TPU v7x, 32 devices: a whole 2x2x4 slice. The times are simulated.
32 devices in a mesh: dp: 4 (over y, x), seq: 4 (over z), col: 2 (over core).
Axes of the slice: x: 2, y: 2, z: 4, core: 2. Of those that a mesh axis runs over, the one named last changes fastest.
Arguments:
- latents: bfloat16 [4, 16, 32, 10240], P('dp', 'seq', None, 'col'), may hold values from -62 to 62
- spatial_kernel: bfloat16 [3, 3, 320, 320], replicated, may hold values from -0.109375 to 0.109375
- temporal_kernel: bfloat16 [3, 320, 320], replicated, may hold values from -0.1875 to 0.1875
- cotangent: bfloat16 [4, 16, 32, 10240], P('dp', 'seq', None, 'col'), may hold values from -6 to 6
Outputs:
- grad_latents: float32 [4, 16, 32, 10240], P('dp', 'seq', None, 'col')
- grad_spatial: float32 [3, 3, 320, 320], replicated
- grad_temporal: float32 [3, 320, 320], replicated
All inputs are finite; a program needn't handle non-finite values.
Results may differ from a plain program's by a relative error of at most 0.0049.
Values may be sent and summed in bfloat16 or wider, within the bound.
No kernel may reach another device: no remote copies, remote signals or barrier semaphores. Data moves between devices by JAX's collectives and lax.ppermute only.
A program may use at most 128 MiB of HBM per device.

v0:
```python
import functools
import math

import jax
import jax.numpy as jnp
from jax import lax
from jax.experimental import pallas as pl
from jax.experimental.pallas import tpu as pltpu
from jax.sharding import PartitionSpec as P

GROUPS = 32
EPSILON = 1e-05
F32 = jnp.float32
BF16 = jnp.bfloat16
VMEM_LIMIT = 56 * 1024 * 1024


def whole(count):
    return [pl.BlockSpec(memory_space=pltpu.VMEM)] * count


def call(body, outs, scratch=(), flops=0, moved=0):
    return pl.pallas_call(
        body,
        out_shape=outs,
        out_specs=jax.tree.map(lambda _: pl.BlockSpec(memory_space=pltpu.VMEM), outs),
        scratch_shapes=list(scratch),
        compiler_params=pltpu.CompilerParams(vmem_limit_bytes=VMEM_LIMIT),
        cost_estimate=pl.CostEstimate(flops=flops, bytes_accessed=moved, transcendentals=0),
    )


def struct(shape, kind):
    return jax.ShapeDtypeStruct(shape, kind)


class Sizes:
    def __init__(self, frames, rows, columns, channels):
        self.frames = frames
        self.rows = rows
        self.columns = columns
        self.channels = channels
        self.pixels = frames * rows
        self.width = columns * channels
        self.pair = 2 * channels
        self.pairs = columns // 2
        self.edge = -(-channels // 128) * 128
        self.slack = self.edge - channels
        self.window = 3 * channels + self.slack
        self.padded = self.width + 2 * self.edge


def group_totals(sums, sizes):
    size = sizes.channels // GROUPS

    def member(shape, lane_dim):
        lane = lax.broadcasted_iota(jnp.int32, shape, lane_dim)
        group = lax.broadcasted_iota(jnp.int32, shape, 1 - lane_dim)
        channel = jnp.where(lane >= sizes.channels, lane - sizes.channels, lane)
        return ((channel >= group * size) & (channel < group * size + size)).astype(F32)

    high = lax.Precision.HIGHEST
    by_group = jnp.dot(sums, member((sizes.pair, 128), 0), precision=high, preferred_element_type=F32)
    return jnp.dot(by_group, member((128, sizes.pair), 1), precision=high, preferred_element_type=F32)


def moments(sums, half, entries, sizes):
    totals = group_totals(sums, sizes) * (1.0 / entries)
    mean = totals[0:half]
    rate = lax.rsqrt(totals[half : 2 * half] - mean * mean + EPSILON)
    return mean, rate


def fold(values):
    return jnp.sum(values.reshape(values.shape[0] // 8, 8, values.shape[1]), axis=0)


def pair_lanes(p, sizes):
    return pl.ds(pl.multiple_of(p * sizes.pair, 128), sizes.pair)


def join(even, odd, sizes):
    cut = sizes.edge - 128
    middle = even[:, cut:] + odd[:, :128]
    return jnp.concatenate([even[:, :cut], middle, odd[:, 128:]], axis=1)


def latent_sums_body(sizes, x_ref, sums_ref, edge_ref):
    def frame(f):
        rows = pl.ds(f * sizes.rows, sizes.rows)

        def step(p, carry):
            plain, square = carry
            v = x_ref[rows, pair_lanes(p, sizes)].astype(F32)
            return plain + fold(v), square + fold(v * v)

        zero = jnp.zeros((8, sizes.pair), F32)
        plain, square = lax.fori_loop(0, sizes.pairs, step, (zero, zero))
        return jnp.sum(plain, axis=0, keepdims=True), jnp.sum(square, axis=0, keepdims=True)

    found = [frame(f) for f in range(sizes.frames)]
    for f, (plain, square) in enumerate(found):
        sums_ref[f : f + 1, :] = plain
        sums_ref[sizes.frames + f : sizes.frames + f + 1, :] = square
    store_edge(sizes, x_ref, edge_ref)


def store_edge(sizes, source, target, at=0):
    left = lax.axis_index("col") == 0
    rows = pl.ds(at, sizes.pixels)

    @pl.when(left)
    def _():
        target[rows, :] = source[:, sizes.width - sizes.edge : sizes.width].astype(target.dtype)

    @pl.when(jnp.logical_not(left))
    def _():
        target[rows, :] = source[:, 0 : sizes.edge].astype(target.dtype)


def row_shifts(values, sizes):
    row = lax.broadcasted_iota(jnp.int32, values.shape, 0)
    down = jnp.where(row == 0, 0.0, pltpu.roll(values, 1, 0))
    up = jnp.where(row == sizes.rows - 1, 0.0, pltpu.roll(values, sizes.rows - 1, 0))
    return down, values, up


def put_shifts(values, frame, lanes, target, sizes):
    rows = pl.ds(frame * sizes.rows, sizes.rows)
    for i, moved in enumerate(row_shifts(values, sizes)):
        target[i, rows, lanes] = moved.astype(BF16)


def put_halo(of_frame, target, sizes):
    left = lax.axis_index("col") == 0
    for f in range(sizes.frames):
        rows = pl.ds(f * sizes.rows, sizes.rows)
        before, after = of_frame(rows, f, True), of_frame(rows, f, False)
        put_shifts(jnp.where(left, 0.0, before), f, pl.ds(0, sizes.edge), target, sizes)
        put_shifts(
            jnp.where(left, after, 0.0), f, pl.ds(sizes.edge + sizes.width, sizes.edge), target, sizes
        )


def windows(padded_ref, p, count, odd, sizes):
    found = []
    for q in range(count):
        start = pl.multiple_of((p + q) * sizes.pair, 128) + (sizes.edge if odd else 0)
        lanes = pl.ds(pl.multiple_of(start, 128), sizes.window)
        found.append(jnp.concatenate([padded_ref[i, :, lanes] for i in range(3)], axis=1))
    return jnp.concatenate(found, axis=0)


def silu_parts(v):
    s = 1.0 / (1.0 + jnp.exp(-v))
    return v * s, s


def forward_body(
    sizes, frame_entries, block, x_ref, sums_ref, other_ref, rim_ref, even_ref, odd_ref,
    hidden_ref, act_ref, clip_ref, padded,
):
    mean, rate = moments(sums_ref[...] + other_ref[...], sizes.frames, frame_entries, sizes)

    def rim(rows, f, before):
        lanes = slice(sizes.pair - sizes.edge, sizes.pair) if before else slice(0, sizes.edge)
        v = rim_ref[rows, :].astype(F32)
        return silu_parts((v - mean[f : f + 1, lanes]) * rate[f : f + 1, lanes])[0]

    put_halo(rim, padded, sizes)

    def activate(p, _):
        for f in range(sizes.frames):
            v = x_ref[pl.ds(f * sizes.rows, sizes.rows), pair_lanes(p, sizes)].astype(F32)
            act = silu_parts((v - mean[f : f + 1]) * rate[f : f + 1])[0]
            lanes = pl.ds(pl.multiple_of(p * sizes.pair + sizes.edge, 128), sizes.pair)
            put_shifts(act, f, lanes, padded, sizes)
        return 0

    lax.fori_loop(0, sizes.pairs, activate, 0)
    act_ref[...] = padded[1]

    def step(b, carry):
        plain, square = carry
        p = b * block
        even = jnp.dot(windows(padded, p, block, False, sizes), even_ref[...], preferred_element_type=F32)
        odd = jnp.dot(windows(padded, p, block, True, sizes), odd_ref[...], preferred_element_type=F32)
        for q in range(block):
            rows = slice(q * sizes.pixels, (q + 1) * sizes.pixels)
            spatial = join(even[rows], odd[rows], sizes)
            lanes = pair_lanes(p + q, sizes)
            hidden = (x_ref[:, lanes].astype(F32) + spatial).astype(BF16)
            hidden_ref[:, lanes] = hidden
            wide = hidden.astype(F32)
            plain = plain + fold(wide)
            square = square + fold(wide * wide)
        return plain, square

    zero = jnp.zeros((8, sizes.pair), F32)
    plain, square = lax.fori_loop(0, sizes.pairs // block, step, (zero, zero))
    put_sums(clip_ref, plain, square)


def put_sums(target, plain, square):
    target[...] = jnp.zeros(target.shape, F32)
    target[0:1, :] = jnp.sum(plain, axis=0, keepdims=True)
    target[1:2, :] = jnp.sum(square, axis=0, keepdims=True)


def frame_taps(cot_ref, before_ref, after_ref, lanes, sizes):
    own = cot_ref[:, lanes]
    later = jnp.concatenate([own[sizes.rows :], after_ref[:, lanes]], axis=0)
    earlier = jnp.concatenate([before_ref[:, lanes], own[: sizes.pixels - sizes.rows]], axis=0)
    return later, own, earlier


def temporal_body(
    sizes, clip_entries, block, hidden_ref, cot_ref, before_ref, after_ref, clip_ref, even_ref, odd_ref,
    act_ref, grad_ref, sums_ref, rim_ref, normed,
):
    mean, rate = moments(clip_ref[...], 1, clip_entries, sizes)

    def step(b, carry):
        plain, cross = carry
        p = b * block
        found = []
        for odd, weights in ((False, even_ref), (True, odd_ref)):
            rows = []
            for q in range(block):
                start = (p + q) * sizes.pair + (sizes.pair - sizes.edge if odd else 0)
                lanes = pl.ds(pl.multiple_of(start, 128), sizes.edge)
                rows.append(
                    jnp.concatenate(frame_taps(cot_ref, before_ref, after_ref, lanes, sizes), axis=1)
                )
            found.append(
                lax.dot_general(
                    jnp.concatenate(rows, axis=0), weights[...], (((1,), (1,)), ((), ())),
                    preferred_element_type=F32,
                )
            )
        for q in range(block):
            rows = slice(q * sizes.pixels, (q + 1) * sizes.pixels)
            dact = join(found[0][rows], found[1][rows], sizes)
            lanes = pair_lanes(p + q, sizes)
            tnormed = (hidden_ref[:, lanes].astype(F32) - mean) * rate
            act, s = silu_parts(tnormed)
            act_ref[:, lanes] = act.astype(BF16)
            normed[:, lanes] = tnormed
            grad = dact * (s * (1.0 + tnormed * (1.0 - s)))
            grad_ref[:, lanes] = grad
            plain = plain + fold(grad)
            cross = cross + fold(grad * tnormed)
        return plain, cross

    zero = jnp.zeros((8, sizes.pair), F32)
    plain, cross = lax.fori_loop(0, sizes.pairs // block, step, (zero, zero))
    put_sums(sums_ref, plain, cross)
    for k, source in enumerate((grad_ref, normed, cot_ref)):
        store_edge(sizes, source, rim_ref, k * sizes.pixels)


def temporal_grad_body(sizes, act_ref, cot_ref, before_ref, after_ref, out_ref, total):
    total[...] = jnp.zeros(total.shape, F32)
    channels = sizes.channels
    zeros = jnp.zeros((sizes.pixels, sizes.slack), BF16)

    def step(p, _):
        lanes = pair_lanes(p, sizes)
        act = act_ref[:, lanes]
        act = jnp.concatenate([act[:, :channels], act[:, channels:]], axis=0)
        taps = frame_taps(cot_ref, before_ref, after_ref, lanes, sizes)
        even = jnp.concatenate([jnp.concatenate([t[:, :channels], zeros], axis=1) for t in taps], axis=1)
        odd = jnp.concatenate([jnp.concatenate([t[:, channels:], zeros], axis=1) for t in taps], axis=1)
        total[...] += lax.dot_general(
            act, jnp.concatenate([even, odd], axis=0), (((0,), (0,)), ((), ())),
            preferred_element_type=F32,
        )
        return 0

    lax.fori_loop(0, sizes.pairs, step, 0)
    for i in range(3):
        out_ref[i] = total[:, i * sizes.edge : i * sizes.edge + channels]


def spatial_grad_body(
    sizes, clip_entries, hidden_ref, cot_ref, grad_ref, clip_ref, mean_ref, rim_ref, act_ref,
    dtemp_ref, dspat_ref, out_ref, padded, total,
):
    mean, rate = moments(clip_ref[...], 1, clip_entries, sizes)
    means = group_totals(mean_ref[...], sizes) * (1.0 / clip_entries)
    plain, cross = means[0:1], means[1:2]

    def rim(rows, f, before):
        lanes = slice(sizes.pair - sizes.edge, sizes.pair) if before else slice(0, sizes.edge)
        at = [pl.ds(k * sizes.pixels + f * sizes.rows, sizes.rows) for k in range(3)]
        grad, tnormed, cot = (rim_ref[r, :] for r in at)
        dtemp = rate[:, lanes] * (grad - plain[:, lanes] - tnormed * cross[:, lanes])
        return (cot + dtemp.astype(BF16).astype(F32)).astype(BF16).astype(F32)

    put_halo(rim, padded, sizes)

    def combine(p, _):
        lanes = pair_lanes(p, sizes)
        for f in range(sizes.frames):
            rows = pl.ds(f * sizes.rows, sizes.rows)
            tnormed = (hidden_ref[rows, lanes].astype(F32) - mean) * rate
            dtemp = (rate * (grad_ref[rows, lanes] - plain - tnormed * cross)).astype(BF16)
            dtemp_ref[rows, lanes] = dtemp
            dspat = cot_ref[rows, lanes].astype(F32) + dtemp.astype(F32)
            put_shifts(
                dspat, f, pl.ds(pl.multiple_of(p * sizes.pair + sizes.edge, 128), sizes.pair), padded, sizes
            )
        return 0

    lax.fori_loop(0, sizes.pairs, combine, 0)
    dspat_ref[...] = padded[1]

    channels = sizes.channels
    zeros = jnp.zeros((sizes.pixels, sizes.slack), BF16)
    total[...] = jnp.zeros(total.shape, F32)

    def step(b, _):
        for odd in (False, True):
            left, right = [], []
            for q in range(2):
                p = 2 * b + q
                start = p * sizes.pair + (sizes.edge if odd else 0)
                left.append(act_ref[:, pl.ds(pl.multiple_of(start, 128), sizes.window)])
                both = pl.ds(pl.multiple_of(p * sizes.pair + sizes.edge, 128), sizes.pair)
                taps = []
                for i in range(3):
                    d = padded[2 - i, :, both]
                    d = d[:, channels:] if odd else d[:, :channels]
                    taps.append(jnp.concatenate([d, zeros], axis=1))
                right.append(jnp.concatenate(taps, axis=1))
            part = lax.dot_general(
                jnp.concatenate(left, axis=0), jnp.concatenate(right, axis=0), (((0,), (0,)), ((), ())),
                preferred_element_type=F32,
            )
            total[...] += part[: 3 * channels] if odd else part[sizes.slack :]
        return 0

    lax.fori_loop(0, sizes.pairs // 2, step, 0)
    for i in range(3):
        out_ref[i] = total[:, i * sizes.edge : i * sizes.edge + channels]


def backward_body(
    sizes, frame_entries, block, x_ref, sums_ref, other_ref, dspat_ref, even_ref, odd_ref,
    grad_ref, out_ref, padded, plains,
):
    mean, rate = moments(sums_ref[...] + other_ref[...], sizes.frames, frame_entries, sizes)

    def spread(k, _):
        lanes = pl.ds(pl.multiple_of(k * 128, 128), 128)
        for f in range(sizes.frames):
            rows = pl.ds(f * sizes.rows, sizes.rows)
            put_shifts(dspat_ref[rows, lanes].astype(F32), f, lanes, padded, sizes)
        return 0

    lax.fori_loop(0, sizes.padded // 128, spread, 0)
    plains[...] = jnp.zeros(plains.shape, F32)
    contract = (((1,), (1,)), ((), ()))

    def step(b, _):
        p = b * block
        even = lax.dot_general(
            windows(padded, p, block, False, sizes), even_ref[...], contract, preferred_element_type=F32
        )
        odd = lax.dot_general(
            windows(padded, p, block, True, sizes), odd_ref[...], contract, preferred_element_type=F32
        )
        for q in range(block):
            base = q * sizes.pixels
            for f in range(sizes.frames):
                at = slice(base + f * sizes.rows, base + (f + 1) * sizes.rows)
                dact = join(even[at], odd[at], sizes)
                rows, lanes = pl.ds(f * sizes.rows, sizes.rows), pair_lanes(p + q, sizes)
                normed = (x_ref[rows, lanes].astype(F32) - mean[f : f + 1]) * rate[f : f + 1]
                _, s = silu_parts(normed)
                grad = dact * (s * (1.0 + normed * (1.0 - s)))
                grad_ref[rows, lanes] = grad
                plains[f] += fold(grad)
                plains[sizes.frames + f] += fold(grad * normed)
        return 0

    lax.fori_loop(0, sizes.pairs // block, step, 0)
    for k in range(2 * sizes.frames):
        out_ref[k : k + 1, :] = jnp.sum(plains[k], axis=0, keepdims=True)


def finish_body(
    sizes, frame_entries, x_ref, sums_ref, other_ref, cot_ref, dtemp_ref, grad_ref, mine_ref, theirs_ref, out_ref
):
    mean, rate = moments(sums_ref[...] + other_ref[...], sizes.frames, frame_entries, sizes)
    means = group_totals(mine_ref[...] + theirs_ref[...], sizes) * (1.0 / frame_entries)

    def step(p, _):
        lanes = pair_lanes(p, sizes)
        for f in range(sizes.frames):
            rows = pl.ds(f * sizes.rows, sizes.rows)
            normed = (x_ref[rows, lanes].astype(F32) - mean[f : f + 1]) * rate[f : f + 1]
            dhidden = cot_ref[rows, lanes].astype(F32) + dtemp_ref[rows, lanes].astype(F32)
            plain, cross = means[f : f + 1], means[sizes.frames + f : sizes.frames + f + 1]
            out_ref[rows, lanes] = dhidden + rate[f : f + 1] * (grad_ref[rows, lanes] - plain - normed * cross)
        return 0

    lax.fori_loop(0, sizes.pairs, step, 0)


def swap(values, axis, bit):
    count = lax.axis_size(axis)
    return lax.ppermute(values, axis, [(i, i ^ bit) for i in range(count)])


def sum_over(values, axes):
    for axis in axes:
        bit = 1
        while bit < lax.axis_size(axis):
            values = values + swap(values, axis, bit)
            bit *= 2
    return values


def shards(latents, spatial_kernel, temporal_kernel, cotangent):
    _, frames, rows, width = latents.shape
    channels = spatial_kernel.shape[2]
    sizes = Sizes(frames, rows, width // channels, channels)
    cols, seqs = lax.axis_size("col"), lax.axis_size("seq")
    frame_entries = float(rows * sizes.columns * cols * (channels // GROUPS))
    clip_entries = frame_entries * frames * seqs
    pixels = lax.axis_size("dp") * seqs * cols * sizes.pixels * sizes.columns
    grad_scale = 1.0 / math.sqrt(pixels)

    x = latents.reshape(sizes.pixels, width)
    cot = cotangent.reshape(sizes.pixels, width)
    sum_shape = struct((8, sizes.pair), F32)
    frame_shape = struct((2 * frames, sizes.pair), F32)
    padded_scratch = pltpu.VMEM((3, sizes.pixels, sizes.padded), BF16)
    slack = sizes.slack

    flat = spatial_kernel.reshape(3, 3 * channels, channels)
    fwd_even = jnp.pad(flat, ((0, 0), (slack, 0), (0, slack))).reshape(3 * sizes.window, sizes.edge)
    fwd_odd = jnp.pad(flat, ((0, 0), (0, slack), (slack, 0))).reshape(3 * sizes.window, sizes.edge)
    back = jnp.flip(spatial_kernel, (0, 1)).transpose(2, 0, 1, 3).reshape(channels, 3, 3 * channels)
    bwd_even = jnp.pad(back, ((0, slack), (0, 0), (slack, 0))).reshape(sizes.edge, 3 * sizes.window)
    bwd_odd = jnp.pad(back, ((slack, 0), (0, 0), (0, slack))).reshape(sizes.edge, 3 * sizes.window)
    times = temporal_kernel.transpose(1, 0, 2)
    time_even = jnp.pad(times, ((0, slack), (0, 0), (0, slack))).reshape(sizes.edge, 3 * sizes.edge)
    time_odd = jnp.pad(times, ((slack, 0), (0, 0), (slack, 0))).reshape(sizes.edge, 3 * sizes.edge)

    forth = [(i, i + 1) for i in range(seqs - 1)]
    before = lax.ppermute(cot[sizes.pixels - rows :], "seq", forth)
    after = lax.ppermute(cot[:rows], "seq", [(j, i) for i, j in forth])

    sums, edge = call(
        functools.partial(latent_sums_body, sizes),
        [frame_shape, struct((sizes.pixels, sizes.edge), BF16)],
    )(x)
    other = swap(sums, "col", 1)
    rim = swap(edge, "col", 1)
    hidden, act, clip = call(
        functools.partial(forward_body, sizes, frame_entries, min(4, sizes.pairs)),
        [struct((sizes.pixels, width), BF16), struct((sizes.pixels, sizes.padded), BF16), sum_shape],
        [padded_scratch],
    )(x, sums, other, rim, fwd_even, fwd_odd)
    clip = sum_over(clip, ("col", "seq"))
    tact, tgrad, means, pack = call(
        functools.partial(temporal_body, sizes, clip_entries, min(4, sizes.pairs)),
        [
            struct((sizes.pixels, width), BF16),
            struct((sizes.pixels, width), F32),
            sum_shape,
            struct((3 * sizes.pixels, sizes.edge), F32),
        ],
        [pltpu.VMEM((sizes.pixels, width), F32)],
    )(hidden, cot, before, after, clip, time_even, time_odd)
    means = sum_over(means, ("col", "seq"))
    pack = swap(pack, "col", 1)
    temporal_grad = call(
        functools.partial(temporal_grad_body, sizes),
        struct((3, channels, channels), F32),
        [pltpu.VMEM((channels, 3 * sizes.edge), F32)],
    )(tact, cot, before, after)
    dtemp, dspat, spatial_grad = call(
        functools.partial(spatial_grad_body, sizes, clip_entries),
        [
            struct((sizes.pixels, width), BF16),
            struct((sizes.pixels, sizes.padded), BF16),
            struct((3, 3 * channels, channels), F32),
        ],
        [padded_scratch, pltpu.VMEM((3 * channels, 3 * sizes.edge), F32)],
    )(hidden, cot, tgrad, clip, means, pack, act)
    dnormed, mine = call(
        functools.partial(backward_body, sizes, frame_entries, min(4, sizes.pairs)),
        [struct((sizes.pixels, width), F32), frame_shape],
        [padded_scratch, pltpu.VMEM((2 * frames, 8, sizes.pair), F32)],
    )(x, sums, other, dspat, bwd_even, bwd_odd)
    theirs = swap(mine, "col", 1)
    grad_latents = call(
        functools.partial(finish_body, sizes, frame_entries), struct((sizes.pixels, width), F32)
    )(x, sums, other, cot, dtemp, dnormed, mine, theirs)

    spatial_grad, temporal_grad = lax.psum((spatial_grad, temporal_grad), ("dp", "seq", "col"))
    spatial_grad = spatial_grad.reshape(spatial_kernel.shape)
    return (grad_latents.reshape(latents.shape), spatial_grad * grad_scale, temporal_grad * grad_scale)


def solution(mesh):
    in_specs = (P("dp", "seq", None, "col"), P(), P(), P("dp", "seq", None, "col"))
    out_specs = (P("dp", "seq", None, "col"), P(), P())
    return jax.shard_map(shards, mesh=mesh, in_specs=in_specs, out_specs=out_specs, check_vma=False)
```

profile of v0, /device:TPU:0, one launch (start us, length us, event | category | flops | bytes accessed | tf_op | source)
XLA Modules:
  0.0 262.3 jit_solution(10939091594735015436)
XLA Ops:
  7.2 0.0 copy-start
  7.2 0.0 all-reduce.9.cloned.1.call-start
  7.2 2.7 %shard_map.67 = (f32[8,640]{1,0:T(8,128)}, bf16[128,384]{1,0:T(8,128)(2,1)}) custom-call(bf16[128,5120]{1,0:T(8,128)(2,1)} %bitcast.23), custom_call_target="tpu_custom_call" | custom-call | tf_op jit(solution)/shard_map/pallas_call | solution.py:456
  9.9 0.5 collective-permute-start
  10.4 0.1 collective-permute-start.1
  10.5 2.0 slice_bitcast_fusion
  12.4 4.9 %collective-permute-start.2 = (bf16[32,5120]{1,0:T(8,128)(2,1)}, bf16[32,5120]{1,0:T(8,128)(2,1)S(1)}, u32[]{:S(2)}, u32[]{:S(2)}) collective-permute-start(bf16[32,5120]{1,0:T(8,128)(2,1)} %get-tuple-element.38), channel_id=1, source_target_pairs={{0,2},{2,4},{4,6},{1,3},{3,5},{5,7},{8,10},{10,12},{12,14},{9,11},... | collective-permute-start | bytes 983048 | tf_op jit(solution)/shard_map/ppermute | solution.py:453
  17.4 1.3 collective-permute-start.3
  18.7 0.0 copy-done
  18.7 3.5 %fusion.1 = (bf16[3,1024,384]{2,1,0:T(8,128)(2,1)}, bf16[3,1024,384]{2,1,0:T(8,128)(2,1)}) fusion(bf16[3,960,320]{2,1,0:T(8,128)(2,1)S(1)} %bitcast.31), kind=kLoop, calls=%fused_computation.6 | loop fusion | bytes 6561792 | tf_op jit(solution)/shard_map/jit(_pad)/pad | solution.py:444
  22.2 0.0 collective-permute-done.other_ref
  22.2 0.0 copy-start.5
  22.2 0.0 collective-permute-done.1.rim_ref
  22.2 0.0 copy-start.6
  22.2 0.6 copy-done.5
  22.8 0.1 copy-done.6
  22.8 0.0 copy-start.3
  22.8 13.4 %shard_map.68 = (bf16[128,5120]{1,0:T(8,128)(2,1)}, bf16[128,5888]{1,0:T(8,128)(2,1)}, f32[8,640]{1,0:T(8,128)}) custom-call(bf16[128,5120]{1,0:T(8,128)(2,1)} %bitcast.24, f32[8,640]{1,0:T(8,128)} %get-tuple-element.17.sums_ref, f32[8,640]{1,0:T(8,128)} %copy-done.5, bf16[128,384]{1,0:T(8,128)(2,1)} %copy-done.6, bf16[3072,384]{1,0:T(8,128)(2,1)} %bitcast.28, ...), custom_call_target="tpu_custom_call" | custom-call | tf_op jit(solution)/shard_map/pallas_call | solution.py:462
  36.2 0.0 collective-permute-start.4
  36.2 1.4 collective-permute-done.4
  37.6 0.7 add.34
  38.4 2.6 %collective-permute-start.5 = (f32[8,640]{1,0:T(8,128)S(1)}, f32[8,640]{1,0:T(8,128)S(1)}, u32[]{:S(2)}, u32[]{:S(2)}) collective-permute-start(f32[8,640]{1,0:T(8,128)S(1)} %add.34), channel_id=1, source_target_pairs={{0,2},{2,0},{4,6},{6,4},{1,3},{3,1},{5,7},{7,5},{8,10},{10,8},{12,... | collective-permute-start | bytes 61448 | tf_op jit(solution)/shard_map/ppermute | solution.py:413
  41.0 0.0 copy-done.3
  41.0 1.2 copy.9
  42.2 0.6 collective-permute-done.5
  42.8 3.3 %collective-permute-start.6 = (f32[8,640]{1,0:T(8,128)S(1)}, f32[8,640]{1,0:T(8,128)S(1)}, u32[]{:S(2)}, u32[]{:S(2)}) collective-permute-start(f32[8,640]{1,0:T(8,128)S(1)} %add.35), channel_id=1, source_target_pairs={{0,4},{2,6},{4,0},{6,2},{1,5},{3,7},{5,1},{7,3},{8,12},{10,14},{12... | collective-permute-start | bytes 61448 | tf_op jit(solution)/shard_map/ppermute | solution.py:413
  46.1 2.7 %fusion.2 = (bf16[384,3,384]{0,2,1:T(8,128)(2,1)S(1)}, bf16[384,3,384]{0,2,1:T(8,128)(2,1)}) fusion(bf16[320,3,320]{0,2,1:T(8,128)(2,1)} %bitcast.36), kind=kLoop, calls=%fused_computation.7 | loop fusion | bytes 2383872 | tf_op jit(solution)/shard_map/jit(_pad)/pad | solution.py:450
  48.8 2.3 copy.10.even_ref
  51.0 1.5 copy.11.odd_ref
  52.5 0.0 collective-permute-done.6
  52.5 0.6 add.36.clip_ref
  53.1 0.0 collective-permute-done.2.before_ref
  53.1 0.0 copy-start.2
  53.1 0.0 collective-permute-done.3.after_ref
  53.1 0.7 copy-done.2
  53.9 9.4 %shard_map.69 = (bf16[128,5120]{1,0:T(8,128)(2,1)}, f32[128,5120]{1,0:T(8,128)}, f32[8,640]{1,0:T(8,128)}, f32[384,384]{1,0:T(8,128)}) custom-call(bf16[128,5120]{1,0:T(8,128)(2,1)} %get-tuple-element.19.hidden_ref, bf16[128,5120]{1,0:T(8,128)(2,1)} %bitcast.19, bf16[32,5120]{1,0:T(8,128)(2,1)} %copy-done.2, ...), custom_call_target="tpu_custom_call" | custom-call | tf_op jit(solution)/shard_map/pallas_call | solution.py:468
  63.3 0.0 collective-permute-start.10
  63.3 0.5 collective-permute-start.7
  63.8 1.7 collective-permute-done.7
  65.5 0.7 add.37
  66.3 2.0 collective-permute-start.8
  68.3 1.8 collective-permute-done.8
  70.1 0.0 collective-permute-start.9
  70.1 7.1 %shard_map.73 = f32[3,320,320]{2,1,0:T(8,128)} custom-call(bf16[128,5120]{1,0:T(8,128)(2,1)} %get-tuple-element.30.act_ref, bf16[128,5120]{1,0:T(8,128)(2,1)} %bitcast.20, bf16[32,5120]{1,0:T(8,128)(2,1)} %copy-done.2, bf16[32,5120]{1,0:T(8,128)(2,1)} %collective-permute-done.3.after_ref), custom_call_target="tpu_custom_call" | custom-call | tf_op jit(solution)/shard_map/pallas_call | solution.py:480
  77.2 0.0 collective-permute-done.9
  77.2 0.6 add.39.mean_ref
  77.8 0.0 collective-permute-done.10.rim_ref
  77.8 0.8 copy-done.4
  78.6 15.1 %shard_map.70 = (bf16[128,5120]{1,0:T(8,128)(2,1)}, bf16[128,5888]{1,0:T(8,128)(2,1)}, f32[3,960,320]{2,1,0:T(8,128)}) custom-call(bf16[128,5120]{1,0:T(8,128)(2,1)} %get-tuple-element.19.hidden_ref, bf16[128,5120]{1,0:T(8,128)(2,1)} %bitcast.21, f32[128,5120]{1,0:T(8,128)} %get-tuple-element.21.grad_ref, f32[8,640]{1,0:T(8,128)} %add.36.clip_ref, ...), custom_call_target="tpu_custom_call" | custom-call | tf_op jit(solution)/shard_map/pallas_call | solution.py:485
  93.7 0.0 all-reduce.9.cloned.1.call-update
  93.7 1.6 reverse_bitcast_fusion
  95.3 4.2 %copy.12 = bf16[320,3,3,320]{0,3,2,1:T(8,128)(2,1)} copy(bf16[320,3,3,320]{3,0,2,1:T(8,128)(2,1)} %reverse_bitcast_fusion) | data formatting | bytes 3686400 | tf_op jit(solution)/shard_map/transpose | solution.py:445
  99.5 5.5 %fusion = (bf16[384,3,1024]{0,2,1:T(8,128)(2,1)S(1)}, bf16[384,3,1024]{0,2,1:T(8,128)(2,1)}) fusion(bf16[320,3,960]{0,2,1:T(8,128)(2,1)} %bitcast.32), kind=kLoop, calls=%fused_computation.5 | loop fusion | bytes 6561792 | tf_op jit(solution)/shard_map/jit(_pad)/pad | solution.py:447
  105.0 4.3 %copy.13.even_ref = bf16[384,3072]{1,0:T(8,128)(2,1)} copy(bf16[384,3072]{0,1:T(8,128)(2,1)} %bitcast.30) | data formatting | bytes 4718592 | tf_op jit(solution)/shard_map/reshape | solution.py:446
  109.3 2.6 copy.14.odd_ref
  111.9 14.1 %shard_map.71 = (f32[128,5120]{1,0:T(8,128)}, f32[8,640]{1,0:T(8,128)}) custom-call(bf16[128,5120]{1,0:T(8,128)(2,1)} %bitcast.25, f32[8,640]{1,0:T(8,128)} %get-tuple-element.17.sums_ref, f32[8,640]{1,0:T(8,128)} %copy-done.5, bf16[128,5888]{1,0:T(8,128)(2,1)} %get-tuple-element.26.dspat_ref, bf16[384,3072]{1,0:T(8,128)(2,1)} %copy.13.even_ref, ...), custom_call_target="tpu_custom_call" | custom-call | tf_op jit(solution)/shard_map/pallas_call | solution.py:494
  126.0 0.0 collective-permute-start.11
  126.0 1.4 collective-permute-done.11.theirs_ref
  127.4 0.6 copy-done.7
  128.0 6.9 %shard_map.72 = f32[128,5120]{1,0:T(8,128)} custom-call(bf16[128,5120]{1,0:T(8,128)(2,1)} %bitcast.26, f32[8,640]{1,0:T(8,128)} %get-tuple-element.17.sums_ref, f32[8,640]{1,0:T(8,128)} %copy-done.5, bf16[128,5120]{1,0:T(8,128)(2,1)} %bitcast.22, bf16[128,5120]{1,0:T(8,128)(2,1)} %get-tuple-element.25.dtemp_ref, f32[128,5120]{1,0:T(8,128)} %get-tuple-element.27.grad_ref, ...), custom_call_target="tpu_custom_call" | custom-call | tf_op jit(solution)/shard_map/pallas_call | solution.py:500
  134.9 114.6 %all-reduce.9.cloned.1.call-done = (f32[3,960,320]{2,1,0:T(8,128)}, f32[3,320,320]{2,1,0:T(8,128)}) async-done(((f32[3,960,320]{2,1,0:T(8,128)}, f32[3,320,320]{2,1,0:T(8,128)}), (f32[3,960,320]{2,1,0:T(8,128)}, f32[3,320,320]{2,1,0:T(8,128)})) %all-reduce.9.cloned.1.call-update) | async-done | bytes 4915216 | tf_op jit(solution)/shard_map/psum | solution.py:504
  249.5 4.7 %broadcast_multiply_fusion = f32[3,960,320]{2,1,0:T(8,128)} fusion(f32[3,960,320]{2,1,0:T(8,128)} %get-tuple-element.31), kind=kLoop, calls=%fused_computation | loop fusion | flops 921600 | bytes 7372800 | tf_op jit(solution)/shard_map/mul | solution.py:506
  254.2 0.0 copy-done.1
  254.2 1.2 broadcast_multiply_fusion.1
  (5 shorter events, 0.0 us)
Async XLA Ops:
  7.2 11.5 %copy-start = (bf16[3,3,320,320]{3,2,1,0:T(8,128)(2,1)S(1)}, bf16[3,3,320,320]{3,2,1,0:T(8,128)(2,1)}, u32[]{:S(2)}) copy-start(bf16[3,3,320,320]{3,2,1,0:T(8,128)(2,1)} %param.5) | copy-start | bytes 5529604
  7.2 242.3 %all-reduce.9.cloned.1.call-start = ((), (), s32[]{:S(2)}) async-start(), calls=%async_computation | async-start | bytes 11796480 | tf_op jit(solution)/shard_map/psum | solution.py:504
  9.9 12.2 %collective-permute-start = (f32[8,640]{1,0:T(8,128)}, f32[8,640]{1,0:T(8,128)S(1)}, u32[]{:S(2)}, u32[]{:S(2)}) collective-permute-start(f32[8,640]{1,0:T(8,128)} %get-tuple-element.17.sums_ref), channel_id=1, source_target_pairs={{0,1},{1,0},{2,3},{3,2},{4,5},{5,4},{6,7},{7,6},{8,9},{9,8},{10,11... | collective-permute-start | bytes 61448 | tf_op jit(solution)/shard_map/ppermute | solution.py:413
  10.4 11.8 %collective-permute-start.1 = (bf16[128,384]{1,0:T(8,128)(2,1)}, bf16[128,384]{1,0:T(8,128)(2,1)S(1)}, u32[]{:S(2)}, u32[]{:S(2)}) collective-permute-start(bf16[128,384]{1,0:T(8,128)(2,1)} %get-tuple-element.18), channel_id=1, source_target_pairs={{0,1},{1,0},{2,3},{3,2},{4,5},{5,4},{6,7},{7,6},{8,9},{9,8},{10,11... | collective-permute-start | bytes 294920 | tf_op jit(solution)/shard_map/ppermute | solution.py:413
  12.4 40.7 %collective-permute-start.2 = (bf16[32,5120]{1,0:T(8,128)(2,1)}, bf16[32,5120]{1,0:T(8,128)(2,1)S(1)}, u32[]{:S(2)}, u32[]{:S(2)}) collective-permute-start(bf16[32,5120]{1,0:T(8,128)(2,1)} %get-tuple-element.38), channel_id=1, source_target_pairs={{0,2},{2,4},{4,6},{1,3},{3,5},{5,7},{8,10},{10,12},{12,14},{9,11},... | collective-permute-start | bytes 983048 | tf_op jit(solution)/shard_map/ppermute | solution.py:453
  17.4 35.8 %collective-permute-start.3 = (bf16[32,5120]{1,0:T(8,128)(2,1)}, bf16[32,5120]{1,0:T(8,128)(2,1)}, u32[]{:S(2)}, u32[]{:S(2)}) collective-permute-start(bf16[32,5120]{1,0:T(8,128)(2,1)} %get-tuple-element.37), channel_id=1, source_target_pairs={{2,0},{4,2},{6,4},{3,1},{5,3},{7,5},{10,8},{12,10},{14,12},{11,9},... | collective-permute-start | bytes 983048 | tf_op jit(solution)/shard_map/ppermute | solution.py:454
  22.2 0.6 copy-start.5
  22.2 0.6 copy-start.6
  22.8 18.2 %copy-start.3 = (bf16[3,320,320]{2,1,0:T(8,128)(2,1)S(1)}, bf16[3,320,320]{2,1,0:T(8,128)(2,1)}, u32[]{:S(2)}) copy-start(bf16[3,320,320]{2,1,0:T(8,128)(2,1)} %param.6) | copy-start | bytes 1843204
  36.2 1.4 collective-permute-start.4
  38.4 4.4 %collective-permute-start.5 = (f32[8,640]{1,0:T(8,128)S(1)}, f32[8,640]{1,0:T(8,128)S(1)}, u32[]{:S(2)}, u32[]{:S(2)}) collective-permute-start(f32[8,640]{1,0:T(8,128)S(1)} %add.34), channel_id=1, source_target_pairs={{0,2},{2,0},{4,6},{6,4},{1,3},{3,1},{5,7},{7,5},{8,10},{10,8},{12,... | collective-permute-start | bytes 61448 | tf_op jit(solution)/shard_map/ppermute | solution.py:413
  42.8 9.7 %collective-permute-start.6 = (f32[8,640]{1,0:T(8,128)S(1)}, f32[8,640]{1,0:T(8,128)S(1)}, u32[]{:S(2)}, u32[]{:S(2)}) collective-permute-start(f32[8,640]{1,0:T(8,128)S(1)} %add.35), channel_id=1, source_target_pairs={{0,4},{2,6},{4,0},{6,2},{1,5},{3,7},{5,1},{7,3},{8,12},{10,14},{12... | collective-permute-start | bytes 61448 | tf_op jit(solution)/shard_map/ppermute | solution.py:413
  53.1 0.7 copy-start.2
  63.3 14.5 %collective-permute-start.10 = (f32[384,384]{1,0:T(8,128)}, f32[384,384]{1,0:T(8,128)S(1)}, u32[]{:S(2)}, u32[]{:S(2)}) collective-permute-start(f32[384,384]{1,0:T(8,128)} %get-tuple-element.23), channel_id=1, source_target_pairs={{0,1},{1,0},{2,3},{3,2},{4,5},{5,4},{6,7},{7,6},{8,9},{9,8},{10,11... | collective-permute-start | bytes 1769480 | tf_op jit(solution)/shard_map/ppermute | solution.py:413
  63.3 2.2 collective-permute-start.7
  66.3 3.8 %collective-permute-start.8 = (f32[8,640]{1,0:T(8,128)S(1)}, f32[8,640]{1,0:T(8,128)S(1)}, u32[]{:S(2)}, u32[]{:S(2)}) collective-permute-start(f32[8,640]{1,0:T(8,128)S(1)} %add.37), channel_id=1, source_target_pairs={{0,2},{2,0},{4,6},{6,4},{1,3},{3,1},{5,7},{7,5},{8,10},{10,8},{12,... | collective-permute-start | bytes 61448 | tf_op jit(solution)/shard_map/ppermute | solution.py:413
  70.1 7.1 %collective-permute-start.9 = (f32[8,640]{1,0:T(8,128)S(1)}, f32[8,640]{1,0:T(8,128)S(1)}, u32[]{:S(2)}, u32[]{:S(2)}) collective-permute-start(f32[8,640]{1,0:T(8,128)S(1)} %add.38), channel_id=1, source_target_pairs={{0,4},{2,6},{4,0},{6,2},{1,5},{3,7},{5,1},{7,3},{8,12},{10,14},{12... | collective-permute-start | bytes 61448 | tf_op jit(solution)/shard_map/ppermute | solution.py:413
  77.8 0.8 copy-start.4
  126.0 1.4 collective-permute-start.11
  127.4 0.6 copy-start.7
  249.5 4.7 %copy-start.1 = (f32[3,320,320]{2,1,0:T(8,128)S(1)}, f32[3,320,320]{2,1,0:T(8,128)}, u32[]{:S(2)}) copy-start(f32[3,320,320]{2,1,0:T(8,128)} %get-tuple-element.32) | copy-start | bytes 3686404
Sparse Core Ops, SparseCore 0:
  93.8 155.6 all-reduce.8
where the time goes:
time: 263 us; the launch traced here: 262 us
  waiting for transfers between devices  121 us (46%)
  Pallas kernels  68.8 us (26%)
  local copies, waits for them, and re-layouts  34 us (13%)
  starting transfers between devices  15.3 us (6%)
  between operations  14.1 us (5%)
  other arithmetic  8.63 us (3%)
    psum x1, waiting for transfers between devices, shards(): lax.psum((spatial_grad, temporal_grad), ('dp', 'seq', 'col'))  115 us
    pallas_call x1, Pallas kernels, shards(): call(functools.partial(spatial_grad_body, sizes, clip_entries), [struct((...  15.1 us
    pallas_call x1, Pallas kernels, shards(): call(functools.partial(backward_body, sizes, frame_entries, min(4, sizes....  14.1 us
    pallas_call x1, Pallas kernels, shards(): call(functools.partial(forward_body, sizes, frame_entries, min(4, sizes.p...  13.4 us
    pallas_call x1, Pallas kernels, shards(): call(functools.partial(temporal_body, sizes, clip_entries, min(4, sizes.p...  9.44 us
    ppermute x10, starting transfers between devices, swap(): return lax.ppermute(values, axis, [(i, i ^ bit) for i in range(count)])  9 us
    pallas_call x1, Pallas kernels, shards(): call(functools.partial(temporal_grad_body, sizes), struct((3, channels, c...  7.12 us
    pallas_call x1, Pallas kernels, shards(): call(functools.partial(finish_body, sizes, frame_entries), struct((sizes....  6.91 us
  transfers between devices with their start and end apart: 13, of which 6 were waited for; matrix products, arithmetic and copies ran while one was open for 13% of the time, Pallas kernels for 16%

commit v1 on v0

--- a/solution.py
+++ b/solution.py
@@ -13,6 +13,7 @@
 F32 = jnp.float32
 BF16 = jnp.bfloat16
 VMEM_LIMIT = 56 * 1024 * 1024
+CONV_COST = 12_000_000_000
 
 
 def whole(count):
@@ -142,6 +143,42 @@
         )
 
 
+def forward_weights(kernel_ref, even_ref, odd_ref, sizes):
+    channels, slack, window = sizes.channels, sizes.slack, sizes.window
+    for weights in (even_ref, odd_ref):
+        weights[...] = jnp.zeros(weights.shape, BF16)
+    for i in range(3):
+        for j in range(3):
+            taps = kernel_ref[i, j]
+            zeros = jnp.zeros((channels, slack), BF16)
+            at = i * window + j * channels
+            even_ref[at + slack : at + slack + channels, :] = jnp.concatenate([taps, zeros], axis=1)
+            odd_ref[at : at + channels, :] = jnp.concatenate([zeros, taps], axis=1)
+
+
+def backward_weights(kernel_ref, even_ref, odd_ref, sizes):
+    channels, slack, window = sizes.channels, sizes.slack, sizes.window
+    for weights in (even_ref, odd_ref):
+        weights[...] = jnp.zeros(weights.shape, BF16)
+    zeros = jnp.zeros((channels, slack), BF16)
+    for i in range(3):
+        taps = [kernel_ref[2 - i, 2 - j] for j in range(3)]
+        lanes = slice(i * window, (i + 1) * window)
+        even_ref[0:channels, lanes] = jnp.concatenate([zeros] + taps, axis=1)
+        odd_ref[slack : slack + channels, lanes] = jnp.concatenate(taps + [zeros], axis=1)
+
+
+def temporal_weights(kernel_ref, even_ref, odd_ref, sizes):
+    channels, slack, edge = sizes.channels, sizes.slack, sizes.edge
+    for weights in (even_ref, odd_ref):
+        weights[...] = jnp.zeros(weights.shape, BF16)
+    zeros = jnp.zeros((channels, slack), BF16)
+    for i in range(3):
+        lanes = slice(i * edge, (i + 1) * edge)
+        even_ref[0:channels, lanes] = jnp.concatenate([kernel_ref[i], zeros], axis=1)
+        odd_ref[slack : slack + channels, lanes] = jnp.concatenate([zeros, kernel_ref[i]], axis=1)
+
+
 def windows(padded_ref, p, count, odd, sizes):
     found = []
     for q in range(count):
@@ -157,9 +194,10 @@
 
 
 def forward_body(
-    sizes, frame_entries, block, x_ref, sums_ref, other_ref, rim_ref, even_ref, odd_ref,
-    hidden_ref, act_ref, clip_ref, padded,
+    sizes, frame_entries, block, x_ref, sums_ref, other_ref, rim_ref, kernel_ref,
+    hidden_ref, act_ref, clip_ref, padded, even_ref, odd_ref,
 ):
+    forward_weights(kernel_ref, even_ref, odd_ref, sizes)
     mean, rate = moments(sums_ref[...] + other_ref[...], sizes.frames, frame_entries, sizes)
 
     def rim(rows, f, before):
@@ -201,6 +239,13 @@
     put_sums(clip_ref, plain, square)
 
 
+def add_up(refs):
+    total = refs[0][...]
+    for ref in refs[1:]:
+        total = total + ref[...]
+    return total
+
+
 def put_sums(target, plain, square):
     target[...] = jnp.zeros(target.shape, F32)
     target[0:1, :] = jnp.sum(plain, axis=0, keepdims=True)
@@ -214,14 +259,10 @@
     return later, own, earlier
 
 
-def temporal_body(
-    sizes, clip_entries, block, hidden_ref, cot_ref, before_ref, after_ref, clip_ref, even_ref, odd_ref,
-    act_ref, grad_ref, sums_ref, rim_ref, normed,
-):
-    mean, rate = moments(clip_ref[...], 1, clip_entries, sizes)
-
-    def step(b, carry):
-        plain, cross = carry
+def activation_grad_body(sizes, block, cot_ref, before_ref, after_ref, kernel_ref, dact_ref, even_ref, odd_ref):
+    temporal_weights(kernel_ref, even_ref, odd_ref, sizes)
+
+    def step(b, _):
         p = b * block
         found = []
         for odd, weights in ((False, even_ref), (True, odd_ref)):
@@ -240,54 +281,92 @@
             )
         for q in range(block):
             rows = slice(q * sizes.pixels, (q + 1) * sizes.pixels)
-            dact = join(found[0][rows], found[1][rows], sizes)
-            lanes = pair_lanes(p + q, sizes)
-            tnormed = (hidden_ref[:, lanes].astype(F32) - mean) * rate
+            dact_ref[:, pair_lanes(p + q, sizes)] = join(found[0][rows], found[1][rows], sizes)
+        return 0
+
+    lax.fori_loop(0, sizes.pairs // block, step, 0)
+
+
+def temporal_body(
+    sizes, clip_entries, terms, hidden_ref, cot_ref, dact_ref, *refs
+):
+    clips, (act_ref, grad_ref, sums_ref, rim_ref, normed) = refs[:terms], refs[terms:]
+    mean, rate = moments(add_up(clips), 1, clip_entries, sizes)
+
+    def step(p, carry):
+        plain, cross = carry
+        lanes = pair_lanes(p, sizes)
+        for f in range(sizes.frames):
+            rows = pl.ds(f * sizes.rows, sizes.rows)
+            tnormed = (hidden_ref[rows, lanes].astype(F32) - mean) * rate
             act, s = silu_parts(tnormed)
-            act_ref[:, lanes] = act.astype(BF16)
-            normed[:, lanes] = tnormed
-            grad = dact * (s * (1.0 + tnormed * (1.0 - s)))
-            grad_ref[:, lanes] = grad
+            act_ref[rows, lanes] = act.astype(BF16)
+            normed[rows, lanes] = tnormed
+            grad = dact_ref[rows, lanes] * (s * (1.0 + tnormed * (1.0 - s)))
+            grad_ref[rows, lanes] = grad
             plain = plain + fold(grad)
             cross = cross + fold(grad * tnormed)
         return plain, cross
 
     zero = jnp.zeros((8, sizes.pair), F32)
-    plain, cross = lax.fori_loop(0, sizes.pairs // block, step, (zero, zero))
+    plain, cross = lax.fori_loop(0, sizes.pairs, step, (zero, zero))
     put_sums(sums_ref, plain, cross)
     for k, source in enumerate((grad_ref, normed, cot_ref)):
         store_edge(sizes, source, rim_ref, k * sizes.pixels)
 
 
-def temporal_grad_body(sizes, act_ref, cot_ref, before_ref, after_ref, out_ref, total):
+def pack(total, target, at, sizes):
+    rows, channels = total.shape[0], sizes.channels
+    full = channels // 128
+    count = 3 * rows
+    for i in range(3):
+        for k in range(full):
+            lanes = slice(i * sizes.edge + k * 128, i * sizes.edge + (k + 1) * 128)
+            target[at + k * count + i * rows : at + k * count + (i + 1) * rows, :] = total[:, lanes]
+    ends = jnp.concatenate([total[:, i * sizes.edge + full * 128 : (i + 1) * sizes.edge] for i in range(3)], axis=0)
+    half = count // 2
+    target[at + full * count : at + full * count + half, :] = jnp.concatenate(
+        [ends[:half, : 128 - sizes.slack], ends[half:, : 128 - sizes.slack]], axis=1
+    )
+
+
+def packed_rows(rows, sizes):
+    return 3 * rows * sizes.channels // 128
+
+
+def temporal_grad_body(sizes, block, act_ref, cot_ref, before_ref, after_ref, out_ref, total):
     total[...] = jnp.zeros(total.shape, F32)
     channels = sizes.channels
     zeros = jnp.zeros((sizes.pixels, sizes.slack), BF16)
 
-    def step(p, _):
-        lanes = pair_lanes(p, sizes)
-        act = act_ref[:, lanes]
-        act = jnp.concatenate([act[:, :channels], act[:, channels:]], axis=0)
-        taps = frame_taps(cot_ref, before_ref, after_ref, lanes, sizes)
-        even = jnp.concatenate([jnp.concatenate([t[:, :channels], zeros], axis=1) for t in taps], axis=1)
-        odd = jnp.concatenate([jnp.concatenate([t[:, channels:], zeros], axis=1) for t in taps], axis=1)
+    def step(b, _):
+        acts, cots = [], []
+        for q in range(block):
+            lanes = pair_lanes(b * block + q, sizes)
+            act = act_ref[:, lanes]
+            acts += [act[:, :channels], act[:, channels:]]
+            taps = frame_taps(cot_ref, before_ref, after_ref, lanes, sizes)
+            for part in (slice(0, channels), slice(channels, 2 * channels)):
+                cots.append(
+                    jnp.concatenate([jnp.concatenate([t[:, part], zeros], axis=1) for t in taps], axis=1)
+                )
         total[...] += lax.dot_general(
-            act, jnp.concatenate([even, odd], axis=0), (((0,), (0,)), ((), ())),
+            jnp.concatenate(acts, axis=0), jnp.concatenate(cots, axis=0), (((0,), (0,)), ((), ())),
             preferred_element_type=F32,
         )
         return 0
 
-    lax.fori_loop(0, sizes.pairs, step, 0)
-    for i in range(3):
-        out_ref[i] = total[:, i * sizes.edge : i * sizes.edge + channels]
+    lax.fori_loop(0, sizes.pairs // block, step, 0)
+    pack(total, out_ref, 0, sizes)
 
 
 def spatial_grad_body(
-    sizes, clip_entries, hidden_ref, cot_ref, grad_ref, clip_ref, mean_ref, rim_ref, act_ref,
-    dtemp_ref, dspat_ref, out_ref, padded, total,
+    sizes, clip_entries, terms, hidden_ref, cot_ref, grad_ref, rim_ref, act_ref, time_ref, *refs
 ):
-    mean, rate = moments(clip_ref[...], 1, clip_entries, sizes)
-    means = group_totals(mean_ref[...], sizes) * (1.0 / clip_entries)
+    clips, sums = refs[:terms], refs[terms : 2 * terms]
+    dtemp_ref, dspat_ref, keep_ref, send_ref, padded, total, packed = refs[2 * terms :]
+    mean, rate = moments(add_up(clips), 1, clip_entries, sizes)
+    means = group_totals(add_up(sums), sizes) * (1.0 / clip_entries)
     plain, cross = means[0:1], means[1:2]
 
     def rim(rows, f, before):
@@ -319,11 +398,13 @@
     zeros = jnp.zeros((sizes.pixels, sizes.slack), BF16)
     total[...] = jnp.zeros(total.shape, F32)
 
+    block = min(4, sizes.pairs)
+
     def step(b, _):
         for odd in (False, True):
             left, right = [], []
-            for q in range(2):
-                p = 2 * b + q
+            for q in range(block):
+                p = block * b + q
                 start = p * sizes.pair + (sizes.edge if odd else 0)
                 left.append(act_ref[:, pl.ds(pl.multiple_of(start, 128), sizes.window)])
                 both = pl.ds(pl.multiple_of(p * sizes.pair + sizes.edge, 128), sizes.pair)
@@ -340,15 +421,22 @@
             total[...] += part[: 3 * channels] if odd else part[sizes.slack :]
         return 0
 
-    lax.fori_loop(0, sizes.pairs // 2, step, 0)
-    for i in range(3):
-        out_ref[i] = total[:, i * sizes.edge : i * sizes.edge + channels]
+    lax.fori_loop(0, sizes.pairs // block, step, 0)
+    pack(total, packed, 0, sizes)
+    own, half = packed_rows(3 * channels, sizes), packed.shape[0] // 2
+    packed[own : own + time_ref.shape[0], :] = time_ref[...]
+    used = own + time_ref.shape[0]
+    packed[used:, :] = jnp.zeros((packed.shape[0] - used, 128), F32)
+    core = lax.axis_index("col")
+    keep_ref[...] = packed[pl.ds(pl.multiple_of(core * half, 16), half), :]
+    send_ref[...] = packed[pl.ds(pl.multiple_of((1 - core) * half, 16), half), :].astype(BF16)
 
 
 def backward_body(
-    sizes, frame_entries, block, x_ref, sums_ref, other_ref, dspat_ref, even_ref, odd_ref,
-    grad_ref, out_ref, padded, plains,
+    sizes, frame_entries, block, x_ref, sums_ref, other_ref, dspat_ref, kernel_ref,
+    grad_ref, out_ref, padded, plains, even_ref, odd_ref,
 ):
+    backward_weights(kernel_ref, even_ref, odd_ref, sizes)
     mean, rate = moments(sums_ref[...] + other_ref[...], sizes.frames, frame_entries, sizes)
 
     def spread(k, _):
@@ -408,18 +496,69 @@
     lax.fori_loop(0, sizes.pairs, step, 0)
 
 
+def unpack_body(sizes, scale, parts, *refs):
+    mine, theirs = refs[:parts], refs[parts : 2 * parts]
+    spatial_ref, temporal_ref, packed = refs[2 * parts :]
+    rows = mine[0].shape[0]
+    half = packed.shape[0] // 2
+    core, me = lax.axis_index("col"), lax.axis_index("dp")
+    for s in range(parts):
+        place = (me ^ s) * rows
+        packed[pl.ds(pl.multiple_of(core * half + place, 16), rows), :] = mine[s][...]
+        packed[pl.ds(pl.multiple_of((1 - core) * half + place, 16), rows), :] = theirs[s][...]
+    full = sizes.channels // 128
+    at = 0
+    for target in (spatial_ref, temporal_ref):
+        count = target.shape[0]
+        tile = math.gcd(count // 2, 240)
+
+        def step(k, _, at=at, target=target, count=count, tile=tile):
+            for second in range(2):
+                row = pl.multiple_of(k * tile, 16) + second * (count // 2)
+                found = [
+                    packed[pl.ds(pl.multiple_of(at + b * count + row, 16), tile), :].astype(F32) for b in range(full)
+                ]
+                ends = packed[pl.ds(pl.multiple_of(at + full * count + k * tile, 16), tile), :].astype(F32)
+                cut = 128 - sizes.slack
+                found.append(ends[:, cut:] if second else ends[:, :cut])
+                target[pl.ds(pl.multiple_of(row, 16), tile), :] = jnp.concatenate(found, axis=1) * scale
+            return 0
+
+        lax.fori_loop(0, count // 2 // tile, step, 0)
+        at += count * sizes.channels // 128
+
+
 def swap(values, axis, bit):
     count = lax.axis_size(axis)
     return lax.ppermute(values, axis, [(i, i ^ bit) for i in range(count)])
 
 
-def sum_over(values, axes):
-    for axis in axes:
-        bit = 1
-        while bit < lax.axis_size(axis):
-            values = values + swap(values, axis, bit)
-            bit *= 2
-    return values
+def from_all(values, axis):
+    return [values] + [swap(values, axis, s) for s in range(1, lax.axis_size(axis))]
+
+
+def scattered(total, axis, beside=None):
+    count = lax.axis_size(axis)
+    rows = total.shape[0] // count
+    me = lax.axis_index(axis)
+    chunks = [lax.dynamic_slice_in_dim(total, (me ^ s) * rows, rows, 0) for s in range(count)]
+    found = [swap(chunks[s].astype(BF16), axis, s) for s in range(1, count)]
+    if beside is not None:
+        found, beside = lax.optimization_barrier((found, beside))
+    total = chunks[0]
+    for chunk in found:
+        total = total + chunk.astype(F32)
+    return total, beside
+
+
+def gathered(chunk, axis):
+    parts = from_all(chunk, axis)
+    me = lax.axis_index(axis)
+    rows = chunk.shape[0]
+    out = jnp.zeros((rows * len(parts), chunk.shape[1]), chunk.dtype)
+    for s, part in enumerate(parts):
+        out = lax.dynamic_update_slice_in_dim(out, part, (me ^ s) * rows, 0)
+    return out
 
 
 def shards(latents, spatial_kernel, temporal_kernel, cotangent):
@@ -439,16 +578,6 @@
     padded_scratch = pltpu.VMEM((3, sizes.pixels, sizes.padded), BF16)
     slack = sizes.slack
 
-    flat = spatial_kernel.reshape(3, 3 * channels, channels)
-    fwd_even = jnp.pad(flat, ((0, 0), (slack, 0), (0, slack))).reshape(3 * sizes.window, sizes.edge)
-    fwd_odd = jnp.pad(flat, ((0, 0), (0, slack), (slack, 0))).reshape(3 * sizes.window, sizes.edge)
-    back = jnp.flip(spatial_kernel, (0, 1)).transpose(2, 0, 1, 3).reshape(channels, 3, 3 * channels)
-    bwd_even = jnp.pad(back, ((0, slack), (0, 0), (slack, 0))).reshape(sizes.edge, 3 * sizes.window)
-    bwd_odd = jnp.pad(back, ((slack, 0), (0, 0), (0, slack))).reshape(sizes.edge, 3 * sizes.window)
-    times = temporal_kernel.transpose(1, 0, 2)
-    time_even = jnp.pad(times, ((0, slack), (0, 0), (0, slack))).reshape(sizes.edge, 3 * sizes.edge)
-    time_odd = jnp.pad(times, ((slack, 0), (0, 0), (slack, 0))).reshape(sizes.edge, 3 * sizes.edge)
-
     forth = [(i, i + 1) for i in range(seqs - 1)]
     before = lax.ppermute(cot[sizes.pixels - rows :], "seq", forth)
     after = lax.ppermute(cot[:rows], "seq", [(j, i) for i, j in forth])
@@ -459,14 +588,22 @@
     )(x)
     other = swap(sums, "col", 1)
     rim = swap(edge, "col", 1)
+    window_weights = [pltpu.VMEM((3 * sizes.window, sizes.edge), BF16)] * 2
     hidden, act, clip = call(
         functools.partial(forward_body, sizes, frame_entries, min(4, sizes.pairs)),
         [struct((sizes.pixels, width), BF16), struct((sizes.pixels, sizes.padded), BF16), sum_shape],
-        [padded_scratch],
-    )(x, sums, other, rim, fwd_even, fwd_odd)
-    clip = sum_over(clip, ("col", "seq"))
-    tact, tgrad, means, pack = call(
-        functools.partial(temporal_body, sizes, clip_entries, min(4, sizes.pairs)),
+        [padded_scratch] + window_weights,
+        flops=CONV_COST,
+    )(x, sums, other, rim, spatial_kernel)
+    clips = from_all(clip + swap(clip, "col", 1), "seq")
+    dact = call(
+        functools.partial(activation_grad_body, sizes, min(4, sizes.pairs)),
+        struct((sizes.pixels, width), F32),
+        [pltpu.VMEM((sizes.edge, 3 * sizes.edge), BF16)] * 2,
+        flops=CONV_COST // 3,
+    )(cot, before, after, temporal_kernel)
+    tact, tgrad, means, rims = call(
+        functools.partial(temporal_body, sizes, clip_entries, seqs),
         [
             struct((sizes.pixels, width), BF16),
             struct((sizes.pixels, width), F32),
@@ -474,36 +611,66 @@
             struct((3 * sizes.pixels, sizes.edge), F32),
         ],
         [pltpu.VMEM((sizes.pixels, width), F32)],
-    )(hidden, cot, before, after, clip, time_even, time_odd)
-    means = sum_over(means, ("col", "seq"))
-    pack = swap(pack, "col", 1)
+        flops=CONV_COST // 3,
+    )(hidden, cot, dact, *clips)
+    means = from_all(means + swap(means, "col", 1), "seq")
+    rims = swap(rims, "col", 1)
     temporal_grad = call(
-        functools.partial(temporal_grad_body, sizes),
-        struct((3, channels, channels), F32),
+        functools.partial(temporal_grad_body, sizes, min(4, sizes.pairs)),
+        struct((packed_rows(channels, sizes), 128), F32),
         [pltpu.VMEM((channels, 3 * sizes.edge), F32)],
+        flops=CONV_COST // 3,
     )(tact, cot, before, after)
-    dtemp, dspat, spatial_grad = call(
-        functools.partial(spatial_grad_body, sizes, clip_entries),
+
+    devices = lax.axis_size("dp") * seqs * cols
+    used = packed_rows(3 * channels, sizes) + packed_rows(channels, sizes)
+    all_rows = -(-used // (16 * devices)) * 16 * devices
+    half = all_rows // 2
+    dtemp, dspat, keep, send = call(
+        functools.partial(spatial_grad_body, sizes, clip_entries, seqs),
         [
             struct((sizes.pixels, width), BF16),
             struct((sizes.pixels, sizes.padded), BF16),
-            struct((3, 3 * channels, channels), F32),
+            struct((half, 128), F32),
+            struct((half, 128), BF16),
         ],
-        [padded_scratch, pltpu.VMEM((3 * channels, 3 * sizes.edge), F32)],
-    )(hidden, cot, tgrad, clip, means, pack, act)
+        [
+            padded_scratch,
+            pltpu.VMEM((3 * channels, 3 * sizes.edge), F32),
+            pltpu.VMEM((all_rows, 128), F32),
+        ],
+        flops=CONV_COST,
+    )(hidden, cot, tgrad, rims, act, temporal_grad, *clips, *means)
     dnormed, mine = call(
         functools.partial(backward_body, sizes, frame_entries, min(4, sizes.pairs)),
         [struct((sizes.pixels, width), F32), frame_shape],
-        [padded_scratch, pltpu.VMEM((2 * frames, 8, sizes.pair), F32)],
-    )(x, sums, other, dspat, bwd_even, bwd_odd)
+        [padded_scratch, pltpu.VMEM((2 * frames, 8, sizes.pair), F32)]
+        + [pltpu.VMEM((sizes.edge, 3 * sizes.window), BF16)] * 2,
+        flops=CONV_COST,
+    )(x, sums, other, dspat, spatial_kernel)
+    total = keep + swap(send, "col", 1).astype(F32)
+    total, (dnormed, mine) = scattered(total, "dp", (dnormed, mine))
+    total, _ = scattered(total, "seq")
     theirs = swap(mine, "col", 1)
     grad_latents = call(
-        functools.partial(finish_body, sizes, frame_entries), struct((sizes.pixels, width), F32)
+        functools.partial(finish_body, sizes, frame_entries), struct((sizes.pixels, width), F32),
+        flops=CONV_COST // 3,
     )(x, sums, other, cot, dtemp, dnormed, mine, theirs)
-
-    spatial_grad, temporal_grad = lax.psum((spatial_grad, temporal_grad), ("dp", "seq", "col"))
-    spatial_grad = spatial_grad.reshape(spatial_kernel.shape)
-    return (grad_latents.reshape(latents.shape), spatial_grad * grad_scale, temporal_grad * grad_scale)
+    parts = from_all(gathered(total.astype(BF16), "seq"), "dp")
+    parts[1], grad_latents = lax.optimization_barrier((parts[1], grad_latents))
+    others = [swap(part, "col", 1) for part in parts]
+    spatial_grad, temporal_grad = call(
+        functools.partial(unpack_body, sizes, grad_scale, len(parts)),
+        [struct((9 * channels, channels), F32), struct((3 * channels, channels), F32)],
+        [pltpu.VMEM((all_rows, 128), BF16)],
+        flops=CONV_COST // 4,
+    )(*parts, *others)
+
+    return (
+        grad_latents.reshape(latents.shape),
+        spatial_grad.reshape(spatial_kernel.shape),
+        temporal_grad.reshape(temporal_kernel.shape),
+    )
 
 
 def solution(mesh):

time: 263 us -> 146 us (0.56)
  waiting for transfers between devices: 121 us -> 25.2 us
  local copies, waits for them, and re-layouts: 34 us -> 6.5 us
  starting transfers between devices: 15.3 us -> 33.9 us
  between operations: 14.1 us -> 0.99 us
  Pallas kernels: 68.8 us -> 75.9 us
  other arithmetic: 8.63 us -> 3.56 us
    psum x1 -> x0, waiting for transfers between devices: 115 us -> none  [shards(): lax.psum((spatial_grad, temporal_grad), ('dp', 'seq', 'col'))]
    ppermute x10 -> x29, starting transfers between devices: 9 us -> 27.7 us  [swap(): return lax.ppermute(values, axis, [(i, i ^ bit) for i in range(count)])]
    ppermute x10 -> x29, waiting for transfers between devices: 6.9 us -> 25.2 us  [swap(): return lax.ppermute(values, axis, [(i, i ^ bit) for i in range(count)])]
    pad x3 -> x0, local copies, waits for them, and re-layouts: 11.7 us -> none  [the longest x1 5.47 us: shards(): jnp.pad(back, ((slack, 0), (0, 0), (0, slack)))]
    reshape x4 -> x0, local copies, waits for them, and re-layouts: 10.6 us -> none  [the longest x1 4.3 us: shards(): jnp.pad(back, ((0, slack), (0, 0), (slack, 0)))]
    pallas_call x3 -> x5, Pallas kernels: 31.6 us -> 40.3 us  [the longest x1 15.3 us: shards(): call(functools.partial(spatial_grad_body, sizes, clip_entries, seqs), [st...]
    mul x2 -> x0, other arithmetic: 5.95 us -> none  [the longest x1 4.74 us: shards(): spatial_grad * grad_scale]
    transpose x2 -> x0, local copies, waits for them, and re-layouts: 5.8 us -> none  [shards(): jnp.flip(spatial_kernel, (0, 1)).transpose(2, 0, 1, 3)]
  transfers between devices with their start and end apart: 13 -> 31, of which waited for: 6 -> 11; matrix products, arithmetic and copies ran while one was open for 13% -> 2% of each run, Pallas kernels for 16% -> 31%
where the time goes in v1:
time: 146 us
  Pallas kernels  75.9 us (52%)
  starting transfers between devices  33.9 us (23%)
  waiting for transfers between devices  25.2 us (17%)
  local copies, waits for them, and re-layouts  6.5 us (4%)
  other arithmetic  3.56 us (2%)
    ppermute x29, starting transfers between devices, swap(): return lax.ppermute(values, axis, [(i, i ^ bit) for i in range(count)])  27.7 us
    ppermute x29, waiting for transfers between devices, swap(): return lax.ppermute(values, axis, [(i, i ^ bit) for i in range(count)])  25.2 us
    pallas_call x1, Pallas kernels, shards(): call(functools.partial(spatial_grad_body, sizes, clip_entries, seqs), [st...  15.3 us
    pallas_call x1, Pallas kernels, shards(): call(functools.partial(backward_body, sizes, frame_entries, min(4, sizes....  13.4 us
    pallas_call x1, Pallas kernels, shards(): call(functools.partial(forward_body, sizes, frame_entries, min(4, sizes.p...  13 us
    pallas_call x1, Pallas kernels, shards(): call(functools.partial(temporal_body, sizes, clip_entries, seqs), [struct...  7.2 us
    pallas_call x1, Pallas kernels, shards(): call(functools.partial(finish_body, sizes, frame_entries), struct((sizes....  6.69 us
    pallas_call x1, Pallas kernels, shards(): call(functools.partial(activation_grad_body, sizes, min(4, sizes.pairs)),...  6.57 us
  transfers between devices with their start and end apart: 31, of which 11 were waited for; matrix products, arithmetic and copies ran while one was open for 2% of the time, Pallas kernels for 31%

profile of v1, /device:TPU:0, one launch (start us, length us, event | category | flops | bytes accessed | tf_op | source)
XLA Modules:
  0.0 146.0 jit_solution(7311960761248810203)
XLA Ops:
  0.6 2.6 %shard_map.67 = (f32[8,640]{1,0:T(8,128)}, bf16[128,384]{1,0:T(8,128)(2,1)}) custom-call(bf16[128,5120]{1,0:T(8,128)(2,1)} %bitcast.9), custom_call_target="tpu_custom_call" | custom-call | tf_op jit(solution)/shard_map/pallas_call | solution.py:585
  3.2 0.5 collective-permute-start
  3.7 0.1 collective-permute-start.1
  3.7 1.1 slice_bitcast_fusion
  4.8 4.9 %collective-permute-start.2 = (bf16[32,5120]{1,0:T(8,128)(2,1)S(1)}, bf16[32,5120]{1,0:T(8,128)(2,1)S(1)}, u32[]{:S(2)}, u32[]{:S(2)}) collective-permute-start(bf16[32,5120]{1,0:T(8,128)(2,1)S(1)} %get-tuple-element.57), channel_id=1, source_target_pairs={{0,2},{2,4},{4,6},{1,3},{3,5},{5,7},{8,10},{10,12},{12,14},{9,11},... | collective-permute-start | bytes 983048 | tf_op jit(solution)/shard_map/ppermute | solution.py:582
  9.8 1.3 collective-permute-start.3
  11.1 0.6 copy-done.14
  11.7 0.6 copy-done.13
  12.3 13.0 %shard_map.68 = (bf16[128,5120]{1,0:T(8,128)(2,1)}, bf16[128,5888]{1,0:T(8,128)(2,1)}, f32[8,640]{1,0:T(8,128)}) custom-call(bf16[128,5120]{1,0:T(8,128)(2,1)} %bitcast.10, f32[8,640]{1,0:T(8,128)} %get-tuple-element.27.sums_ref, f32[8,640]{1,0:T(8,128)} %copy-done.14, bf16[128,384]{1,0:T(8,128)(2,1)} %copy-done.13, bf16[3,3,320,320]{3,2,1,0:T(8,128)(2,1)} %kernel_ref.5), custom_call_target="tpu_custom_call" | custom-call | flops 12000000000 | tf_op jit(solution)/shard_map/pallas_call | solution.py:592
  25.3 1.4 collective-permute-done.4
  26.7 0.7 add.55.refs_0_
  27.5 2.6 %collective-permute-start.5 = (f32[8,640]{1,0:T(8,128)S(1)}, f32[8,640]{1,0:T(8,128)S(1)}, u32[]{:S(2)}, u32[]{:S(2)}) collective-permute-start(f32[8,640]{1,0:T(8,128)S(1)} %add.55.refs_0_), channel_id=1, source_target_pairs={{0,2},{2,0},{4,6},{6,4},{1,3},{3,1},{5,7},{7,5},{8,10},{10,8},{12,... | collective-permute-start | bytes 61448 | tf_op jit(solution)/shard_map/ppermute | solution.py:533
  30.1 2.6 %collective-permute-start.6 = (f32[8,640]{1,0:T(8,128)S(1)}, f32[8,640]{1,0:T(8,128)S(1)}, u32[]{:S(2)}, u32[]{:S(2)}) collective-permute-start(f32[8,640]{1,0:T(8,128)S(1)} %add.55.refs_0_), channel_id=1, source_target_pairs={{0,4},{2,6},{4,0},{6,2},{1,5},{3,7},{5,1},{7,3},{8,12},{10,14},{12... | collective-permute-start | bytes 61448 | tf_op jit(solution)/shard_map/ppermute | solution.py:533
  32.7 0.7 copy-done.4
  33.4 0.1 copy-done.5
  33.6 6.6 %shard_map.69.dact_ref = f32[128,5120]{1,0:T(8,128)} custom-call(bf16[128,5120]{1,0:T(8,128)(2,1)} %bitcast.13, bf16[32,5120]{1,0:T(8,128)(2,1)} %copy-done.4, bf16[32,5120]{1,0:T(8,128)(2,1)} %copy-done.5, bf16[3,320,320]{2,1,0:T(8,128)(2,1)} %kernel_ref.4), custom_call_target="tpu_custom_call" | custom-call | flops 4000000000 | tf_op jit(solution)/shard_map/pallas_call | solution.py:599
  40.2 0.6 copy-done.16
  40.7 0.0 copy-done.17
  40.8 0.0 copy-done.18
  40.8 7.2 %shard_map.70 = (bf16[128,5120]{1,0:T(8,128)(2,1)}, f32[128,5120]{1,0:T(8,128)}, f32[8,640]{1,0:T(8,128)}, f32[384,384]{1,0:T(8,128)}) custom-call(bf16[128,5120]{1,0:T(8,128)(2,1)} %get-tuple-element.29.hidden_ref, bf16[128,5120]{1,0:T(8,128)(2,1)} %bitcast.14, f32[128,5120]{1,0:T(8,128)} %shard_map.69.dact_ref, f32[8,640]{1,0:T(8,128)} %copy-done.1, ...), custom_call_target="tpu_custom_call" | custom-call | flops 4000000000 | tf_op jit(solution)/shard_map/pallas_call | solution.py:605
  48.0 0.5 collective-permute-start.9
  48.5 1.7 %collective-permute-done.9 = f32[8,640]{1,0:T(8,128)S(1)} collective-permute-done((f32[8,640]{1,0:T(8,128)}, f32[8,640]{1,0:T(8,128)S(1)}, u32[]{:S(2)}, u32[]{:S(2)}) %collective-permute-start.9) | collective-permute-done | bytes 20512 | tf_op jit(solution)/shard_map/ppermute | solution.py:533
  50.2 0.7 add.56.refs_4_
  50.9 0.9 collective-permute-start.10
  51.8 3.5 %collective-permute-start.11 = (f32[8,640]{1,0:T(8,128)S(1)}, f32[8,640]{1,0:T(8,128)S(1)}, u32[]{:S(2)}, u32[]{:S(2)}) collective-permute-start(f32[8,640]{1,0:T(8,128)S(1)} %add.56.refs_4_), channel_id=1, source_target_pairs={{0,4},{2,6},{4,0},{6,2},{1,5},{3,7},{5,1},{7,3},{8,12},{10,14},{12... | collective-permute-start | bytes 61448 | tf_op jit(solution)/shard_map/ppermute | solution.py:533
  55.3 0.0 collective-permute-start.12
  55.3 5.8 %shard_map.71.time_ref = f32[2400,128]{1,0:T(8,128)} custom-call(bf16[128,5120]{1,0:T(8,128)(2,1)} %get-tuple-element.34.act_ref, bf16[128,5120]{1,0:T(8,128)(2,1)} %bitcast.15, bf16[32,5120]{1,0:T(8,128)(2,1)} %copy-done.4, bf16[32,5120]{1,0:T(8,128)(2,1)} %copy-done.5), custom_call_target="tpu_custom_call" | custom-call | flops 4000000000 | tf_op jit(solution)/shard_map/pallas_call | solution.py:618
  61.2 0.5 copy-done.20
  61.8 0.0 copy-done.21
  61.8 0.0 copy-done.22
  61.8 0.3 copy-done.3
  62.1 15.3 %shard_map.72 = (bf16[128,5120]{1,0:T(8,128)(2,1)}, bf16[128,5888]{1,0:T(8,128)(2,1)}, f32[4864,128]{1,0:T(8,128)}, bf16[4864,128]{1,0:T(8,128)(2,1)}) custom-call(bf16[128,5120]{1,0:T(8,128)(2,1)} %get-tuple-element.29.hidden_ref, bf16[128,5120]{1,0:T(8,128)(2,1)} %bitcast.16, f32[128,5120]{1,0:T(8,128)} %get-tuple-element.31.grad_ref, ...), custom_call_target="tpu_custom_call" | custom-call | flops 12000000000 | tf_op jit(solution)/shard_map/pallas_call | solution.py:629
  77.4 3.1 %collective-permute-done.13 = bf16[4864,128]{1,0:T(8,128)(2,1)S(1)} collective-permute-done((bf16[4864,128]{1,0:T(8,128)(2,1)}, bf16[4864,128]{1,0:T(8,128)(2,1)S(1)}, u32[]{:S(2)}, u32[]{:S(2)}) %collective-permute-start.13) | collective-permute-done | bytes 1245216 | tf_op jit(solution)/shard_map/ppermute | solution.py:533
  80.5 1.9 %convert_add_fusion = f32[4864,128]{1,0:T(8,128)S(1)} fusion(f32[4864,128]{1,0:T(8,128)} %get-tuple-element.36, bf16[4864,128]{1,0:T(8,128)(2,1)S(1)} %collective-permute-done.13), kind=kLoop, calls=%fused_computation | loop fusion | flops 1245184 | bytes 6225920 | tf_op jit(solution)/shard_map/add | solution.py:651
  82.4 0.1 dynamic-slice_convert_fusion
  82.6 1.6 %collective-permute-start.14 = (bf16[1216,128]{1,0:T(8,128)(2,1)S(1)}, bf16[1216,128]{1,0:T(8,128)(2,1)S(1)}, u32[]{:S(2)}, u32[]{:S(2)}) collective-permute-start(bf16[1216,128]{1,0:T(8,128)(2,1)S(1)} %get-tuple-element.55), channel_id=1, source_target_pairs={{0,8},{8,0},{16,24},{24,16},{1,9},{9,1},{17,25},{25,17},{2,10},{10... | collective-permute-start | bytes 933896 | tf_op jit(solution)/shard_map/ppermute | solution.py:533
  84.1 1.5 %collective-permute-start.15 = (bf16[1216,128]{1,0:T(8,128)(2,1)S(1)}, bf16[1216,128]{1,0:T(8,128)(2,1)S(1)}, u32[]{:S(2)}, u32[]{:S(2)}) collective-permute-start(bf16[1216,128]{1,0:T(8,128)(2,1)S(1)} %get-tuple-element.54), channel_id=1, source_target_pairs={{0,16},{8,24},{16,0},{24,8},{1,17},{9,25},{17,1},{25,9},{2,18},{10... | collective-permute-start | bytes 933896 | tf_op jit(solution)/shard_map/ppermute | solution.py:533
  85.6 0.5 collective-permute-start.16
  86.1 13.4 %shard_map.73 = (f32[128,5120]{1,0:T(8,128)}, f32[8,640]{1,0:T(8,128)}) custom-call(bf16[128,5120]{1,0:T(8,128)(2,1)} %bitcast.11, f32[8,640]{1,0:T(8,128)} %get-tuple-element.27.sums_ref, f32[8,640]{1,0:T(8,128)} %copy-done.14, bf16[128,5888]{1,0:T(8,128)(2,1)} %get-tuple-element.38.dspat_ref, bf16[3,3,320,320]{3,2,1,0:T(8,128)(2,1)} %kernel_ref.5), custom_call_target="tpu_custom_call" | custom-call | flops 12000000000 | tf_op jit(solution)/shard_map/pallas_call | solution.py:644
  99.5 0.4 collective-permute-done.15
  99.9 0.1 convert_add_fusion.1
  100.1 0.6 collective-permute-start.17
  100.7 3.8 %collective-permute-start.18 = (bf16[304,128]{1,0:T(8,128)(2,1)S(1)}, bf16[304,128]{1,0:T(8,128)(2,1)S(1)}, u32[]{:S(2)}, u32[]{:S(2)}) collective-permute-start(bf16[304,128]{1,0:T(8,128)(2,1)S(1)} %get-tuple-element.60), channel_id=1, source_target_pairs={{0,4},{2,6},{4,0},{6,2},{1,5},{3,7},{5,1},{7,3},{8,12},{10,14},{12... | collective-permute-start | bytes 233480 | tf_op jit(solution)/shard_map/ppermute | solution.py:533
  104.5 0.7 collective-permute-done.17
  105.2 4.0 %collective-permute-done.18 = bf16[304,128]{1,0:T(8,128)(2,1)S(1)} collective-permute-done((bf16[304,128]{1,0:T(8,128)(2,1)S(1)}, bf16[304,128]{1,0:T(8,128)(2,1)S(1)}, u32[]{:S(2)}, u32[]{:S(2)}) %collective-permute-start.18) | collective-permute-done | bytes 77856 | tf_op jit(solution)/shard_map/ppermute | solution.py:533
  109.2 1.6 %collective-permute-done.19 = bf16[304,128]{1,0:T(8,128)(2,1)S(1)} collective-permute-done((bf16[304,128]{1,0:T(8,128)(2,1)S(1)}, bf16[304,128]{1,0:T(8,128)(2,1)S(1)}, u32[]{:S(2)}, u32[]{:S(2)}) %collective-permute-start.19) | collective-permute-done | bytes 77856 | tf_op jit(solution)/shard_map/ppermute | solution.py:533
  110.9 0.1 constant_dynamic-update-slice_fusion.3
  111.0 0.7 collective-permute-start.20
  111.6 1.6 %collective-permute-start.21 = (bf16[304,128]{1,0:T(8,128)(2,1)S(1)}, bf16[304,128]{1,0:T(8,128)(2,1)S(1)}, u32[]{:S(2)}, u32[]{:S(2)}) collective-permute-start(bf16[304,128]{1,0:T(8,128)(2,1)S(1)} %get-tuple-element.52), channel_id=1, source_target_pairs={{0,4},{2,6},{4,0},{6,2},{1,5},{3,7},{5,1},{7,3},{8,12},{10,14},{12... | collective-permute-start | bytes 233480 | tf_op jit(solution)/shard_map/ppermute | solution.py:533
  113.2 2.2 %collective-permute-start.22 = (bf16[304,128]{1,0:T(8,128)(2,1)S(1)}, bf16[304,128]{1,0:T(8,128)(2,1)S(1)}, u32[]{:S(2)}, u32[]{:S(2)}) collective-permute-start(bf16[304,128]{1,0:T(8,128)(2,1)S(1)} %get-tuple-element.52), channel_id=1, source_target_pairs={{0,6},{2,4},{4,2},{6,0},{1,7},{3,5},{5,3},{7,1},{8,14},{10,12},{12... | collective-permute-start | bytes 233480 | tf_op jit(solution)/shard_map/ppermute | solution.py:533
  115.4 5.6 %collective-permute-done.21 = bf16[304,128]{1,0:T(8,128)(2,1)S(1)} collective-permute-done((bf16[304,128]{1,0:T(8,128)(2,1)S(1)}, bf16[304,128]{1,0:T(8,128)(2,1)S(1)}, u32[]{:S(2)}, u32[]{:S(2)}) %collective-permute-start.21) | collective-permute-done | bytes 77856 | tf_op jit(solution)/shard_map/ppermute | solution.py:533
  121.1 1.5 %collective-permute-start.23 = (bf16[1216,128]{1,0:T(8,128)(2,1)S(1)}, bf16[1216,128]{1,0:T(8,128)(2,1)S(1)}, u32[]{:S(2)}, u32[]{:S(2)}) collective-permute-start(bf16[1216,128]{1,0:T(8,128)(2,1)S(1)} %constant_dynamic-update-slice_fusion.refs_0_), channel_id=1, source_target_pairs={{0,8},{8,0},{16,24},{24,16},{1,9},{9,1},{17,25},{25,17},{2,10},{10... | collective-permute-start | bytes 933896 | tf_op jit(solution)/shard_map/ppermute | solution.py:533
  122.6 1.4 collective-permute-start.25
  124.0 0.7 collective-permute-start.26
  124.6 0.6 copy-done.19
  125.2 6.7 %shard_map.74 = f32[128,5120]{1,0:T(8,128)} custom-call(bf16[128,5120]{1,0:T(8,128)(2,1)} %bitcast.12, f32[8,640]{1,0:T(8,128)} %get-tuple-element.27.sums_ref, f32[8,640]{1,0:T(8,128)} %copy-done.14, bf16[128,5120]{1,0:T(8,128)(2,1)} %bitcast.17, bf16[128,5120]{1,0:T(8,128)(2,1)} %get-tuple-element.44.dtemp_ref, f32[128,5120]{1,0:T(8,128)} %get-tuple-element.45.grad_ref, ...), custom_call_target="tpu_custom_call" | custom-call | flops 4000000000 | tf_op jit(solution)/shard_map/pallas_call | solution.py:655
  132.0 0.5 collective-permute-start.28
  132.4 5.1 %collective-permute-done.25.refs_2_ = bf16[1216,128]{1,0:T(8,128)(2,1)S(1)} collective-permute-done((bf16[1216,128]{1,0:T(8,128)(2,1)S(1)}, bf16[1216,128]{1,0:T(8,128)(2,1)S(1)}, u32[]{:S(2)}, u32[]{:S(2)}) %collective-permute-start.25) | collective-permute-done | bytes 311328 | tf_op jit(solution)/shard_map/ppermute | solution.py:533
  137.6 0.5 collective-permute-start.30
  138.1 1.1 collective-permute-done.29.refs_6_
  139.2 0.4 collective-permute-done.30.refs_7_
  139.7 0.3 copy-done.11
  139.9 0.7 copy-done.12
  140.7 5.4 %shard_map.75 = (f32[2880,320]{1,0:T(8,128)}, f32[960,320]{1,0:T(8,128)}) custom-call(bf16[1216,128]{1,0:T(8,128)(2,1)} %copy-done, bf16[1216,128]{1,0:T(8,128)(2,1)} %copy-done.6, bf16[1216,128]{1,0:T(8,128)(2,1)} %copy-done.7, bf16[1216,128]{1,0:T(8,128)(2,1)} %copy-done.8, bf16[1216,128]{1,0:T(8,128)(2,1)} %copy-done.9, bf16[1216,128]{1,0:T(8,128)(2,1)} %copy-done.10, ...), custom_call_target="tpu_custom_call" | custom-call | flops 3000000000 | tf_op jit(solution)/shard_map/pallas_call | solution.py:662
  (65 shorter events, 0.3 us)
Async XLA Ops:
  3.2 7.9 %collective-permute-start = (f32[8,640]{1,0:T(8,128)}, f32[8,640]{1,0:T(8,128)S(1)}, u32[]{:S(2)}, u32[]{:S(2)}) collective-permute-start(f32[8,640]{1,0:T(8,128)} %get-tuple-element.27.sums_ref), channel_id=1, source_target_pairs={{0,1},{1,0},{2,3},{3,2},{4,5},{5,4},{6,7},{7,6},{8,9},{9,8},{10,11... | collective-permute-start | bytes 61448 | tf_op jit(solution)/shard_map/ppermute | solution.py:533
  3.7 7.4 %collective-permute-start.1 = (bf16[128,384]{1,0:T(8,128)(2,1)}, bf16[128,384]{1,0:T(8,128)(2,1)S(1)}, u32[]{:S(2)}, u32[]{:S(2)}) collective-permute-start(bf16[128,384]{1,0:T(8,128)(2,1)} %get-tuple-element.28), channel_id=1, source_target_pairs={{0,1},{1,0},{2,3},{3,2},{4,5},{5,4},{6,7},{7,6},{8,9},{9,8},{10,11... | collective-permute-start | bytes 294920 | tf_op jit(solution)/shard_map/ppermute | solution.py:533
  4.8 27.9 %collective-permute-start.2 = (bf16[32,5120]{1,0:T(8,128)(2,1)S(1)}, bf16[32,5120]{1,0:T(8,128)(2,1)S(1)}, u32[]{:S(2)}, u32[]{:S(2)}) collective-permute-start(bf16[32,5120]{1,0:T(8,128)(2,1)S(1)} %get-tuple-element.57), channel_id=1, source_target_pairs={{0,2},{2,4},{4,6},{1,3},{3,5},{5,7},{8,10},{10,12},{12,14},{9,11},... | collective-permute-start | bytes 983048 | tf_op jit(solution)/shard_map/ppermute | solution.py:582
  9.8 22.9 %collective-permute-start.3 = (bf16[32,5120]{1,0:T(8,128)(2,1)S(1)}, bf16[32,5120]{1,0:T(8,128)(2,1)S(1)}, u32[]{:S(2)}, u32[]{:S(2)}) collective-permute-start(bf16[32,5120]{1,0:T(8,128)(2,1)S(1)} %get-tuple-element.56), channel_id=1, source_target_pairs={{2,0},{4,2},{6,4},{3,1},{5,3},{7,5},{10,8},{12,10},{14,12},{11,9},... | collective-permute-start | bytes 983048 | tf_op jit(solution)/shard_map/ppermute | solution.py:583
  11.1 0.6 copy-start.14
  11.7 0.6 copy-start.13
  25.3 1.4 collective-permute-start.4
  27.5 12.7 %copy-start.1 = (f32[8,640]{1,0:T(8,128)}, f32[8,640]{1,0:T(8,128)S(1)}, u32[]{:S(2)}) copy-start(f32[8,640]{1,0:T(8,128)S(1)} %add.55.refs_0_) | copy-start | bytes 61444
  27.5 12.7 %collective-permute-start.5 = (f32[8,640]{1,0:T(8,128)S(1)}, f32[8,640]{1,0:T(8,128)S(1)}, u32[]{:S(2)}, u32[]{:S(2)}) collective-permute-start(f32[8,640]{1,0:T(8,128)S(1)} %add.55.refs_0_), channel_id=1, source_target_pairs={{0,2},{2,0},{4,6},{6,4},{1,3},{3,1},{5,7},{7,5},{8,10},{10,8},{12,... | collective-permute-start | bytes 61448 | tf_op jit(solution)/shard_map/ppermute | solution.py:533
  30.1 10.0 %collective-permute-start.6 = (f32[8,640]{1,0:T(8,128)S(1)}, f32[8,640]{1,0:T(8,128)S(1)}, u32[]{:S(2)}, u32[]{:S(2)}) collective-permute-start(f32[8,640]{1,0:T(8,128)S(1)} %add.55.refs_0_), channel_id=1, source_target_pairs={{0,4},{2,6},{4,0},{6,2},{1,5},{3,7},{5,1},{7,3},{8,12},{10,14},{12... | collective-permute-start | bytes 61448 | tf_op jit(solution)/shard_map/ppermute | solution.py:533
  32.7 7.5 %collective-permute-start.7 = (f32[8,640]{1,0:T(8,128)S(1)}, f32[8,640]{1,0:T(8,128)S(1)}, u32[]{:S(2)}, u32[]{:S(2)}) collective-permute-start(f32[8,640]{1,0:T(8,128)S(1)} %add.55.refs_0_), channel_id=1, source_target_pairs={{0,6},{2,4},{4,2},{6,0},{1,7},{3,5},{5,3},{7,1},{8,14},{10,12},{12... | collective-permute-start | bytes 61448 | tf_op jit(solution)/shard_map/ppermute | solution.py:533
  32.7 0.7 copy-start.4
  32.7 0.8 copy-start.5
  40.1 0.6 copy-start.16
  40.1 0.6 copy-start.17
  40.2 0.6 copy-start.18
  48.0 13.2 %collective-permute-start.8 = (f32[384,384]{1,0:T(8,128)}, f32[384,384]{1,0:T(8,128)S(1)}, u32[]{:S(2)}, u32[]{:S(2)}) collective-permute-start(f32[384,384]{1,0:T(8,128)} %get-tuple-element.32), channel_id=1, source_target_pairs={{0,1},{1,0},{2,3},{3,2},{4,5},{5,4},{6,7},{7,6},{8,9},{9,8},{10,11... | collective-permute-start | bytes 1769480 | tf_op jit(solution)/shard_map/ppermute | solution.py:533
  48.0 2.2 %collective-permute-start.9 = (f32[8,640]{1,0:T(8,128)}, f32[8,640]{1,0:T(8,128)S(1)}, u32[]{:S(2)}, u32[]{:S(2)}) collective-permute-start(f32[8,640]{1,0:T(8,128)} %get-tuple-element.35), channel_id=1, source_target_pairs={{0,1},{1,0},{2,3},{3,2},{4,5},{5,4},{6,7},{7,6},{8,9},{9,8},{10,11... | collective-permute-start | bytes 61448 | tf_op jit(solution)/shard_map/ppermute | solution.py:533
  50.9 10.2 %copy-start.2 = (f32[8,640]{1,0:T(8,128)}, f32[8,640]{1,0:T(8,128)S(1)}, u32[]{:S(2)}) copy-start(f32[8,640]{1,0:T(8,128)S(1)} %add.56.refs_4_) | copy-start | bytes 61444
  50.9 10.2 %collective-permute-start.10 = (f32[8,640]{1,0:T(8,128)S(1)}, f32[8,640]{1,0:T(8,128)S(1)}, u32[]{:S(2)}, u32[]{:S(2)}) collective-permute-start(f32[8,640]{1,0:T(8,128)S(1)} %add.56.refs_4_), channel_id=1, source_target_pairs={{0,2},{2,0},{4,6},{6,4},{1,3},{3,1},{5,7},{7,5},{8,10},{10,8},{12,... | collective-permute-start | bytes 61448 | tf_op jit(solution)/shard_map/ppermute | solution.py:533
  51.8 9.3 %collective-permute-start.11 = (f32[8,640]{1,0:T(8,128)S(1)}, f32[8,640]{1,0:T(8,128)S(1)}, u32[]{:S(2)}, u32[]{:S(2)}) collective-permute-start(f32[8,640]{1,0:T(8,128)S(1)} %add.56.refs_4_), channel_id=1, source_target_pairs={{0,4},{2,6},{4,0},{6,2},{1,5},{3,7},{5,1},{7,3},{8,12},{10,14},{12... | collective-permute-start | bytes 61448 | tf_op jit(solution)/shard_map/ppermute | solution.py:533
  55.3 5.9 %collective-permute-start.12 = (f32[8,640]{1,0:T(8,128)S(1)}, f32[8,640]{1,0:T(8,128)S(1)}, u32[]{:S(2)}, u32[]{:S(2)}) collective-permute-start(f32[8,640]{1,0:T(8,128)S(1)} %add.56.refs_4_), channel_id=1, source_target_pairs={{0,6},{2,4},{4,2},{6,0},{1,7},{3,5},{5,3},{7,1},{8,14},{10,12},{12... | collective-permute-start | bytes 61448 | tf_op jit(solution)/shard_map/ppermute | solution.py:533
  61.2 0.6 copy-start.20
  61.2 0.6 copy-start.21
  61.2 0.6 copy-start.22
  61.2 0.9 copy-start.3
  77.4 3.2 %collective-permute-start.13 = (bf16[4864,128]{1,0:T(8,128)(2,1)}, bf16[4864,128]{1,0:T(8,128)(2,1)S(1)}, u32[]{:S(2)}, u32[]{:S(2)}) collective-permute-start(bf16[4864,128]{1,0:T(8,128)(2,1)} %get-tuple-element.37), channel_id=1, source_target_pairs={{0,1},{1,0},{2,3},{3,2},{4,5},{5,4},{6,7},{7,6},{8,9},{9,8},{10,11... | collective-permute-start | bytes 3735560 | tf_op jit(solution)/shard_map/ppermute | solution.py:533
  82.6 16.9 %collective-permute-start.14 = (bf16[1216,128]{1,0:T(8,128)(2,1)S(1)}, bf16[1216,128]{1,0:T(8,128)(2,1)S(1)}, u32[]{:S(2)}, u32[]{:S(2)}) collective-permute-start(bf16[1216,128]{1,0:T(8,128)(2,1)S(1)} %get-tuple-element.55), channel_id=1, source_target_pairs={{0,8},{8,0},{16,24},{24,16},{1,9},{9,1},{17,25},{25,17},{2,10},{10... | collective-permute-start | bytes 933896 | tf_op jit(solution)/shard_map/ppermute | solution.py:533
  84.1 15.8 %collective-permute-start.15 = (bf16[1216,128]{1,0:T(8,128)(2,1)S(1)}, bf16[1216,128]{1,0:T(8,128)(2,1)S(1)}, u32[]{:S(2)}, u32[]{:S(2)}) collective-permute-start(bf16[1216,128]{1,0:T(8,128)(2,1)S(1)} %get-tuple-element.54), channel_id=1, source_target_pairs={{0,16},{8,24},{16,0},{24,8},{1,17},{9,25},{17,1},{25,9},{2,18},{10... | collective-permute-start | bytes 933896 | tf_op jit(solution)/shard_map/ppermute | solution.py:533
  85.6 14.3 %collective-permute-start.16 = (bf16[1216,128]{1,0:T(8,128)(2,1)S(1)}, bf16[1216,128]{1,0:T(8,128)(2,1)S(1)}, u32[]{:S(2)}, u32[]{:S(2)}) collective-permute-start(bf16[1216,128]{1,0:T(8,128)(2,1)S(1)} %get-tuple-element.53), channel_id=1, source_target_pairs={{0,24},{8,16},{16,8},{24,0},{1,25},{9,17},{17,9},{25,1},{2,26},{10... | collective-permute-start | bytes 933896 | tf_op jit(solution)/shard_map/ppermute | solution.py:533
  99.5 12.1 %copy-start.15 = (f32[8,640]{1,0:T(8,128)S(1)}, f32[8,640]{1,0:T(8,128)}, u32[]{:S(2)}) copy-start(f32[8,640]{1,0:T(8,128)} %get-tuple-element.46.mine_ref) | copy-start | bytes 61444
  100.1 5.1 %collective-permute-start.17 = (bf16[304,128]{1,0:T(8,128)(2,1)S(1)}, bf16[304,128]{1,0:T(8,128)(2,1)S(1)}, u32[]{:S(2)}, u32[]{:S(2)}) collective-permute-start(bf16[304,128]{1,0:T(8,128)(2,1)S(1)} %get-tuple-element.58), channel_id=1, source_target_pairs={{0,2},{2,0},{4,6},{6,4},{1,3},{3,1},{5,7},{7,5},{8,10},{10,8},{12,... | collective-permute-start | bytes 233480 | tf_op jit(solution)/shard_map/ppermute | solution.py:533
  100.7 8.5 %collective-permute-start.18 = (bf16[304,128]{1,0:T(8,128)(2,1)S(1)}, bf16[304,128]{1,0:T(8,128)(2,1)S(1)}, u32[]{:S(2)}, u32[]{:S(2)}) collective-permute-start(bf16[304,128]{1,0:T(8,128)(2,1)S(1)} %get-tuple-element.60), channel_id=1, source_target_pairs={{0,4},{2,6},{4,0},{6,2},{1,5},{3,7},{5,1},{7,3},{8,12},{10,14},{12... | collective-permute-start | bytes 233480 | tf_op jit(solution)/shard_map/ppermute | solution.py:533
  104.5 6.3 %collective-permute-start.19 = (bf16[304,128]{1,0:T(8,128)(2,1)S(1)}, bf16[304,128]{1,0:T(8,128)(2,1)S(1)}, u32[]{:S(2)}, u32[]{:S(2)}) collective-permute-start(bf16[304,128]{1,0:T(8,128)(2,1)S(1)} %get-tuple-element.59), channel_id=1, source_target_pairs={{0,6},{2,4},{4,2},{6,0},{1,7},{3,5},{5,3},{7,1},{8,14},{10,12},{12... | collective-permute-start | bytes 233480 | tf_op jit(solution)/shard_map/ppermute | solution.py:533
  111.0 4.5 %collective-permute-start.20 = (bf16[304,128]{1,0:T(8,128)(2,1)S(1)}, bf16[304,128]{1,0:T(8,128)(2,1)S(1)}, u32[]{:S(2)}, u32[]{:S(2)}) collective-permute-start(bf16[304,128]{1,0:T(8,128)(2,1)S(1)} %get-tuple-element.52), channel_id=1, source_target_pairs={{0,2},{2,0},{4,6},{6,4},{1,3},{3,1},{5,7},{7,5},{8,10},{10,8},{12,... | collective-permute-start | bytes 233480 | tf_op jit(solution)/shard_map/ppermute | solution.py:533
  111.6 13.0 %collective-permute-start.24 = (f32[8,640]{1,0:T(8,128)S(1)}, f32[8,640]{1,0:T(8,128)S(1)}, u32[]{:S(2)}, u32[]{:S(2)}) collective-permute-start(f32[8,640]{1,0:T(8,128)S(1)} %copy-done.15), channel_id=1, source_target_pairs={{0,1},{1,0},{2,3},{3,2},{4,5},{5,4},{6,7},{7,6},{8,9},{9,8},{10,11... | collective-permute-start | bytes 61448 | tf_op jit(solution)/shard_map/ppermute | solution.py:533
  111.6 9.4 %collective-permute-start.21 = (bf16[304,128]{1,0:T(8,128)(2,1)S(1)}, bf16[304,128]{1,0:T(8,128)(2,1)S(1)}, u32[]{:S(2)}, u32[]{:S(2)}) collective-permute-start(bf16[304,128]{1,0:T(8,128)(2,1)S(1)} %get-tuple-element.52), channel_id=1, source_target_pairs={{0,4},{2,6},{4,0},{6,2},{1,5},{3,7},{5,1},{7,3},{8,12},{10,14},{12... | collective-permute-start | bytes 233480 | tf_op jit(solution)/shard_map/ppermute | solution.py:533
  113.2 7.8 %collective-permute-start.22 = (bf16[304,128]{1,0:T(8,128)(2,1)S(1)}, bf16[304,128]{1,0:T(8,128)(2,1)S(1)}, u32[]{:S(2)}, u32[]{:S(2)}) collective-permute-start(bf16[304,128]{1,0:T(8,128)(2,1)S(1)} %get-tuple-element.52), channel_id=1, source_target_pairs={{0,6},{2,4},{4,2},{6,0},{1,7},{3,5},{5,3},{7,1},{8,14},{10,12},{12... | collective-permute-start | bytes 233480 | tf_op jit(solution)/shard_map/ppermute | solution.py:533
  121.1 10.9 %copy-start = (bf16[1216,128]{1,0:T(8,128)(2,1)}, bf16[1216,128]{1,0:T(8,128)(2,1)S(1)}, u32[]{:S(2)}) copy-start(bf16[1216,128]{1,0:T(8,128)(2,1)S(1)} %constant_dynamic-update-slice_fusion.refs_0_) | copy-start | bytes 933892
  121.1 10.9 %collective-permute-start.23 = (bf16[1216,128]{1,0:T(8,128)(2,1)S(1)}, bf16[1216,128]{1,0:T(8,128)(2,1)S(1)}, u32[]{:S(2)}, u32[]{:S(2)}) collective-permute-start(bf16[1216,128]{1,0:T(8,128)(2,1)S(1)} %constant_dynamic-update-slice_fusion.refs_0_), channel_id=1, source_target_pairs={{0,8},{8,0},{16,24},{24,16},{1,9},{9,1},{17,25},{25,17},{2,10},{10... | collective-permute-start | bytes 933896 | tf_op jit(solution)/shard_map/ppermute | solution.py:533
  122.6 15.0 %collective-permute-start.25 = (bf16[1216,128]{1,0:T(8,128)(2,1)S(1)}, bf16[1216,128]{1,0:T(8,128)(2,1)S(1)}, u32[]{:S(2)}, u32[]{:S(2)}) collective-permute-start(bf16[1216,128]{1,0:T(8,128)(2,1)S(1)} %constant_dynamic-update-slice_fusion.refs_0_), channel_id=1, source_target_pairs={{0,16},{8,24},{16,0},{24,8},{1,17},{9,25},{17,1},{25,9},{2,18},{10... | collective-permute-start | bytes 933896 | tf_op jit(solution)/shard_map/ppermute | solution.py:533
  124.0 13.6 %collective-permute-start.26 = (bf16[1216,128]{1,0:T(8,128)(2,1)S(1)}, bf16[1216,128]{1,0:T(8,128)(2,1)S(1)}, u32[]{:S(2)}, u32[]{:S(2)}) collective-permute-start(bf16[1216,128]{1,0:T(8,128)(2,1)S(1)} %constant_dynamic-update-slice_fusion.refs_0_), channel_id=1, source_target_pairs={{0,24},{8,16},{16,8},{24,0},{1,25},{9,17},{17,9},{25,1},{2,26},{10... | collective-permute-start | bytes 933896 | tf_op jit(solution)/shard_map/ppermute | solution.py:533
  124.6 0.6 copy-start.19
  131.9 6.2 %collective-permute-start.27 = (bf16[1216,128]{1,0:T(8,128)(2,1)S(1)}, bf16[1216,128]{1,0:T(8,128)(2,1)S(1)}, u32[]{:S(2)}, u32[]{:S(2)}) collective-permute-start(bf16[1216,128]{1,0:T(8,128)(2,1)S(1)} %constant_dynamic-update-slice_fusion.refs_0_), channel_id=1, source_target_pairs={{0,1},{1,0},{2,3},{3,2},{4,5},{5,4},{6,7},{7,6},{8,9},{9,8},{10,11... | collective-permute-start | bytes 933896 | tf_op jit(solution)/shard_map/ppermute | solution.py:533
  131.9 7.7 %copy-start.6 = (bf16[1216,128]{1,0:T(8,128)(2,1)}, bf16[1216,128]{1,0:T(8,128)(2,1)S(1)}, u32[]{:S(2)}) copy-start(bf16[1216,128]{1,0:T(8,128)(2,1)S(1)} %collective-permute-done.23.refs_1_) | copy-start | bytes 933892
  132.0 6.2 %collective-permute-start.28 = (bf16[1216,128]{1,0:T(8,128)(2,1)S(1)}, bf16[1216,128]{1,0:T(8,128)(2,1)S(1)}, u32[]{:S(2)}, u32[]{:S(2)}) collective-permute-start(bf16[1216,128]{1,0:T(8,128)(2,1)S(1)} %collective-permute-done.23.refs_1_), channel_id=1, source_target_pairs={{0,1},{1,0},{2,3},{3,2},{4,5},{5,4},{6,7},{7,6},{8,9},{9,8},{10,11... | collective-permute-start | bytes 933896 | tf_op jit(solution)/shard_map/ppermute | solution.py:533
  137.6 2.1 %copy-start.7 = (bf16[1216,128]{1,0:T(8,128)(2,1)}, bf16[1216,128]{1,0:T(8,128)(2,1)S(1)}, u32[]{:S(2)}) copy-start(bf16[1216,128]{1,0:T(8,128)(2,1)S(1)} %collective-permute-done.25.refs_2_) | copy-start | bytes 933892
  137.6 1.6 %collective-permute-start.29 = (bf16[1216,128]{1,0:T(8,128)(2,1)S(1)}, bf16[1216,128]{1,0:T(8,128)(2,1)S(1)}, u32[]{:S(2)}, u32[]{:S(2)}) collective-permute-start(bf16[1216,128]{1,0:T(8,128)(2,1)S(1)} %collective-permute-done.25.refs_2_), channel_id=1, source_target_pairs={{0,1},{1,0},{2,3},{3,2},{4,5},{5,4},{6,7},{7,6},{8,9},{9,8},{10,11... | collective-permute-start | bytes 933896 | tf_op jit(solution)/shard_map/ppermute | solution.py:533
  137.6 2.0 %copy-start.8 = (bf16[1216,128]{1,0:T(8,128)(2,1)}, bf16[1216,128]{1,0:T(8,128)(2,1)S(1)}, u32[]{:S(2)}) copy-start(bf16[1216,128]{1,0:T(8,128)(2,1)S(1)} %collective-permute-done.26.refs_3_) | copy-start | bytes 933892
  137.6 2.0 %collective-permute-start.30 = (bf16[1216,128]{1,0:T(8,128)(2,1)S(1)}, bf16[1216,128]{1,0:T(8,128)(2,1)S(1)}, u32[]{:S(2)}, u32[]{:S(2)}) collective-permute-start(bf16[1216,128]{1,0:T(8,128)(2,1)S(1)} %collective-permute-done.26.refs_3_), channel_id=1, source_target_pairs={{0,1},{1,0},{2,3},{3,2},{4,5},{5,4},{6,7},{7,6},{8,9},{9,8},{10,11... | collective-permute-start | bytes 933896 | tf_op jit(solution)/shard_map/ppermute | solution.py:533
  138.1 1.5 %copy-start.9 = (bf16[1216,128]{1,0:T(8,128)(2,1)}, bf16[1216,128]{1,0:T(8,128)(2,1)S(1)}, u32[]{:S(2)}) copy-start(bf16[1216,128]{1,0:T(8,128)(2,1)S(1)} %collective-permute-done.27.refs_4_) | copy-start | bytes 933892
  138.1 1.5 %copy-start.10 = (bf16[1216,128]{1,0:T(8,128)(2,1)}, bf16[1216,128]{1,0:T(8,128)(2,1)S(1)}, u32[]{:S(2)}) copy-start(bf16[1216,128]{1,0:T(8,128)(2,1)S(1)} %collective-permute-done.28.refs_5_) | copy-start | bytes 933892
  139.2 0.7 copy-start.11
  139.9 0.7 copy-start.12

commit v2 on v1

--- a/solution.py
+++ b/solution.py
@@ -12,7 +12,7 @@
 EPSILON = 1e-05
 F32 = jnp.float32
 BF16 = jnp.bfloat16
-VMEM_LIMIT = 56 * 1024 * 1024
+VMEM_LIMIT = 28 * 1024 * 1024
 CONV_COST = 12_000_000_000
 
 

time: 146 us -> 125 us (0.86)
  Pallas kernels: 75.9 us -> 47.3 us
  waiting for transfers between devices: 25.2 us -> 29.2 us
  local copies, waits for them, and re-layouts: 6.5 us -> 10.1 us
    pallas_call x1, Pallas kernels: 7.2 us -> 2.5 us  [shards(): call(functools.partial(temporal_body, sizes, clip_entries, seqs), [struct...]
    pallas_call x1, Pallas kernels: 15.3 us -> 10.9 us  [shards(): call(functools.partial(spatial_grad_body, sizes, clip_entries, seqs), [st...]
    ppermute x29, waiting for transfers between devices: 25.2 us -> 29.2 us  [swap(): return lax.ppermute(values, axis, [(i, i ^ bit) for i in range(count)])]
    pallas_call x1, Pallas kernels: 13.4 us -> 9.69 us  [shards(): call(functools.partial(backward_body, sizes, frame_entries, min(4, sizes....]
    pallas_call x1, Pallas kernels: 6.57 us -> 3.26 us  [shards(): call(functools.partial(activation_grad_body, sizes, min(4, sizes.pairs)),...]
    pallas_call x1, Pallas kernels: 13 us -> 9.89 us  [shards(): call(functools.partial(forward_body, sizes, frame_entries, min(4, sizes.p...]
    pallas_call x1, Pallas kernels: 6.69 us -> 3.74 us  [shards(): call(functools.partial(finish_body, sizes, frame_entries), struct((sizes....]
    unnamed x46 -> x28, local copies, waits for them, and re-layouts: 5.12 us -> 8.06 us
  transfers between devices with their start and end apart: 31 -> 31, of which waited for: 11 -> 13; matrix products, arithmetic and copies ran while one was open for 2% -> 1% of each run, Pallas kernels for 31% -> 24%
where the time goes in v2:
time: 125 us; the launch traced here: 124 us
  Pallas kernels  47.3 us (38%)
  starting transfers between devices  34.2 us (27%)
  waiting for transfers between devices  29.2 us (23%)
  local copies, waits for them, and re-layouts  10.1 us (8%)
  other arithmetic  2.73 us (2%)
    ppermute x29, waiting for transfers between devices, swap(): return lax.ppermute(values, axis, [(i, i ^ bit) for i in range(count)])  29.2 us
    ppermute x29, starting transfers between devices, swap(): return lax.ppermute(values, axis, [(i, i ^ bit) for i in range(count)])  27.8 us
    pallas_call x1, Pallas kernels, shards(): call(functools.partial(spatial_grad_body, sizes, clip_entries, seqs), [st...  10.9 us
    pallas_call x1, Pallas kernels, shards(): call(functools.partial(forward_body, sizes, frame_entries, min(4, sizes.p...  9.89 us
    pallas_call x1, Pallas kernels, shards(): call(functools.partial(backward_body, sizes, frame_entries, min(4, sizes....  9.69 us
    unnamed x28, local copies, waits for them, and re-layouts  8.06 us
    ppermute x1, starting transfers between devices, shards(): before = lax.ppermute(cot[sizes.pixels - rows:], 'seq', forth)  4.92 us
    pallas_call x1, Pallas kernels, shards(): call(functools.partial(unpack_body, sizes, grad_scale, len(parts)), [stru...  3.76 us
  transfers between devices with their start and end apart: 31, of which 13 were waited for; matrix products, arithmetic and copies ran while one was open for 1% of the time, Pallas kernels for 24%

profile of v2, /device:TPU:0, one launch (start us, length us, event | category | flops | bytes accessed | tf_op | source)
XLA Modules:
  0.0 124.5 jit_solution(16715127169617879490)
XLA Ops:
  0.6 0.0 copy-start
  0.6 1.3 %copy-done = bf16[1,4,32,5120]{3,2,1,0:T(8,128)(2,1)S(1)} copy-done((bf16[1,4,32,5120]{3,2,1,0:T(8,128)(2,1)S(1)}, bf16[1,4,32,5120]{3,2,1,0:T(8,128)(2,1)}, u32[]{:S(2)}) %copy-start) | copy-done | bytes 1310744
  2.0 0.6 shard_map.67
  2.6 0.5 collective-permute-start
  3.1 0.1 collective-permute-start.1
  3.2 1.1 slice_bitcast_fusion
  4.3 4.9 %collective-permute-start.2 = (bf16[32,5120]{1,0:T(8,128)(2,1)S(1)}, bf16[32,5120]{1,0:T(8,128)(2,1)S(1)}, u32[]{:S(2)}, u32[]{:S(2)}) collective-permute-start(bf16[32,5120]{1,0:T(8,128)(2,1)S(1)} %get-tuple-element.57), channel_id=1, source_target_pairs={{0,2},{2,4},{4,6},{1,3},{3,5},{5,7},{8,10},{10,12},{12,14},{9,11},... | collective-permute-start | bytes 983048 | tf_op jit(solution)/shard_map/ppermute | solution.py:582
  9.2 0.0 copy-start.3
  9.2 0.0 copy-start.7
  9.2 1.4 %collective-permute-start.3 = (bf16[32,5120]{1,0:T(8,128)(2,1)S(1)}, bf16[32,5120]{1,0:T(8,128)(2,1)S(1)}, u32[]{:S(2)}, u32[]{:S(2)}) collective-permute-start(bf16[32,5120]{1,0:T(8,128)(2,1)S(1)} %get-tuple-element.56), channel_id=1, source_target_pairs={{2,0},{4,2},{6,4},{3,1},{5,3},{7,5},{10,8},{12,10},{14,12},{11,9},... | collective-permute-start | bytes 983048 | tf_op jit(solution)/shard_map/ppermute | solution.py:583
  10.7 9.9 %shard_map.68 = (bf16[128,5120]{1,0:T(8,128)(2,1)S(1)}, bf16[128,5888]{1,0:T(8,128)(2,1)S(1)}, f32[8,640]{1,0:T(8,128)S(1)}) custom-call(bf16[128,5120]{1,0:T(8,128)(2,1)S(1)} %bitcast.10, f32[8,640]{1,0:T(8,128)S(1)} %get-tuple-element.27.sums_ref, f32[8,640]{1,0:T(8,128)S(1)} %collective-permute-done.other_ref, ...), custom_call_target="tpu_custom_call" | custom-call | flops 12000000000 | tf_op jit(solution)/shard_map/pallas_call | solution.py:592
  20.6 0.1 collective-permute-start.4
  20.7 1.2 collective-permute-done.4
  21.9 2.6 %collective-permute-start.5 = (f32[8,640]{1,0:T(8,128)S(1)}, f32[8,640]{1,0:T(8,128)S(1)}, u32[]{:S(2)}, u32[]{:S(2)}) collective-permute-start(f32[8,640]{1,0:T(8,128)S(1)} %add.55.refs_0_), channel_id=1, source_target_pairs={{0,2},{2,0},{4,6},{6,4},{1,3},{3,1},{5,7},{7,5},{8,10},{10,8},{12,... | collective-permute-start | bytes 61448 | tf_op jit(solution)/shard_map/ppermute | solution.py:533
  24.5 2.6 %collective-permute-start.6 = (f32[8,640]{1,0:T(8,128)S(1)}, f32[8,640]{1,0:T(8,128)S(1)}, u32[]{:S(2)}, u32[]{:S(2)}) collective-permute-start(f32[8,640]{1,0:T(8,128)S(1)} %add.55.refs_0_), channel_id=1, source_target_pairs={{0,4},{2,6},{4,0},{6,2},{1,5},{3,7},{5,1},{7,3},{8,12},{10,14},{12... | collective-permute-start | bytes 61448 | tf_op jit(solution)/shard_map/ppermute | solution.py:533
  27.1 3.3 %shard_map.69.dact_ref = f32[128,5120]{1,0:T(8,128)S(1)} custom-call(bf16[128,5120]{1,0:T(8,128)(2,1)S(1)} %bitcast.13, bf16[32,5120]{1,0:T(8,128)(2,1)S(1)} %collective-permute-done.2.before_ref, bf16[32,5120]{1,0:T(8,128)(2,1)S(1)} %collective-permute-done.3.after_ref, bf16[3,320,320]{2,1,0:T(8,128)(2,1)S(1)} %copy-done.7), custom_call_target="tpu_custom_call" | custom-call | flops 4000000000 | tf_op jit(solution)/shard_map/pallas_call | solution.py:599
  30.4 2.3 %collective-permute-done.7.refs_3_ = f32[8,640]{1,0:T(8,128)S(1)} collective-permute-done((f32[8,640]{1,0:T(8,128)S(1)}, f32[8,640]{1,0:T(8,128)S(1)}, u32[]{:S(2)}, u32[]{:S(2)}) %collective-permute-start.7) | collective-permute-done | bytes 20512 | tf_op jit(solution)/shard_map/ppermute | solution.py:533
  32.7 2.5 %shard_map.70 = (bf16[128,5120]{1,0:T(8,128)(2,1)S(1)}, f32[128,5120]{1,0:T(8,128)S(1)}, f32[8,640]{1,0:T(8,128)S(1)}, f32[384,384]{1,0:T(8,128)S(1)}) custom-call(bf16[128,5120]{1,0:T(8,128)(2,1)S(1)} %get-tuple-element.29.hidden_ref, bf16[128,5120]{1,0:T(8,128)(2,1)S(1)} %bitcast.14, f32[128,5120]{1,0:T(8,128)S(1)} %shard_map.69.dact_ref, ...), custom_call_target="tpu_custom_call" | custom-call | flops 4000000000 | tf_op jit(solution)/shard_map/pallas_call | solution.py:605
  35.2 0.1 collective-permute-start.8
  35.3 0.5 collective-permute-start.9
  35.8 1.5 %collective-permute-done.9 = f32[8,640]{1,0:T(8,128)S(1)} collective-permute-done((f32[8,640]{1,0:T(8,128)S(1)}, f32[8,640]{1,0:T(8,128)S(1)}, u32[]{:S(2)}, u32[]{:S(2)}) %collective-permute-start.9) | collective-permute-done | bytes 20512 | tf_op jit(solution)/shard_map/ppermute | solution.py:533
  37.3 2.1 %collective-permute-start.11 = (f32[8,640]{1,0:T(8,128)S(1)}, f32[8,640]{1,0:T(8,128)S(1)}, u32[]{:S(2)}, u32[]{:S(2)}) collective-permute-start(f32[8,640]{1,0:T(8,128)S(1)} %add.56.refs_4_), channel_id=1, source_target_pairs={{0,4},{2,6},{4,0},{6,2},{1,5},{3,7},{5,1},{7,3},{8,12},{10,14},{12... | collective-permute-start | bytes 61448 | tf_op jit(solution)/shard_map/ppermute | solution.py:533
  39.4 2.3 %collective-permute-start.12 = (f32[8,640]{1,0:T(8,128)S(1)}, f32[8,640]{1,0:T(8,128)S(1)}, u32[]{:S(2)}, u32[]{:S(2)}) collective-permute-start(f32[8,640]{1,0:T(8,128)S(1)} %add.56.refs_4_), channel_id=1, source_target_pairs={{0,6},{2,4},{4,2},{6,0},{1,7},{3,5},{5,3},{7,1},{8,14},{10,12},{12... | collective-permute-start | bytes 61448 | tf_op jit(solution)/shard_map/ppermute | solution.py:533
  41.7 2.9 %shard_map.71.time_ref = f32[2400,128]{1,0:T(8,128)S(1)} custom-call(bf16[128,5120]{1,0:T(8,128)(2,1)S(1)} %get-tuple-element.34.act_ref, bf16[128,5120]{1,0:T(8,128)(2,1)S(1)} %bitcast.15, bf16[32,5120]{1,0:T(8,128)(2,1)S(1)} %collective-permute-done.2.before_ref, bf16[32,5120]{1,0:T(8,128)(2,1)S(1)} %collective-permute-done.3.after_ref), custom_call_target="tpu_custom_call" | custom-call | flops 4000000000 | tf_op jit(solution)/shard_map/pallas_call | solution.py:618
  44.6 0.4 collective-permute-done.12.refs_7_
  45.0 10.9 %shard_map.72 = (bf16[128,5120]{1,0:T(8,128)(2,1)S(1)}, bf16[128,5888]{1,0:T(8,128)(2,1)S(1)}, f32[4864,128]{1,0:T(8,128)S(1)}, bf16[4864,128]{1,0:T(8,128)(2,1)}) custom-call(bf16[128,5120]{1,0:T(8,128)(2,1)S(1)} %get-tuple-element.29.hidden_ref, bf16[128,5120]{1,0:T(8,128)(2,1)S(1)} %bitcast.16, f32[128,5120]{1,0:T(8,128)S(1)} %get-tuple-element.31.grad_ref, ...), custom_call_target="tpu_custom_call" | custom-call | flops 12000000000 | tf_op jit(solution)/shard_map/pallas_call | solution.py:629
  55.9 1.1 copy-done.10
  57.0 1.1 copy-done.12
  58.1 3.3 %collective-permute-done.13 = bf16[4864,128]{1,0:T(8,128)(2,1)} collective-permute-done((bf16[4864,128]{1,0:T(8,128)(2,1)}, bf16[4864,128]{1,0:T(8,128)(2,1)}, u32[]{:S(2)}, u32[]{:S(2)}) %collective-permute-start.13) | collective-permute-done | bytes 1245216 | tf_op jit(solution)/shard_map/ppermute | solution.py:533
  61.4 1.6 %convert_add_fusion = f32[4864,128]{1,0:T(8,128)S(1)} fusion(f32[4864,128]{1,0:T(8,128)S(1)} %get-tuple-element.36, bf16[4864,128]{1,0:T(8,128)(2,1)} %collective-permute-done.13), kind=kLoop, calls=%fused_computation | loop fusion | flops 1245184 | bytes 6225920 | tf_op jit(solution)/shard_map/add | solution.py:651
  63.1 0.1 dynamic-slice_convert_fusion
  63.2 1.6 %collective-permute-start.14 = (bf16[1216,128]{1,0:T(8,128)(2,1)S(1)}, bf16[1216,128]{1,0:T(8,128)(2,1)S(1)}, u32[]{:S(2)}, u32[]{:S(2)}) collective-permute-start(bf16[1216,128]{1,0:T(8,128)(2,1)S(1)} %get-tuple-element.55), channel_id=1, source_target_pairs={{0,8},{8,0},{16,24},{24,16},{1,9},{9,1},{17,25},{25,17},{2,10},{10... | collective-permute-start | bytes 933896 | tf_op jit(solution)/shard_map/ppermute | solution.py:533
  64.8 1.5 %collective-permute-start.15 = (bf16[1216,128]{1,0:T(8,128)(2,1)S(1)}, bf16[1216,128]{1,0:T(8,128)(2,1)S(1)}, u32[]{:S(2)}, u32[]{:S(2)}) collective-permute-start(bf16[1216,128]{1,0:T(8,128)(2,1)S(1)} %get-tuple-element.54), channel_id=1, source_target_pairs={{0,16},{8,24},{16,0},{24,8},{1,17},{9,25},{17,1},{25,9},{2,18},{10... | collective-permute-start | bytes 933896 | tf_op jit(solution)/shard_map/ppermute | solution.py:533
  66.3 0.5 collective-permute-start.16
  66.8 9.7 %shard_map.73 = (f32[128,5120]{1,0:T(8,128)S(1)}, f32[8,640]{1,0:T(8,128)S(1)}) custom-call(bf16[128,5120]{1,0:T(8,128)(2,1)S(1)} %bitcast.11, f32[8,640]{1,0:T(8,128)S(1)} %get-tuple-element.27.sums_ref, f32[8,640]{1,0:T(8,128)S(1)} %collective-permute-done.other_ref, bf16[128,5888]{1,0:T(8,128)(2,1)S(1)} %copy-done.13, bf16[3,3,320,320]{3,2,1,0:T(8,128)(2,1)S(1)} %copy-done.6), custom_call_target="tpu_custom_call" | custom-call | flops 12000000000 | tf_op jit(solution)/shard_map/pallas_call | solution.py:644
  76.5 0.0 copy-start.8
  76.5 1.5 %copy-done.8 = f32[128,5120]{1,0:T(8,128)} copy-done((f32[128,5120]{1,0:T(8,128)}, f32[128,5120]{1,0:T(8,128)S(1)}, u32[]{:S(2)}) %copy-start.8) | copy-done | bytes 2621464
  78.0 2.6 %collective-permute-done.15 = bf16[1216,128]{1,0:T(8,128)(2,1)S(1)} collective-permute-done((bf16[1216,128]{1,0:T(8,128)(2,1)S(1)}, bf16[1216,128]{1,0:T(8,128)(2,1)S(1)}, u32[]{:S(2)}, u32[]{:S(2)}) %collective-permute-start.15) | collective-permute-done | bytes 311328 | tf_op jit(solution)/shard_map/ppermute | solution.py:533
  80.6 0.1 convert_add_fusion.1
  80.7 0.7 dynamic-slice_convert_fusion.5
  81.4 2.8 %collective-permute-start.18 = (bf16[304,128]{1,0:T(8,128)(2,1)}, bf16[304,128]{1,0:T(8,128)(2,1)S(1)}, u32[]{:S(2)}, u32[]{:S(2)}) collective-permute-start(bf16[304,128]{1,0:T(8,128)(2,1)} %get-tuple-element.60), channel_id=1, source_target_pairs={{0,4},{2,6},{4,0},{6,2},{1,5},{3,7},{5,1},{7,3},{8,12},{10,14},{12... | collective-permute-start | bytes 233480 | tf_op jit(solution)/shard_map/ppermute | solution.py:533
  84.2 1.6 %collective-permute-start.19 = (bf16[304,128]{1,0:T(8,128)(2,1)S(1)}, bf16[304,128]{1,0:T(8,128)(2,1)}, u32[]{:S(2)}, u32[]{:S(2)}) collective-permute-start(bf16[304,128]{1,0:T(8,128)(2,1)S(1)} %get-tuple-element.59), channel_id=1, source_target_pairs={{0,6},{2,4},{4,2},{6,0},{1,7},{3,5},{5,3},{7,1},{8,14},{10,12},{12... | collective-permute-start | bytes 233480 | tf_op jit(solution)/shard_map/ppermute | solution.py:533
  85.8 0.2 collective-permute-done.17
  86.0 3.2 %collective-permute-done.18 = bf16[304,128]{1,0:T(8,128)(2,1)S(1)} collective-permute-done((bf16[304,128]{1,0:T(8,128)(2,1)}, bf16[304,128]{1,0:T(8,128)(2,1)S(1)}, u32[]{:S(2)}, u32[]{:S(2)}) %collective-permute-start.18) | collective-permute-done | bytes 77856 | tf_op jit(solution)/shard_map/ppermute | solution.py:533
  89.2 1.4 %collective-permute-done.19 = bf16[304,128]{1,0:T(8,128)(2,1)} collective-permute-done((bf16[304,128]{1,0:T(8,128)(2,1)S(1)}, bf16[304,128]{1,0:T(8,128)(2,1)}, u32[]{:S(2)}, u32[]{:S(2)}) %collective-permute-start.19) | collective-permute-done | bytes 77856 | tf_op jit(solution)/shard_map/ppermute | solution.py:533
  90.7 1.0 constant_dynamic-update-slice_fusion.3
  91.6 1.0 collective-permute-start.20
  92.6 1.3 %collective-permute-start.21 = (bf16[304,128]{1,0:T(8,128)(2,1)S(1)}, bf16[304,128]{1,0:T(8,128)(2,1)S(1)}, u32[]{:S(2)}, u32[]{:S(2)}) collective-permute-start(bf16[304,128]{1,0:T(8,128)(2,1)S(1)} %get-tuple-element.52), channel_id=1, source_target_pairs={{0,4},{2,6},{4,0},{6,2},{1,5},{3,7},{5,1},{7,3},{8,12},{10,14},{12... | collective-permute-start | bytes 233480 | tf_op jit(solution)/shard_map/ppermute | solution.py:533
  93.9 2.2 %collective-permute-start.22 = (bf16[304,128]{1,0:T(8,128)(2,1)S(1)}, bf16[304,128]{1,0:T(8,128)(2,1)S(1)}, u32[]{:S(2)}, u32[]{:S(2)}) collective-permute-start(bf16[304,128]{1,0:T(8,128)(2,1)S(1)} %get-tuple-element.52), channel_id=1, source_target_pairs={{0,6},{2,4},{4,2},{6,0},{1,7},{3,5},{5,3},{7,1},{8,14},{10,12},{12... | collective-permute-start | bytes 233480 | tf_op jit(solution)/shard_map/ppermute | solution.py:533
  96.1 0.0 collective-permute-done.20
  96.1 5.9 %collective-permute-done.21 = bf16[304,128]{1,0:T(8,128)(2,1)S(1)} collective-permute-done((bf16[304,128]{1,0:T(8,128)(2,1)S(1)}, bf16[304,128]{1,0:T(8,128)(2,1)S(1)}, u32[]{:S(2)}, u32[]{:S(2)}) %collective-permute-start.21) | collective-permute-done | bytes 77856 | tf_op jit(solution)/shard_map/ppermute | solution.py:533
  102.1 1.4 %collective-permute-start.23 = (bf16[1216,128]{1,0:T(8,128)(2,1)S(1)}, bf16[1216,128]{1,0:T(8,128)(2,1)S(1)}, u32[]{:S(2)}, u32[]{:S(2)}) collective-permute-start(bf16[1216,128]{1,0:T(8,128)(2,1)S(1)} %constant_dynamic-update-slice_fusion.refs_0_), channel_id=1, source_target_pairs={{0,8},{8,0},{16,24},{24,16},{1,9},{9,1},{17,25},{25,17},{2,10},{10... | collective-permute-start | bytes 933896 | tf_op jit(solution)/shard_map/ppermute | solution.py:533
  103.5 0.6 collective-permute-start.25
  104.1 1.5 %collective-permute-start.26 = (bf16[1216,128]{1,0:T(8,128)(2,1)S(1)}, bf16[1216,128]{1,0:T(8,128)(2,1)S(1)}, u32[]{:S(2)}, u32[]{:S(2)}) collective-permute-start(bf16[1216,128]{1,0:T(8,128)(2,1)S(1)} %constant_dynamic-update-slice_fusion.refs_0_), channel_id=1, source_target_pairs={{0,24},{8,16},{16,8},{24,0},{1,25},{9,17},{17,9},{25,1},{2,26},{10... | collective-permute-start | bytes 933896 | tf_op jit(solution)/shard_map/ppermute | solution.py:533
  105.6 0.0 copy-start.9
  105.7 1.7 %copy-done.9 = f32[128,5120]{1,0:T(8,128)S(1)} copy-done((f32[128,5120]{1,0:T(8,128)S(1)}, f32[128,5120]{1,0:T(8,128)}, u32[]{:S(2)}) %copy-start.9) | copy-done | bytes 2621464
  107.4 1.3 %copy-done.11 = bf16[128,5120]{1,0:T(8,128)(2,1)S(1)} copy-done((bf16[128,5120]{1,0:T(8,128)(2,1)S(1)}, bf16[128,5120]{1,0:T(8,128)(2,1)}, u32[]{:S(2)}) %copy-start.11) | copy-done | bytes 1310744
  108.7 3.7 %shard_map.74 = f32[128,5120]{1,0:T(8,128)} custom-call(bf16[128,5120]{1,0:T(8,128)(2,1)S(1)} %bitcast.12, f32[8,640]{1,0:T(8,128)S(1)} %get-tuple-element.27.sums_ref, f32[8,640]{1,0:T(8,128)S(1)} %collective-permute-done.other_ref, bf16[128,5120]{1,0:T(8,128)(2,1)S(1)} %bitcast.17, bf16[128,5120]{1,0:T(8,128)(2,1)S(1)} %copy-done.11, ...), custom_call_target="tpu_custom_call" | custom-call | flops 4000000000 | tf_op jit(solution)/shard_map/pallas_call | solution.py:655
  112.4 0.5 collective-permute-start.28
  113.0 5.7 %collective-permute-done.25.refs_2_ = bf16[1216,128]{1,0:T(8,128)(2,1)S(1)} collective-permute-done((bf16[1216,128]{1,0:T(8,128)(2,1)S(1)}, bf16[1216,128]{1,0:T(8,128)(2,1)S(1)}, u32[]{:S(2)}, u32[]{:S(2)}) %collective-permute-start.25) | collective-permute-done | bytes 311328 | tf_op jit(solution)/shard_map/ppermute | solution.py:533
  118.6 0.5 collective-permute-start.30
  119.2 1.1 collective-permute-done.29.refs_6_
  120.2 0.4 collective-permute-done.30.refs_7_
  120.7 3.8 %shard_map.75 = (f32[2880,320]{1,0:T(8,128)}, f32[960,320]{1,0:T(8,128)}) custom-call(bf16[1216,128]{1,0:T(8,128)(2,1)S(1)} %constant_dynamic-update-slice_fusion.refs_0_, bf16[1216,128]{1,0:T(8,128)(2,1)S(1)} %collective-permute-done.23.refs_1_, bf16[1216,128]{1,0:T(8,128)(2,1)S(1)} %collective-permute-done.25.refs_2_, ...), custom_call_target="tpu_custom_call" | custom-call | flops 3000000000 | tf_op jit(solution)/shard_map/pallas_call | solution.py:662
  (47 shorter events, 0.2 us)
Async XLA Ops:
  0.6 1.3 %copy-start = (bf16[1,4,32,5120]{3,2,1,0:T(8,128)(2,1)S(1)}, bf16[1,4,32,5120]{3,2,1,0:T(8,128)(2,1)}, u32[]{:S(2)}) copy-start(bf16[1,4,32,5120]{3,2,1,0:T(8,128)(2,1)} %param.4) | copy-start | bytes 3932164
  1.9 8.8 %copy-start.5 = (bf16[3,3,320,320]{3,2,1,0:T(8,128)(2,1)S(1)}, bf16[3,3,320,320]{3,2,1,0:T(8,128)(2,1)}, u32[]{:S(2)}) copy-start(bf16[3,3,320,320]{3,2,1,0:T(8,128)(2,1)} %kernel_ref.5) | copy-start | bytes 5529604
  2.6 8.1 %collective-permute-start = (f32[8,640]{1,0:T(8,128)S(1)}, f32[8,640]{1,0:T(8,128)S(1)}, u32[]{:S(2)}, u32[]{:S(2)}) collective-permute-start(f32[8,640]{1,0:T(8,128)S(1)} %get-tuple-element.27.sums_ref), channel_id=1, source_target_pairs={{0,1},{1,0},{2,3},{3,2},{4,5},{5,4},{6,7},{7,6},{8,9},{9,8},{10,11... | collective-permute-start | bytes 61448 | tf_op jit(solution)/shard_map/ppermute | solution.py:533
  3.1 7.6 %collective-permute-start.1 = (bf16[128,384]{1,0:T(8,128)(2,1)S(1)}, bf16[128,384]{1,0:T(8,128)(2,1)S(1)}, u32[]{:S(2)}, u32[]{:S(2)}) collective-permute-start(bf16[128,384]{1,0:T(8,128)(2,1)S(1)} %get-tuple-element.28), channel_id=1, source_target_pairs={{0,1},{1,0},{2,3},{3,2},{4,5},{5,4},{6,7},{7,6},{8,9},{9,8},{10,11... | collective-permute-start | bytes 294920 | tf_op jit(solution)/shard_map/ppermute | solution.py:533
  4.3 22.8 %collective-permute-start.2 = (bf16[32,5120]{1,0:T(8,128)(2,1)S(1)}, bf16[32,5120]{1,0:T(8,128)(2,1)S(1)}, u32[]{:S(2)}, u32[]{:S(2)}) collective-permute-start(bf16[32,5120]{1,0:T(8,128)(2,1)S(1)} %get-tuple-element.57), channel_id=1, source_target_pairs={{0,2},{2,4},{4,6},{1,3},{3,5},{5,7},{8,10},{10,12},{12,14},{9,11},... | collective-permute-start | bytes 983048 | tf_op jit(solution)/shard_map/ppermute | solution.py:582
  9.2 17.9 %copy-start.3 = (bf16[1,4,32,5120]{3,2,1,0:T(8,128)(2,1)S(1)}, bf16[1,4,32,5120]{3,2,1,0:T(8,128)(2,1)}, u32[]{:S(2)}) copy-start(bf16[1,4,32,5120]{3,2,1,0:T(8,128)(2,1)} %param.7) | copy-start | bytes 3932164
  9.2 17.9 %copy-start.7 = (bf16[3,320,320]{2,1,0:T(8,128)(2,1)S(1)}, bf16[3,320,320]{2,1,0:T(8,128)(2,1)}, u32[]{:S(2)}) copy-start(bf16[3,320,320]{2,1,0:T(8,128)(2,1)} %kernel_ref.4) | copy-start | bytes 1843204
  9.2 17.9 %collective-permute-start.3 = (bf16[32,5120]{1,0:T(8,128)(2,1)S(1)}, bf16[32,5120]{1,0:T(8,128)(2,1)S(1)}, u32[]{:S(2)}, u32[]{:S(2)}) collective-permute-start(bf16[32,5120]{1,0:T(8,128)(2,1)S(1)} %get-tuple-element.56), channel_id=1, source_target_pairs={{2,0},{4,2},{6,4},{3,1},{5,3},{7,5},{10,8},{12,10},{14,12},{11,9},... | collective-permute-start | bytes 983048 | tf_op jit(solution)/shard_map/ppermute | solution.py:583
  20.6 1.3 %collective-permute-start.4 = (f32[8,640]{1,0:T(8,128)S(1)}, f32[8,640]{1,0:T(8,128)S(1)}, u32[]{:S(2)}, u32[]{:S(2)}) collective-permute-start(f32[8,640]{1,0:T(8,128)S(1)} %get-tuple-element.30), channel_id=1, source_target_pairs={{0,1},{1,0},{2,3},{3,2},{4,5},{5,4},{6,7},{7,6},{8,9},{9,8},{10,11... | collective-permute-start | bytes 61448 | tf_op jit(solution)/shard_map/ppermute | solution.py:533
  21.9 8.5 %collective-permute-start.5 = (f32[8,640]{1,0:T(8,128)S(1)}, f32[8,640]{1,0:T(8,128)S(1)}, u32[]{:S(2)}, u32[]{:S(2)}) collective-permute-start(f32[8,640]{1,0:T(8,128)S(1)} %add.55.refs_0_), channel_id=1, source_target_pairs={{0,2},{2,0},{4,6},{6,4},{1,3},{3,1},{5,7},{7,5},{8,10},{10,8},{12,... | collective-permute-start | bytes 61448 | tf_op jit(solution)/shard_map/ppermute | solution.py:533
  24.5 5.9 %collective-permute-start.6 = (f32[8,640]{1,0:T(8,128)S(1)}, f32[8,640]{1,0:T(8,128)S(1)}, u32[]{:S(2)}, u32[]{:S(2)}) collective-permute-start(f32[8,640]{1,0:T(8,128)S(1)} %add.55.refs_0_), channel_id=1, source_target_pairs={{0,4},{2,6},{4,0},{6,2},{1,5},{3,7},{5,1},{7,3},{8,12},{10,14},{12... | collective-permute-start | bytes 61448 | tf_op jit(solution)/shard_map/ppermute | solution.py:533
  27.1 5.6 %collective-permute-start.7 = (f32[8,640]{1,0:T(8,128)S(1)}, f32[8,640]{1,0:T(8,128)S(1)}, u32[]{:S(2)}, u32[]{:S(2)}) collective-permute-start(f32[8,640]{1,0:T(8,128)S(1)} %add.55.refs_0_), channel_id=1, source_target_pairs={{0,6},{2,4},{4,2},{6,0},{1,7},{3,5},{5,3},{7,1},{8,14},{10,12},{12... | collective-permute-start | bytes 61448 | tf_op jit(solution)/shard_map/ppermute | solution.py:533
  35.2 9.8 %collective-permute-start.8 = (f32[384,384]{1,0:T(8,128)S(1)}, f32[384,384]{1,0:T(8,128)S(1)}, u32[]{:S(2)}, u32[]{:S(2)}) collective-permute-start(f32[384,384]{1,0:T(8,128)S(1)} %get-tuple-element.32), channel_id=1, source_target_pairs={{0,1},{1,0},{2,3},{3,2},{4,5},{5,4},{6,7},{7,6},{8,9},{9,8},{10,11... | collective-permute-start | bytes 1769480 | tf_op jit(solution)/shard_map/ppermute | solution.py:533
  35.3 2.0 %collective-permute-start.9 = (f32[8,640]{1,0:T(8,128)S(1)}, f32[8,640]{1,0:T(8,128)S(1)}, u32[]{:S(2)}, u32[]{:S(2)}) collective-permute-start(f32[8,640]{1,0:T(8,128)S(1)} %get-tuple-element.35), channel_id=1, source_target_pairs={{0,1},{1,0},{2,3},{3,2},{4,5},{5,4},{6,7},{7,6},{8,9},{9,8},{10,11... | collective-permute-start | bytes 61448 | tf_op jit(solution)/shard_map/ppermute | solution.py:533
  37.3 7.3 %collective-permute-start.10 = (f32[8,640]{1,0:T(8,128)S(1)}, f32[8,640]{1,0:T(8,128)S(1)}, u32[]{:S(2)}, u32[]{:S(2)}) collective-permute-start(f32[8,640]{1,0:T(8,128)S(1)} %add.56.refs_4_), channel_id=1, source_target_pairs={{0,2},{2,0},{4,6},{6,4},{1,3},{3,1},{5,7},{7,5},{8,10},{10,8},{12,... | collective-permute-start | bytes 61448 | tf_op jit(solution)/shard_map/ppermute | solution.py:533
  37.3 7.3 %collective-permute-start.11 = (f32[8,640]{1,0:T(8,128)S(1)}, f32[8,640]{1,0:T(8,128)S(1)}, u32[]{:S(2)}, u32[]{:S(2)}) collective-permute-start(f32[8,640]{1,0:T(8,128)S(1)} %add.56.refs_4_), channel_id=1, source_target_pairs={{0,4},{2,6},{4,0},{6,2},{1,5},{3,7},{5,1},{7,3},{8,12},{10,14},{12... | collective-permute-start | bytes 61448 | tf_op jit(solution)/shard_map/ppermute | solution.py:533
  39.4 5.6 %collective-permute-start.12 = (f32[8,640]{1,0:T(8,128)S(1)}, f32[8,640]{1,0:T(8,128)S(1)}, u32[]{:S(2)}, u32[]{:S(2)}) collective-permute-start(f32[8,640]{1,0:T(8,128)S(1)} %add.56.refs_4_), channel_id=1, source_target_pairs={{0,6},{2,4},{4,2},{6,0},{1,7},{3,5},{5,3},{7,1},{8,14},{10,12},{12... | collective-permute-start | bytes 61448 | tf_op jit(solution)/shard_map/ppermute | solution.py:533
  55.9 1.1 copy-start.10
  57.0 1.1 copy-start.12
  58.1 3.3 %collective-permute-start.13 = (bf16[4864,128]{1,0:T(8,128)(2,1)}, bf16[4864,128]{1,0:T(8,128)(2,1)}, u32[]{:S(2)}, u32[]{:S(2)}) collective-permute-start(bf16[4864,128]{1,0:T(8,128)(2,1)} %get-tuple-element.37), channel_id=1, source_target_pairs={{0,1},{1,0},{2,3},{3,2},{4,5},{5,4},{6,7},{7,6},{8,9},{9,8},{10,11... | collective-permute-start | bytes 3735560 | tf_op jit(solution)/shard_map/ppermute | solution.py:533
  61.4 5.4 %copy-start.1 = (bf16[1,4,32,5120]{3,2,1,0:T(8,128)(2,1)S(1)}, bf16[1,4,32,5120]{3,2,1,0:T(8,128)(2,1)}, u32[]{:S(2)}) copy-start(bf16[1,4,32,5120]{3,2,1,0:T(8,128)(2,1)} %param.4) | copy-start | bytes 3932164
  61.4 5.4 %copy-start.6 = (bf16[3,3,320,320]{3,2,1,0:T(8,128)(2,1)S(1)}, bf16[3,3,320,320]{3,2,1,0:T(8,128)(2,1)}, u32[]{:S(2)}) copy-start(bf16[3,3,320,320]{3,2,1,0:T(8,128)(2,1)} %kernel_ref.5) | copy-start | bytes 5529604
  61.4 5.4 %copy-start.13 = (bf16[128,5888]{1,0:T(8,128)(2,1)S(1)}, bf16[128,5888]{1,0:T(8,128)(2,1)}, u32[]{:S(2)}) copy-start(bf16[128,5888]{1,0:T(8,128)(2,1)} %copy-done.12) | copy-start | bytes 4521988
  63.2 14.8 %collective-permute-start.14 = (bf16[1216,128]{1,0:T(8,128)(2,1)S(1)}, bf16[1216,128]{1,0:T(8,128)(2,1)S(1)}, u32[]{:S(2)}, u32[]{:S(2)}) collective-permute-start(bf16[1216,128]{1,0:T(8,128)(2,1)S(1)} %get-tuple-element.55), channel_id=1, source_target_pairs={{0,8},{8,0},{16,24},{24,16},{1,9},{9,1},{17,25},{25,17},{2,10},{10... | collective-permute-start | bytes 933896 | tf_op jit(solution)/shard_map/ppermute | solution.py:533
  64.8 15.8 %collective-permute-start.15 = (bf16[1216,128]{1,0:T(8,128)(2,1)S(1)}, bf16[1216,128]{1,0:T(8,128)(2,1)S(1)}, u32[]{:S(2)}, u32[]{:S(2)}) collective-permute-start(bf16[1216,128]{1,0:T(8,128)(2,1)S(1)} %get-tuple-element.54), channel_id=1, source_target_pairs={{0,16},{8,24},{16,0},{24,8},{1,17},{9,25},{17,1},{25,9},{2,18},{10... | collective-permute-start | bytes 933896 | tf_op jit(solution)/shard_map/ppermute | solution.py:533
  66.3 14.3 %collective-permute-start.16 = (bf16[1216,128]{1,0:T(8,128)(2,1)S(1)}, bf16[1216,128]{1,0:T(8,128)(2,1)S(1)}, u32[]{:S(2)}, u32[]{:S(2)}) collective-permute-start(bf16[1216,128]{1,0:T(8,128)(2,1)S(1)} %get-tuple-element.53), channel_id=1, source_target_pairs={{0,24},{8,16},{16,8},{24,0},{1,25},{9,17},{17,9},{25,1},{2,26},{10... | collective-permute-start | bytes 933896 | tf_op jit(solution)/shard_map/ppermute | solution.py:533
  76.5 1.5 %copy-start.8 = (f32[128,5120]{1,0:T(8,128)}, f32[128,5120]{1,0:T(8,128)S(1)}, u32[]{:S(2)}) copy-start(f32[128,5120]{1,0:T(8,128)S(1)} %get-tuple-element.45.grad_ref) | copy-start | bytes 7864324
  78.0 27.7 %copy-start.2 = (bf16[1,4,32,5120]{3,2,1,0:T(8,128)(2,1)S(1)}, bf16[1,4,32,5120]{3,2,1,0:T(8,128)(2,1)}, u32[]{:S(2)}) copy-start(bf16[1,4,32,5120]{3,2,1,0:T(8,128)(2,1)} %param.4) | copy-start | bytes 3932164
  78.0 27.7 %copy-start.4 = (bf16[1,4,32,5120]{3,2,1,0:T(8,128)(2,1)S(1)}, bf16[1,4,32,5120]{3,2,1,0:T(8,128)(2,1)}, u32[]{:S(2)}) copy-start(bf16[1,4,32,5120]{3,2,1,0:T(8,128)(2,1)} %param.7) | copy-start | bytes 3932164
  81.4 4.6 %collective-permute-start.17 = (bf16[304,128]{1,0:T(8,128)(2,1)}, bf16[304,128]{1,0:T(8,128)(2,1)S(1)}, u32[]{:S(2)}, u32[]{:S(2)}) collective-permute-start(bf16[304,128]{1,0:T(8,128)(2,1)} %get-tuple-element.58), channel_id=1, source_target_pairs={{0,2},{2,0},{4,6},{6,4},{1,3},{3,1},{5,7},{7,5},{8,10},{10,8},{12,... | collective-permute-start | bytes 233480 | tf_op jit(solution)/shard_map/ppermute | solution.py:533
  81.4 7.8 %collective-permute-start.18 = (bf16[304,128]{1,0:T(8,128)(2,1)}, bf16[304,128]{1,0:T(8,128)(2,1)S(1)}, u32[]{:S(2)}, u32[]{:S(2)}) collective-permute-start(bf16[304,128]{1,0:T(8,128)(2,1)} %get-tuple-element.60), channel_id=1, source_target_pairs={{0,4},{2,6},{4,0},{6,2},{1,5},{3,7},{5,1},{7,3},{8,12},{10,14},{12... | collective-permute-start | bytes 233480 | tf_op jit(solution)/shard_map/ppermute | solution.py:533
  84.2 6.4 %collective-permute-start.19 = (bf16[304,128]{1,0:T(8,128)(2,1)S(1)}, bf16[304,128]{1,0:T(8,128)(2,1)}, u32[]{:S(2)}, u32[]{:S(2)}) collective-permute-start(bf16[304,128]{1,0:T(8,128)(2,1)S(1)} %get-tuple-element.59), channel_id=1, source_target_pairs={{0,6},{2,4},{4,2},{6,0},{1,7},{3,5},{5,3},{7,1},{8,14},{10,12},{12... | collective-permute-start | bytes 233480 | tf_op jit(solution)/shard_map/ppermute | solution.py:533
  91.6 4.5 %collective-permute-start.20 = (bf16[304,128]{1,0:T(8,128)(2,1)S(1)}, bf16[304,128]{1,0:T(8,128)(2,1)S(1)}, u32[]{:S(2)}, u32[]{:S(2)}) collective-permute-start(bf16[304,128]{1,0:T(8,128)(2,1)S(1)} %get-tuple-element.52), channel_id=1, source_target_pairs={{0,2},{2,0},{4,6},{6,4},{1,3},{3,1},{5,7},{7,5},{8,10},{10,8},{12,... | collective-permute-start | bytes 233480 | tf_op jit(solution)/shard_map/ppermute | solution.py:533
  92.6 13.0 %collective-permute-start.24 = (f32[8,640]{1,0:T(8,128)S(1)}, f32[8,640]{1,0:T(8,128)S(1)}, u32[]{:S(2)}, u32[]{:S(2)}) collective-permute-start(f32[8,640]{1,0:T(8,128)S(1)} %get-tuple-element.46.mine_ref), channel_id=1, source_target_pairs={{0,1},{1,0},{2,3},{3,2},{4,5},{5,4},{6,7},{7,6},{8,9},{9,8},{10,11... | collective-permute-start | bytes 61448 | tf_op jit(solution)/shard_map/ppermute | solution.py:533
  92.6 9.4 %collective-permute-start.21 = (bf16[304,128]{1,0:T(8,128)(2,1)S(1)}, bf16[304,128]{1,0:T(8,128)(2,1)S(1)}, u32[]{:S(2)}, u32[]{:S(2)}) collective-permute-start(bf16[304,128]{1,0:T(8,128)(2,1)S(1)} %get-tuple-element.52), channel_id=1, source_target_pairs={{0,4},{2,6},{4,0},{6,2},{1,5},{3,7},{5,1},{7,3},{8,12},{10,14},{12... | collective-permute-start | bytes 233480 | tf_op jit(solution)/shard_map/ppermute | solution.py:533
  93.9 8.1 %collective-permute-start.22 = (bf16[304,128]{1,0:T(8,128)(2,1)S(1)}, bf16[304,128]{1,0:T(8,128)(2,1)S(1)}, u32[]{:S(2)}, u32[]{:S(2)}) collective-permute-start(bf16[304,128]{1,0:T(8,128)(2,1)S(1)} %get-tuple-element.52), channel_id=1, source_target_pairs={{0,6},{2,4},{4,2},{6,0},{1,7},{3,5},{5,3},{7,1},{8,14},{10,12},{12... | collective-permute-start | bytes 233480 | tf_op jit(solution)/shard_map/ppermute | solution.py:533
  102.1 10.4 %collective-permute-start.23 = (bf16[1216,128]{1,0:T(8,128)(2,1)S(1)}, bf16[1216,128]{1,0:T(8,128)(2,1)S(1)}, u32[]{:S(2)}, u32[]{:S(2)}) collective-permute-start(bf16[1216,128]{1,0:T(8,128)(2,1)S(1)} %constant_dynamic-update-slice_fusion.refs_0_), channel_id=1, source_target_pairs={{0,8},{8,0},{16,24},{24,16},{1,9},{9,1},{17,25},{25,17},{2,10},{10... | collective-permute-start | bytes 933896 | tf_op jit(solution)/shard_map/ppermute | solution.py:533
  103.5 15.1 %collective-permute-start.25 = (bf16[1216,128]{1,0:T(8,128)(2,1)S(1)}, bf16[1216,128]{1,0:T(8,128)(2,1)S(1)}, u32[]{:S(2)}, u32[]{:S(2)}) collective-permute-start(bf16[1216,128]{1,0:T(8,128)(2,1)S(1)} %constant_dynamic-update-slice_fusion.refs_0_), channel_id=1, source_target_pairs={{0,16},{8,24},{16,0},{24,8},{1,17},{9,25},{17,1},{25,9},{2,18},{10... | collective-permute-start | bytes 933896 | tf_op jit(solution)/shard_map/ppermute | solution.py:533
  104.1 14.5 %collective-permute-start.26 = (bf16[1216,128]{1,0:T(8,128)(2,1)S(1)}, bf16[1216,128]{1,0:T(8,128)(2,1)S(1)}, u32[]{:S(2)}, u32[]{:S(2)}) collective-permute-start(bf16[1216,128]{1,0:T(8,128)(2,1)S(1)} %constant_dynamic-update-slice_fusion.refs_0_), channel_id=1, source_target_pairs={{0,24},{8,16},{16,8},{24,0},{1,25},{9,17},{17,9},{25,1},{2,26},{10... | collective-permute-start | bytes 933896 | tf_op jit(solution)/shard_map/ppermute | solution.py:533
  105.6 1.7 %copy-start.9 = (f32[128,5120]{1,0:T(8,128)S(1)}, f32[128,5120]{1,0:T(8,128)}, u32[]{:S(2)}) copy-start(f32[128,5120]{1,0:T(8,128)} %copy-done.8) | copy-start | bytes 7864324
  107.4 1.3 %copy-start.11 = (bf16[128,5120]{1,0:T(8,128)(2,1)S(1)}, bf16[128,5120]{1,0:T(8,128)(2,1)}, u32[]{:S(2)}) copy-start(bf16[128,5120]{1,0:T(8,128)(2,1)} %copy-done.10) | copy-start | bytes 3932164
  112.4 6.7 %collective-permute-start.27 = (bf16[1216,128]{1,0:T(8,128)(2,1)S(1)}, bf16[1216,128]{1,0:T(8,128)(2,1)S(1)}, u32[]{:S(2)}, u32[]{:S(2)}) collective-permute-start(bf16[1216,128]{1,0:T(8,128)(2,1)S(1)} %constant_dynamic-update-slice_fusion.refs_0_), channel_id=1, source_target_pairs={{0,1},{1,0},{2,3},{3,2},{4,5},{5,4},{6,7},{7,6},{8,9},{9,8},{10,11... | collective-permute-start | bytes 933896 | tf_op jit(solution)/shard_map/ppermute | solution.py:533
  112.4 6.7 %collective-permute-start.28 = (bf16[1216,128]{1,0:T(8,128)(2,1)S(1)}, bf16[1216,128]{1,0:T(8,128)(2,1)S(1)}, u32[]{:S(2)}, u32[]{:S(2)}) collective-permute-start(bf16[1216,128]{1,0:T(8,128)(2,1)S(1)} %collective-permute-done.23.refs_1_), channel_id=1, source_target_pairs={{0,1},{1,0},{2,3},{3,2},{4,5},{5,4},{6,7},{7,6},{8,9},{9,8},{10,11... | collective-permute-start | bytes 933896 | tf_op jit(solution)/shard_map/ppermute | solution.py:533
  118.6 1.6 %collective-permute-start.29 = (bf16[1216,128]{1,0:T(8,128)(2,1)S(1)}, bf16[1216,128]{1,0:T(8,128)(2,1)S(1)}, u32[]{:S(2)}, u32[]{:S(2)}) collective-permute-start(bf16[1216,128]{1,0:T(8,128)(2,1)S(1)} %collective-permute-done.25.refs_2_), channel_id=1, source_target_pairs={{0,1},{1,0},{2,3},{3,2},{4,5},{5,4},{6,7},{7,6},{8,9},{9,8},{10,11... | collective-permute-start | bytes 933896 | tf_op jit(solution)/shard_map/ppermute | solution.py:533
  118.6 2.0 %collective-permute-start.30 = (bf16[1216,128]{1,0:T(8,128)(2,1)S(1)}, bf16[1216,128]{1,0:T(8,128)(2,1)S(1)}, u32[]{:S(2)}, u32[]{:S(2)}) collective-permute-start(bf16[1216,128]{1,0:T(8,128)(2,1)S(1)} %collective-permute-done.26.refs_3_), channel_id=1, source_target_pairs={{0,1},{1,0},{2,3},{3,2},{4,5},{5,4},{6,7},{7,6},{8,9},{9,8},{10,11... | collective-permute-start | bytes 933896 | tf_op jit(solution)/shard_map/ppermute | solution.py:533

commit v3 on v2

--- a/solution.py
+++ b/solution.py
@@ -12,12 +12,8 @@
 EPSILON = 1e-05
 F32 = jnp.float32
 BF16 = jnp.bfloat16
-VMEM_LIMIT = 28 * 1024 * 1024
+VMEM_LIMIT = 20 * 1024 * 1024
 CONV_COST = 12_000_000_000
-
-
-def whole(count):
-    return [pl.BlockSpec(memory_space=pltpu.VMEM)] * count
 
 
 def call(body, outs, scratch=(), flops=0, moved=0):
@@ -364,7 +360,9 @@
     sizes, clip_entries, terms, hidden_ref, cot_ref, grad_ref, rim_ref, act_ref, time_ref, *refs
 ):
     clips, sums = refs[:terms], refs[terms : 2 * terms]
-    dtemp_ref, dspat_ref, keep_ref, send_ref, padded, total, packed = refs[2 * terms :]
+    dtemp_ref, dspat_ref = refs[2 * terms : 2 * terms + 2]
+    chunks, (padded, total, packed) = refs[2 * terms + 2 : -3], refs[-3:]
+    count = len(chunks) // 2
     mean, rate = moments(add_up(clips), 1, clip_entries, sizes)
     means = group_totals(add_up(sums), sizes) * (1.0 / clip_entries)
     plain, cross = means[0:1], means[1:2]
@@ -423,13 +421,15 @@
 
     lax.fori_loop(0, sizes.pairs // block, step, 0)
     pack(total, packed, 0, sizes)
-    own, half = packed_rows(3 * channels, sizes), packed.shape[0] // 2
+    own = packed_rows(3 * channels, sizes)
     packed[own : own + time_ref.shape[0], :] = time_ref[...]
     used = own + time_ref.shape[0]
     packed[used:, :] = jnp.zeros((packed.shape[0] - used, 128), F32)
     core = lax.axis_index("col")
-    keep_ref[...] = packed[pl.ds(pl.multiple_of(core * half, 16), half), :]
-    send_ref[...] = packed[pl.ds(pl.multiple_of((1 - core) * half, 16), half), :].astype(BF16)
+    for n in range(count):
+        keep_ref, send_ref = chunks[n], chunks[count + n]
+        keep_ref[...] = packed[chunk_rows(core, n, packed.shape[0], count), :]
+        send_ref[...] = packed[chunk_rows(1 - core, n, packed.shape[0], count), :].astype(BF16)
 
 
 def backward_body(
@@ -496,16 +496,44 @@
     lax.fori_loop(0, sizes.pairs, step, 0)
 
 
+PHASES = ("dp", "seq")
+
+
+def crossed():
+    return lax.axis_size("col") == 2 and lax.axis_size("dp") == lax.axis_size("seq")
+
+
+def place_of(core, phase):
+    place = lax.axis_index(PHASES[phase])
+    if crossed():
+        place = jnp.where(core == 0, place, lax.axis_index(PHASES[1 - phase]))
+    return place
+
+
+def exchange(values, phase, bits):
+    names = ("dp", "seq", "col")
+    dps, seqs, cols = (lax.axis_size(name) for name in names)
+    pairs = []
+    for i in range(dps * seqs * cols):
+        place = [i // (seqs * cols), i // cols % seqs, i % cols]
+        place[phase ^ place[2] if crossed() else phase] ^= bits
+        pairs.append((i, (place[0] * seqs + place[1]) * cols + place[2]))
+    return lax.ppermute(values, names, pairs)
+
+
+def chunk_rows(core, bits, rows, count):
+    chunk = rows // 2 // count
+    start = core * (rows // 2) + (place_of(core, 0) ^ bits) * chunk
+    return pl.ds(pl.multiple_of(start, 16), chunk)
+
+
 def unpack_body(sizes, scale, parts, *refs):
     mine, theirs = refs[:parts], refs[parts : 2 * parts]
     spatial_ref, temporal_ref, packed = refs[2 * parts :]
-    rows = mine[0].shape[0]
-    half = packed.shape[0] // 2
-    core, me = lax.axis_index("col"), lax.axis_index("dp")
-    for s in range(parts):
-        place = (me ^ s) * rows
-        packed[pl.ds(pl.multiple_of(core * half + place, 16), rows), :] = mine[s][...]
-        packed[pl.ds(pl.multiple_of((1 - core) * half + place, 16), rows), :] = theirs[s][...]
+    core = lax.axis_index("col")
+    for n in range(parts):
+        packed[chunk_rows(core, n, packed.shape[0], parts), :] = mine[n][...]
+        packed[chunk_rows(1 - core, n, packed.shape[0], parts), :] = theirs[n][...]
     full = sizes.channels // 128
     at = 0
     for target in (spatial_ref, temporal_ref):
@@ -537,27 +565,29 @@
     return [values] + [swap(values, axis, s) for s in range(1, lax.axis_size(axis))]
 
 
-def scattered(total, axis, beside=None):
-    count = lax.axis_size(axis)
+def added(terms):
+    total = terms[0].astype(F32)
+    for term in terms[1:]:
+        total = total + term.astype(F32)
+    return total
+
+
+def scattered(total, phase):
+    count = lax.axis_size(PHASES[phase])
     rows = total.shape[0] // count
-    me = lax.axis_index(axis)
-    chunks = [lax.dynamic_slice_in_dim(total, (me ^ s) * rows, rows, 0) for s in range(count)]
-    found = [swap(chunks[s].astype(BF16), axis, s) for s in range(1, count)]
-    if beside is not None:
-        found, beside = lax.optimization_barrier((found, beside))
-    total = chunks[0]
-    for chunk in found:
-        total = total + chunk.astype(F32)
-    return total, beside
-
-
-def gathered(chunk, axis):
-    parts = from_all(chunk, axis)
-    me = lax.axis_index(axis)
+    place = place_of(lax.axis_index("col"), phase)
+    chunks = [lax.dynamic_slice_in_dim(total, (place ^ n) * rows, rows, 0) for n in range(count)]
+    return added(chunks[:1] + [exchange(chunks[n].astype(BF16), phase, n) for n in range(1, count)])
+
+
+def gathered(chunk, phase):
+    count = lax.axis_size(PHASES[phase])
+    parts = [chunk] + [exchange(chunk, phase, n) for n in range(1, count)]
+    place = place_of(lax.axis_index("col"), phase)
     rows = chunk.shape[0]
-    out = jnp.zeros((rows * len(parts), chunk.shape[1]), chunk.dtype)
-    for s, part in enumerate(parts):
-        out = lax.dynamic_update_slice_in_dim(out, part, (me ^ s) * rows, 0)
+    out = jnp.zeros((rows * count, chunk.shape[1]), chunk.dtype)
+    for n, part in enumerate(parts):
+        out = lax.dynamic_update_slice_in_dim(out, part, (place ^ n) * rows, 0)
     return out
 
 
@@ -625,15 +655,16 @@
     devices = lax.axis_size("dp") * seqs * cols
     used = packed_rows(3 * channels, sizes) + packed_rows(channels, sizes)
     all_rows = -(-used // (16 * devices)) * 16 * devices
-    half = all_rows // 2
-    dtemp, dspat, keep, send = call(
+    count = lax.axis_size(PHASES[0])
+    chunk = (all_rows // 2 // count, 128)
+    dtemp, dspat, *chunks = call(
         functools.partial(spatial_grad_body, sizes, clip_entries, seqs),
         [
             struct((sizes.pixels, width), BF16),
             struct((sizes.pixels, sizes.padded), BF16),
-            struct((half, 128), F32),
-            struct((half, 128), BF16),
-        ],
+        ]
+        + [struct(chunk, F32)] * count
+        + [struct(chunk, BF16)] * count,
         [
             padded_scratch,
             pltpu.VMEM((3 * channels, 3 * sizes.edge), F32),
@@ -648,15 +679,17 @@
         + [pltpu.VMEM((sizes.edge, 3 * sizes.window), BF16)] * 2,
         flops=CONV_COST,
     )(x, sums, other, dspat, spatial_kernel)
-    total = keep + swap(send, "col", 1).astype(F32)
-    total, (dnormed, mine) = scattered(total, "dp", (dnormed, mine))
-    total, _ = scattered(total, "seq")
+    chunks = [chunks[n] + swap(chunks[count + n], "col", 1).astype(F32) for n in range(count)]
+    found = [exchange(chunks[n].astype(BF16), 0, n) for n in range(1, count)]
+    found, (dnormed, mine) = lax.optimization_barrier((found, (dnormed, mine)))
+    total = scattered(added(chunks[:1] + found), 1)
     theirs = swap(mine, "col", 1)
     grad_latents = call(
         functools.partial(finish_body, sizes, frame_entries), struct((sizes.pixels, width), F32),
         flops=CONV_COST // 3,
     )(x, sums, other, cot, dtemp, dnormed, mine, theirs)
-    parts = from_all(gathered(total.astype(BF16), "seq"), "dp")
+    part = gathered(total.astype(BF16), 1)
+    parts = [part] + [exchange(part, 0, n) for n in range(1, count)]
     parts[1], grad_latents = lax.optimization_barrier((parts[1], grad_latents))
     others = [swap(part, "col", 1) for part in parts]
     spatial_grad, temporal_grad = call(

time: 125 us -> 117 us (0.936)
  waiting for transfers between devices: 29.2 us -> 17.4 us
  local copies, waits for them, and re-layouts: 10.1 us -> 13.4 us
  starting transfers between devices: 34.2 us -> 35.7 us
  other arithmetic: 2.73 us -> 1.36 us
    ppermute x29 -> x20, waiting for transfers between devices: 29.2 us -> 7.8 us  [swap(): return lax.ppermute(values, axis, [(i, i ^ bit) for i in range(count)])]
    ppermute x0 -> x12, starting transfers between devices: none -> 16 us  [exchange(): return lax.ppermute(values, names, pairs)]
    ppermute x29 -> x20, starting transfers between devices: 27.8 us -> 13.4 us  [swap(): return lax.ppermute(values, axis, [(i, i ^ bit) for i in range(count)])]
    ppermute x0 -> x12, waiting for transfers between devices: none -> 9.58 us  [exchange(): return lax.ppermute(values, names, pairs)]
    unnamed x28 -> x30, local copies, waits for them, and re-layouts: 8.06 us -> 12.6 us
    add x2 -> x1, other arithmetic: 1.77 us -> 0.17 us  [added(): total = total + term.astype(F32)]
  transfers between devices with their start and end apart: 31 -> 34, of which waited for: 13 -> 13; matrix products, arithmetic and copies ran while one was open for 1% -> 0% of each run, Pallas kernels for 24% -> 25%
where the time goes in v3:
time: 117 us; the launch traced here: 116 us
  Pallas kernels  46.9 us (40%)
  starting transfers between devices  35.7 us (31%)
  waiting for transfers between devices  17.4 us (15%)
  local copies, waits for them, and re-layouts  13.4 us (11%)
  other arithmetic  1.36 us (1%)
    ppermute x12, starting transfers between devices, exchange(): return lax.ppermute(values, names, pairs)  16 us
    ppermute x20, starting transfers between devices, swap(): return lax.ppermute(values, axis, [(i, i ^ bit) for i in range(count)])  13.4 us
    unnamed x30, local copies, waits for them, and re-layouts  12.6 us
    pallas_call x1, Pallas kernels, shards(): call(functools.partial(spatial_grad_body, sizes, clip_entries, seqs), [st...  10.5 us
    pallas_call x1, Pallas kernels, shards(): call(functools.partial(forward_body, sizes, frame_entries, min(4, sizes.p...  9.89 us
    pallas_call x1, Pallas kernels, shards(): call(functools.partial(backward_body, sizes, frame_entries, min(4, sizes....  9.68 us
    ppermute x12, waiting for transfers between devices, exchange(): return lax.ppermute(values, names, pairs)  9.58 us
    ppermute x20, waiting for transfers between devices, swap(): return lax.ppermute(values, axis, [(i, i ^ bit) for i in range(count)])  7.8 us
  transfers between devices with their start and end apart: 34, of which 13 were waited for; matrix products, arithmetic and copies ran while one was open for 0% of the time, Pallas kernels for 25%

profile of v3, /device:TPU:0, one launch (start us, length us, event | category | flops | bytes accessed | tf_op | source)
XLA Modules:
  0.0 115.7 jit_solution(17428832628952288471)
XLA Ops:
  0.6 1.3 %copy-done = bf16[1,4,32,5120]{3,2,1,0:T(8,128)(2,1)S(1)} copy-done((bf16[1,4,32,5120]{3,2,1,0:T(8,128)(2,1)S(1)}, bf16[1,4,32,5120]{3,2,1,0:T(8,128)(2,1)}, u32[]{:S(2)}) %copy-start) | copy-done | bytes 1310744
  2.0 0.6 shard_map.67
  2.6 0.5 collective-permute-start
  3.1 0.1 collective-permute-start.1
  3.2 0.1 copy-done.2
  3.3 4.9 %collective-permute-start.2 = (bf16[32,5120]{1,0:T(8,128)(2,1)S(1)}, bf16[32,5120]{1,0:T(8,128)(2,1)S(1)}, u32[]{:S(2)}, u32[]{:S(2)}) collective-permute-start(bf16[32,5120]{1,0:T(8,128)(2,1)S(1)} %get-tuple-element.66), channel_id=1, source_target_pairs={{0,2},{2,4},{4,6},{1,3},{3,5},{5,7},{8,10},{10,12},{12,14},{9,11},... | collective-permute-start | bytes 983048 | tf_op jit(solution)/shard_map/ppermute | solution.py:612
  8.3 1.3 %collective-permute-start.3 = (bf16[32,5120]{1,0:T(8,128)(2,1)S(1)}, bf16[32,5120]{1,0:T(8,128)(2,1)S(1)}, u32[]{:S(2)}, u32[]{:S(2)}) collective-permute-start(bf16[32,5120]{1,0:T(8,128)(2,1)S(1)} %get-tuple-element.65), channel_id=1, source_target_pairs={{2,0},{4,2},{6,4},{3,1},{5,3},{7,5},{10,8},{12,10},{14,12},{11,9},... | collective-permute-start | bytes 983048 | tf_op jit(solution)/shard_map/ppermute | solution.py:613
  9.6 1.6 %copy-done.4 = bf16[3,3,320,320]{3,2,1,0:T(8,128)(2,1)S(1)} copy-done((bf16[3,3,320,320]{3,2,1,0:T(8,128)(2,1)S(1)}, bf16[3,3,320,320]{3,2,1,0:T(8,128)(2,1)}, u32[]{:S(2)}) %copy-start.4) | copy-done | bytes 1843224
  11.2 9.9 %shard_map.68 = (bf16[128,5120]{1,0:T(8,128)(2,1)S(1)}, bf16[128,5888]{1,0:T(8,128)(2,1)S(1)}, f32[8,640]{1,0:T(8,128)S(1)}) custom-call(bf16[128,5120]{1,0:T(8,128)(2,1)S(1)} %bitcast.10, f32[8,640]{1,0:T(8,128)S(1)} %get-tuple-element.33.sums_ref, f32[8,640]{1,0:T(8,128)S(1)} %collective-permute-done.other_ref, ...), custom_call_target="tpu_custom_call" | custom-call | flops 12000000000 | tf_op jit(solution)/shard_map/pallas_call | solution.py:622
  21.1 0.1 collective-permute-start.4
  21.2 1.2 %collective-permute-done.4 = f32[8,640]{1,0:T(8,128)S(1)} collective-permute-done((f32[8,640]{1,0:T(8,128)S(1)}, f32[8,640]{1,0:T(8,128)S(1)}, u32[]{:S(2)}, u32[]{:S(2)}) %collective-permute-start.4) | collective-permute-done | bytes 20512 | tf_op jit(solution)/shard_map/ppermute | solution.py:561
  22.4 2.6 %collective-permute-start.5 = (f32[8,640]{1,0:T(8,128)S(1)}, f32[8,640]{1,0:T(8,128)S(1)}, u32[]{:S(2)}, u32[]{:S(2)}) collective-permute-start(f32[8,640]{1,0:T(8,128)S(1)} %add.52.refs_0_), channel_id=1, source_target_pairs={{0,2},{2,0},{4,6},{6,4},{1,3},{3,1},{5,7},{7,5},{8,10},{10,8},{12,... | collective-permute-start | bytes 61448 | tf_op jit(solution)/shard_map/ppermute | solution.py:561
  25.0 2.6 %collective-permute-start.6 = (f32[8,640]{1,0:T(8,128)S(1)}, f32[8,640]{1,0:T(8,128)S(1)}, u32[]{:S(2)}, u32[]{:S(2)}) collective-permute-start(f32[8,640]{1,0:T(8,128)S(1)} %add.52.refs_0_), channel_id=1, source_target_pairs={{0,4},{2,6},{4,0},{6,2},{1,5},{3,7},{5,1},{7,3},{8,12},{10,14},{12... | collective-permute-start | bytes 61448 | tf_op jit(solution)/shard_map/ppermute | solution.py:561
  27.6 3.3 %shard_map.69.dact_ref = f32[128,5120]{1,0:T(8,128)S(1)} custom-call(bf16[128,5120]{1,0:T(8,128)(2,1)S(1)} %bitcast.13, bf16[32,5120]{1,0:T(8,128)(2,1)S(1)} %collective-permute-done.2.before_ref, bf16[32,5120]{1,0:T(8,128)(2,1)S(1)} %collective-permute-done.3.after_ref, bf16[3,320,320]{2,1,0:T(8,128)(2,1)S(1)} %copy-done.6), custom_call_target="tpu_custom_call" | custom-call | flops 4000000000 | tf_op jit(solution)/shard_map/pallas_call | solution.py:629
  30.9 2.3 %collective-permute-done.7.refs_3_ = f32[8,640]{1,0:T(8,128)S(1)} collective-permute-done((f32[8,640]{1,0:T(8,128)S(1)}, f32[8,640]{1,0:T(8,128)S(1)}, u32[]{:S(2)}, u32[]{:S(2)}) %collective-permute-start.7) | collective-permute-done | bytes 20512 | tf_op jit(solution)/shard_map/ppermute | solution.py:561
  33.2 2.5 %shard_map.70 = (bf16[128,5120]{1,0:T(8,128)(2,1)S(1)}, f32[128,5120]{1,0:T(8,128)S(1)}, f32[8,640]{1,0:T(8,128)S(1)}, f32[384,384]{1,0:T(8,128)S(1)}) custom-call(bf16[128,5120]{1,0:T(8,128)(2,1)S(1)} %get-tuple-element.35.hidden_ref, bf16[128,5120]{1,0:T(8,128)(2,1)S(1)} %bitcast.14, f32[128,5120]{1,0:T(8,128)S(1)} %shard_map.69.dact_ref, ...), custom_call_target="tpu_custom_call" | custom-call | flops 4000000000 | tf_op jit(solution)/shard_map/pallas_call | solution.py:635
  35.7 0.1 collective-permute-start.8
  35.8 0.5 collective-permute-start.9
  36.3 1.5 %collective-permute-done.9 = f32[8,640]{1,0:T(8,128)S(1)} collective-permute-done((f32[8,640]{1,0:T(8,128)S(1)}, f32[8,640]{1,0:T(8,128)S(1)}, u32[]{:S(2)}, u32[]{:S(2)}) %collective-permute-start.9) | collective-permute-done | bytes 20512 | tf_op jit(solution)/shard_map/ppermute | solution.py:561
  37.8 2.1 %collective-permute-start.11 = (f32[8,640]{1,0:T(8,128)S(1)}, f32[8,640]{1,0:T(8,128)S(1)}, u32[]{:S(2)}, u32[]{:S(2)}) collective-permute-start(f32[8,640]{1,0:T(8,128)S(1)} %add.53.refs_4_), channel_id=1, source_target_pairs={{0,4},{2,6},{4,0},{6,2},{1,5},{3,7},{5,1},{7,3},{8,12},{10,14},{12... | collective-permute-start | bytes 61448 | tf_op jit(solution)/shard_map/ppermute | solution.py:561
  39.9 2.3 %collective-permute-start.12 = (f32[8,640]{1,0:T(8,128)S(1)}, f32[8,640]{1,0:T(8,128)S(1)}, u32[]{:S(2)}, u32[]{:S(2)}) collective-permute-start(f32[8,640]{1,0:T(8,128)S(1)} %add.53.refs_4_), channel_id=1, source_target_pairs={{0,6},{2,4},{4,2},{6,0},{1,7},{3,5},{5,3},{7,1},{8,14},{10,12},{12... | collective-permute-start | bytes 61448 | tf_op jit(solution)/shard_map/ppermute | solution.py:561
  42.2 2.9 %shard_map.71.time_ref = f32[2400,128]{1,0:T(8,128)S(1)} custom-call(bf16[128,5120]{1,0:T(8,128)(2,1)S(1)} %get-tuple-element.40.act_ref, bf16[128,5120]{1,0:T(8,128)(2,1)S(1)} %bitcast.15, bf16[32,5120]{1,0:T(8,128)(2,1)S(1)} %collective-permute-done.2.before_ref, bf16[32,5120]{1,0:T(8,128)(2,1)S(1)} %collective-permute-done.3.after_ref), custom_call_target="tpu_custom_call" | custom-call | flops 4000000000 | tf_op jit(solution)/shard_map/pallas_call | solution.py:648
  45.1 0.3 collective-permute-done.12.refs_7_
  45.5 10.5 %shard_map.72 = (bf16[128,5120]{1,0:T(8,128)(2,1)S(1)}, bf16[128,5888]{1,0:T(8,128)(2,1)S(1)}, f32[1216,128]{1,0:T(8,128)S(1)}, f32[1216,128]{1,0:T(8,128)S(1)},...) custom-call(bf16[128,5120]{1,0:T(8,128)(2,1)S(1)} %get-tuple-element, ...), custom_call_target="tpu_custom_call" | custom-call | flops 12000000000 | tf_op jit(solution)/shard_map/pallas_call | solution.py:660
  56.0 0.7 copy-done.7
  56.8 0.7 copy-done.8
  57.5 1.1 copy-done.11
  58.6 1.1 copy-done.13
  59.7 0.5 collective-permute-start.16
  60.2 0.5 collective-permute-start.13
  60.7 0.8 collective-permute-done.18
  61.5 0.1 add_convert_fusion
  61.6 2.5 %collective-permute-start.19 = (bf16[1216,128]{1,0:T(8,128)(2,1)S(1)}, bf16[1216,128]{1,0:T(8,128)(2,1)S(1)}, u32[]{:S(2)}, u32[]{:S(2)}) collective-permute-start(bf16[1216,128]{1,0:T(8,128)(2,1)S(1)} %add_convert_fusion), channel_id=1, source_target_pairs={{0,24},{1,7},{2,26},{3,5},{4,28},{5,3},{6,30},{7,1},{8,16},{9,15},... | collective-permute-start | bytes 933896 | tf_op jit(solution)/shard_map/ppermute | solution.py:521
  64.2 0.6 collective-permute-start.17
  64.8 0.6 collective-permute-start.15
  65.4 1.4 %copy-done.14 = bf16[128,5888]{1,0:T(8,128)(2,1)S(1)} copy-done((bf16[128,5888]{1,0:T(8,128)(2,1)S(1)}, bf16[128,5888]{1,0:T(8,128)(2,1)}, u32[]{:S(2)}) %copy-start.14) | copy-done | bytes 1507352
  66.8 9.7 %shard_map.73 = (f32[128,5120]{1,0:T(8,128)S(1)}, f32[8,640]{1,0:T(8,128)S(1)}) custom-call(bf16[128,5120]{1,0:T(8,128)(2,1)S(1)} %bitcast.11, f32[8,640]{1,0:T(8,128)S(1)} %get-tuple-element.33.sums_ref, f32[8,640]{1,0:T(8,128)S(1)} %collective-permute-done.other_ref, bf16[128,5888]{1,0:T(8,128)(2,1)S(1)} %copy-done.14, bf16[3,3,320,320]{3,2,1,0:T(8,128)(2,1)S(1)} %copy-done.5), custom_call_target="tpu_custom_call" | custom-call | flops 12000000000 | tf_op jit(solution)/shard_map/pallas_call | solution.py:675
  76.5 1.5 %copy-done.9 = f32[128,5120]{1,0:T(8,128)} copy-done((f32[128,5120]{1,0:T(8,128)}, f32[128,5120]{1,0:T(8,128)S(1)}, u32[]{:S(2)}) %copy-start.9) | copy-done | bytes 2621464
  78.0 0.2 convert_add_fusion
  78.2 0.7 dynamic-slice_convert_fusion.2
  78.9 2.8 %collective-permute-start.21 = (bf16[304,128]{1,0:T(8,128)(2,1)}, bf16[304,128]{1,0:T(8,128)(2,1)}, u32[]{:S(2)}, u32[]{:S(2)}) collective-permute-start(bf16[304,128]{1,0:T(8,128)(2,1)} %get-tuple-element.69), channel_id=1, source_target_pairs={{0,4},{1,17},{2,6},{3,19},{4,0},{5,21},{6,2},{7,23},{8,12},{9,25},... | collective-permute-start | bytes 233480 | tf_op jit(solution)/shard_map/ppermute | solution.py:521
  81.7 1.5 %collective-permute-start.22 = (bf16[304,128]{1,0:T(8,128)(2,1)S(1)}, bf16[304,128]{1,0:T(8,128)(2,1)}, u32[]{:S(2)}, u32[]{:S(2)}) collective-permute-start(bf16[304,128]{1,0:T(8,128)(2,1)S(1)} %get-tuple-element.68), channel_id=1, source_target_pairs={{0,6},{1,25},{2,4},{3,27},{4,2},{5,29},{6,0},{7,31},{8,14},{9,17},... | collective-permute-start | bytes 233480 | tf_op jit(solution)/shard_map/ppermute | solution.py:521
  83.3 0.2 collective-permute-done.20
  83.5 1.0 collective-permute-done.21
  84.5 3.5 %collective-permute-done.22 = bf16[304,128]{1,0:T(8,128)(2,1)} collective-permute-done((bf16[304,128]{1,0:T(8,128)(2,1)S(1)}, bf16[304,128]{1,0:T(8,128)(2,1)}, u32[]{:S(2)}, u32[]{:S(2)}) %collective-permute-start.22) | collective-permute-done | bytes 77856 | tf_op jit(solution)/shard_map/ppermute | solution.py:521
  88.1 1.0 constant_dynamic-update-slice_fusion.3
  89.1 0.1 collective-permute-start.23
  89.2 0.1 collective-permute-start.27
  89.2 2.0 %collective-permute-start.24 = (bf16[304,128]{1,0:T(8,128)(2,1)S(1)}, bf16[304,128]{1,0:T(8,128)(2,1)S(1)}, u32[]{:S(2)}, u32[]{:S(2)}) collective-permute-start(bf16[304,128]{1,0:T(8,128)(2,1)S(1)} %get-tuple-element.64), channel_id=1, source_target_pairs={{0,4},{1,17},{2,6},{3,19},{4,0},{5,21},{6,2},{7,23},{8,12},{9,25},... | collective-permute-start | bytes 233480 | tf_op jit(solution)/shard_map/ppermute | solution.py:521
  91.3 2.3 %collective-permute-start.25 = (bf16[304,128]{1,0:T(8,128)(2,1)S(1)}, bf16[304,128]{1,0:T(8,128)(2,1)S(1)}, u32[]{:S(2)}, u32[]{:S(2)}) collective-permute-start(bf16[304,128]{1,0:T(8,128)(2,1)S(1)} %get-tuple-element.64), channel_id=1, source_target_pairs={{0,6},{1,25},{2,4},{3,27},{4,2},{5,29},{6,0},{7,31},{8,14},{9,17},... | collective-permute-start | bytes 233480 | tf_op jit(solution)/shard_map/ppermute | solution.py:521
  93.6 1.0 collective-permute-done.24
  94.6 2.8 %collective-permute-done.25 = bf16[304,128]{1,0:T(8,128)(2,1)S(1)} collective-permute-done((bf16[304,128]{1,0:T(8,128)(2,1)S(1)}, bf16[304,128]{1,0:T(8,128)(2,1)S(1)}, u32[]{:S(2)}, u32[]{:S(2)}) %collective-permute-start.25) | collective-permute-done | bytes 77856 | tf_op jit(solution)/shard_map/ppermute | solution.py:521
  97.5 1.6 %collective-permute-start.26 = (bf16[1216,128]{1,0:T(8,128)(2,1)S(1)}, bf16[1216,128]{1,0:T(8,128)(2,1)S(1)}, u32[]{:S(2)}, u32[]{:S(2)}) collective-permute-start(bf16[1216,128]{1,0:T(8,128)(2,1)S(1)} %constant_dynamic-update-slice_fusion.refs_0_), channel_id=1, source_target_pairs={{0,8},{1,3},{2,10},{3,1},{4,12},{5,7},{6,14},{7,5},{8,0},{9,11},{1... | collective-permute-start | bytes 933896 | tf_op jit(solution)/shard_map/ppermute | solution.py:521
  99.0 1.5 %collective-permute-start.28 = (bf16[1216,128]{1,0:T(8,128)(2,1)S(1)}, bf16[1216,128]{1,0:T(8,128)(2,1)S(1)}, u32[]{:S(2)}, u32[]{:S(2)}) collective-permute-start(bf16[1216,128]{1,0:T(8,128)(2,1)S(1)} %constant_dynamic-update-slice_fusion.refs_0_), channel_id=1, source_target_pairs={{0,16},{1,5},{2,18},{3,7},{4,20},{5,1},{6,22},{7,3},{8,24},{9,13},... | collective-permute-start | bytes 933896 | tf_op jit(solution)/shard_map/ppermute | solution.py:521
  100.6 0.5 collective-permute-start.29
  101.0 1.7 %copy-done.10 = f32[128,5120]{1,0:T(8,128)S(1)} copy-done((f32[128,5120]{1,0:T(8,128)S(1)}, f32[128,5120]{1,0:T(8,128)}, u32[]{:S(2)}) %copy-start.10) | copy-done | bytes 2621464
  102.8 1.3 %copy-done.12 = bf16[128,5120]{1,0:T(8,128)(2,1)S(1)} copy-done((bf16[128,5120]{1,0:T(8,128)(2,1)S(1)}, bf16[128,5120]{1,0:T(8,128)(2,1)}, u32[]{:S(2)}) %copy-start.12) | copy-done | bytes 1310744
  104.1 3.7 %shard_map.74 = f32[128,5120]{1,0:T(8,128)} custom-call(bf16[128,5120]{1,0:T(8,128)(2,1)S(1)} %bitcast.12, f32[8,640]{1,0:T(8,128)S(1)} %get-tuple-element.33.sums_ref, f32[8,640]{1,0:T(8,128)S(1)} %collective-permute-done.other_ref, bf16[128,5120]{1,0:T(8,128)(2,1)S(1)} %bitcast.17, bf16[128,5120]{1,0:T(8,128)(2,1)S(1)} %copy-done.12, ...), custom_call_target="tpu_custom_call" | custom-call | flops 4000000000 | tf_op jit(solution)/shard_map/pallas_call | solution.py:687
  107.8 0.5 collective-permute-start.31
  108.3 0.9 collective-permute-done.28.refs_2_
  109.3 1.0 collective-permute-start.32
  110.3 1.2 %collective-permute-done.32.refs_6_ = bf16[1216,128]{1,0:T(8,128)(2,1)S(1)} collective-permute-done((bf16[1216,128]{1,0:T(8,128)(2,1)S(1)}, bf16[1216,128]{1,0:T(8,128)(2,1)S(1)}, u32[]{:S(2)}, u32[]{:S(2)}) %collective-permute-start.32) | collective-permute-done | bytes 311328 | tf_op jit(solution)/shard_map/ppermute | solution.py:561
  111.5 0.4 collective-permute-done.33.refs_7_
  111.9 3.8 %shard_map.75 = (f32[2880,320]{1,0:T(8,128)}, f32[960,320]{1,0:T(8,128)}) custom-call(bf16[1216,128]{1,0:T(8,128)(2,1)S(1)} %constant_dynamic-update-slice_fusion.refs_0_, bf16[1216,128]{1,0:T(8,128)(2,1)S(1)} %collective-permute-done.26.refs_1_, bf16[1216,128]{1,0:T(8,128)(2,1)S(1)} %collective-permute-done.28.refs_2_, ...), custom_call_target="tpu_custom_call" | custom-call | flops 3000000000 | tf_op jit(solution)/shard_map/pallas_call | solution.py:695
  (56 shorter events, 0.4 us)
Async XLA Ops:
  0.6 1.3 %copy-start = (bf16[1,4,32,5120]{3,2,1,0:T(8,128)(2,1)S(1)}, bf16[1,4,32,5120]{3,2,1,0:T(8,128)(2,1)}, u32[]{:S(2)}) copy-start(bf16[1,4,32,5120]{3,2,1,0:T(8,128)(2,1)} %param.4) | copy-start | bytes 3932164
  1.9 1.3 %copy-start.2 = (bf16[1,4,32,5120]{3,2,1,0:T(8,128)(2,1)S(1)}, bf16[1,4,32,5120]{3,2,1,0:T(8,128)(2,1)}, u32[]{:S(2)}) copy-start(bf16[1,4,32,5120]{3,2,1,0:T(8,128)(2,1)} %param.7) | copy-start | bytes 3932164
  2.6 7.0 %collective-permute-start = (f32[8,640]{1,0:T(8,128)S(1)}, f32[8,640]{1,0:T(8,128)S(1)}, u32[]{:S(2)}, u32[]{:S(2)}) collective-permute-start(f32[8,640]{1,0:T(8,128)S(1)} %get-tuple-element.33.sums_ref), channel_id=1, source_target_pairs={{0,1},{1,0},{2,3},{3,2},{4,5},{5,4},{6,7},{7,6},{8,9},{9,8},{10,11... | collective-permute-start | bytes 61448 | tf_op jit(solution)/shard_map/ppermute | solution.py:561
  3.1 6.5 %collective-permute-start.1 = (bf16[128,384]{1,0:T(8,128)(2,1)S(1)}, bf16[128,384]{1,0:T(8,128)(2,1)S(1)}, u32[]{:S(2)}, u32[]{:S(2)}) collective-permute-start(bf16[128,384]{1,0:T(8,128)(2,1)S(1)} %get-tuple-element.34), channel_id=1, source_target_pairs={{0,1},{1,0},{2,3},{3,2},{4,5},{5,4},{6,7},{7,6},{8,9},{9,8},{10,11... | collective-permute-start | bytes 294920 | tf_op jit(solution)/shard_map/ppermute | solution.py:561
  3.3 24.3 %collective-permute-start.2 = (bf16[32,5120]{1,0:T(8,128)(2,1)S(1)}, bf16[32,5120]{1,0:T(8,128)(2,1)S(1)}, u32[]{:S(2)}, u32[]{:S(2)}) collective-permute-start(bf16[32,5120]{1,0:T(8,128)(2,1)S(1)} %get-tuple-element.66), channel_id=1, source_target_pairs={{0,2},{2,4},{4,6},{1,3},{3,5},{5,7},{8,10},{10,12},{12,14},{9,11},... | collective-permute-start | bytes 983048 | tf_op jit(solution)/shard_map/ppermute | solution.py:612
  8.3 19.3 %collective-permute-start.3 = (bf16[32,5120]{1,0:T(8,128)(2,1)S(1)}, bf16[32,5120]{1,0:T(8,128)(2,1)S(1)}, u32[]{:S(2)}, u32[]{:S(2)}) collective-permute-start(bf16[32,5120]{1,0:T(8,128)(2,1)S(1)} %get-tuple-element.65), channel_id=1, source_target_pairs={{2,0},{4,2},{6,4},{3,1},{5,3},{7,5},{10,8},{12,10},{14,12},{11,9},... | collective-permute-start | bytes 983048 | tf_op jit(solution)/shard_map/ppermute | solution.py:613
  9.6 1.6 %copy-start.4 = (bf16[3,3,320,320]{3,2,1,0:T(8,128)(2,1)S(1)}, bf16[3,3,320,320]{3,2,1,0:T(8,128)(2,1)}, u32[]{:S(2)}) copy-start(bf16[3,3,320,320]{3,2,1,0:T(8,128)(2,1)} %kernel_ref.5) | copy-start | bytes 5529604
  11.2 16.4 %copy-start.6 = (bf16[3,320,320]{2,1,0:T(8,128)(2,1)S(1)}, bf16[3,320,320]{2,1,0:T(8,128)(2,1)}, u32[]{:S(2)}) copy-start(bf16[3,320,320]{2,1,0:T(8,128)(2,1)} %kernel_ref.4) | copy-start | bytes 1843204
  21.1 1.3 %collective-permute-start.4 = (f32[8,640]{1,0:T(8,128)S(1)}, f32[8,640]{1,0:T(8,128)S(1)}, u32[]{:S(2)}, u32[]{:S(2)}) collective-permute-start(f32[8,640]{1,0:T(8,128)S(1)} %get-tuple-element.36), channel_id=1, source_target_pairs={{0,1},{1,0},{2,3},{3,2},{4,5},{5,4},{6,7},{7,6},{8,9},{9,8},{10,11... | collective-permute-start | bytes 61448 | tf_op jit(solution)/shard_map/ppermute | solution.py:561
  22.4 8.5 %collective-permute-start.5 = (f32[8,640]{1,0:T(8,128)S(1)}, f32[8,640]{1,0:T(8,128)S(1)}, u32[]{:S(2)}, u32[]{:S(2)}) collective-permute-start(f32[8,640]{1,0:T(8,128)S(1)} %add.52.refs_0_), channel_id=1, source_target_pairs={{0,2},{2,0},{4,6},{6,4},{1,3},{3,1},{5,7},{7,5},{8,10},{10,8},{12,... | collective-permute-start | bytes 61448 | tf_op jit(solution)/shard_map/ppermute | solution.py:561
  25.0 5.9 %collective-permute-start.6 = (f32[8,640]{1,0:T(8,128)S(1)}, f32[8,640]{1,0:T(8,128)S(1)}, u32[]{:S(2)}, u32[]{:S(2)}) collective-permute-start(f32[8,640]{1,0:T(8,128)S(1)} %add.52.refs_0_), channel_id=1, source_target_pairs={{0,4},{2,6},{4,0},{6,2},{1,5},{3,7},{5,1},{7,3},{8,12},{10,14},{12... | collective-permute-start | bytes 61448 | tf_op jit(solution)/shard_map/ppermute | solution.py:561
  27.6 5.6 %collective-permute-start.7 = (f32[8,640]{1,0:T(8,128)S(1)}, f32[8,640]{1,0:T(8,128)S(1)}, u32[]{:S(2)}, u32[]{:S(2)}) collective-permute-start(f32[8,640]{1,0:T(8,128)S(1)} %add.52.refs_0_), channel_id=1, source_target_pairs={{0,6},{2,4},{4,2},{6,0},{1,7},{3,5},{5,3},{7,1},{8,14},{10,12},{12... | collective-permute-start | bytes 61448 | tf_op jit(solution)/shard_map/ppermute | solution.py:561
  35.7 9.8 %collective-permute-start.8 = (f32[384,384]{1,0:T(8,128)S(1)}, f32[384,384]{1,0:T(8,128)S(1)}, u32[]{:S(2)}, u32[]{:S(2)}) collective-permute-start(f32[384,384]{1,0:T(8,128)S(1)} %get-tuple-element.38), channel_id=1, source_target_pairs={{0,1},{1,0},{2,3},{3,2},{4,5},{5,4},{6,7},{7,6},{8,9},{9,8},{10,11... | collective-permute-start | bytes 1769480 | tf_op jit(solution)/shard_map/ppermute | solution.py:561
  35.8 2.0 %collective-permute-start.9 = (f32[8,640]{1,0:T(8,128)S(1)}, f32[8,640]{1,0:T(8,128)S(1)}, u32[]{:S(2)}, u32[]{:S(2)}) collective-permute-start(f32[8,640]{1,0:T(8,128)S(1)} %get-tuple-element.41), channel_id=1, source_target_pairs={{0,1},{1,0},{2,3},{3,2},{4,5},{5,4},{6,7},{7,6},{8,9},{9,8},{10,11... | collective-permute-start | bytes 61448 | tf_op jit(solution)/shard_map/ppermute | solution.py:561
  37.8 7.3 %collective-permute-start.10 = (f32[8,640]{1,0:T(8,128)S(1)}, f32[8,640]{1,0:T(8,128)S(1)}, u32[]{:S(2)}, u32[]{:S(2)}) collective-permute-start(f32[8,640]{1,0:T(8,128)S(1)} %add.53.refs_4_), channel_id=1, source_target_pairs={{0,2},{2,0},{4,6},{6,4},{1,3},{3,1},{5,7},{7,5},{8,10},{10,8},{12,... | collective-permute-start | bytes 61448 | tf_op jit(solution)/shard_map/ppermute | solution.py:561
  37.8 7.3 %collective-permute-start.11 = (f32[8,640]{1,0:T(8,128)S(1)}, f32[8,640]{1,0:T(8,128)S(1)}, u32[]{:S(2)}, u32[]{:S(2)}) collective-permute-start(f32[8,640]{1,0:T(8,128)S(1)} %add.53.refs_4_), channel_id=1, source_target_pairs={{0,4},{2,6},{4,0},{6,2},{1,5},{3,7},{5,1},{7,3},{8,12},{10,14},{12... | collective-permute-start | bytes 61448 | tf_op jit(solution)/shard_map/ppermute | solution.py:561
  39.9 5.6 %collective-permute-start.12 = (f32[8,640]{1,0:T(8,128)S(1)}, f32[8,640]{1,0:T(8,128)S(1)}, u32[]{:S(2)}, u32[]{:S(2)}) collective-permute-start(f32[8,640]{1,0:T(8,128)S(1)} %add.53.refs_4_), channel_id=1, source_target_pairs={{0,6},{2,4},{4,2},{6,0},{1,7},{3,5},{5,3},{7,1},{8,14},{10,12},{12... | collective-permute-start | bytes 61448 | tf_op jit(solution)/shard_map/ppermute | solution.py:561
  56.0 0.7 copy-start.7
  56.8 0.7 copy-start.8
  57.5 1.1 copy-start.11
  58.6 1.1 copy-start.13
  59.7 1.8 %collective-permute-start.18 = (bf16[1216,128]{1,0:T(8,128)(2,1)}, bf16[1216,128]{1,0:T(8,128)(2,1)S(1)}, u32[]{:S(2)}, u32[]{:S(2)}) collective-permute-start(bf16[1216,128]{1,0:T(8,128)(2,1)} %get-tuple-element.49), channel_id=1, source_target_pairs={{0,1},{1,0},{2,3},{3,2},{4,5},{5,4},{6,7},{7,6},{8,9},{9,8},{10,11... | collective-permute-start | bytes 933896 | tf_op jit(solution)/shard_map/ppermute | solution.py:561
  59.7 4.4 %collective-permute-start.16 = (bf16[1216,128]{1,0:T(8,128)(2,1)}, bf16[1216,128]{1,0:T(8,128)(2,1)S(1)}, u32[]{:S(2)}, u32[]{:S(2)}) collective-permute-start(bf16[1216,128]{1,0:T(8,128)(2,1)} %copy-done.8), channel_id=1, source_target_pairs={{0,1},{1,0},{2,3},{3,2},{4,5},{5,4},{6,7},{7,6},{8,9},{9,8},{10,11... | collective-permute-start | bytes 933896 | tf_op jit(solution)/shard_map/ppermute | solution.py:561
  60.2 4.6 %collective-permute-start.14 = (bf16[1216,128]{1,0:T(8,128)(2,1)}, bf16[1216,128]{1,0:T(8,128)(2,1)S(1)}, u32[]{:S(2)}, u32[]{:S(2)}) collective-permute-start(bf16[1216,128]{1,0:T(8,128)(2,1)} %copy-done.7), channel_id=1, source_target_pairs={{0,1},{1,0},{2,3},{3,2},{4,5},{5,4},{6,7},{7,6},{8,9},{9,8},{10,11... | collective-permute-start | bytes 933896 | tf_op jit(solution)/shard_map/ppermute | solution.py:561
  60.2 17.8 %collective-permute-start.13 = (bf16[1216,128]{1,0:T(8,128)(2,1)S(1)}, bf16[1216,128]{1,0:T(8,128)(2,1)S(1)}, u32[]{:S(2)}, u32[]{:S(2)}) collective-permute-start(bf16[1216,128]{1,0:T(8,128)(2,1)S(1)} %get-tuple-element.43), channel_id=1, source_target_pairs={{0,1},{1,0},{2,3},{3,2},{4,5},{5,4},{6,7},{7,6},{8,9},{9,8},{10,11... | collective-permute-start | bytes 933896 | tf_op jit(solution)/shard_map/ppermute | solution.py:561
  61.5 3.9 %copy-start.5 = (bf16[3,3,320,320]{3,2,1,0:T(8,128)(2,1)S(1)}, bf16[3,3,320,320]{3,2,1,0:T(8,128)(2,1)}, u32[]{:S(2)}) copy-start(bf16[3,3,320,320]{3,2,1,0:T(8,128)(2,1)} %kernel_ref.5) | copy-start | bytes 5529604
  61.6 3.8 %copy-start.1 = (bf16[1,4,32,5120]{3,2,1,0:T(8,128)(2,1)S(1)}, bf16[1,4,32,5120]{3,2,1,0:T(8,128)(2,1)}, u32[]{:S(2)}) copy-start(bf16[1,4,32,5120]{3,2,1,0:T(8,128)(2,1)} %param.4) | copy-start | bytes 3932164
  61.6 16.4 %collective-permute-start.19 = (bf16[1216,128]{1,0:T(8,128)(2,1)S(1)}, bf16[1216,128]{1,0:T(8,128)(2,1)S(1)}, u32[]{:S(2)}, u32[]{:S(2)}) collective-permute-start(bf16[1216,128]{1,0:T(8,128)(2,1)S(1)} %add_convert_fusion), channel_id=1, source_target_pairs={{0,24},{1,7},{2,26},{3,5},{4,28},{5,3},{6,30},{7,1},{8,16},{9,15},... | collective-permute-start | bytes 933896 | tf_op jit(solution)/shard_map/ppermute | solution.py:521
  64.2 13.8 %collective-permute-start.17 = (bf16[1216,128]{1,0:T(8,128)(2,1)S(1)}, bf16[1216,128]{1,0:T(8,128)(2,1)S(1)}, u32[]{:S(2)}, u32[]{:S(2)}) collective-permute-start(bf16[1216,128]{1,0:T(8,128)(2,1)S(1)} %add_convert_fusion.1), channel_id=1, source_target_pairs={{0,16},{1,5},{2,18},{3,7},{4,20},{5,1},{6,22},{7,3},{8,24},{9,13},... | collective-permute-start | bytes 933896 | tf_op jit(solution)/shard_map/ppermute | solution.py:521
  64.8 13.2 %collective-permute-start.15 = (bf16[1216,128]{1,0:T(8,128)(2,1)S(1)}, bf16[1216,128]{1,0:T(8,128)(2,1)S(1)}, u32[]{:S(2)}, u32[]{:S(2)}) collective-permute-start(bf16[1216,128]{1,0:T(8,128)(2,1)S(1)} %add_convert_fusion.2), channel_id=1, source_target_pairs={{0,8},{1,3},{2,10},{3,1},{4,12},{5,7},{6,14},{7,5},{8,0},{9,11},{1... | collective-permute-start | bytes 933896 | tf_op jit(solution)/shard_map/ppermute | solution.py:521
  65.4 1.4 %copy-start.14 = (bf16[128,5888]{1,0:T(8,128)(2,1)S(1)}, bf16[128,5888]{1,0:T(8,128)(2,1)}, u32[]{:S(2)}) copy-start(bf16[128,5888]{1,0:T(8,128)(2,1)} %copy-done.13) | copy-start | bytes 4521988
  76.5 1.5 %copy-start.9 = (f32[128,5120]{1,0:T(8,128)}, f32[128,5120]{1,0:T(8,128)S(1)}, u32[]{:S(2)}) copy-start(f32[128,5120]{1,0:T(8,128)S(1)} %get-tuple-element.57.grad_ref) | copy-start | bytes 7864324
  78.2 22.8 %copy-start.3 = (bf16[1,4,32,5120]{3,2,1,0:T(8,128)(2,1)S(1)}, bf16[1,4,32,5120]{3,2,1,0:T(8,128)(2,1)}, u32[]{:S(2)}) copy-start(bf16[1,4,32,5120]{3,2,1,0:T(8,128)(2,1)} %param.7) | copy-start | bytes 3932164
  78.9 4.6 %collective-permute-start.20 = (bf16[304,128]{1,0:T(8,128)(2,1)}, bf16[304,128]{1,0:T(8,128)(2,1)S(1)}, u32[]{:S(2)}, u32[]{:S(2)}) collective-permute-start(bf16[304,128]{1,0:T(8,128)(2,1)} %get-tuple-element.67), channel_id=1, source_target_pairs={{0,2},{1,9},{2,0},{3,11},{4,6},{5,13},{6,4},{7,15},{8,10},{9,1},{1... | collective-permute-start | bytes 233480 | tf_op jit(solution)/shard_map/ppermute | solution.py:521
  78.9 5.6 %collective-permute-start.21 = (bf16[304,128]{1,0:T(8,128)(2,1)}, bf16[304,128]{1,0:T(8,128)(2,1)}, u32[]{:S(2)}, u32[]{:S(2)}) collective-permute-start(bf16[304,128]{1,0:T(8,128)(2,1)} %get-tuple-element.69), channel_id=1, source_target_pairs={{0,4},{1,17},{2,6},{3,19},{4,0},{5,21},{6,2},{7,23},{8,12},{9,25},... | collective-permute-start | bytes 233480 | tf_op jit(solution)/shard_map/ppermute | solution.py:521
  81.7 6.3 %collective-permute-start.22 = (bf16[304,128]{1,0:T(8,128)(2,1)S(1)}, bf16[304,128]{1,0:T(8,128)(2,1)}, u32[]{:S(2)}, u32[]{:S(2)}) collective-permute-start(bf16[304,128]{1,0:T(8,128)(2,1)S(1)} %get-tuple-element.68), channel_id=1, source_target_pairs={{0,6},{1,25},{2,4},{3,27},{4,2},{5,29},{6,0},{7,31},{8,14},{9,17},... | collective-permute-start | bytes 233480 | tf_op jit(solution)/shard_map/ppermute | solution.py:521
  89.1 4.5 %collective-permute-start.23 = (bf16[304,128]{1,0:T(8,128)(2,1)S(1)}, bf16[304,128]{1,0:T(8,128)(2,1)S(1)}, u32[]{:S(2)}, u32[]{:S(2)}) collective-permute-start(bf16[304,128]{1,0:T(8,128)(2,1)S(1)} %get-tuple-element.64), channel_id=1, source_target_pairs={{0,2},{1,9},{2,0},{3,11},{4,6},{5,13},{6,4},{7,15},{8,10},{9,1},{1... | collective-permute-start | bytes 233480 | tf_op jit(solution)/shard_map/ppermute | solution.py:521
  89.2 11.9 %collective-permute-start.27 = (f32[8,640]{1,0:T(8,128)S(1)}, f32[8,640]{1,0:T(8,128)S(1)}, u32[]{:S(2)}, u32[]{:S(2)}) collective-permute-start(f32[8,640]{1,0:T(8,128)S(1)} %get-tuple-element.58.mine_ref), channel_id=1, source_target_pairs={{0,1},{1,0},{2,3},{3,2},{4,5},{5,4},{6,7},{7,6},{8,9},{9,8},{10,11... | collective-permute-start | bytes 61448 | tf_op jit(solution)/shard_map/ppermute | solution.py:561
  89.2 5.4 %collective-permute-start.24 = (bf16[304,128]{1,0:T(8,128)(2,1)S(1)}, bf16[304,128]{1,0:T(8,128)(2,1)S(1)}, u32[]{:S(2)}, u32[]{:S(2)}) collective-permute-start(bf16[304,128]{1,0:T(8,128)(2,1)S(1)} %get-tuple-element.64), channel_id=1, source_target_pairs={{0,4},{1,17},{2,6},{3,19},{4,0},{5,21},{6,2},{7,23},{8,12},{9,25},... | collective-permute-start | bytes 233480 | tf_op jit(solution)/shard_map/ppermute | solution.py:521
  91.3 6.2 %collective-permute-start.25 = (bf16[304,128]{1,0:T(8,128)(2,1)S(1)}, bf16[304,128]{1,0:T(8,128)(2,1)S(1)}, u32[]{:S(2)}, u32[]{:S(2)}) collective-permute-start(bf16[304,128]{1,0:T(8,128)(2,1)S(1)} %get-tuple-element.64), channel_id=1, source_target_pairs={{0,6},{1,25},{2,4},{3,27},{4,2},{5,29},{6,0},{7,31},{8,14},{9,17},... | collective-permute-start | bytes 233480 | tf_op jit(solution)/shard_map/ppermute | solution.py:521
  97.5 10.4 %collective-permute-start.26 = (bf16[1216,128]{1,0:T(8,128)(2,1)S(1)}, bf16[1216,128]{1,0:T(8,128)(2,1)S(1)}, u32[]{:S(2)}, u32[]{:S(2)}) collective-permute-start(bf16[1216,128]{1,0:T(8,128)(2,1)S(1)} %constant_dynamic-update-slice_fusion.refs_0_), channel_id=1, source_target_pairs={{0,8},{1,3},{2,10},{3,1},{4,12},{5,7},{6,14},{7,5},{8,0},{9,11},{1... | collective-permute-start | bytes 933896 | tf_op jit(solution)/shard_map/ppermute | solution.py:521
  99.0 10.2 %collective-permute-start.28 = (bf16[1216,128]{1,0:T(8,128)(2,1)S(1)}, bf16[1216,128]{1,0:T(8,128)(2,1)S(1)}, u32[]{:S(2)}, u32[]{:S(2)}) collective-permute-start(bf16[1216,128]{1,0:T(8,128)(2,1)S(1)} %constant_dynamic-update-slice_fusion.refs_0_), channel_id=1, source_target_pairs={{0,16},{1,5},{2,18},{3,7},{4,20},{5,1},{6,22},{7,3},{8,24},{9,13},... | collective-permute-start | bytes 933896 | tf_op jit(solution)/shard_map/ppermute | solution.py:521
  100.6 9.7 %collective-permute-start.29 = (bf16[1216,128]{1,0:T(8,128)(2,1)S(1)}, bf16[1216,128]{1,0:T(8,128)(2,1)S(1)}, u32[]{:S(2)}, u32[]{:S(2)}) collective-permute-start(bf16[1216,128]{1,0:T(8,128)(2,1)S(1)} %constant_dynamic-update-slice_fusion.refs_0_), channel_id=1, source_target_pairs={{0,24},{1,7},{2,26},{3,5},{4,28},{5,3},{6,30},{7,1},{8,16},{9,15},... | collective-permute-start | bytes 933896 | tf_op jit(solution)/shard_map/ppermute | solution.py:521
  101.0 1.7 %copy-start.10 = (f32[128,5120]{1,0:T(8,128)S(1)}, f32[128,5120]{1,0:T(8,128)}, u32[]{:S(2)}) copy-start(f32[128,5120]{1,0:T(8,128)} %copy-done.9) | copy-start | bytes 7864324
  102.8 1.3 %copy-start.12 = (bf16[128,5120]{1,0:T(8,128)(2,1)S(1)}, bf16[128,5120]{1,0:T(8,128)(2,1)}, u32[]{:S(2)}) copy-start(bf16[128,5120]{1,0:T(8,128)(2,1)} %copy-done.11) | copy-start | bytes 3932164
  107.8 2.4 %collective-permute-start.30 = (bf16[1216,128]{1,0:T(8,128)(2,1)S(1)}, bf16[1216,128]{1,0:T(8,128)(2,1)S(1)}, u32[]{:S(2)}, u32[]{:S(2)}) collective-permute-start(bf16[1216,128]{1,0:T(8,128)(2,1)S(1)} %constant_dynamic-update-slice_fusion.refs_0_), channel_id=1, source_target_pairs={{0,1},{1,0},{2,3},{3,2},{4,5},{5,4},{6,7},{7,6},{8,9},{9,8},{10,11... | collective-permute-start | bytes 933896 | tf_op jit(solution)/shard_map/ppermute | solution.py:561
  107.8 2.4 %collective-permute-start.31 = (bf16[1216,128]{1,0:T(8,128)(2,1)S(1)}, bf16[1216,128]{1,0:T(8,128)(2,1)S(1)}, u32[]{:S(2)}, u32[]{:S(2)}) collective-permute-start(bf16[1216,128]{1,0:T(8,128)(2,1)S(1)} %collective-permute-done.26.refs_1_), channel_id=1, source_target_pairs={{0,1},{1,0},{2,3},{3,2},{4,5},{5,4},{6,7},{7,6},{8,9},{9,8},{10,11... | collective-permute-start | bytes 933896 | tf_op jit(solution)/shard_map/ppermute | solution.py:561
  109.3 2.2 %collective-permute-start.32 = (bf16[1216,128]{1,0:T(8,128)(2,1)S(1)}, bf16[1216,128]{1,0:T(8,128)(2,1)S(1)}, u32[]{:S(2)}, u32[]{:S(2)}) collective-permute-start(bf16[1216,128]{1,0:T(8,128)(2,1)S(1)} %collective-permute-done.28.refs_2_), channel_id=1, source_target_pairs={{0,1},{1,0},{2,3},{3,2},{4,5},{5,4},{6,7},{7,6},{8,9},{9,8},{10,11... | collective-permute-start | bytes 933896 | tf_op jit(solution)/shard_map/ppermute | solution.py:561
  110.2 1.7 %collective-permute-start.33 = (bf16[1216,128]{1,0:T(8,128)(2,1)S(1)}, bf16[1216,128]{1,0:T(8,128)(2,1)S(1)}, u32[]{:S(2)}, u32[]{:S(2)}) collective-permute-start(bf16[1216,128]{1,0:T(8,128)(2,1)S(1)} %collective-permute-done.29.refs_3_), channel_id=1, source_target_pairs={{0,1},{1,0},{2,3},{3,2},{4,5},{5,4},{6,7},{7,6},{8,9},{9,8},{10,11... | collective-permute-start | bytes 933896 | tf_op jit(solution)/shard_map/ppermute | solution.py:561

commit v4 on v3

--- a/solution.py
+++ b/solution.py
@@ -13,16 +13,17 @@
 F32 = jnp.float32
 BF16 = jnp.bfloat16
 VMEM_LIMIT = 20 * 1024 * 1024
+SMALL_LIMIT = 4 * 1024 * 1024
 CONV_COST = 12_000_000_000
 
 
-def call(body, outs, scratch=(), flops=0, moved=0):
+def call(body, outs, scratch=(), flops=0, moved=0, limit=VMEM_LIMIT):
     return pl.pallas_call(
         body,
         out_shape=outs,
         out_specs=jax.tree.map(lambda _: pl.BlockSpec(memory_space=pltpu.VMEM), outs),
         scratch_shapes=list(scratch),
-        compiler_params=pltpu.CompilerParams(vmem_limit_bytes=VMEM_LIMIT),
+        compiler_params=pltpu.CompilerParams(vmem_limit_bytes=limit),
         cost_estimate=pl.CostEstimate(flops=flops, bytes_accessed=moved, transcendentals=0),
     )
 
@@ -572,23 +573,41 @@
     return total
 
 
-def scattered(total, phase):
+def place_rows(phase, bits, rows):
+    place = place_of(lax.axis_index("col"), phase)
+    return pl.ds(pl.multiple_of((place ^ bits) * rows, 16), rows)
+
+
+def split_body(phase, terms, *refs):
+    for bits, target in enumerate(refs[terms:]):
+        rows = place_rows(phase, bits, target.shape[0])
+        target[...] = added([ref[rows, :] for ref in refs[:terms]]).astype(target.dtype)
+
+
+def scattered(terms, phase):
     count = lax.axis_size(PHASES[phase])
-    rows = total.shape[0] // count
-    place = place_of(lax.axis_index("col"), phase)
-    chunks = [lax.dynamic_slice_in_dim(total, (place ^ n) * rows, rows, 0) for n in range(count)]
-    return added(chunks[:1] + [exchange(chunks[n].astype(BF16), phase, n) for n in range(1, count)])
+    chunk = (terms[0].shape[0] // count, terms[0].shape[1])
+    own, *others = call(
+        functools.partial(split_body, phase, len(terms)),
+        [struct(chunk, F32)] + [struct(chunk, BF16)] * (count - 1),
+        limit=SMALL_LIMIT,
+    )(*terms)
+    return [own] + [exchange(values, phase, n + 1) for n, values in enumerate(others)]
+
+
+def gather_body(phase, *refs):
+    for bits, part in enumerate(refs[:-1]):
+        refs[-1][place_rows(phase, bits, part.shape[0]), :] = part[...]
 
 
 def gathered(chunk, phase):
     count = lax.axis_size(PHASES[phase])
     parts = [chunk] + [exchange(chunk, phase, n) for n in range(1, count)]
-    place = place_of(lax.axis_index("col"), phase)
-    rows = chunk.shape[0]
-    out = jnp.zeros((rows * count, chunk.shape[1]), chunk.dtype)
-    for n, part in enumerate(parts):
-        out = lax.dynamic_update_slice_in_dim(out, part, (place ^ n) * rows, 0)
-    return out
+    return call(
+        functools.partial(gather_body, phase),
+        struct((chunk.shape[0] * count, chunk.shape[1]), chunk.dtype),
+        limit=SMALL_LIMIT,
+    )(*parts)
 
 
 def shards(latents, spatial_kernel, temporal_kernel, cotangent):
@@ -672,6 +691,10 @@
         ],
         flops=CONV_COST,
     )(hidden, cot, tgrad, rims, act, temporal_grad, *clips, *means)
+    chunks = [chunks[n] + swap(chunks[count + n], "col", 1).astype(F32) for n in range(count)]
+    sends = [values.astype(BF16) for values in chunks[1:]]
+    sends, dspat = lax.optimization_barrier((sends, dspat))
+    found = [exchange(values, 0, n + 1) for n, values in enumerate(sends)]
     dnormed, mine = call(
         functools.partial(backward_body, sizes, frame_entries, min(4, sizes.pairs)),
         [struct((sizes.pixels, width), F32), frame_shape],
@@ -679,10 +702,8 @@
         + [pltpu.VMEM((sizes.edge, 3 * sizes.window), BF16)] * 2,
         flops=CONV_COST,
     )(x, sums, other, dspat, spatial_kernel)
-    chunks = [chunks[n] + swap(chunks[count + n], "col", 1).astype(F32) for n in range(count)]
-    found = [exchange(chunks[n].astype(BF16), 0, n) for n in range(1, count)]
     found, (dnormed, mine) = lax.optimization_barrier((found, (dnormed, mine)))
-    total = scattered(added(chunks[:1] + found), 1)
+    total = added(scattered(chunks[:1] + found, 1))
     theirs = swap(mine, "col", 1)
     grad_latents = call(
         functools.partial(finish_body, sizes, frame_entries), struct((sizes.pixels, width), F32),

time: 117 us -> 106 us (0.906); the launches traced: 116 us -> 106 us
  local copies, waits for them, and re-layouts: 13.4 us -> 3.08 us
  starting transfers between devices: 35.7 us -> 37.3 us
    unnamed x30 -> x12, local copies, waits for them, and re-layouts: 12.6 us -> 3.04 us
    ppermute x12, waiting for transfers between devices: 9.58 us -> 12 us  [exchange(): return lax.ppermute(values, names, pairs)]
    ppermute x20, waiting for transfers between devices: 7.8 us -> 6.16 us  [swap(): return lax.ppermute(values, axis, [(i, i ^ bit) for i in range(count)])]
  transfers between devices with their start and end apart: 34 -> 34, of which waited for: 13 -> 12; matrix products, arithmetic and copies ran while one was open for 0% -> 0% of each run, Pallas kernels for 25% -> 28%
where the time goes in v4:
time: 106 us
  Pallas kernels  46.2 us (44%)
  starting transfers between devices  37.3 us (35%)
  waiting for transfers between devices  18.1 us (17%)
  local copies, waits for them, and re-layouts  3.08 us (3%)
    ppermute x12, starting transfers between devices, exchange(): return lax.ppermute(values, names, pairs)  16 us
    ppermute x20, starting transfers between devices, swap(): return lax.ppermute(values, axis, [(i, i ^ bit) for i in range(count)])  14.4 us
    ppermute x12, waiting for transfers between devices, exchange(): return lax.ppermute(values, names, pairs)  12 us
    pallas_call x1, Pallas kernels, shards(): call(functools.partial(forward_body, sizes, frame_entries, min(4, sizes.p...  9.89 us
    pallas_call x1, Pallas kernels, shards(): call(functools.partial(spatial_grad_body, sizes, clip_entries, seqs), [st...  9.83 us
    pallas_call x1, Pallas kernels, shards(): call(functools.partial(backward_body, sizes, frame_entries, min(4, sizes....  9.46 us
    ppermute x20, waiting for transfers between devices, swap(): return lax.ppermute(values, axis, [(i, i ^ bit) for i in range(count)])  6.16 us
    ppermute x1, starting transfers between devices, shards(): before = lax.ppermute(cot[sizes.pixels - rows:], 'seq', forth)  5.58 us
  transfers between devices with their start and end apart: 34, of which 12 were waited for; matrix products, arithmetic and copies ran while one was open for 0% of the time, Pallas kernels for 28%

profile of v4, /device:TPU:0, one launch (start us, length us, event | category | flops | bytes accessed | tf_op | source)
XLA Modules:
  0.0 105.9 jit_solution(17486057765934635196)
XLA Ops:
  0.6 0.0 copy-start
  0.6 1.3 %copy-done = bf16[1,4,32,5120]{3,2,1,0:T(8,128)(2,1)S(1)} copy-done((bf16[1,4,32,5120]{3,2,1,0:T(8,128)(2,1)S(1)}, bf16[1,4,32,5120]{3,2,1,0:T(8,128)(2,1)}, u32[]{:S(2)}) %copy-start) | copy-done | bytes 1310744
  2.0 0.6 shard_map.67
  2.6 0.5 collective-permute-start
  3.1 0.1 collective-permute-start.1
  3.2 0.1 copy-done.2
  3.3 1.3 %collective-permute-start.3 = (bf16[32,5120]{1,0:T(8,128)(2,1)S(1)}, bf16[32,5120]{1,0:T(8,128)(2,1)S(1)}, u32[]{:S(2)}, u32[]{:S(2)}) collective-permute-start(bf16[32,5120]{1,0:T(8,128)(2,1)S(1)} %get-tuple-element.79), channel_id=1, source_target_pairs={{2,0},{4,2},{6,4},{3,1},{5,3},{7,5},{10,8},{12,10},{14,12},{11,9},... | collective-permute-start | bytes 983048 | tf_op jit(solution)/shard_map/ppermute | solution.py:632
  4.6 5.6 %collective-permute-start.2 = (bf16[32,5120]{1,0:T(8,128)(2,1)S(1)}, bf16[32,5120]{1,0:T(8,128)(2,1)S(1)}, u32[]{:S(2)}, u32[]{:S(2)}) collective-permute-start(bf16[32,5120]{1,0:T(8,128)(2,1)S(1)} %get-tuple-element.80), channel_id=1, source_target_pairs={{0,2},{2,4},{4,6},{1,3},{3,5},{5,7},{8,10},{10,12},{12,14},{9,11},... | collective-permute-start | bytes 983048 | tf_op jit(solution)/shard_map/ppermute | solution.py:631
  10.2 0.0 collective-permute-done.other_ref
  10.2 0.0 copy-start.3
  10.2 1.6 %copy-done.3 = bf16[3,3,320,320]{3,2,1,0:T(8,128)(2,1)S(1)} copy-done((bf16[3,3,320,320]{3,2,1,0:T(8,128)(2,1)S(1)}, bf16[3,3,320,320]{3,2,1,0:T(8,128)(2,1)}, u32[]{:S(2)}) %copy-start.3) | copy-done | bytes 1843224
  11.8 9.9 %shard_map.68 = (bf16[128,5120]{1,0:T(8,128)(2,1)S(1)}, bf16[128,5888]{1,0:T(8,128)(2,1)S(1)}, f32[8,640]{1,0:T(8,128)S(1)}) custom-call(bf16[128,5120]{1,0:T(8,128)(2,1)S(1)} %bitcast.10, f32[8,640]{1,0:T(8,128)S(1)} %get-tuple-element.41.sums_ref, f32[8,640]{1,0:T(8,128)S(1)} %collective-permute-done.other_ref, ...), custom_call_target="tpu_custom_call" | custom-call | flops 12000000000 | tf_op jit(solution)/shard_map/pallas_call | solution.py:641
  21.7 0.1 collective-permute-start.4
  21.8 1.2 %collective-permute-done.4 = f32[8,640]{1,0:T(8,128)S(1)} collective-permute-done((f32[8,640]{1,0:T(8,128)S(1)}, f32[8,640]{1,0:T(8,128)S(1)}, u32[]{:S(2)}, u32[]{:S(2)}) %collective-permute-start.4) | collective-permute-done | bytes 20512 | tf_op jit(solution)/shard_map/ppermute | solution.py:562
  23.0 1.8 %collective-permute-start.7 = (f32[8,640]{1,0:T(8,128)S(1)}, f32[8,640]{1,0:T(8,128)S(1)}, u32[]{:S(2)}, u32[]{:S(2)}) collective-permute-start(f32[8,640]{1,0:T(8,128)S(1)} %add.27.refs_0_), channel_id=1, source_target_pairs={{0,6},{2,4},{4,2},{6,0},{1,7},{3,5},{5,3},{7,1},{8,14},{10,12},{12... | collective-permute-start | bytes 61448 | tf_op jit(solution)/shard_map/ppermute | solution.py:562
  24.8 1.6 %collective-permute-start.6 = (f32[8,640]{1,0:T(8,128)S(1)}, f32[8,640]{1,0:T(8,128)S(1)}, u32[]{:S(2)}, u32[]{:S(2)}) collective-permute-start(f32[8,640]{1,0:T(8,128)S(1)} %add.27.refs_0_), channel_id=1, source_target_pairs={{0,4},{2,6},{4,0},{6,2},{1,5},{3,7},{5,1},{7,3},{8,12},{10,14},{12... | collective-permute-start | bytes 61448 | tf_op jit(solution)/shard_map/ppermute | solution.py:562
  26.5 0.9 collective-permute-start.5
  27.4 3.3 %shard_map.69.dact_ref = f32[128,5120]{1,0:T(8,128)S(1)} custom-call(bf16[128,5120]{1,0:T(8,128)(2,1)S(1)} %bitcast.13, bf16[32,5120]{1,0:T(8,128)(2,1)S(1)} %collective-permute-done.2.before_ref, bf16[32,5120]{1,0:T(8,128)(2,1)S(1)} %collective-permute-done.3.after_ref, bf16[3,320,320]{2,1,0:T(8,128)(2,1)S(1)} %copy-done.5), custom_call_target="tpu_custom_call" | custom-call | flops 4000000000 | tf_op jit(solution)/shard_map/pallas_call | solution.py:648
  30.7 2.3 %shard_map.70 = (bf16[128,5120]{1,0:T(8,128)(2,1)S(1)}, f32[128,5120]{1,0:T(8,128)S(1)}, f32[8,640]{1,0:T(8,128)S(1)}, f32[384,384]{1,0:T(8,128)S(1)}) custom-call(bf16[128,5120]{1,0:T(8,128)(2,1)S(1)} %get-tuple-element.43.hidden_ref, bf16[128,5120]{1,0:T(8,128)(2,1)S(1)} %bitcast.14, f32[128,5120]{1,0:T(8,128)S(1)} %shard_map.69.dact_ref, ...), custom_call_target="tpu_custom_call" | custom-call | flops 4000000000 | tf_op jit(solution)/shard_map/pallas_call | solution.py:654
  33.0 0.1 collective-permute-start.8
  33.1 0.5 collective-permute-start.9
  33.6 1.5 %collective-permute-done.9 = f32[8,640]{1,0:T(8,128)S(1)} collective-permute-done((f32[8,640]{1,0:T(8,128)S(1)}, f32[8,640]{1,0:T(8,128)S(1)}, u32[]{:S(2)}, u32[]{:S(2)}) %collective-permute-start.9) | collective-permute-done | bytes 20512 | tf_op jit(solution)/shard_map/ppermute | solution.py:562
  35.1 2.0 %collective-permute-start.12 = (f32[8,640]{1,0:T(8,128)S(1)}, f32[8,640]{1,0:T(8,128)S(1)}, u32[]{:S(2)}, u32[]{:S(2)}) collective-permute-start(f32[8,640]{1,0:T(8,128)S(1)} %add.28.refs_4_), channel_id=1, source_target_pairs={{0,6},{2,4},{4,2},{6,0},{1,7},{3,5},{5,3},{7,1},{8,14},{10,12},{12... | collective-permute-start | bytes 61448 | tf_op jit(solution)/shard_map/ppermute | solution.py:562
  37.2 0.5 collective-permute-start.11
  37.7 1.8 %collective-permute-start.10 = (f32[8,640]{1,0:T(8,128)S(1)}, f32[8,640]{1,0:T(8,128)S(1)}, u32[]{:S(2)}, u32[]{:S(2)}) collective-permute-start(f32[8,640]{1,0:T(8,128)S(1)} %add.28.refs_4_), channel_id=1, source_target_pairs={{0,2},{2,0},{4,6},{6,4},{1,3},{3,1},{5,7},{7,5},{8,10},{10,8},{12,... | collective-permute-start | bytes 61448 | tf_op jit(solution)/shard_map/ppermute | solution.py:562
  39.5 3.1 %shard_map.71.time_ref = f32[2400,128]{1,0:T(8,128)S(1)} custom-call(bf16[128,5120]{1,0:T(8,128)(2,1)S(1)} %get-tuple-element.48.act_ref, bf16[128,5120]{1,0:T(8,128)(2,1)S(1)} %bitcast.15, bf16[32,5120]{1,0:T(8,128)(2,1)S(1)} %collective-permute-done.2.before_ref, bf16[32,5120]{1,0:T(8,128)(2,1)S(1)} %collective-permute-done.3.after_ref), custom_call_target="tpu_custom_call" | custom-call | flops 4000000000 | tf_op jit(solution)/shard_map/pallas_call | solution.py:667
  42.7 9.8 %shard_map.72 = (bf16[128,5120]{1,0:T(8,128)(2,1)S(1)}, bf16[128,5888]{1,0:T(8,128)(2,1)S(1)}, f32[1216,128]{1,0:T(8,128)S(1)}, f32[1216,128]{1,0:T(8,128)S(1)},...) custom-call(bf16[128,5120]{1,0:T(8,128)(2,1)S(1)} %get-tuple-element, ...), custom_call_target="tpu_custom_call" | custom-call | flops 12000000000 | tf_op jit(solution)/shard_map/pallas_call | solution.py:679
  52.5 0.1 collective-permute-start.14
  52.6 0.5 collective-permute-start.13
  53.1 0.1 collective-permute-start.15
  53.2 0.4 collective-permute-start.16
  53.6 0.6 collective-permute-done.14
  54.2 0.1 add_convert_fusion.2
  54.3 0.0 copy-start.1
  54.3 0.8 collective-permute-done.15
  55.1 0.1 add_convert_fusion.1
  55.2 0.4 collective-permute-done.16
  55.5 0.1 add_convert_fusion
  55.6 2.0 %collective-permute-start.17 = (bf16[1216,128]{1,0:T(8,128)(2,1)S(1)}, bf16[1216,128]{1,0:T(8,128)(2,1)S(1)}, u32[]{:S(2)}, u32[]{:S(2)}) collective-permute-start(bf16[1216,128]{1,0:T(8,128)(2,1)S(1)} %add_convert_fusion.2), channel_id=1, source_target_pairs={{0,8},{1,3},{2,10},{3,1},{4,12},{5,7},{6,14},{7,5},{8,0},{9,11},{1... | collective-permute-start | bytes 933896 | tf_op jit(solution)/shard_map/ppermute | solution.py:522
  57.6 1.5 %collective-permute-start.18 = (bf16[1216,128]{1,0:T(8,128)(2,1)S(1)}, bf16[1216,128]{1,0:T(8,128)(2,1)S(1)}, u32[]{:S(2)}, u32[]{:S(2)}) collective-permute-start(bf16[1216,128]{1,0:T(8,128)(2,1)S(1)} %add_convert_fusion.1), channel_id=1, source_target_pairs={{0,16},{1,5},{2,18},{3,7},{4,20},{5,1},{6,22},{7,3},{8,24},{9,13},... | collective-permute-start | bytes 933896 | tf_op jit(solution)/shard_map/ppermute | solution.py:522
  59.1 0.0 collective-permute-start.19
  59.2 9.5 %shard_map.73 = (f32[128,5120]{1,0:T(8,128)S(1)}, f32[8,640]{1,0:T(8,128)S(1)}) custom-call(bf16[128,5120]{1,0:T(8,128)(2,1)S(1)} %bitcast.11, f32[8,640]{1,0:T(8,128)S(1)} %get-tuple-element.41.sums_ref, f32[8,640]{1,0:T(8,128)S(1)} %collective-permute-done.other_ref, bf16[128,5888]{1,0:T(8,128)(2,1)S(1)} %get-tuple-element.62.dspat_ref, ...), custom_call_target="tpu_custom_call" | custom-call | flops 12000000000 | tf_op jit(solution)/shard_map/pallas_call | solution.py:698
  68.6 0.1 convert_add_fusion.refs_0_
  68.7 0.2 shard_map.74
  68.9 0.7 collective-permute-start.20
  69.6 2.0 %collective-permute-start.21 = (bf16[304,128]{1,0:T(8,128)(2,1)S(1)}, bf16[304,128]{1,0:T(8,128)(2,1)S(1)}, u32[]{:S(2)}, u32[]{:S(2)}) collective-permute-start(bf16[304,128]{1,0:T(8,128)(2,1)S(1)} %get-tuple-element.70), channel_id=1, source_target_pairs={{0,4},{1,17},{2,6},{3,19},{4,0},{5,21},{6,2},{7,23},{8,12},{9,25},... | collective-permute-start | bytes 233480 | tf_op jit(solution)/shard_map/ppermute | solution.py:522
  71.6 1.8 %collective-permute-start.22 = (bf16[304,128]{1,0:T(8,128)(2,1)S(1)}, bf16[304,128]{1,0:T(8,128)(2,1)S(1)}, u32[]{:S(2)}, u32[]{:S(2)}) collective-permute-start(bf16[304,128]{1,0:T(8,128)(2,1)S(1)} %get-tuple-element.71), channel_id=1, source_target_pairs={{0,6},{1,25},{2,4},{3,27},{4,2},{5,29},{6,0},{7,31},{8,14},{9,17},... | collective-permute-start | bytes 233480 | tf_op jit(solution)/shard_map/ppermute | solution.py:522
  73.3 0.0 collective-permute-done.20
  73.4 1.5 %collective-permute-done.21 = bf16[304,128]{1,0:T(8,128)(2,1)S(1)} collective-permute-done((bf16[304,128]{1,0:T(8,128)(2,1)S(1)}, bf16[304,128]{1,0:T(8,128)(2,1)S(1)}, u32[]{:S(2)}, u32[]{:S(2)}) %collective-permute-start.21) | collective-permute-done | bytes 77856 | tf_op jit(solution)/shard_map/ppermute | solution.py:522
  74.9 2.9 %collective-permute-done.22 = bf16[304,128]{1,0:T(8,128)(2,1)S(1)} collective-permute-done((bf16[304,128]{1,0:T(8,128)(2,1)S(1)}, bf16[304,128]{1,0:T(8,128)(2,1)S(1)}, u32[]{:S(2)}, u32[]{:S(2)}) %collective-permute-start.22) | collective-permute-done | bytes 77856 | tf_op jit(solution)/shard_map/ppermute | solution.py:522
  77.8 1.8 %collective-permute-start.25 = (bf16[304,128]{1,0:T(8,128)(2,1)S(1)}, bf16[304,128]{1,0:T(8,128)(2,1)S(1)}, u32[]{:S(2)}, u32[]{:S(2)}) collective-permute-start(bf16[304,128]{1,0:T(8,128)(2,1)S(1)} %add_convert_fusion.3.refs_0_), channel_id=1, source_target_pairs={{0,6},{1,25},{2,4},{3,27},{4,2},{5,29},{6,0},{7,31},{8,14},{9,17},... | collective-permute-start | bytes 233480 | tf_op jit(solution)/shard_map/ppermute | solution.py:522
  79.7 2.6 %collective-permute-start.23 = (bf16[304,128]{1,0:T(8,128)(2,1)S(1)}, bf16[304,128]{1,0:T(8,128)(2,1)S(1)}, u32[]{:S(2)}, u32[]{:S(2)}) collective-permute-start(bf16[304,128]{1,0:T(8,128)(2,1)S(1)} %add_convert_fusion.3.refs_0_), channel_id=1, source_target_pairs={{0,2},{1,9},{2,0},{3,11},{4,6},{5,13},{6,4},{7,15},{8,10},{9,1},{1... | collective-permute-start | bytes 233480 | tf_op jit(solution)/shard_map/ppermute | solution.py:522
  82.3 1.8 %collective-permute-done.25.refs_3_ = bf16[304,128]{1,0:T(8,128)(2,1)S(1)} collective-permute-done((bf16[304,128]{1,0:T(8,128)(2,1)S(1)}, bf16[304,128]{1,0:T(8,128)(2,1)S(1)}, u32[]{:S(2)}, u32[]{:S(2)}) %collective-permute-start.25) | collective-permute-done | bytes 77856 | tf_op jit(solution)/shard_map/ppermute | solution.py:522
  84.1 1.6 %collective-permute-done.24.refs_2_ = bf16[304,128]{1,0:T(8,128)(2,1)S(1)} collective-permute-done((bf16[304,128]{1,0:T(8,128)(2,1)S(1)}, bf16[304,128]{1,0:T(8,128)(2,1)S(1)}, u32[]{:S(2)}, u32[]{:S(2)}) %collective-permute-start.24) | collective-permute-done | bytes 77856 | tf_op jit(solution)/shard_map/ppermute | solution.py:522
  85.8 2.6 %collective-permute-start.29 = (bf16[1216,128]{1,0:T(8,128)(2,1)S(1)}, bf16[1216,128]{1,0:T(8,128)(2,1)S(1)}, u32[]{:S(2)}, u32[]{:S(2)}) collective-permute-start(bf16[1216,128]{1,0:T(8,128)(2,1)S(1)} %shard_map.75.refs_0_), channel_id=1, source_target_pairs={{0,24},{1,7},{2,26},{3,5},{4,28},{5,3},{6,30},{7,1},{8,16},{9,15},... | collective-permute-start | bytes 933896 | tf_op jit(solution)/shard_map/ppermute | solution.py:522
  88.4 0.5 collective-permute-start.28
  88.9 0.5 collective-permute-start.26
  89.3 3.7 %shard_map.76 = f32[128,5120]{1,0:T(8,128)} custom-call(bf16[128,5120]{1,0:T(8,128)(2,1)S(1)} %bitcast.12, f32[8,640]{1,0:T(8,128)S(1)} %get-tuple-element.41.sums_ref, f32[8,640]{1,0:T(8,128)S(1)} %collective-permute-done.other_ref, bf16[128,5120]{1,0:T(8,128)(2,1)S(1)} %bitcast.17, bf16[128,5120]{1,0:T(8,128)(2,1)S(1)} %get-tuple-element.72.dtemp_ref, ...), custom_call_target="tpu_custom_call" | custom-call | flops 4000000000 | tf_op jit(solution)/shard_map/pallas_call | solution.py:708
  93.1 4.1 %collective-permute-done.26.refs_1_ = bf16[1216,128]{1,0:T(8,128)(2,1)S(1)} collective-permute-done((bf16[1216,128]{1,0:T(8,128)(2,1)S(1)}, bf16[1216,128]{1,0:T(8,128)(2,1)S(1)}, u32[]{:S(2)}, u32[]{:S(2)}) %collective-permute-start.26) | collective-permute-done | bytes 311328 | tf_op jit(solution)/shard_map/ppermute | solution.py:522
  97.2 3.3 %collective-permute-start.32 = (bf16[1216,128]{1,0:T(8,128)(2,1)S(1)}, bf16[1216,128]{1,0:T(8,128)(2,1)S(1)}, u32[]{:S(2)}, u32[]{:S(2)}) collective-permute-start(bf16[1216,128]{1,0:T(8,128)(2,1)S(1)} %collective-permute-done.28.refs_2_), channel_id=1, source_target_pairs={{0,1},{1,0},{2,3},{3,2},{4,5},{5,4},{6,7},{7,6},{8,9},{9,8},{10,11... | collective-permute-start | bytes 933896 | tf_op jit(solution)/shard_map/ppermute | solution.py:562
  100.5 0.0 collective-permute-start.31
  100.5 1.2 %collective-permute-done.32.refs_6_ = bf16[1216,128]{1,0:T(8,128)(2,1)S(1)} collective-permute-done((bf16[1216,128]{1,0:T(8,128)(2,1)S(1)}, bf16[1216,128]{1,0:T(8,128)(2,1)S(1)}, u32[]{:S(2)}, u32[]{:S(2)}) %collective-permute-start.32) | collective-permute-done | bytes 311328 | tf_op jit(solution)/shard_map/ppermute | solution.py:562
  101.7 0.4 collective-permute-done.31.refs_5_
  102.1 3.8 %shard_map.77 = (f32[2880,320]{1,0:T(8,128)}, f32[960,320]{1,0:T(8,128)}) custom-call(bf16[1216,128]{1,0:T(8,128)(2,1)S(1)} %shard_map.75.refs_0_, bf16[1216,128]{1,0:T(8,128)(2,1)S(1)} %collective-permute-done.26.refs_1_, bf16[1216,128]{1,0:T(8,128)(2,1)S(1)} %collective-permute-done.28.refs_2_, bf16[1216,128]{1,0:T(8,128)(2,1)S(1)} %collective-permute-done.29.refs_3_, ...), custom_call_target="tpu_custom_call" | custom-call | flops 3000000000 | tf_op jit(solution)/shard_map/pallas_call | solution.py:716
  (35 shorter events, 0.2 us)
Async XLA Ops:
  0.6 1.3 %copy-start = (bf16[1,4,32,5120]{3,2,1,0:T(8,128)(2,1)S(1)}, bf16[1,4,32,5120]{3,2,1,0:T(8,128)(2,1)}, u32[]{:S(2)}) copy-start(bf16[1,4,32,5120]{3,2,1,0:T(8,128)(2,1)} %param.4) | copy-start | bytes 3932164
  1.9 1.3 %copy-start.2 = (bf16[1,4,32,5120]{3,2,1,0:T(8,128)(2,1)S(1)}, bf16[1,4,32,5120]{3,2,1,0:T(8,128)(2,1)}, u32[]{:S(2)}) copy-start(bf16[1,4,32,5120]{3,2,1,0:T(8,128)(2,1)} %param.7) | copy-start | bytes 3932164
  2.6 7.6 %collective-permute-start = (f32[8,640]{1,0:T(8,128)S(1)}, f32[8,640]{1,0:T(8,128)S(1)}, u32[]{:S(2)}, u32[]{:S(2)}) collective-permute-start(f32[8,640]{1,0:T(8,128)S(1)} %get-tuple-element.41.sums_ref), channel_id=1, source_target_pairs={{0,1},{1,0},{2,3},{3,2},{4,5},{5,4},{6,7},{7,6},{8,9},{9,8},{10,11... | collective-permute-start | bytes 61448 | tf_op jit(solution)/shard_map/ppermute | solution.py:562
  3.1 7.1 %collective-permute-start.1 = (bf16[128,384]{1,0:T(8,128)(2,1)S(1)}, bf16[128,384]{1,0:T(8,128)(2,1)S(1)}, u32[]{:S(2)}, u32[]{:S(2)}) collective-permute-start(bf16[128,384]{1,0:T(8,128)(2,1)S(1)} %get-tuple-element.42), channel_id=1, source_target_pairs={{0,1},{1,0},{2,3},{3,2},{4,5},{5,4},{6,7},{7,6},{8,9},{9,8},{10,11... | collective-permute-start | bytes 294920 | tf_op jit(solution)/shard_map/ppermute | solution.py:562
  3.3 24.1 %collective-permute-start.3 = (bf16[32,5120]{1,0:T(8,128)(2,1)S(1)}, bf16[32,5120]{1,0:T(8,128)(2,1)S(1)}, u32[]{:S(2)}, u32[]{:S(2)}) collective-permute-start(bf16[32,5120]{1,0:T(8,128)(2,1)S(1)} %get-tuple-element.79), channel_id=1, source_target_pairs={{2,0},{4,2},{6,4},{3,1},{5,3},{7,5},{10,8},{12,10},{14,12},{11,9},... | collective-permute-start | bytes 983048 | tf_op jit(solution)/shard_map/ppermute | solution.py:632
  4.6 22.8 %collective-permute-start.2 = (bf16[32,5120]{1,0:T(8,128)(2,1)S(1)}, bf16[32,5120]{1,0:T(8,128)(2,1)S(1)}, u32[]{:S(2)}, u32[]{:S(2)}) collective-permute-start(bf16[32,5120]{1,0:T(8,128)(2,1)S(1)} %get-tuple-element.80), channel_id=1, source_target_pairs={{0,2},{2,4},{4,6},{1,3},{3,5},{5,7},{8,10},{10,12},{12,14},{9,11},... | collective-permute-start | bytes 983048 | tf_op jit(solution)/shard_map/ppermute | solution.py:631
  10.2 1.6 %copy-start.3 = (bf16[3,3,320,320]{3,2,1,0:T(8,128)(2,1)S(1)}, bf16[3,3,320,320]{3,2,1,0:T(8,128)(2,1)}, u32[]{:S(2)}) copy-start(bf16[3,3,320,320]{3,2,1,0:T(8,128)(2,1)} %kernel_ref.5) | copy-start | bytes 5529604
  11.8 15.6 %copy-start.5 = (bf16[3,320,320]{2,1,0:T(8,128)(2,1)S(1)}, bf16[3,320,320]{2,1,0:T(8,128)(2,1)}, u32[]{:S(2)}) copy-start(bf16[3,320,320]{2,1,0:T(8,128)(2,1)} %kernel_ref.4) | copy-start | bytes 1843204
  21.7 1.3 %collective-permute-start.4 = (f32[8,640]{1,0:T(8,128)S(1)}, f32[8,640]{1,0:T(8,128)S(1)}, u32[]{:S(2)}, u32[]{:S(2)}) collective-permute-start(f32[8,640]{1,0:T(8,128)S(1)} %get-tuple-element.44), channel_id=1, source_target_pairs={{0,1},{1,0},{2,3},{3,2},{4,5},{5,4},{6,7},{7,6},{8,9},{9,8},{10,11... | collective-permute-start | bytes 61448 | tf_op jit(solution)/shard_map/ppermute | solution.py:562
  23.0 7.7 %collective-permute-start.7 = (f32[8,640]{1,0:T(8,128)S(1)}, f32[8,640]{1,0:T(8,128)S(1)}, u32[]{:S(2)}, u32[]{:S(2)}) collective-permute-start(f32[8,640]{1,0:T(8,128)S(1)} %add.27.refs_0_), channel_id=1, source_target_pairs={{0,6},{2,4},{4,2},{6,0},{1,7},{3,5},{5,3},{7,1},{8,14},{10,12},{12... | collective-permute-start | bytes 61448 | tf_op jit(solution)/shard_map/ppermute | solution.py:562
  24.8 5.8 %collective-permute-start.6 = (f32[8,640]{1,0:T(8,128)S(1)}, f32[8,640]{1,0:T(8,128)S(1)}, u32[]{:S(2)}, u32[]{:S(2)}) collective-permute-start(f32[8,640]{1,0:T(8,128)S(1)} %add.27.refs_0_), channel_id=1, source_target_pairs={{0,4},{2,6},{4,0},{6,2},{1,5},{3,7},{5,1},{7,3},{8,12},{10,14},{12... | collective-permute-start | bytes 61448 | tf_op jit(solution)/shard_map/ppermute | solution.py:562
  26.5 4.2 %collective-permute-start.5 = (f32[8,640]{1,0:T(8,128)S(1)}, f32[8,640]{1,0:T(8,128)S(1)}, u32[]{:S(2)}, u32[]{:S(2)}) collective-permute-start(f32[8,640]{1,0:T(8,128)S(1)} %add.27.refs_0_), channel_id=1, source_target_pairs={{0,2},{2,0},{4,6},{6,4},{1,3},{3,1},{5,7},{7,5},{8,10},{10,8},{12,... | collective-permute-start | bytes 61448 | tf_op jit(solution)/shard_map/ppermute | solution.py:562
  33.0 9.6 %collective-permute-start.8 = (f32[384,384]{1,0:T(8,128)S(1)}, f32[384,384]{1,0:T(8,128)S(1)}, u32[]{:S(2)}, u32[]{:S(2)}) collective-permute-start(f32[384,384]{1,0:T(8,128)S(1)} %get-tuple-element.46), channel_id=1, source_target_pairs={{0,1},{1,0},{2,3},{3,2},{4,5},{5,4},{6,7},{7,6},{8,9},{9,8},{10,11... | collective-permute-start | bytes 1769480 | tf_op jit(solution)/shard_map/ppermute | solution.py:562
  33.1 2.0 %collective-permute-start.9 = (f32[8,640]{1,0:T(8,128)S(1)}, f32[8,640]{1,0:T(8,128)S(1)}, u32[]{:S(2)}, u32[]{:S(2)}) collective-permute-start(f32[8,640]{1,0:T(8,128)S(1)} %get-tuple-element.49), channel_id=1, source_target_pairs={{0,1},{1,0},{2,3},{3,2},{4,5},{5,4},{6,7},{7,6},{8,9},{9,8},{10,11... | collective-permute-start | bytes 61448 | tf_op jit(solution)/shard_map/ppermute | solution.py:562
  35.1 7.5 %collective-permute-start.12 = (f32[8,640]{1,0:T(8,128)S(1)}, f32[8,640]{1,0:T(8,128)S(1)}, u32[]{:S(2)}, u32[]{:S(2)}) collective-permute-start(f32[8,640]{1,0:T(8,128)S(1)} %add.28.refs_4_), channel_id=1, source_target_pairs={{0,6},{2,4},{4,2},{6,0},{1,7},{3,5},{5,3},{7,1},{8,14},{10,12},{12... | collective-permute-start | bytes 61448 | tf_op jit(solution)/shard_map/ppermute | solution.py:562
  37.2 5.5 %collective-permute-start.11 = (f32[8,640]{1,0:T(8,128)S(1)}, f32[8,640]{1,0:T(8,128)S(1)}, u32[]{:S(2)}, u32[]{:S(2)}) collective-permute-start(f32[8,640]{1,0:T(8,128)S(1)} %add.28.refs_4_), channel_id=1, source_target_pairs={{0,4},{2,6},{4,0},{6,2},{1,5},{3,7},{5,1},{7,3},{8,12},{10,14},{12... | collective-permute-start | bytes 61448 | tf_op jit(solution)/shard_map/ppermute | solution.py:562
  37.7 5.0 %collective-permute-start.10 = (f32[8,640]{1,0:T(8,128)S(1)}, f32[8,640]{1,0:T(8,128)S(1)}, u32[]{:S(2)}, u32[]{:S(2)}) collective-permute-start(f32[8,640]{1,0:T(8,128)S(1)} %add.28.refs_4_), channel_id=1, source_target_pairs={{0,2},{2,0},{4,6},{6,4},{1,3},{3,1},{5,7},{7,5},{8,10},{10,8},{12,... | collective-permute-start | bytes 61448 | tf_op jit(solution)/shard_map/ppermute | solution.py:562
  52.5 1.7 %collective-permute-start.14 = (bf16[1216,128]{1,0:T(8,128)(2,1)S(1)}, bf16[1216,128]{1,0:T(8,128)(2,1)S(1)}, u32[]{:S(2)}, u32[]{:S(2)}) collective-permute-start(bf16[1216,128]{1,0:T(8,128)(2,1)S(1)} %get-tuple-element.53), channel_id=1, source_target_pairs={{0,1},{1,0},{2,3},{3,2},{4,5},{5,4},{6,7},{7,6},{8,9},{9,8},{10,11... | collective-permute-start | bytes 933896 | tf_op jit(solution)/shard_map/ppermute | solution.py:562
  52.6 16.0 %collective-permute-start.13 = (bf16[1216,128]{1,0:T(8,128)(2,1)S(1)}, bf16[1216,128]{1,0:T(8,128)(2,1)S(1)}, u32[]{:S(2)}, u32[]{:S(2)}) collective-permute-start(bf16[1216,128]{1,0:T(8,128)(2,1)S(1)} %get-tuple-element.51), channel_id=1, source_target_pairs={{0,1},{1,0},{2,3},{3,2},{4,5},{5,4},{6,7},{7,6},{8,9},{9,8},{10,11... | collective-permute-start | bytes 933896 | tf_op jit(solution)/shard_map/ppermute | solution.py:562
  53.1 2.0 %collective-permute-start.15 = (bf16[1216,128]{1,0:T(8,128)(2,1)S(1)}, bf16[1216,128]{1,0:T(8,128)(2,1)S(1)}, u32[]{:S(2)}, u32[]{:S(2)}) collective-permute-start(bf16[1216,128]{1,0:T(8,128)(2,1)S(1)} %get-tuple-element.55), channel_id=1, source_target_pairs={{0,1},{1,0},{2,3},{3,2},{4,5},{5,4},{6,7},{7,6},{8,9},{9,8},{10,11... | collective-permute-start | bytes 933896 | tf_op jit(solution)/shard_map/ppermute | solution.py:562
  53.2 2.4 %collective-permute-start.16 = (bf16[1216,128]{1,0:T(8,128)(2,1)S(1)}, bf16[1216,128]{1,0:T(8,128)(2,1)S(1)}, u32[]{:S(2)}, u32[]{:S(2)}) collective-permute-start(bf16[1216,128]{1,0:T(8,128)(2,1)S(1)} %get-tuple-element.57), channel_id=1, source_target_pairs={{0,1},{1,0},{2,3},{3,2},{4,5},{5,4},{6,7},{7,6},{8,9},{9,8},{10,11... | collective-permute-start | bytes 933896 | tf_op jit(solution)/shard_map/ppermute | solution.py:562
  54.2 5.0 %copy-start.4 = (bf16[3,3,320,320]{3,2,1,0:T(8,128)(2,1)S(1)}, bf16[3,3,320,320]{3,2,1,0:T(8,128)(2,1)}, u32[]{:S(2)}) copy-start(bf16[3,3,320,320]{3,2,1,0:T(8,128)(2,1)} %kernel_ref.5) | copy-start | bytes 5529604
  54.3 4.9 %copy-start.1 = (bf16[1,4,32,5120]{3,2,1,0:T(8,128)(2,1)S(1)}, bf16[1,4,32,5120]{3,2,1,0:T(8,128)(2,1)}, u32[]{:S(2)}) copy-start(bf16[1,4,32,5120]{3,2,1,0:T(8,128)(2,1)} %param.4) | copy-start | bytes 3932164
  55.6 13.1 %collective-permute-start.17 = (bf16[1216,128]{1,0:T(8,128)(2,1)S(1)}, bf16[1216,128]{1,0:T(8,128)(2,1)S(1)}, u32[]{:S(2)}, u32[]{:S(2)}) collective-permute-start(bf16[1216,128]{1,0:T(8,128)(2,1)S(1)} %add_convert_fusion.2), channel_id=1, source_target_pairs={{0,8},{1,3},{2,10},{3,1},{4,12},{5,7},{6,14},{7,5},{8,0},{9,11},{1... | collective-permute-start | bytes 933896 | tf_op jit(solution)/shard_map/ppermute | solution.py:522
  57.6 11.1 %collective-permute-start.18 = (bf16[1216,128]{1,0:T(8,128)(2,1)S(1)}, bf16[1216,128]{1,0:T(8,128)(2,1)S(1)}, u32[]{:S(2)}, u32[]{:S(2)}) collective-permute-start(bf16[1216,128]{1,0:T(8,128)(2,1)S(1)} %add_convert_fusion.1), channel_id=1, source_target_pairs={{0,16},{1,5},{2,18},{3,7},{4,20},{5,1},{6,22},{7,3},{8,24},{9,13},... | collective-permute-start | bytes 933896 | tf_op jit(solution)/shard_map/ppermute | solution.py:522
  59.1 9.6 %collective-permute-start.19 = (bf16[1216,128]{1,0:T(8,128)(2,1)S(1)}, bf16[1216,128]{1,0:T(8,128)(2,1)S(1)}, u32[]{:S(2)}, u32[]{:S(2)}) collective-permute-start(bf16[1216,128]{1,0:T(8,128)(2,1)S(1)} %add_convert_fusion), channel_id=1, source_target_pairs={{0,24},{1,7},{2,26},{3,5},{4,28},{5,3},{6,30},{7,1},{8,16},{9,15},... | collective-permute-start | bytes 933896 | tf_op jit(solution)/shard_map/ppermute | solution.py:522
  68.9 4.5 %collective-permute-start.20 = (bf16[304,128]{1,0:T(8,128)(2,1)S(1)}, bf16[304,128]{1,0:T(8,128)(2,1)S(1)}, u32[]{:S(2)}, u32[]{:S(2)}) collective-permute-start(bf16[304,128]{1,0:T(8,128)(2,1)S(1)} %get-tuple-element.69), channel_id=1, source_target_pairs={{0,2},{1,9},{2,0},{3,11},{4,6},{5,13},{6,4},{7,15},{8,10},{9,1},{1... | collective-permute-start | bytes 233480 | tf_op jit(solution)/shard_map/ppermute | solution.py:522
  69.6 5.3 %collective-permute-start.21 = (bf16[304,128]{1,0:T(8,128)(2,1)S(1)}, bf16[304,128]{1,0:T(8,128)(2,1)S(1)}, u32[]{:S(2)}, u32[]{:S(2)}) collective-permute-start(bf16[304,128]{1,0:T(8,128)(2,1)S(1)} %get-tuple-element.70), channel_id=1, source_target_pairs={{0,4},{1,17},{2,6},{3,19},{4,0},{5,21},{6,2},{7,23},{8,12},{9,25},... | collective-permute-start | bytes 233480 | tf_op jit(solution)/shard_map/ppermute | solution.py:522
  71.6 6.2 %collective-permute-start.22 = (bf16[304,128]{1,0:T(8,128)(2,1)S(1)}, bf16[304,128]{1,0:T(8,128)(2,1)S(1)}, u32[]{:S(2)}, u32[]{:S(2)}) collective-permute-start(bf16[304,128]{1,0:T(8,128)(2,1)S(1)} %get-tuple-element.71), channel_id=1, source_target_pairs={{0,6},{1,25},{2,4},{3,27},{4,2},{5,29},{6,0},{7,31},{8,14},{9,17},... | collective-permute-start | bytes 233480 | tf_op jit(solution)/shard_map/ppermute | solution.py:522
  77.8 6.3 %collective-permute-start.25 = (bf16[304,128]{1,0:T(8,128)(2,1)S(1)}, bf16[304,128]{1,0:T(8,128)(2,1)S(1)}, u32[]{:S(2)}, u32[]{:S(2)}) collective-permute-start(bf16[304,128]{1,0:T(8,128)(2,1)S(1)} %add_convert_fusion.3.refs_0_), channel_id=1, source_target_pairs={{0,6},{1,25},{2,4},{3,27},{4,2},{5,29},{6,0},{7,31},{8,14},{9,17},... | collective-permute-start | bytes 233480 | tf_op jit(solution)/shard_map/ppermute | solution.py:522
  79.7 6.1 %collective-permute-start.24 = (bf16[304,128]{1,0:T(8,128)(2,1)S(1)}, bf16[304,128]{1,0:T(8,128)(2,1)S(1)}, u32[]{:S(2)}, u32[]{:S(2)}) collective-permute-start(bf16[304,128]{1,0:T(8,128)(2,1)S(1)} %add_convert_fusion.3.refs_0_), channel_id=1, source_target_pairs={{0,4},{1,17},{2,6},{3,19},{4,0},{5,21},{6,2},{7,23},{8,12},{9,25},... | collective-permute-start | bytes 233480 | tf_op jit(solution)/shard_map/ppermute | solution.py:522
  79.7 6.1 %collective-permute-start.23 = (bf16[304,128]{1,0:T(8,128)(2,1)S(1)}, bf16[304,128]{1,0:T(8,128)(2,1)S(1)}, u32[]{:S(2)}, u32[]{:S(2)}) collective-permute-start(bf16[304,128]{1,0:T(8,128)(2,1)S(1)} %add_convert_fusion.3.refs_0_), channel_id=1, source_target_pairs={{0,2},{1,9},{2,0},{3,11},{4,6},{5,13},{6,4},{7,15},{8,10},{9,1},{1... | collective-permute-start | bytes 233480 | tf_op jit(solution)/shard_map/ppermute | solution.py:522
  82.3 7.1 %collective-permute-start.27 = (f32[8,640]{1,0:T(8,128)S(1)}, f32[8,640]{1,0:T(8,128)S(1)}, u32[]{:S(2)}, u32[]{:S(2)}) collective-permute-start(f32[8,640]{1,0:T(8,128)S(1)} %get-tuple-element.74.mine_ref), channel_id=1, source_target_pairs={{0,1},{1,0},{2,3},{3,2},{4,5},{5,4},{6,7},{7,6},{8,9},{9,8},{10,11... | collective-permute-start | bytes 61448 | tf_op jit(solution)/shard_map/ppermute | solution.py:562
  85.8 11.4 %collective-permute-start.29 = (bf16[1216,128]{1,0:T(8,128)(2,1)S(1)}, bf16[1216,128]{1,0:T(8,128)(2,1)S(1)}, u32[]{:S(2)}, u32[]{:S(2)}) collective-permute-start(bf16[1216,128]{1,0:T(8,128)(2,1)S(1)} %shard_map.75.refs_0_), channel_id=1, source_target_pairs={{0,24},{1,7},{2,26},{3,5},{4,28},{5,3},{6,30},{7,1},{8,16},{9,15},... | collective-permute-start | bytes 933896 | tf_op jit(solution)/shard_map/ppermute | solution.py:522
  88.4 8.8 %collective-permute-start.28 = (bf16[1216,128]{1,0:T(8,128)(2,1)S(1)}, bf16[1216,128]{1,0:T(8,128)(2,1)S(1)}, u32[]{:S(2)}, u32[]{:S(2)}) collective-permute-start(bf16[1216,128]{1,0:T(8,128)(2,1)S(1)} %shard_map.75.refs_0_), channel_id=1, source_target_pairs={{0,16},{1,5},{2,18},{3,7},{4,20},{5,1},{6,22},{7,3},{8,24},{9,13},... | collective-permute-start | bytes 933896 | tf_op jit(solution)/shard_map/ppermute | solution.py:522
  88.9 8.3 %collective-permute-start.26 = (bf16[1216,128]{1,0:T(8,128)(2,1)S(1)}, bf16[1216,128]{1,0:T(8,128)(2,1)S(1)}, u32[]{:S(2)}, u32[]{:S(2)}) collective-permute-start(bf16[1216,128]{1,0:T(8,128)(2,1)S(1)} %shard_map.75.refs_0_), channel_id=1, source_target_pairs={{0,8},{1,3},{2,10},{3,1},{4,12},{5,7},{6,14},{7,5},{8,0},{9,11},{1... | collective-permute-start | bytes 933896 | tf_op jit(solution)/shard_map/ppermute | solution.py:522
  93.1 7.4 %collective-permute-start.30 = (bf16[1216,128]{1,0:T(8,128)(2,1)S(1)}, bf16[1216,128]{1,0:T(8,128)(2,1)S(1)}, u32[]{:S(2)}, u32[]{:S(2)}) collective-permute-start(bf16[1216,128]{1,0:T(8,128)(2,1)S(1)} %shard_map.75.refs_0_), channel_id=1, source_target_pairs={{0,1},{1,0},{2,3},{3,2},{4,5},{5,4},{6,7},{7,6},{8,9},{9,8},{10,11... | collective-permute-start | bytes 933896 | tf_op jit(solution)/shard_map/ppermute | solution.py:562
  97.1 3.3 %collective-permute-start.33 = (bf16[1216,128]{1,0:T(8,128)(2,1)S(1)}, bf16[1216,128]{1,0:T(8,128)(2,1)S(1)}, u32[]{:S(2)}, u32[]{:S(2)}) collective-permute-start(bf16[1216,128]{1,0:T(8,128)(2,1)S(1)} %collective-permute-done.29.refs_3_), channel_id=1, source_target_pairs={{0,1},{1,0},{2,3},{3,2},{4,5},{5,4},{6,7},{7,6},{8,9},{9,8},{10,11... | collective-permute-start | bytes 933896 | tf_op jit(solution)/shard_map/ppermute | solution.py:562
  97.2 4.5 %collective-permute-start.32 = (bf16[1216,128]{1,0:T(8,128)(2,1)S(1)}, bf16[1216,128]{1,0:T(8,128)(2,1)S(1)}, u32[]{:S(2)}, u32[]{:S(2)}) collective-permute-start(bf16[1216,128]{1,0:T(8,128)(2,1)S(1)} %collective-permute-done.28.refs_2_), channel_id=1, source_target_pairs={{0,1},{1,0},{2,3},{3,2},{4,5},{5,4},{6,7},{7,6},{8,9},{9,8},{10,11... | collective-permute-start | bytes 933896 | tf_op jit(solution)/shard_map/ppermute | solution.py:562
  100.5 1.7 %collective-permute-start.31 = (bf16[1216,128]{1,0:T(8,128)(2,1)S(1)}, bf16[1216,128]{1,0:T(8,128)(2,1)S(1)}, u32[]{:S(2)}, u32[]{:S(2)}) collective-permute-start(bf16[1216,128]{1,0:T(8,128)(2,1)S(1)} %collective-permute-done.26.refs_1_), channel_id=1, source_target_pairs={{0,1},{1,0},{2,3},{3,2},{4,5},{5,4},{6,7},{7,6},{8,9},{9,8},{10,11... | collective-permute-start | bytes 933896 | tf_op jit(solution)/shard_map/ppermute | solution.py:562

commit v5 on v4

--- a/solution.py
+++ b/solution.py
@@ -17,11 +17,17 @@
 CONV_COST = 12_000_000_000
 
 
-def call(body, outs, scratch=(), flops=0, moved=0, limit=VMEM_LIMIT):
+def call(body, outs, scratch=(), flops=0, moved=0, limit=VMEM_LIMIT, spaces=None, out_spaces=None):
+    specs = {} if spaces is None else {"in_specs": [pl.BlockSpec(memory_space=space) for space in spaces]}
     return pl.pallas_call(
         body,
         out_shape=outs,
-        out_specs=jax.tree.map(lambda _: pl.BlockSpec(memory_space=pltpu.VMEM), outs),
+        **specs,
+        out_specs=(
+            jax.tree.map(lambda _: pl.BlockSpec(memory_space=pltpu.VMEM), outs)
+            if out_spaces is None
+            else [pl.BlockSpec(memory_space=space) for space in out_spaces]
+        ),
         scratch_shapes=list(scratch),
         compiler_params=pltpu.CompilerParams(vmem_limit_bytes=limit),
         cost_estimate=pl.CostEstimate(flops=flops, bytes_accessed=moved, transcendentals=0),
@@ -186,7 +192,7 @@
 
 
 def silu_parts(v):
-    s = 1.0 / (1.0 + jnp.exp(-v))
+    s = 0.5 * jnp.tanh(0.5 * v) + 0.5
     return v * s, s
 
 
@@ -249,10 +255,44 @@
     target[1:2, :] = jnp.sum(square, axis=0, keepdims=True)
 
 
-def frame_taps(cot_ref, before_ref, after_ref, lanes, sizes):
-    own = cot_ref[:, lanes]
-    later = jnp.concatenate([own[sizes.rows :], after_ref[:, lanes]], axis=0)
-    earlier = jnp.concatenate([before_ref[:, lanes], own[: sizes.pixels - sizes.rows]], axis=0)
+def end_frames_body(sizes, cot_hbm, first_ref, second_ref, sems):
+    even = lax.axis_index("seq") % 2 == 0
+    last = sizes.pixels - sizes.rows
+    copies = []
+    for k, target in enumerate((first_ref, second_ref)):
+        start = jnp.where(even, last, 0) if k == 0 else jnp.where(even, 0, last)
+        rows = pl.ds(pl.multiple_of(start, 16), sizes.rows)
+        copies.append(pltpu.make_async_copy(cot_hbm.at[rows, :], target, sems.at[k]))
+    for copy in copies:
+        copy.start()
+    for copy in copies:
+        copy.wait()
+
+
+def neighbour_frames(cot, sizes):
+    seqs = lax.axis_size("seq")
+    first, second = call(
+        functools.partial(end_frames_body, sizes),
+        [struct((sizes.rows, sizes.width), BF16)] * 2,
+        [pltpu.SemaphoreType.DMA((2,))],
+        limit=SMALL_LIMIT,
+        spaces=[pltpu.HBM],
+        flops=CONV_COST // 3,
+    )(cot)
+    found = []
+    for low, values in ((0, first), (1, second)):
+        pairs = []
+        for i in range(low, seqs - 1, 2):
+            pairs += [(i, i + 1), (i + 1, i)]
+        found.append(lax.ppermute(values, "seq", pairs))
+    return found
+
+
+def frame_taps(cot_ref, first_ref, second_ref, lanes, sizes):
+    even = lax.axis_index("seq") % 2 == 0
+    own, first, second = cot_ref[:, lanes], first_ref[:, lanes], second_ref[:, lanes]
+    later = jnp.concatenate([own[sizes.rows :], jnp.where(even, first, second)], axis=0)
+    earlier = jnp.concatenate([jnp.where(even, second, first), own[: sizes.pixels - sizes.rows]], axis=0)
     return later, own, earlier
 
 
@@ -313,18 +353,13 @@
 
 
 def pack(total, target, at, sizes):
-    rows, channels = total.shape[0], sizes.channels
-    full = channels // 128
-    count = 3 * rows
-    for i in range(3):
-        for k in range(full):
-            lanes = slice(i * sizes.edge + k * 128, i * sizes.edge + (k + 1) * 128)
-            target[at + k * count + i * rows : at + k * count + (i + 1) * rows, :] = total[:, lanes]
-    ends = jnp.concatenate([total[:, i * sizes.edge + full * 128 : (i + 1) * sizes.edge] for i in range(3)], axis=0)
-    half = count // 2
-    target[at + full * count : at + full * count + half, :] = jnp.concatenate(
-        [ends[:half, : 128 - sizes.slack], ends[half:, : 128 - sizes.slack]], axis=1
-    )
+    rows, width = total.shape
+    full = width // 128
+    for k in range(full):
+        target[at + k * rows : at + (k + 1) * rows, :] = total[:, k * 128 : (k + 1) * 128]
+    if width % 128:
+        ends, half = total[:, full * 128 :], rows // 2
+        target[at + full * rows : at + full * rows + half, :] = jnp.concatenate([ends[:half], ends[half:]], axis=1)
 
 
 def packed_rows(rows, sizes):
@@ -334,7 +369,6 @@
 def temporal_grad_body(sizes, block, act_ref, cot_ref, before_ref, after_ref, out_ref, total):
     total[...] = jnp.zeros(total.shape, F32)
     channels = sizes.channels
-    zeros = jnp.zeros((sizes.pixels, sizes.slack), BF16)
 
     def step(b, _):
         acts, cots = [], []
@@ -344,9 +378,7 @@
             acts += [act[:, :channels], act[:, channels:]]
             taps = frame_taps(cot_ref, before_ref, after_ref, lanes, sizes)
             for part in (slice(0, channels), slice(channels, 2 * channels)):
-                cots.append(
-                    jnp.concatenate([jnp.concatenate([t[:, part], zeros], axis=1) for t in taps], axis=1)
-                )
+                cots.append(jnp.concatenate([t[:, part] for t in taps], axis=1))
         total[...] += lax.dot_general(
             jnp.concatenate(acts, axis=0), jnp.concatenate(cots, axis=0), (((0,), (0,)), ((), ())),
             preferred_element_type=F32,
@@ -394,7 +426,6 @@
     dspat_ref[...] = padded[1]
 
     channels = sizes.channels
-    zeros = jnp.zeros((sizes.pixels, sizes.slack), BF16)
     total[...] = jnp.zeros(total.shape, F32)
 
     block = min(4, sizes.pairs)
@@ -411,7 +442,7 @@
                 for i in range(3):
                     d = padded[2 - i, :, both]
                     d = d[:, channels:] if odd else d[:, :channels]
-                    taps.append(jnp.concatenate([d, zeros], axis=1))
+                    taps.append(d)
                 right.append(jnp.concatenate(taps, axis=1))
             part = lax.dot_general(
                 jnp.concatenate(left, axis=0), jnp.concatenate(right, axis=0), (((0,), (0,)), ((), ())),
@@ -530,31 +561,44 @@
 
 def unpack_body(sizes, scale, parts, *refs):
     mine, theirs = refs[:parts], refs[parts : 2 * parts]
-    spatial_ref, temporal_ref, packed = refs[2 * parts :]
+    spatial_hbm, temporal_hbm, packed, spatial_ref, temporal_ref, sems = refs[2 * parts :]
     core = lax.axis_index("col")
     for n in range(parts):
         packed[chunk_rows(core, n, packed.shape[0], parts), :] = mine[n][...]
         packed[chunk_rows(1 - core, n, packed.shape[0], parts), :] = theirs[n][...]
-    full = sizes.channels // 128
+    width = 3 * sizes.channels
+    full, left = width // 128, width % 128
     at = 0
-    for target in (spatial_ref, temporal_ref):
-        count = target.shape[0]
-        tile = math.gcd(count // 2, 240)
-
-        def step(k, _, at=at, target=target, count=count, tile=tile):
-            for second in range(2):
-                row = pl.multiple_of(k * tile, 16) + second * (count // 2)
-                found = [
-                    packed[pl.ds(pl.multiple_of(at + b * count + row, 16), tile), :].astype(F32) for b in range(full)
-                ]
-                ends = packed[pl.ds(pl.multiple_of(at + full * count + k * tile, 16), tile), :].astype(F32)
-                cut = 128 - sizes.slack
-                found.append(ends[:, cut:] if second else ends[:, :cut])
-                target[pl.ds(pl.multiple_of(row, 16), tile), :] = jnp.concatenate(found, axis=1) * scale
-            return 0
-
-        lax.fori_loop(0, count // 2 // tile, step, 0)
-        at += count * sizes.channels // 128
+    copies = []
+    for target, hbm in ((spatial_ref, spatial_hbm), (temporal_ref, temporal_hbm)):
+        count = target.shape[0] // 3
+        tile = math.gcd(count // 2, 80)
+        block = math.gcd(count // 2, 240)
+        for first in range(0, count // 2, block):
+
+            def step(k, _, at=at, target=target, count=count, first=first, tile=tile):
+                line = first + k * tile
+                ends = packed[pl.ds(pl.multiple_of(at + full * count + line, 16), tile), :].astype(F32)
+                for second in range(2):
+                    row = line + second * (count // 2)
+                    found = [
+                        packed[pl.ds(pl.multiple_of(at + b * count + row, 16), tile), :].astype(F32) for b in range(full)
+                    ]
+                    found.append(ends[:, left:] if second else ends[:, :left])
+                    wide = jnp.concatenate(found, axis=1) * scale
+                    for i in range(3):
+                        rows = pl.ds(pl.multiple_of(i * count + row, 16), tile)
+                        target[rows, :] = wide[:, i * sizes.channels : (i + 1) * sizes.channels]
+                return 0
+
+            lax.fori_loop(0, block // tile, step, 0)
+            for start in range(first, 3 * count, count // 2):
+                rows = pl.ds(start, block)
+                copies.append(pltpu.make_async_copy(target.at[rows, :], hbm.at[rows, :], sems.at[len(copies)]))
+                copies[-1].start()
+        at += count * width // 128
+    for copy in copies:
+        copy.wait()
 
 
 def swap(values, axis, bit):
@@ -627,21 +671,19 @@
     padded_scratch = pltpu.VMEM((3, sizes.pixels, sizes.padded), BF16)
     slack = sizes.slack
 
-    forth = [(i, i + 1) for i in range(seqs - 1)]
-    before = lax.ppermute(cot[sizes.pixels - rows :], "seq", forth)
-    after = lax.ppermute(cot[:rows], "seq", [(j, i) for i, j in forth])
+    before, after = neighbour_frames(cot, sizes)
 
     sums, edge = call(
         functools.partial(latent_sums_body, sizes),
         [frame_shape, struct((sizes.pixels, sizes.edge), BF16)],
+        flops=CONV_COST // 3,
     )(x)
     other = swap(sums, "col", 1)
     rim = swap(edge, "col", 1)
-    window_weights = [pltpu.VMEM((3 * sizes.window, sizes.edge), BF16)] * 2
     hidden, act, clip = call(
         functools.partial(forward_body, sizes, frame_entries, min(4, sizes.pairs)),
         [struct((sizes.pixels, width), BF16), struct((sizes.pixels, sizes.padded), BF16), sum_shape],
-        [padded_scratch] + window_weights,
+        [padded_scratch] + [pltpu.VMEM((3 * sizes.window, sizes.edge), BF16)] * 2,
         flops=CONV_COST,
     )(x, sums, other, rim, spatial_kernel)
     clips = from_all(clip + swap(clip, "col", 1), "seq")
@@ -667,7 +709,7 @@
     temporal_grad = call(
         functools.partial(temporal_grad_body, sizes, min(4, sizes.pairs)),
         struct((packed_rows(channels, sizes), 128), F32),
-        [pltpu.VMEM((channels, 3 * sizes.edge), F32)],
+        [pltpu.VMEM((channels, 3 * channels), F32)],
         flops=CONV_COST // 3,
     )(tact, cot, before, after)
 
@@ -686,7 +728,7 @@
         + [struct(chunk, BF16)] * count,
         [
             padded_scratch,
-            pltpu.VMEM((3 * channels, 3 * sizes.edge), F32),
+            pltpu.VMEM((3 * channels, 3 * channels), F32),
             pltpu.VMEM((all_rows, 128), F32),
         ],
         flops=CONV_COST,
@@ -716,8 +758,14 @@
     spatial_grad, temporal_grad = call(
         functools.partial(unpack_body, sizes, grad_scale, len(parts)),
         [struct((9 * channels, channels), F32), struct((3 * channels, channels), F32)],
-        [pltpu.VMEM((all_rows, 128), BF16)],
+        [
+            pltpu.VMEM((all_rows, 128), BF16),
+            pltpu.VMEM((9 * channels, channels), F32),
+            pltpu.VMEM((3 * channels, channels), F32),
+            pltpu.SemaphoreType.DMA((64,)),
+        ],
         flops=CONV_COST // 4,
+        out_spaces=[pltpu.HBM] * 2,
     )(*parts, *others)
 
     return (

time: 106 us -> 102 us (0.962)
  local copies, waits for them, and re-layouts: 3.08 us -> 1.42 us
  starting transfers between devices: 37.3 us -> 35.8 us
  Pallas kernels: 46.2 us -> 45 us
    ppermute x2, starting transfers between devices: 6.87 us -> 3.89 us  [neighbour_frames(): found.append(lax.ppermute(values, 'seq', pairs))]
    unnamed x12 -> x10, local copies, waits for them, and re-layouts: 3.04 us -> 1.42 us
    ppermute x20, starting transfers between devices: 14.4 us -> 15.9 us  [swap(): return lax.ppermute(values, axis, [(i, i ^ bit) for i in range(count)])]
  transfers between devices with their start and end apart: 34 -> 34, of which waited for: 12 -> 13; matrix products, arithmetic and copies ran while one was open for 0% -> 0% of each run, Pallas kernels for 28% -> 29%
where the time goes in v5:
time: 102 us; the launch traced here: 101 us
  Pallas kernels  45 us (44%)
  starting transfers between devices  35.8 us (35%)
  waiting for transfers between devices  17.8 us (17%)
  local copies, waits for them, and re-layouts  1.42 us (1%)
  between operations  1.08 us (1%)
    ppermute x12, starting transfers between devices, exchange(): return lax.ppermute(values, names, pairs)  16 us
    ppermute x20, starting transfers between devices, swap(): return lax.ppermute(values, axis, [(i, i ^ bit) for i in range(count)])  15.9 us
    ppermute x12, waiting for transfers between devices, exchange(): return lax.ppermute(values, names, pairs)  11.1 us
    pallas_call x1, Pallas kernels, shards(): call(functools.partial(forward_body, sizes, frame_entries, min(4, sizes.p...  9.77 us
    pallas_call x1, Pallas kernels, shards(): call(functools.partial(backward_body, sizes, frame_entries, min(4, sizes....  9.4 us
    pallas_call x1, Pallas kernels, shards(): call(functools.partial(spatial_grad_body, sizes, clip_entries, seqs), [st...  8.83 us
    ppermute x20, waiting for transfers between devices, swap(): return lax.ppermute(values, axis, [(i, i ^ bit) for i in range(count)])  6.64 us
    ppermute x2, starting transfers between devices, neighbour_frames(): found.append(lax.ppermute(values, 'seq', pairs))  3.89 us
  transfers between devices with their start and end apart: 34, of which 13 were waited for; matrix products, arithmetic and copies ran while one was open for 0% of the time, Pallas kernels for 29%

profile of v5, /device:TPU:0, one launch (start us, length us, event | category | flops | bytes accessed | tf_op | source)
XLA Modules:
  0.0 101.4 jit_solution(6146420906667181084)
XLA Ops:
  0.6 0.0 copy-start.1
  0.6 1.3 %copy-done.1 = bf16[1,4,32,5120]{3,2,1,0:T(8,128)(2,1)S(1)} copy-done((bf16[1,4,32,5120]{3,2,1,0:T(8,128)(2,1)S(1)}, bf16[1,4,32,5120]{3,2,1,0:T(8,128)(2,1)}, u32[]{:S(2)}) %copy-start.1) | copy-done | bytes 1310744
  2.0 0.6 shard_map.67
  2.6 0.5 collective-permute-start
  3.1 0.1 collective-permute-start.1
  3.2 0.1 copy-done.3
  3.3 0.2 shard_map.69
  3.5 3.1 %collective-permute-start.2 = (bf16[32,5120]{1,0:T(8,128)(2,1)S(1)}, bf16[32,5120]{1,0:T(8,128)(2,1)S(1)}, u32[]{:S(2)}, u32[]{:S(2)}) collective-permute-start(bf16[32,5120]{1,0:T(8,128)(2,1)S(1)} %get-tuple-element.46), channel_id=1, source_target_pairs={{0,2},{2,0},{4,6},{6,4},{1,3},{3,1},{5,7},{7,5},{8,10},{10,8},{12,... | collective-permute-start | bytes 983048 | tf_op jit(solution)/shard_map/ppermute | solution.py:287
  6.6 0.8 collective-permute-start.3
  7.4 0.0 collective-permute-done.other_ref
  7.4 9.8 %shard_map.68 = (bf16[128,5120]{1,0:T(8,128)(2,1)S(1)}, bf16[128,5888]{1,0:T(8,128)(2,1)S(1)}, f32[8,640]{1,0:T(8,128)S(1)}) custom-call(bf16[128,5120]{1,0:T(8,128)(2,1)S(1)} %bitcast.6, f32[8,640]{1,0:T(8,128)S(1)} %get-tuple-element.43.sums_ref, f32[8,640]{1,0:T(8,128)S(1)} %collective-permute-done.other_ref, ...), custom_call_target="tpu_custom_call" | custom-call | flops 12000000000 | tf_op jit(solution)/shard_map/pallas_call | solution.py:683
  17.2 0.1 collective-permute-start.4
  17.3 1.2 %collective-permute-done.4 = f32[8,640]{1,0:T(8,128)S(1)} collective-permute-done((f32[8,640]{1,0:T(8,128)S(1)}, f32[8,640]{1,0:T(8,128)S(1)}, u32[]{:S(2)}, u32[]{:S(2)}) %collective-permute-start.4) | collective-permute-done | bytes 20512 | tf_op jit(solution)/shard_map/ppermute | solution.py:606
  18.5 2.5 %collective-permute-start.7 = (f32[8,640]{1,0:T(8,128)S(1)}, f32[8,640]{1,0:T(8,128)S(1)}, u32[]{:S(2)}, u32[]{:S(2)}) collective-permute-start(f32[8,640]{1,0:T(8,128)S(1)} %add.27.refs_0_), channel_id=1, source_target_pairs={{0,6},{2,4},{4,2},{6,0},{1,7},{3,5},{5,3},{7,1},{8,14},{10,12},{12... | collective-permute-start | bytes 61448 | tf_op jit(solution)/shard_map/ppermute | solution.py:606
  21.0 3.3 %collective-permute-start.6 = (f32[8,640]{1,0:T(8,128)S(1)}, f32[8,640]{1,0:T(8,128)S(1)}, u32[]{:S(2)}, u32[]{:S(2)}) collective-permute-start(f32[8,640]{1,0:T(8,128)S(1)} %add.27.refs_0_), channel_id=1, source_target_pairs={{0,4},{2,6},{4,0},{6,2},{1,5},{3,7},{5,1},{7,3},{8,12},{10,14},{12... | collective-permute-start | bytes 61448 | tf_op jit(solution)/shard_map/ppermute | solution.py:606
  24.3 3.3 %shard_map.70.dact_ref = f32[128,5120]{1,0:T(8,128)S(1)} custom-call(bf16[128,5120]{1,0:T(8,128)(2,1)S(1)} %bitcast.10, bf16[32,5120]{1,0:T(8,128)(2,1)S(1)} %collective-permute-done.2.before_ref, bf16[32,5120]{1,0:T(8,128)(2,1)S(1)} %collective-permute-done.3.after_ref, bf16[3,320,320]{2,1,0:T(8,128)(2,1)S(1)} %copy-done.4), custom_call_target="tpu_custom_call" | custom-call | flops 4000000000 | tf_op jit(solution)/shard_map/pallas_call | solution.py:690
  27.6 0.5 collective-permute-done.5.refs_1_
  28.1 2.2 %shard_map.71 = (bf16[128,5120]{1,0:T(8,128)(2,1)S(1)}, f32[128,5120]{1,0:T(8,128)S(1)}, f32[8,640]{1,0:T(8,128)S(1)}, f32[384,384]{1,0:T(8,128)S(1)}) custom-call(bf16[128,5120]{1,0:T(8,128)(2,1)S(1)} %get-tuple-element.45.hidden_ref, bf16[128,5120]{1,0:T(8,128)(2,1)S(1)} %bitcast.11, f32[128,5120]{1,0:T(8,128)S(1)} %shard_map.70.dact_ref, ...), custom_call_target="tpu_custom_call" | custom-call | flops 4000000000 | tf_op jit(solution)/shard_map/pallas_call | solution.py:696
  30.3 0.1 collective-permute-start.8
  30.4 0.5 collective-permute-start.9
  30.9 1.5 %collective-permute-done.9 = f32[8,640]{1,0:T(8,128)S(1)} collective-permute-done((f32[8,640]{1,0:T(8,128)S(1)}, f32[8,640]{1,0:T(8,128)S(1)}, u32[]{:S(2)}, u32[]{:S(2)}) %collective-permute-start.9) | collective-permute-done | bytes 20512 | tf_op jit(solution)/shard_map/ppermute | solution.py:606
  32.4 1.0 collective-permute-start.12
  33.4 2.0 %collective-permute-start.11 = (f32[8,640]{1,0:T(8,128)S(1)}, f32[8,640]{1,0:T(8,128)S(1)}, u32[]{:S(2)}, u32[]{:S(2)}) collective-permute-start(f32[8,640]{1,0:T(8,128)S(1)} %add.28.refs_4_), channel_id=1, source_target_pairs={{0,4},{2,6},{4,0},{6,2},{1,5},{3,7},{5,1},{7,3},{8,12},{10,14},{12... | collective-permute-start | bytes 61448 | tf_op jit(solution)/shard_map/ppermute | solution.py:606
  35.5 1.4 %collective-permute-start.10 = (f32[8,640]{1,0:T(8,128)S(1)}, f32[8,640]{1,0:T(8,128)S(1)}, u32[]{:S(2)}, u32[]{:S(2)}) collective-permute-start(f32[8,640]{1,0:T(8,128)S(1)} %add.28.refs_4_), channel_id=1, source_target_pairs={{0,2},{2,0},{4,6},{6,4},{1,3},{3,1},{5,7},{7,5},{8,10},{10,8},{12,... | collective-permute-start | bytes 61448 | tf_op jit(solution)/shard_map/ppermute | solution.py:606
  36.8 2.9 %shard_map.72.time_ref = f32[2400,128]{1,0:T(8,128)S(1)} custom-call(bf16[128,5120]{1,0:T(8,128)(2,1)S(1)} %get-tuple-element.52.act_ref, bf16[128,5120]{1,0:T(8,128)(2,1)S(1)} %bitcast.12, bf16[32,5120]{1,0:T(8,128)(2,1)S(1)} %collective-permute-done.2.before_ref, bf16[32,5120]{1,0:T(8,128)(2,1)S(1)} %collective-permute-done.3.after_ref), custom_call_target="tpu_custom_call" | custom-call | flops 4000000000 | tf_op jit(solution)/shard_map/pallas_call | solution.py:709
  39.8 8.8 %shard_map.73 = (bf16[128,5120]{1,0:T(8,128)(2,1)S(1)}, bf16[128,5888]{1,0:T(8,128)(2,1)S(1)}, f32[1216,128]{1,0:T(8,128)S(1)}, f32[1216,128]{1,0:T(8,128)S(1)},...) custom-call(bf16[128,5120]{1,0:T(8,128)(2,1)S(1)} %get-tuple-element, ...), custom_call_target="tpu_custom_call" | custom-call | flops 12000000000 | tf_op jit(solution)/shard_map/pallas_call | solution.py:721
  48.7 0.1 collective-permute-start.14
  48.7 0.5 collective-permute-start.13
  49.2 0.1 collective-permute-start.15
  49.3 0.4 collective-permute-start.16
  49.7 0.6 collective-permute-done.14
  50.3 0.1 add_convert_fusion.2
  50.4 0.0 copy-start.2
  50.4 0.8 collective-permute-done.15
  51.2 0.1 add_convert_fusion.1
  51.3 0.4 collective-permute-done.16
  51.7 0.1 add_convert_fusion
  51.7 1.6 %collective-permute-start.17 = (bf16[1216,128]{1,0:T(8,128)(2,1)S(1)}, bf16[1216,128]{1,0:T(8,128)(2,1)S(1)}, u32[]{:S(2)}, u32[]{:S(2)}) collective-permute-start(bf16[1216,128]{1,0:T(8,128)(2,1)S(1)} %add_convert_fusion.2), channel_id=1, source_target_pairs={{0,8},{1,3},{2,10},{3,1},{4,12},{5,7},{6,14},{7,5},{8,0},{9,11},{1... | collective-permute-start | bytes 933896 | tf_op jit(solution)/shard_map/ppermute | solution.py:553
  53.3 1.5 %collective-permute-start.18 = (bf16[1216,128]{1,0:T(8,128)(2,1)S(1)}, bf16[1216,128]{1,0:T(8,128)(2,1)S(1)}, u32[]{:S(2)}, u32[]{:S(2)}) collective-permute-start(bf16[1216,128]{1,0:T(8,128)(2,1)S(1)} %add_convert_fusion.1), channel_id=1, source_target_pairs={{0,16},{1,5},{2,18},{3,7},{4,20},{5,1},{6,22},{7,3},{8,24},{9,13},... | collective-permute-start | bytes 933896 | tf_op jit(solution)/shard_map/ppermute | solution.py:553
  54.8 0.5 collective-permute-start.19
  55.3 9.4 %shard_map.74 = (f32[128,5120]{1,0:T(8,128)S(1)}, f32[8,640]{1,0:T(8,128)S(1)}) custom-call(bf16[128,5120]{1,0:T(8,128)(2,1)S(1)} %bitcast.7, f32[8,640]{1,0:T(8,128)S(1)} %get-tuple-element.43.sums_ref, f32[8,640]{1,0:T(8,128)S(1)} %collective-permute-done.other_ref, bf16[128,5888]{1,0:T(8,128)(2,1)S(1)} %get-tuple-element.66.dspat_ref, ...), custom_call_target="tpu_custom_call" | custom-call | flops 12000000000 | tf_op jit(solution)/shard_map/pallas_call | solution.py:740
  64.7 0.1 convert_add_fusion.refs_0_
  64.8 0.2 shard_map.75
  65.0 0.9 collective-permute-start.20
  65.8 1.0 %collective-permute-start.21 = (bf16[304,128]{1,0:T(8,128)(2,1)S(1)}, bf16[304,128]{1,0:T(8,128)(2,1)S(1)}, u32[]{:S(2)}, u32[]{:S(2)}) collective-permute-start(bf16[304,128]{1,0:T(8,128)(2,1)S(1)} %get-tuple-element.74), channel_id=1, source_target_pairs={{0,4},{1,17},{2,6},{3,19},{4,0},{5,21},{6,2},{7,23},{8,12},{9,25},... | collective-permute-start | bytes 233480 | tf_op jit(solution)/shard_map/ppermute | solution.py:553
  66.9 2.6 %collective-permute-start.22 = (bf16[304,128]{1,0:T(8,128)(2,1)S(1)}, bf16[304,128]{1,0:T(8,128)(2,1)S(1)}, u32[]{:S(2)}, u32[]{:S(2)}) collective-permute-start(bf16[304,128]{1,0:T(8,128)(2,1)S(1)} %get-tuple-element.75), channel_id=1, source_target_pairs={{0,6},{1,25},{2,4},{3,27},{4,2},{5,29},{6,0},{7,31},{8,14},{9,17},... | collective-permute-start | bytes 233480 | tf_op jit(solution)/shard_map/ppermute | solution.py:553
  69.4 0.0 collective-permute-done.20
  69.4 2.5 %collective-permute-done.21 = bf16[304,128]{1,0:T(8,128)(2,1)S(1)} collective-permute-done((bf16[304,128]{1,0:T(8,128)(2,1)S(1)}, bf16[304,128]{1,0:T(8,128)(2,1)S(1)}, u32[]{:S(2)}, u32[]{:S(2)}) %collective-permute-start.21) | collective-permute-done | bytes 77856 | tf_op jit(solution)/shard_map/ppermute | solution.py:553
  72.0 1.1 %collective-permute-done.22 = bf16[304,128]{1,0:T(8,128)(2,1)S(1)} collective-permute-done((bf16[304,128]{1,0:T(8,128)(2,1)S(1)}, bf16[304,128]{1,0:T(8,128)(2,1)S(1)}, u32[]{:S(2)}, u32[]{:S(2)}) %collective-permute-start.22) | collective-permute-done | bytes 77856 | tf_op jit(solution)/shard_map/ppermute | solution.py:553
  73.2 2.6 %collective-permute-start.25 = (bf16[304,128]{1,0:T(8,128)(2,1)S(1)}, bf16[304,128]{1,0:T(8,128)(2,1)S(1)}, u32[]{:S(2)}, u32[]{:S(2)}) collective-permute-start(bf16[304,128]{1,0:T(8,128)(2,1)S(1)} %add_convert_fusion.3.refs_0_), channel_id=1, source_target_pairs={{0,6},{1,25},{2,4},{3,27},{4,2},{5,29},{6,0},{7,31},{8,14},{9,17},... | collective-permute-start | bytes 233480 | tf_op jit(solution)/shard_map/ppermute | solution.py:553
  75.7 0.0 collective-permute-start.24
  75.8 1.8 %collective-permute-start.23 = (bf16[304,128]{1,0:T(8,128)(2,1)S(1)}, bf16[304,128]{1,0:T(8,128)(2,1)S(1)}, u32[]{:S(2)}, u32[]{:S(2)}) collective-permute-start(bf16[304,128]{1,0:T(8,128)(2,1)S(1)} %add_convert_fusion.3.refs_0_), channel_id=1, source_target_pairs={{0,2},{1,9},{2,0},{3,11},{4,6},{5,13},{6,4},{7,15},{8,10},{9,1},{1... | collective-permute-start | bytes 233480 | tf_op jit(solution)/shard_map/ppermute | solution.py:553
  77.6 1.8 %collective-permute-done.25.refs_3_ = bf16[304,128]{1,0:T(8,128)(2,1)S(1)} collective-permute-done((bf16[304,128]{1,0:T(8,128)(2,1)S(1)}, bf16[304,128]{1,0:T(8,128)(2,1)S(1)}, u32[]{:S(2)}, u32[]{:S(2)}) %collective-permute-start.25) | collective-permute-done | bytes 77856 | tf_op jit(solution)/shard_map/ppermute | solution.py:553
  79.4 1.7 %collective-permute-done.24.refs_2_ = bf16[304,128]{1,0:T(8,128)(2,1)S(1)} collective-permute-done((bf16[304,128]{1,0:T(8,128)(2,1)S(1)}, bf16[304,128]{1,0:T(8,128)(2,1)S(1)}, u32[]{:S(2)}, u32[]{:S(2)}) %collective-permute-start.24) | collective-permute-done | bytes 77856 | tf_op jit(solution)/shard_map/ppermute | solution.py:553
  81.1 2.5 %collective-permute-start.29 = (bf16[1216,128]{1,0:T(8,128)(2,1)S(1)}, bf16[1216,128]{1,0:T(8,128)(2,1)S(1)}, u32[]{:S(2)}, u32[]{:S(2)}) collective-permute-start(bf16[1216,128]{1,0:T(8,128)(2,1)S(1)} %shard_map.76.refs_0_), channel_id=1, source_target_pairs={{0,24},{1,7},{2,26},{3,5},{4,28},{5,3},{6,30},{7,1},{8,16},{9,15},... | collective-permute-start | bytes 933896 | tf_op jit(solution)/shard_map/ppermute | solution.py:553
  83.6 0.5 collective-permute-start.28
  84.2 0.5 collective-permute-start.26
  84.7 3.7 %shard_map.77 = f32[128,5120]{1,0:T(8,128)} custom-call(bf16[128,5120]{1,0:T(8,128)(2,1)S(1)} %bitcast.8, f32[8,640]{1,0:T(8,128)S(1)} %get-tuple-element.43.sums_ref, f32[8,640]{1,0:T(8,128)S(1)} %collective-permute-done.other_ref, bf16[128,5120]{1,0:T(8,128)(2,1)S(1)} %bitcast.14, bf16[128,5120]{1,0:T(8,128)(2,1)S(1)} %get-tuple-element.76.dtemp_ref, ...), custom_call_target="tpu_custom_call" | custom-call | flops 4000000000 | tf_op jit(solution)/shard_map/pallas_call | solution.py:750
  88.4 4.0 %collective-permute-done.26.refs_1_ = bf16[1216,128]{1,0:T(8,128)(2,1)S(1)} collective-permute-done((bf16[1216,128]{1,0:T(8,128)(2,1)S(1)}, bf16[1216,128]{1,0:T(8,128)(2,1)S(1)}, u32[]{:S(2)}, u32[]{:S(2)}) %collective-permute-start.26) | collective-permute-done | bytes 311328 | tf_op jit(solution)/shard_map/ppermute | solution.py:553
  92.4 3.4 %collective-permute-start.32 = (bf16[1216,128]{1,0:T(8,128)(2,1)S(1)}, bf16[1216,128]{1,0:T(8,128)(2,1)S(1)}, u32[]{:S(2)}, u32[]{:S(2)}) collective-permute-start(bf16[1216,128]{1,0:T(8,128)(2,1)S(1)} %collective-permute-done.28.refs_2_), channel_id=1, source_target_pairs={{0,1},{1,0},{2,3},{3,2},{4,5},{5,4},{6,7},{7,6},{8,9},{9,8},{10,11... | collective-permute-start | bytes 933896 | tf_op jit(solution)/shard_map/ppermute | solution.py:606
  95.8 0.0 collective-permute-start.31
  95.8 1.2 %collective-permute-done.32.refs_6_ = bf16[1216,128]{1,0:T(8,128)(2,1)S(1)} collective-permute-done((bf16[1216,128]{1,0:T(8,128)(2,1)S(1)}, bf16[1216,128]{1,0:T(8,128)(2,1)S(1)}, u32[]{:S(2)}, u32[]{:S(2)}) %collective-permute-start.32) | collective-permute-done | bytes 311328 | tf_op jit(solution)/shard_map/ppermute | solution.py:606
  97.0 0.4 collective-permute-done.31.refs_5_
  97.5 3.7 %shard_map.78 = (f32[2880,320]{1,0:T(8,128)}, f32[960,320]{1,0:T(8,128)}) custom-call(bf16[1216,128]{1,0:T(8,128)(2,1)S(1)} %shard_map.76.refs_0_, bf16[1216,128]{1,0:T(8,128)(2,1)S(1)} %collective-permute-done.26.refs_1_, bf16[1216,128]{1,0:T(8,128)(2,1)S(1)} %collective-permute-done.28.refs_2_, bf16[1216,128]{1,0:T(8,128)(2,1)S(1)} %collective-permute-done.29.refs_3_, ...), custom_call_target="tpu_custom_call" | custom-call | flops 3000000000 | tf_op jit(solution)/shard_map/pallas_call | solution.py:758
  (33 shorter events, 0.2 us)
Async XLA Ops:
  0.6 1.3 %copy-start.1 = (bf16[1,4,32,5120]{3,2,1,0:T(8,128)(2,1)S(1)}, bf16[1,4,32,5120]{3,2,1,0:T(8,128)(2,1)}, u32[]{:S(2)}) copy-start(bf16[1,4,32,5120]{3,2,1,0:T(8,128)(2,1)} %param.4) | copy-start | bytes 3932164
  1.9 1.3 %copy-start.3 = (bf16[1,4,32,5120]{3,2,1,0:T(8,128)(2,1)S(1)}, bf16[1,4,32,5120]{3,2,1,0:T(8,128)(2,1)}, u32[]{:S(2)}) copy-start(bf16[1,4,32,5120]{3,2,1,0:T(8,128)(2,1)} %param.7) | copy-start | bytes 3932164
  2.6 4.8 %collective-permute-start = (f32[8,640]{1,0:T(8,128)S(1)}, f32[8,640]{1,0:T(8,128)S(1)}, u32[]{:S(2)}, u32[]{:S(2)}) collective-permute-start(f32[8,640]{1,0:T(8,128)S(1)} %get-tuple-element.43.sums_ref), channel_id=1, source_target_pairs={{0,1},{1,0},{2,3},{3,2},{4,5},{5,4},{6,7},{7,6},{8,9},{9,8},{10,11... | collective-permute-start | bytes 61448 | tf_op jit(solution)/shard_map/ppermute | solution.py:606
  3.1 4.3 %collective-permute-start.1 = (bf16[128,384]{1,0:T(8,128)(2,1)S(1)}, bf16[128,384]{1,0:T(8,128)(2,1)S(1)}, u32[]{:S(2)}, u32[]{:S(2)}) collective-permute-start(bf16[128,384]{1,0:T(8,128)(2,1)S(1)} %get-tuple-element.44), channel_id=1, source_target_pairs={{0,1},{1,0},{2,3},{3,2},{4,5},{5,4},{6,7},{7,6},{8,9},{9,8},{10,11... | collective-permute-start | bytes 294920 | tf_op jit(solution)/shard_map/ppermute | solution.py:606
  3.3 4.2 %copy-start = (bf16[3,3,320,320]{3,2,1,0:T(8,128)(2,1)S(1)}, bf16[3,3,320,320]{3,2,1,0:T(8,128)(2,1)}, u32[]{:S(2)}) copy-start(bf16[3,3,320,320]{3,2,1,0:T(8,128)(2,1)} %kernel_ref.5) | copy-start | bytes 5529604
  3.5 20.8 %collective-permute-start.2 = (bf16[32,5120]{1,0:T(8,128)(2,1)S(1)}, bf16[32,5120]{1,0:T(8,128)(2,1)S(1)}, u32[]{:S(2)}, u32[]{:S(2)}) collective-permute-start(bf16[32,5120]{1,0:T(8,128)(2,1)S(1)} %get-tuple-element.46), channel_id=1, source_target_pairs={{0,2},{2,0},{4,6},{6,4},{1,3},{3,1},{5,7},{7,5},{8,10},{10,8},{12,... | collective-permute-start | bytes 983048 | tf_op jit(solution)/shard_map/ppermute | solution.py:287
  6.6 17.7 %copy-start.4 = (bf16[3,320,320]{2,1,0:T(8,128)(2,1)S(1)}, bf16[3,320,320]{2,1,0:T(8,128)(2,1)}, u32[]{:S(2)}) copy-start(bf16[3,320,320]{2,1,0:T(8,128)(2,1)} %kernel_ref.4) | copy-start | bytes 1843204
  6.6 17.7 %collective-permute-start.3 = (bf16[32,5120]{1,0:T(8,128)(2,1)S(1)}, bf16[32,5120]{1,0:T(8,128)(2,1)S(1)}, u32[]{:S(2)}, u32[]{:S(2)}) collective-permute-start(bf16[32,5120]{1,0:T(8,128)(2,1)S(1)} %get-tuple-element.47), channel_id=1, source_target_pairs={{2,4},{4,2},{3,5},{5,3},{10,12},{12,10},{11,13},{13,11},{18,20},{2... | collective-permute-start | bytes 983048 | tf_op jit(solution)/shard_map/ppermute | solution.py:287
  17.2 1.3 %collective-permute-start.4 = (f32[8,640]{1,0:T(8,128)S(1)}, f32[8,640]{1,0:T(8,128)S(1)}, u32[]{:S(2)}, u32[]{:S(2)}) collective-permute-start(f32[8,640]{1,0:T(8,128)S(1)} %get-tuple-element.48), channel_id=1, source_target_pairs={{0,1},{1,0},{2,3},{3,2},{4,5},{5,4},{6,7},{7,6},{8,9},{9,8},{10,11... | collective-permute-start | bytes 61448 | tf_op jit(solution)/shard_map/ppermute | solution.py:606
  18.5 9.1 %collective-permute-start.7 = (f32[8,640]{1,0:T(8,128)S(1)}, f32[8,640]{1,0:T(8,128)S(1)}, u32[]{:S(2)}, u32[]{:S(2)}) collective-permute-start(f32[8,640]{1,0:T(8,128)S(1)} %add.27.refs_0_), channel_id=1, source_target_pairs={{0,6},{2,4},{4,2},{6,0},{1,7},{3,5},{5,3},{7,1},{8,14},{10,12},{12... | collective-permute-start | bytes 61448 | tf_op jit(solution)/shard_map/ppermute | solution.py:606
  21.0 6.6 %collective-permute-start.6 = (f32[8,640]{1,0:T(8,128)S(1)}, f32[8,640]{1,0:T(8,128)S(1)}, u32[]{:S(2)}, u32[]{:S(2)}) collective-permute-start(f32[8,640]{1,0:T(8,128)S(1)} %add.27.refs_0_), channel_id=1, source_target_pairs={{0,4},{2,6},{4,0},{6,2},{1,5},{3,7},{5,1},{7,3},{8,12},{10,14},{12... | collective-permute-start | bytes 61448 | tf_op jit(solution)/shard_map/ppermute | solution.py:606
  24.3 3.8 %collective-permute-start.5 = (f32[8,640]{1,0:T(8,128)S(1)}, f32[8,640]{1,0:T(8,128)S(1)}, u32[]{:S(2)}, u32[]{:S(2)}) collective-permute-start(f32[8,640]{1,0:T(8,128)S(1)} %add.27.refs_0_), channel_id=1, source_target_pairs={{0,2},{2,0},{4,6},{6,4},{1,3},{3,1},{5,7},{7,5},{8,10},{10,8},{12,... | collective-permute-start | bytes 61448 | tf_op jit(solution)/shard_map/ppermute | solution.py:606
  30.3 9.5 %collective-permute-start.8 = (f32[384,384]{1,0:T(8,128)S(1)}, f32[384,384]{1,0:T(8,128)S(1)}, u32[]{:S(2)}, u32[]{:S(2)}) collective-permute-start(f32[384,384]{1,0:T(8,128)S(1)} %get-tuple-element.50), channel_id=1, source_target_pairs={{0,1},{1,0},{2,3},{3,2},{4,5},{5,4},{6,7},{7,6},{8,9},{9,8},{10,11... | collective-permute-start | bytes 1769480 | tf_op jit(solution)/shard_map/ppermute | solution.py:606
  30.4 2.0 %collective-permute-start.9 = (f32[8,640]{1,0:T(8,128)S(1)}, f32[8,640]{1,0:T(8,128)S(1)}, u32[]{:S(2)}, u32[]{:S(2)}) collective-permute-start(f32[8,640]{1,0:T(8,128)S(1)} %get-tuple-element.53), channel_id=1, source_target_pairs={{0,1},{1,0},{2,3},{3,2},{4,5},{5,4},{6,7},{7,6},{8,9},{9,8},{10,11... | collective-permute-start | bytes 61448 | tf_op jit(solution)/shard_map/ppermute | solution.py:606
  32.4 7.3 %collective-permute-start.12 = (f32[8,640]{1,0:T(8,128)S(1)}, f32[8,640]{1,0:T(8,128)S(1)}, u32[]{:S(2)}, u32[]{:S(2)}) collective-permute-start(f32[8,640]{1,0:T(8,128)S(1)} %add.28.refs_4_), channel_id=1, source_target_pairs={{0,6},{2,4},{4,2},{6,0},{1,7},{3,5},{5,3},{7,1},{8,14},{10,12},{12... | collective-permute-start | bytes 61448 | tf_op jit(solution)/shard_map/ppermute | solution.py:606
  33.4 6.4 %collective-permute-start.11 = (f32[8,640]{1,0:T(8,128)S(1)}, f32[8,640]{1,0:T(8,128)S(1)}, u32[]{:S(2)}, u32[]{:S(2)}) collective-permute-start(f32[8,640]{1,0:T(8,128)S(1)} %add.28.refs_4_), channel_id=1, source_target_pairs={{0,4},{2,6},{4,0},{6,2},{1,5},{3,7},{5,1},{7,3},{8,12},{10,14},{12... | collective-permute-start | bytes 61448 | tf_op jit(solution)/shard_map/ppermute | solution.py:606
  35.5 4.3 %collective-permute-start.10 = (f32[8,640]{1,0:T(8,128)S(1)}, f32[8,640]{1,0:T(8,128)S(1)}, u32[]{:S(2)}, u32[]{:S(2)}) collective-permute-start(f32[8,640]{1,0:T(8,128)S(1)} %add.28.refs_4_), channel_id=1, source_target_pairs={{0,2},{2,0},{4,6},{6,4},{1,3},{3,1},{5,7},{7,5},{8,10},{10,8},{12,... | collective-permute-start | bytes 61448 | tf_op jit(solution)/shard_map/ppermute | solution.py:606
  48.7 1.7 %collective-permute-start.14 = (bf16[1216,128]{1,0:T(8,128)(2,1)S(1)}, bf16[1216,128]{1,0:T(8,128)(2,1)S(1)}, u32[]{:S(2)}, u32[]{:S(2)}) collective-permute-start(bf16[1216,128]{1,0:T(8,128)(2,1)S(1)} %get-tuple-element.57), channel_id=1, source_target_pairs={{0,1},{1,0},{2,3},{3,2},{4,5},{5,4},{6,7},{7,6},{8,9},{9,8},{10,11... | collective-permute-start | bytes 933896 | tf_op jit(solution)/shard_map/ppermute | solution.py:606
  48.7 16.0 %collective-permute-start.13 = (bf16[1216,128]{1,0:T(8,128)(2,1)S(1)}, bf16[1216,128]{1,0:T(8,128)(2,1)S(1)}, u32[]{:S(2)}, u32[]{:S(2)}) collective-permute-start(bf16[1216,128]{1,0:T(8,128)(2,1)S(1)} %get-tuple-element.55), channel_id=1, source_target_pairs={{0,1},{1,0},{2,3},{3,2},{4,5},{5,4},{6,7},{7,6},{8,9},{9,8},{10,11... | collective-permute-start | bytes 933896 | tf_op jit(solution)/shard_map/ppermute | solution.py:606
  49.2 2.0 %collective-permute-start.15 = (bf16[1216,128]{1,0:T(8,128)(2,1)S(1)}, bf16[1216,128]{1,0:T(8,128)(2,1)S(1)}, u32[]{:S(2)}, u32[]{:S(2)}) collective-permute-start(bf16[1216,128]{1,0:T(8,128)(2,1)S(1)} %get-tuple-element.59), channel_id=1, source_target_pairs={{0,1},{1,0},{2,3},{3,2},{4,5},{5,4},{6,7},{7,6},{8,9},{9,8},{10,11... | collective-permute-start | bytes 933896 | tf_op jit(solution)/shard_map/ppermute | solution.py:606
  49.3 2.4 %collective-permute-start.16 = (bf16[1216,128]{1,0:T(8,128)(2,1)S(1)}, bf16[1216,128]{1,0:T(8,128)(2,1)S(1)}, u32[]{:S(2)}, u32[]{:S(2)}) collective-permute-start(bf16[1216,128]{1,0:T(8,128)(2,1)S(1)} %get-tuple-element.61), channel_id=1, source_target_pairs={{0,1},{1,0},{2,3},{3,2},{4,5},{5,4},{6,7},{7,6},{8,9},{9,8},{10,11... | collective-permute-start | bytes 933896 | tf_op jit(solution)/shard_map/ppermute | solution.py:606
  50.4 4.9 %copy-start.2 = (bf16[1,4,32,5120]{3,2,1,0:T(8,128)(2,1)S(1)}, bf16[1,4,32,5120]{3,2,1,0:T(8,128)(2,1)}, u32[]{:S(2)}) copy-start(bf16[1,4,32,5120]{3,2,1,0:T(8,128)(2,1)} %param.4) | copy-start | bytes 3932164
  51.7 13.0 %collective-permute-start.17 = (bf16[1216,128]{1,0:T(8,128)(2,1)S(1)}, bf16[1216,128]{1,0:T(8,128)(2,1)S(1)}, u32[]{:S(2)}, u32[]{:S(2)}) collective-permute-start(bf16[1216,128]{1,0:T(8,128)(2,1)S(1)} %add_convert_fusion.2), channel_id=1, source_target_pairs={{0,8},{1,3},{2,10},{3,1},{4,12},{5,7},{6,14},{7,5},{8,0},{9,11},{1... | collective-permute-start | bytes 933896 | tf_op jit(solution)/shard_map/ppermute | solution.py:553
  53.3 11.5 %collective-permute-start.18 = (bf16[1216,128]{1,0:T(8,128)(2,1)S(1)}, bf16[1216,128]{1,0:T(8,128)(2,1)S(1)}, u32[]{:S(2)}, u32[]{:S(2)}) collective-permute-start(bf16[1216,128]{1,0:T(8,128)(2,1)S(1)} %add_convert_fusion.1), channel_id=1, source_target_pairs={{0,16},{1,5},{2,18},{3,7},{4,20},{5,1},{6,22},{7,3},{8,24},{9,13},... | collective-permute-start | bytes 933896 | tf_op jit(solution)/shard_map/ppermute | solution.py:553
  54.8 10.0 %collective-permute-start.19 = (bf16[1216,128]{1,0:T(8,128)(2,1)S(1)}, bf16[1216,128]{1,0:T(8,128)(2,1)S(1)}, u32[]{:S(2)}, u32[]{:S(2)}) collective-permute-start(bf16[1216,128]{1,0:T(8,128)(2,1)S(1)} %add_convert_fusion), channel_id=1, source_target_pairs={{0,24},{1,7},{2,26},{3,5},{4,28},{5,3},{6,30},{7,1},{8,16},{9,15},... | collective-permute-start | bytes 933896 | tf_op jit(solution)/shard_map/ppermute | solution.py:553
  65.0 4.5 %collective-permute-start.20 = (bf16[304,128]{1,0:T(8,128)(2,1)S(1)}, bf16[304,128]{1,0:T(8,128)(2,1)S(1)}, u32[]{:S(2)}, u32[]{:S(2)}) collective-permute-start(bf16[304,128]{1,0:T(8,128)(2,1)S(1)} %get-tuple-element.73), channel_id=1, source_target_pairs={{0,2},{1,9},{2,0},{3,11},{4,6},{5,13},{6,4},{7,15},{8,10},{9,1},{1... | collective-permute-start | bytes 233480 | tf_op jit(solution)/shard_map/ppermute | solution.py:553
  65.8 6.1 %collective-permute-start.21 = (bf16[304,128]{1,0:T(8,128)(2,1)S(1)}, bf16[304,128]{1,0:T(8,128)(2,1)S(1)}, u32[]{:S(2)}, u32[]{:S(2)}) collective-permute-start(bf16[304,128]{1,0:T(8,128)(2,1)S(1)} %get-tuple-element.74), channel_id=1, source_target_pairs={{0,4},{1,17},{2,6},{3,19},{4,0},{5,21},{6,2},{7,23},{8,12},{9,25},... | collective-permute-start | bytes 233480 | tf_op jit(solution)/shard_map/ppermute | solution.py:553
  66.9 6.3 %collective-permute-start.22 = (bf16[304,128]{1,0:T(8,128)(2,1)S(1)}, bf16[304,128]{1,0:T(8,128)(2,1)S(1)}, u32[]{:S(2)}, u32[]{:S(2)}) collective-permute-start(bf16[304,128]{1,0:T(8,128)(2,1)S(1)} %get-tuple-element.75), channel_id=1, source_target_pairs={{0,6},{1,25},{2,4},{3,27},{4,2},{5,29},{6,0},{7,31},{8,14},{9,17},... | collective-permute-start | bytes 233480 | tf_op jit(solution)/shard_map/ppermute | solution.py:553
  73.2 6.3 %collective-permute-start.25 = (bf16[304,128]{1,0:T(8,128)(2,1)S(1)}, bf16[304,128]{1,0:T(8,128)(2,1)S(1)}, u32[]{:S(2)}, u32[]{:S(2)}) collective-permute-start(bf16[304,128]{1,0:T(8,128)(2,1)S(1)} %add_convert_fusion.3.refs_0_), channel_id=1, source_target_pairs={{0,6},{1,25},{2,4},{3,27},{4,2},{5,29},{6,0},{7,31},{8,14},{9,17},... | collective-permute-start | bytes 233480 | tf_op jit(solution)/shard_map/ppermute | solution.py:553
  75.7 5.3 %collective-permute-start.24 = (bf16[304,128]{1,0:T(8,128)(2,1)S(1)}, bf16[304,128]{1,0:T(8,128)(2,1)S(1)}, u32[]{:S(2)}, u32[]{:S(2)}) collective-permute-start(bf16[304,128]{1,0:T(8,128)(2,1)S(1)} %add_convert_fusion.3.refs_0_), channel_id=1, source_target_pairs={{0,4},{1,17},{2,6},{3,19},{4,0},{5,21},{6,2},{7,23},{8,12},{9,25},... | collective-permute-start | bytes 233480 | tf_op jit(solution)/shard_map/ppermute | solution.py:553
  75.8 5.3 %collective-permute-start.23 = (bf16[304,128]{1,0:T(8,128)(2,1)S(1)}, bf16[304,128]{1,0:T(8,128)(2,1)S(1)}, u32[]{:S(2)}, u32[]{:S(2)}) collective-permute-start(bf16[304,128]{1,0:T(8,128)(2,1)S(1)} %add_convert_fusion.3.refs_0_), channel_id=1, source_target_pairs={{0,2},{1,9},{2,0},{3,11},{4,6},{5,13},{6,4},{7,15},{8,10},{9,1},{1... | collective-permute-start | bytes 233480 | tf_op jit(solution)/shard_map/ppermute | solution.py:553
  77.6 7.1 %collective-permute-start.27 = (f32[8,640]{1,0:T(8,128)S(1)}, f32[8,640]{1,0:T(8,128)S(1)}, u32[]{:S(2)}, u32[]{:S(2)}) collective-permute-start(f32[8,640]{1,0:T(8,128)S(1)} %get-tuple-element.78.mine_ref), channel_id=1, source_target_pairs={{0,1},{1,0},{2,3},{3,2},{4,5},{5,4},{6,7},{7,6},{8,9},{9,8},{10,11... | collective-permute-start | bytes 61448 | tf_op jit(solution)/shard_map/ppermute | solution.py:606
  81.1 11.3 %collective-permute-start.29 = (bf16[1216,128]{1,0:T(8,128)(2,1)S(1)}, bf16[1216,128]{1,0:T(8,128)(2,1)S(1)}, u32[]{:S(2)}, u32[]{:S(2)}) collective-permute-start(bf16[1216,128]{1,0:T(8,128)(2,1)S(1)} %shard_map.76.refs_0_), channel_id=1, source_target_pairs={{0,24},{1,7},{2,26},{3,5},{4,28},{5,3},{6,30},{7,1},{8,16},{9,15},... | collective-permute-start | bytes 933896 | tf_op jit(solution)/shard_map/ppermute | solution.py:553
  83.6 8.8 %collective-permute-start.28 = (bf16[1216,128]{1,0:T(8,128)(2,1)S(1)}, bf16[1216,128]{1,0:T(8,128)(2,1)S(1)}, u32[]{:S(2)}, u32[]{:S(2)}) collective-permute-start(bf16[1216,128]{1,0:T(8,128)(2,1)S(1)} %shard_map.76.refs_0_), channel_id=1, source_target_pairs={{0,16},{1,5},{2,18},{3,7},{4,20},{5,1},{6,22},{7,3},{8,24},{9,13},... | collective-permute-start | bytes 933896 | tf_op jit(solution)/shard_map/ppermute | solution.py:553
  84.2 8.3 %collective-permute-start.26 = (bf16[1216,128]{1,0:T(8,128)(2,1)S(1)}, bf16[1216,128]{1,0:T(8,128)(2,1)S(1)}, u32[]{:S(2)}, u32[]{:S(2)}) collective-permute-start(bf16[1216,128]{1,0:T(8,128)(2,1)S(1)} %shard_map.76.refs_0_), channel_id=1, source_target_pairs={{0,8},{1,3},{2,10},{3,1},{4,12},{5,7},{6,14},{7,5},{8,0},{9,11},{1... | collective-permute-start | bytes 933896 | tf_op jit(solution)/shard_map/ppermute | solution.py:553
  88.4 7.4 %collective-permute-start.30 = (bf16[1216,128]{1,0:T(8,128)(2,1)S(1)}, bf16[1216,128]{1,0:T(8,128)(2,1)S(1)}, u32[]{:S(2)}, u32[]{:S(2)}) collective-permute-start(bf16[1216,128]{1,0:T(8,128)(2,1)S(1)} %shard_map.76.refs_0_), channel_id=1, source_target_pairs={{0,1},{1,0},{2,3},{3,2},{4,5},{5,4},{6,7},{7,6},{8,9},{9,8},{10,11... | collective-permute-start | bytes 933896 | tf_op jit(solution)/shard_map/ppermute | solution.py:606
  92.4 3.4 %collective-permute-start.33 = (bf16[1216,128]{1,0:T(8,128)(2,1)S(1)}, bf16[1216,128]{1,0:T(8,128)(2,1)S(1)}, u32[]{:S(2)}, u32[]{:S(2)}) collective-permute-start(bf16[1216,128]{1,0:T(8,128)(2,1)S(1)} %collective-permute-done.29.refs_3_), channel_id=1, source_target_pairs={{0,1},{1,0},{2,3},{3,2},{4,5},{5,4},{6,7},{7,6},{8,9},{9,8},{10,11... | collective-permute-start | bytes 933896 | tf_op jit(solution)/shard_map/ppermute | solution.py:606
  92.4 4.6 %collective-permute-start.32 = (bf16[1216,128]{1,0:T(8,128)(2,1)S(1)}, bf16[1216,128]{1,0:T(8,128)(2,1)S(1)}, u32[]{:S(2)}, u32[]{:S(2)}) collective-permute-start(bf16[1216,128]{1,0:T(8,128)(2,1)S(1)} %collective-permute-done.28.refs_2_), channel_id=1, source_target_pairs={{0,1},{1,0},{2,3},{3,2},{4,5},{5,4},{6,7},{7,6},{8,9},{9,8},{10,11... | collective-permute-start | bytes 933896 | tf_op jit(solution)/shard_map/ppermute | solution.py:606
  95.8 1.7 %collective-permute-start.31 = (bf16[1216,128]{1,0:T(8,128)(2,1)S(1)}, bf16[1216,128]{1,0:T(8,128)(2,1)S(1)}, u32[]{:S(2)}, u32[]{:S(2)}) collective-permute-start(bf16[1216,128]{1,0:T(8,128)(2,1)S(1)} %collective-permute-done.26.refs_1_), channel_id=1, source_target_pairs={{0,1},{1,0},{2,3},{3,2},{4,5},{5,4},{6,7},{7,6},{8,9},{9,8},{10,11... | collective-permute-start | bytes 933896 | tf_op jit(solution)/shard_map/ppermute | solution.py:606

commit v6 on v5

--- a/solution.py
+++ b/solution.py
@@ -17,7 +17,7 @@
 CONV_COST = 12_000_000_000
 
 
-def call(body, outs, scratch=(), flops=0, moved=0, limit=VMEM_LIMIT, spaces=None, out_spaces=None):
+def call(body, outs, scratch=(), flops=0, moved=0, limit=VMEM_LIMIT, spaces=None, out_spaces=None, aliases=None):
     specs = {} if spaces is None else {"in_specs": [pl.BlockSpec(memory_space=space) for space in spaces]}
     return pl.pallas_call(
         body,
@@ -29,6 +29,7 @@
             else [pl.BlockSpec(memory_space=space) for space in out_spaces]
         ),
         scratch_shapes=list(scratch),
+        input_output_aliases=aliases or {},
         compiler_params=pltpu.CompilerParams(vmem_limit_bytes=limit),
         cost_estimate=pl.CostEstimate(flops=flops, bytes_accessed=moved, transcendentals=0),
     )
@@ -352,21 +353,19 @@
         store_edge(sizes, source, rim_ref, k * sizes.pixels)
 
 
-def pack(total, target, at, sizes):
-    rows, width = total.shape
-    full = width // 128
+def pack(total, start, rows, target):
+    width = total.shape[1]
+    full, used, half = width // 128, rows * width // 128, rows // 2
+    lines = pl.ds(pl.multiple_of(start, 16), rows)
     for k in range(full):
-        target[at + k * rows : at + (k + 1) * rows, :] = total[:, k * 128 : (k + 1) * 128]
+        target[k * rows : (k + 1) * rows, :] = total[lines, k * 128 : (k + 1) * 128].astype(target.dtype)
     if width % 128:
-        ends, half = total[:, full * 128 :], rows // 2
-        target[at + full * rows : at + full * rows + half, :] = jnp.concatenate([ends[:half], ends[half:]], axis=1)
-
-
-def packed_rows(rows, sizes):
-    return 3 * rows * sizes.channels // 128
-
-
-def temporal_grad_body(sizes, block, act_ref, cot_ref, before_ref, after_ref, out_ref, total):
+        ends = total[lines, full * 128 :].astype(target.dtype)
+        target[full * rows : used, :] = jnp.concatenate([ends[:half], ends[half:]], axis=1)
+    target[used:, :] = jnp.zeros((target.shape[0] - used, 128), target.dtype)
+
+
+def temporal_grad_body(sizes, block, act_ref, cot_ref, before_ref, after_ref, total):
     total[...] = jnp.zeros(total.shape, F32)
     channels = sizes.channels
 
@@ -386,7 +385,6 @@
         return 0
 
     lax.fori_loop(0, sizes.pairs // block, step, 0)
-    pack(total, out_ref, 0, sizes)
 
 
 def spatial_grad_body(
@@ -394,7 +392,7 @@
 ):
     clips, sums = refs[:terms], refs[terms : 2 * terms]
     dtemp_ref, dspat_ref = refs[2 * terms : 2 * terms + 2]
-    chunks, (padded, total, packed) = refs[2 * terms + 2 : -3], refs[-3:]
+    chunks, (padded, total) = refs[2 * terms + 2 : -2], refs[-2:]
     count = len(chunks) // 2
     mean, rate = moments(add_up(clips), 1, clip_entries, sizes)
     means = group_totals(add_up(sums), sizes) * (1.0 / clip_entries)
@@ -426,8 +424,9 @@
     dspat_ref[...] = padded[1]
 
     channels = sizes.channels
-    total[...] = jnp.zeros(total.shape, F32)
-
+    own = 3 * channels
+    total[:own, :] = jnp.zeros((own, own), F32)
+    total[own:, :] = time_ref[...]
     block = min(4, sizes.pairs)
 
     def step(b, _):
@@ -448,20 +447,15 @@
                 jnp.concatenate(left, axis=0), jnp.concatenate(right, axis=0), (((0,), (0,)), ((), ())),
                 preferred_element_type=F32,
             )
-            total[...] += part[: 3 * channels] if odd else part[sizes.slack :]
+            total[:own, :] += part[:own] if odd else part[sizes.slack :]
         return 0
 
     lax.fori_loop(0, sizes.pairs // block, step, 0)
-    pack(total, packed, 0, sizes)
-    own = packed_rows(3 * channels, sizes)
-    packed[own : own + time_ref.shape[0], :] = time_ref[...]
-    used = own + time_ref.shape[0]
-    packed[used:, :] = jnp.zeros((packed.shape[0] - used, 128), F32)
     core = lax.axis_index("col")
+    rows = total.shape[0] // 2 // count
     for n in range(count):
-        keep_ref, send_ref = chunks[n], chunks[count + n]
-        keep_ref[...] = packed[chunk_rows(core, n, packed.shape[0], count), :]
-        send_ref[...] = packed[chunk_rows(1 - core, n, packed.shape[0], count), :].astype(BF16)
+        pack(total, chunk_place(core, n, count) * rows, rows, chunks[n])
+        pack(total, chunk_place(1 - core, n, count) * rows, rows, chunks[count + n])
 
 
 def backward_body(
@@ -553,52 +547,61 @@
     return lax.ppermute(values, names, pairs)
 
 
-def chunk_rows(core, bits, rows, count):
-    chunk = rows // 2 // count
-    start = core * (rows // 2) + (place_of(core, 0) ^ bits) * chunk
-    return pl.ds(pl.multiple_of(start, 16), chunk)
-
-
-def unpack_body(sizes, scale, parts, *refs):
-    mine, theirs = refs[:parts], refs[parts : 2 * parts]
-    spatial_hbm, temporal_hbm, packed, spatial_ref, temporal_ref, sems = refs[2 * parts :]
+def chunk_place(core, bits, count):
+    return core * count + (place_of(core, 0) ^ bits)
+
+
+def unpack_body(sizes, scale, count, chunks, *refs):
+    found, (spatial_hbm, temporal_hbm, staged, sems) = refs[: len(chunks)], refs[-4:]
     core = lax.axis_index("col")
-    for n in range(parts):
-        packed[chunk_rows(core, n, packed.shape[0], parts), :] = mine[n][...]
-        packed[chunk_rows(1 - core, n, packed.shape[0], parts), :] = theirs[n][...]
     width = 3 * sizes.channels
     full, left = width // 128, width % 128
-    at = 0
-    copies = []
-    for target, hbm in ((spatial_ref, spatial_hbm), (temporal_ref, temporal_hbm)):
-        count = target.shape[0] // 3
-        tile = math.gcd(count // 2, 80)
-        block = math.gcd(count // 2, 240)
-        for first in range(0, count // 2, block):
-
-            def step(k, _, at=at, target=target, count=count, first=first, tile=tile):
-                line = first + k * tile
-                ends = packed[pl.ds(pl.multiple_of(at + full * count + line, 16), tile), :].astype(F32)
-                for second in range(2):
-                    row = line + second * (count // 2)
-                    found = [
-                        packed[pl.ds(pl.multiple_of(at + b * count + row, 16), tile), :].astype(F32) for b in range(full)
-                    ]
-                    found.append(ends[:, left:] if second else ends[:, :left])
-                    wide = jnp.concatenate(found, axis=1) * scale
-                    for i in range(3):
-                        rows = pl.ds(pl.multiple_of(i * count + row, 16), tile)
-                        target[rows, :] = wide[:, i * sizes.channels : (i + 1) * sizes.channels]
-                return 0
-
-            lax.fori_loop(0, block // tile, step, 0)
-            for start in range(first, 3 * count, count // 2):
-                rows = pl.ds(start, block)
-                copies.append(pltpu.make_async_copy(target.at[rows, :], hbm.at[rows, :], sems.at[len(copies)]))
-                copies[-1].start()
-        at += count * width // 128
-    for copy in copies:
-        copy.wait()
+    rows = (width + sizes.channels) // 2 // count
+    half = rows // 2
+
+    def each(k, act):
+        mine, bits = chunks[k]
+        place = chunk_place(core if mine else 1 - core, bits, count)
+        spatial = place < width // rows
+        for inside, target, at in (
+            (spatial, spatial_hbm, place), (jnp.logical_not(spatial), temporal_hbm, place - width // rows)
+        ):
+
+            @pl.when(inside)
+            def _(target=target, at=at):
+                lines = pl.ds(pl.multiple_of(at * rows, 16), rows)
+                for i in range(3):
+                    act(pltpu.make_async_copy(staged.at[k, i], target.at[i, lines, :], sems.at[3 * k + i]))
+
+    for k, chunk in enumerate(found):
+        ends = chunk[full * rows : full * rows + half, :].astype(F32)
+        for second in range(2):
+            at = second * half
+            taken = [chunk[b * rows + at : b * rows + at + half, :].astype(F32) for b in range(full)]
+            taken.append(ends[:, left:] if second else ends[:, :left])
+            wide = jnp.concatenate(taken, axis=1) * scale
+            for i in range(3):
+                staged[k, i, at : at + half, :] = wide[:, i * sizes.channels : (i + 1) * sizes.channels]
+        each(k, lambda copy: copy.start())
+    for k in range(len(found)):
+        each(k, lambda copy: copy.wait())
+
+
+def unpack(sizes, scale, count, found, before=None):
+    channels = sizes.channels
+    outs = [struct((3, 3 * channels, channels), F32), struct((3, channels, channels), F32)]
+    rows = 2 * channels // count
+    carried = [] if before is None else list(before)
+    return call(
+        functools.partial(unpack_body, sizes, scale, count, tuple(found)),
+        outs,
+        [pltpu.VMEM((len(found), 3, rows, channels), F32), pltpu.SemaphoreType.DMA((3 * len(found),))],
+        flops=1000,
+        moved=1000,
+        spaces=[pltpu.VMEM] * len(found) + [pltpu.HBM] * len(carried),
+        out_spaces=[pltpu.HBM] * 2,
+        aliases={len(found) + k: k for k in range(len(carried))},
+    )(*found.values(), *carried)
 
 
 def swap(values, axis, bit):
@@ -708,16 +711,13 @@
     rims = swap(rims, "col", 1)
     temporal_grad = call(
         functools.partial(temporal_grad_body, sizes, min(4, sizes.pairs)),
-        struct((packed_rows(channels, sizes), 128), F32),
-        [pltpu.VMEM((channels, 3 * channels), F32)],
+        struct((channels, 3 * channels), F32),
         flops=CONV_COST // 3,
     )(tact, cot, before, after)
 
-    devices = lax.axis_size("dp") * seqs * cols
-    used = packed_rows(3 * channels, sizes) + packed_rows(channels, sizes)
-    all_rows = -(-used // (16 * devices)) * 16 * devices
-    count = lax.axis_size(PHASES[0])
-    chunk = (all_rows // 2 // count, 128)
+    count, after_count = (lax.axis_size(name) for name in PHASES)
+    chunk_rows = 4 * channels // (2 * count) * 3 * channels // 128
+    chunk = (-(-chunk_rows // (16 * after_count)) * 16 * after_count, 128)
     dtemp, dspat, *chunks = call(
         functools.partial(spatial_grad_body, sizes, clip_entries, seqs),
         [
@@ -728,8 +728,7 @@
         + [struct(chunk, BF16)] * count,
         [
             padded_scratch,
-            pltpu.VMEM((3 * channels, 3 * channels), F32),
-            pltpu.VMEM((all_rows, 128), F32),
+            pltpu.VMEM((4 * channels, 3 * channels), F32),
         ],
         flops=CONV_COST,
     )(hidden, cot, tgrad, rims, act, temporal_grad, *clips, *means)
@@ -745,29 +744,26 @@
         flops=CONV_COST,
     )(x, sums, other, dspat, spatial_kernel)
     found, (dnormed, mine) = lax.optimization_barrier((found, (dnormed, mine)))
-    total = added(scattered(chunks[:1] + found, 1))
     theirs = swap(mine, "col", 1)
+    terms, theirs = lax.optimization_barrier((scattered(chunks[:1] + found, 1), theirs))
+    total = added(terms)
     grad_latents = call(
         functools.partial(finish_body, sizes, frame_entries), struct((sizes.pixels, width), F32),
         flops=CONV_COST // 3,
     )(x, sums, other, cot, dtemp, dnormed, mine, theirs)
     part = gathered(total.astype(BF16), 1)
-    parts = [part] + [exchange(part, 0, n) for n in range(1, count)]
-    parts[1], grad_latents = lax.optimization_barrier((parts[1], grad_latents))
-    others = [swap(part, "col", 1) for part in parts]
-    spatial_grad, temporal_grad = call(
-        functools.partial(unpack_body, sizes, grad_scale, len(parts)),
-        [struct((9 * channels, channels), F32), struct((3 * channels, channels), F32)],
-        [
-            pltpu.VMEM((all_rows, 128), BF16),
-            pltpu.VMEM((9 * channels, channels), F32),
-            pltpu.VMEM((3 * channels, channels), F32),
-            pltpu.SemaphoreType.DMA((64,)),
-        ],
-        flops=CONV_COST // 4,
-        out_spaces=[pltpu.HBM] * 2,
-    )(*parts, *others)
-
+    near = [exchange(part, 0, 1 << k) for k in range(count.bit_length() - 1)]
+    part, near, grad_latents = lax.optimization_barrier((part, near, grad_latents))
+    parts = [part] + [None] * (count - 1)
+    for n in range(1, count):
+        parts[n] = exchange(parts[n & (n - 1)], 0, n & -n) if n & (n - 1) else near[n.bit_length() - 1]
+    found = {}
+    for n, part in enumerate(parts[:-1]):
+        found[True, n], found[False, n] = part, swap(part, "col", 1)
+    grads = unpack(sizes, grad_scale, count, found)
+    part, grads = lax.optimization_barrier((parts[-1], grads))
+    last = {(True, count - 1): part, (False, count - 1): swap(part, "col", 1)}
+    spatial_grad, temporal_grad = unpack(sizes, grad_scale, count, last, grads)
     return (
         grad_latents.reshape(latents.shape),
         spatial_grad.reshape(spatial_kernel.shape),

time: 102 us -> 100 us (0.980)
  starting transfers between devices: 35.8 us -> 34 us
    ppermute x20, starting transfers between devices: 15.9 us -> 13.1 us  [swap(): return lax.ppermute(values, axis, [(i, i ^ bit) for i in range(count)])]
    ppermute x20, waiting for transfers between devices: 6.64 us -> 8.21 us  [swap(): return lax.ppermute(values, axis, [(i, i ^ bit) for i in range(count)])]
    pallas_call x1 -> x2, Pallas kernels: 3.74 us -> 3.65 us  [unpack(): call(functools.partial(unpack_body, sizes, scale, count, tuple(found)), o...]
  transfers between devices with their start and end apart: 34 -> 34, of which waited for: 13 -> 16; matrix products, arithmetic and copies ran while one was open for 0% -> 0% of each run, Pallas kernels for 29% -> 31%
where the time goes in v6:
time: 100 us
  Pallas kernels  44.5 us (44%)
  starting transfers between devices  34 us (34%)
  waiting for transfers between devices  18.7 us (19%)
  local copies, waits for them, and re-layouts  1.42 us (1%)
  between operations  1.07 us (1%)
    ppermute x12, starting transfers between devices, exchange(): return lax.ppermute(values, names, pairs)  17 us
    ppermute x20, starting transfers between devices, swap(): return lax.ppermute(values, axis, [(i, i ^ bit) for i in range(count)])  13.1 us
    ppermute x12, waiting for transfers between devices, exchange(): return lax.ppermute(values, names, pairs)  10.5 us
    pallas_call x1, Pallas kernels, shards(): call(functools.partial(forward_body, sizes, frame_entries, min(4, sizes.p...  9.77 us
    pallas_call x1, Pallas kernels, shards(): call(functools.partial(backward_body, sizes, frame_entries, min(4, sizes....  9.4 us
    pallas_call x1, Pallas kernels, shards(): call(functools.partial(spatial_grad_body, sizes, clip_entries, seqs), [st...  8.6 us
    ppermute x20, waiting for transfers between devices, swap(): return lax.ppermute(values, axis, [(i, i ^ bit) for i in range(count)])  8.21 us
    ppermute x2, starting transfers between devices, neighbour_frames(): found.append(lax.ppermute(values, 'seq', pairs))  3.89 us
  transfers between devices with their start and end apart: 34, of which 16 were waited for; matrix products, arithmetic and copies ran while one was open for 0% of the time, Pallas kernels for 31%

profile of v6, /device:TPU:0, one launch (start us, length us, event | category | flops | bytes accessed | tf_op | source)
XLA Modules:
  0.0 100.1 jit_solution(12085770765903882049)
XLA Ops:
  0.6 1.3 %copy-done.1 = bf16[1,4,32,5120]{3,2,1,0:T(8,128)(2,1)S(1)} copy-done((bf16[1,4,32,5120]{3,2,1,0:T(8,128)(2,1)S(1)}, bf16[1,4,32,5120]{3,2,1,0:T(8,128)(2,1)}, u32[]{:S(2)}) %copy-start.1) | copy-done | bytes 1310744
  2.0 0.6 shard_map.67
  2.6 0.5 collective-permute-start
  3.1 0.1 collective-permute-start.1
  3.2 0.1 copy-done.3
  3.3 0.2 shard_map.69
  3.5 3.1 %collective-permute-start.2 = (bf16[32,5120]{1,0:T(8,128)(2,1)S(1)}, bf16[32,5120]{1,0:T(8,128)(2,1)S(1)}, u32[]{:S(2)}, u32[]{:S(2)}) collective-permute-start(bf16[32,5120]{1,0:T(8,128)(2,1)S(1)} %get-tuple-element.58), channel_id=1, source_target_pairs={{0,2},{2,0},{4,6},{6,4},{1,3},{3,1},{5,7},{7,5},{8,10},{10,8},{12,... | collective-permute-start | bytes 983048 | tf_op jit(solution)/shard_map/ppermute | solution.py:288
  6.6 0.8 collective-permute-start.3
  7.4 9.8 %shard_map.68 = (bf16[128,5120]{1,0:T(8,128)(2,1)S(1)}, bf16[128,5888]{1,0:T(8,128)(2,1)S(1)}, f32[8,640]{1,0:T(8,128)S(1)}) custom-call(bf16[128,5120]{1,0:T(8,128)(2,1)S(1)} %bitcast.5, f32[8,640]{1,0:T(8,128)S(1)} %get-tuple-element.55.sums_ref, f32[8,640]{1,0:T(8,128)S(1)} %collective-permute-done.other_ref, ...), custom_call_target="tpu_custom_call" | custom-call | flops 12000000000 | tf_op jit(solution)/shard_map/pallas_call | solution.py:686
  17.2 0.1 collective-permute-start.4
  17.3 1.2 %collective-permute-done.4 = f32[8,640]{1,0:T(8,128)S(1)} collective-permute-done((f32[8,640]{1,0:T(8,128)S(1)}, f32[8,640]{1,0:T(8,128)S(1)}, u32[]{:S(2)}, u32[]{:S(2)}) %collective-permute-start.4) | collective-permute-done | bytes 20512 | tf_op jit(solution)/shard_map/ppermute | solution.py:609
  18.5 2.5 %collective-permute-start.7 = (f32[8,640]{1,0:T(8,128)S(1)}, f32[8,640]{1,0:T(8,128)S(1)}, u32[]{:S(2)}, u32[]{:S(2)}) collective-permute-start(f32[8,640]{1,0:T(8,128)S(1)} %add.27.refs_0_), channel_id=1, source_target_pairs={{0,6},{2,4},{4,2},{6,0},{1,7},{3,5},{5,3},{7,1},{8,14},{10,12},{12... | collective-permute-start | bytes 61448 | tf_op jit(solution)/shard_map/ppermute | solution.py:609
  21.0 3.3 %collective-permute-start.6 = (f32[8,640]{1,0:T(8,128)S(1)}, f32[8,640]{1,0:T(8,128)S(1)}, u32[]{:S(2)}, u32[]{:S(2)}) collective-permute-start(f32[8,640]{1,0:T(8,128)S(1)} %add.27.refs_0_), channel_id=1, source_target_pairs={{0,4},{2,6},{4,0},{6,2},{1,5},{3,7},{5,1},{7,3},{8,12},{10,14},{12... | collective-permute-start | bytes 61448 | tf_op jit(solution)/shard_map/ppermute | solution.py:609
  24.3 3.3 %shard_map.70.dact_ref = f32[128,5120]{1,0:T(8,128)S(1)} custom-call(bf16[128,5120]{1,0:T(8,128)(2,1)S(1)} %bitcast.9, bf16[32,5120]{1,0:T(8,128)(2,1)S(1)} %collective-permute-done.2.before_ref, bf16[32,5120]{1,0:T(8,128)(2,1)S(1)} %collective-permute-done.3.after_ref, bf16[3,320,320]{2,1,0:T(8,128)(2,1)S(1)} %copy-done.4), custom_call_target="tpu_custom_call" | custom-call | flops 4000000000 | tf_op jit(solution)/shard_map/pallas_call | solution.py:693
  27.6 0.5 collective-permute-done.5.refs_1_
  28.1 2.4 %shard_map.71 = (bf16[128,5120]{1,0:T(8,128)(2,1)S(1)}, f32[128,5120]{1,0:T(8,128)S(1)}, f32[8,640]{1,0:T(8,128)S(1)}, f32[384,384]{1,0:T(8,128)S(1)}) custom-call(bf16[128,5120]{1,0:T(8,128)(2,1)S(1)} %get-tuple-element.57.hidden_ref, bf16[128,5120]{1,0:T(8,128)(2,1)S(1)} %bitcast.10, f32[128,5120]{1,0:T(8,128)S(1)} %shard_map.70.dact_ref, ...), custom_call_target="tpu_custom_call" | custom-call | flops 4000000000 | tf_op jit(solution)/shard_map/pallas_call | solution.py:699
  30.5 0.1 collective-permute-start.8
  30.6 0.5 collective-permute-start.9
  31.1 1.5 %collective-permute-done.9 = f32[8,640]{1,0:T(8,128)S(1)} collective-permute-done((f32[8,640]{1,0:T(8,128)S(1)}, f32[8,640]{1,0:T(8,128)S(1)}, u32[]{:S(2)}, u32[]{:S(2)}) %collective-permute-start.9) | collective-permute-done | bytes 20512 | tf_op jit(solution)/shard_map/ppermute | solution.py:609
  32.6 1.0 collective-permute-start.12
  33.6 2.0 %collective-permute-start.11 = (f32[8,640]{1,0:T(8,128)S(1)}, f32[8,640]{1,0:T(8,128)S(1)}, u32[]{:S(2)}, u32[]{:S(2)}) collective-permute-start(f32[8,640]{1,0:T(8,128)S(1)} %add.28.refs_4_), channel_id=1, source_target_pairs={{0,4},{2,6},{4,0},{6,2},{1,5},{3,7},{5,1},{7,3},{8,12},{10,14},{12... | collective-permute-start | bytes 61448 | tf_op jit(solution)/shard_map/ppermute | solution.py:609
  35.6 1.4 %collective-permute-start.10 = (f32[8,640]{1,0:T(8,128)S(1)}, f32[8,640]{1,0:T(8,128)S(1)}, u32[]{:S(2)}, u32[]{:S(2)}) collective-permute-start(f32[8,640]{1,0:T(8,128)S(1)} %add.28.refs_4_), channel_id=1, source_target_pairs={{0,2},{2,0},{4,6},{6,4},{1,3},{3,1},{5,7},{7,5},{8,10},{10,8},{12,... | collective-permute-start | bytes 61448 | tf_op jit(solution)/shard_map/ppermute | solution.py:609
  37.0 2.6 %shard_map.72.time_ref = f32[320,960]{1,0:T(8,128)S(1)} custom-call(bf16[128,5120]{1,0:T(8,128)(2,1)S(1)} %get-tuple-element.64.act_ref, bf16[128,5120]{1,0:T(8,128)(2,1)S(1)} %bitcast.11, bf16[32,5120]{1,0:T(8,128)(2,1)S(1)} %collective-permute-done.2.before_ref, bf16[32,5120]{1,0:T(8,128)(2,1)S(1)} %collective-permute-done.3.after_ref), custom_call_target="tpu_custom_call" | custom-call | flops 4000000000 | tf_op jit(solution)/shard_map/pallas_call | solution.py:712
  39.7 8.6 %shard_map.73 = (bf16[128,5120]{1,0:T(8,128)(2,1)S(1)}, bf16[128,5888]{1,0:T(8,128)(2,1)S(1)}, f32[1216,128]{1,0:T(8,128)S(1)}, f32[1216,128]{1,0:T(8,128)S(1)},...) custom-call(bf16[128,5120]{1,0:T(8,128)(2,1)S(1)} %get-tuple-element, ...), custom_call_target="tpu_custom_call" | custom-call | flops 12000000000 | tf_op jit(solution)/shard_map/pallas_call | solution.py:721
  48.3 0.1 collective-permute-start.14
  48.4 0.5 collective-permute-start.13
  48.9 0.1 collective-permute-start.15
  48.9 0.4 collective-permute-start.16
  49.4 0.6 collective-permute-done.14
  50.0 0.1 add_convert_fusion.2
  50.1 0.8 collective-permute-done.15
  50.9 0.1 add_convert_fusion.1
  50.9 0.4 collective-permute-done.16
  51.3 0.1 add_convert_fusion
  51.4 1.6 %collective-permute-start.17 = (bf16[1216,128]{1,0:T(8,128)(2,1)S(1)}, bf16[1216,128]{1,0:T(8,128)(2,1)S(1)}, u32[]{:S(2)}, u32[]{:S(2)}) collective-permute-start(bf16[1216,128]{1,0:T(8,128)(2,1)S(1)} %add_convert_fusion.2), channel_id=1, source_target_pairs={{0,8},{1,3},{2,10},{3,1},{4,12},{5,7},{6,14},{7,5},{8,0},{9,11},{1... | collective-permute-start | bytes 933896 | tf_op jit(solution)/shard_map/ppermute | solution.py:547
  52.9 1.5 %collective-permute-start.18 = (bf16[1216,128]{1,0:T(8,128)(2,1)S(1)}, bf16[1216,128]{1,0:T(8,128)(2,1)S(1)}, u32[]{:S(2)}, u32[]{:S(2)}) collective-permute-start(bf16[1216,128]{1,0:T(8,128)(2,1)S(1)} %add_convert_fusion.1), channel_id=1, source_target_pairs={{0,16},{1,5},{2,18},{3,7},{4,20},{5,1},{6,22},{7,3},{8,24},{9,13},... | collective-permute-start | bytes 933896 | tf_op jit(solution)/shard_map/ppermute | solution.py:547
  54.5 0.5 collective-permute-start.19
  54.9 9.4 %shard_map.74 = (f32[128,5120]{1,0:T(8,128)S(1)}, f32[8,640]{1,0:T(8,128)S(1)}) custom-call(bf16[128,5120]{1,0:T(8,128)(2,1)S(1)} %bitcast.6, f32[8,640]{1,0:T(8,128)S(1)} %get-tuple-element.55.sums_ref, f32[8,640]{1,0:T(8,128)S(1)} %collective-permute-done.other_ref, bf16[128,5888]{1,0:T(8,128)(2,1)S(1)} %get-tuple-element.78.dspat_ref, ...), custom_call_target="tpu_custom_call" | custom-call | flops 12000000000 | tf_op jit(solution)/shard_map/pallas_call | solution.py:739
  64.4 0.1 convert_add_fusion.refs_0_
  64.4 0.2 shard_map.75
  64.6 1.2 %collective-permute-start.20 = (bf16[304,128]{1,0:T(8,128)(2,1)S(1)}, bf16[304,128]{1,0:T(8,128)(2,1)S(1)}, u32[]{:S(2)}, u32[]{:S(2)}) collective-permute-start(bf16[304,128]{1,0:T(8,128)(2,1)S(1)} %get-tuple-element.85), channel_id=1, source_target_pairs={{0,2},{1,9},{2,0},{3,11},{4,6},{5,13},{6,4},{7,15},{8,10},{9,1},{1... | collective-permute-start | bytes 233480 | tf_op jit(solution)/shard_map/ppermute | solution.py:547
  65.8 1.0 %collective-permute-start.21 = (bf16[304,128]{1,0:T(8,128)(2,1)S(1)}, bf16[304,128]{1,0:T(8,128)(2,1)S(1)}, u32[]{:S(2)}, u32[]{:S(2)}) collective-permute-start(bf16[304,128]{1,0:T(8,128)(2,1)S(1)} %get-tuple-element.86), channel_id=1, source_target_pairs={{0,4},{1,17},{2,6},{3,19},{4,0},{5,21},{6,2},{7,23},{8,12},{9,25},... | collective-permute-start | bytes 233480 | tf_op jit(solution)/shard_map/ppermute | solution.py:547
  66.8 2.3 %collective-permute-start.22 = (bf16[304,128]{1,0:T(8,128)(2,1)S(1)}, bf16[304,128]{1,0:T(8,128)(2,1)S(1)}, u32[]{:S(2)}, u32[]{:S(2)}) collective-permute-start(bf16[304,128]{1,0:T(8,128)(2,1)S(1)} %get-tuple-element.87), channel_id=1, source_target_pairs={{0,6},{1,25},{2,4},{3,27},{4,2},{5,29},{6,0},{7,31},{8,14},{9,17},... | collective-permute-start | bytes 233480 | tf_op jit(solution)/shard_map/ppermute | solution.py:547
  69.1 1.2 %collective-permute-done.23.theirs_ref = f32[8,640]{1,0:T(8,128)S(1)} collective-permute-done((f32[8,640]{1,0:T(8,128)S(1)}, f32[8,640]{1,0:T(8,128)S(1)}, u32[]{:S(2)}, u32[]{:S(2)}) %collective-permute-start.23) | collective-permute-done | bytes 20512 | tf_op jit(solution)/shard_map/ppermute | solution.py:609
  70.3 1.6 %collective-permute-done.21 = bf16[304,128]{1,0:T(8,128)(2,1)S(1)} collective-permute-done((bf16[304,128]{1,0:T(8,128)(2,1)S(1)}, bf16[304,128]{1,0:T(8,128)(2,1)S(1)}, u32[]{:S(2)}, u32[]{:S(2)}) %collective-permute-start.21) | collective-permute-done | bytes 77856 | tf_op jit(solution)/shard_map/ppermute | solution.py:547
  71.9 1.2 %collective-permute-done.22 = bf16[304,128]{1,0:T(8,128)(2,1)S(1)} collective-permute-done((bf16[304,128]{1,0:T(8,128)(2,1)S(1)}, bf16[304,128]{1,0:T(8,128)(2,1)S(1)}, u32[]{:S(2)}, u32[]{:S(2)}) %collective-permute-start.22) | collective-permute-done | bytes 77856 | tf_op jit(solution)/shard_map/ppermute | solution.py:547
  73.2 2.2 %collective-permute-start.26 = (bf16[304,128]{1,0:T(8,128)(2,1)S(1)}, bf16[304,128]{1,0:T(8,128)(2,1)S(1)}, u32[]{:S(2)}, u32[]{:S(2)}) collective-permute-start(bf16[304,128]{1,0:T(8,128)(2,1)S(1)} %add_convert_fusion.3.refs_0_), channel_id=1, source_target_pairs={{0,6},{1,25},{2,4},{3,27},{4,2},{5,29},{6,0},{7,31},{8,14},{9,17},... | collective-permute-start | bytes 233480 | tf_op jit(solution)/shard_map/ppermute | solution.py:547
  75.4 0.3 collective-permute-start.25
  75.7 1.9 %collective-permute-start.24 = (bf16[304,128]{1,0:T(8,128)(2,1)S(1)}, bf16[304,128]{1,0:T(8,128)(2,1)S(1)}, u32[]{:S(2)}, u32[]{:S(2)}) collective-permute-start(bf16[304,128]{1,0:T(8,128)(2,1)S(1)} %add_convert_fusion.3.refs_0_), channel_id=1, source_target_pairs={{0,2},{1,9},{2,0},{3,11},{4,6},{5,13},{6,4},{7,15},{8,10},{9,1},{1... | collective-permute-start | bytes 233480 | tf_op jit(solution)/shard_map/ppermute | solution.py:547
  77.6 1.8 %collective-permute-done.26.refs_3_ = bf16[304,128]{1,0:T(8,128)(2,1)S(1)} collective-permute-done((bf16[304,128]{1,0:T(8,128)(2,1)S(1)}, bf16[304,128]{1,0:T(8,128)(2,1)S(1)}, u32[]{:S(2)}, u32[]{:S(2)}) %collective-permute-start.26) | collective-permute-done | bytes 77856 | tf_op jit(solution)/shard_map/ppermute | solution.py:547
  79.4 1.7 %collective-permute-done.25.refs_2_ = bf16[304,128]{1,0:T(8,128)(2,1)S(1)} collective-permute-done((bf16[304,128]{1,0:T(8,128)(2,1)S(1)}, bf16[304,128]{1,0:T(8,128)(2,1)S(1)}, u32[]{:S(2)}, u32[]{:S(2)}) %collective-permute-start.25) | collective-permute-done | bytes 77856 | tf_op jit(solution)/shard_map/ppermute | solution.py:547
  81.1 1.6 %collective-permute-start.28 = (bf16[1216,128]{1,0:T(8,128)(2,1)S(1)}, bf16[1216,128]{1,0:T(8,128)(2,1)S(1)}, u32[]{:S(2)}, u32[]{:S(2)}) collective-permute-start(bf16[1216,128]{1,0:T(8,128)(2,1)S(1)} %shard_map.76.refs_0_), channel_id=1, source_target_pairs={{0,16},{1,5},{2,18},{3,7},{4,20},{5,1},{6,22},{7,3},{8,24},{9,13},... | collective-permute-start | bytes 933896 | tf_op jit(solution)/shard_map/ppermute | solution.py:547
  82.7 1.5 %collective-permute-start.27 = (bf16[1216,128]{1,0:T(8,128)(2,1)S(1)}, bf16[1216,128]{1,0:T(8,128)(2,1)S(1)}, u32[]{:S(2)}, u32[]{:S(2)}) collective-permute-start(bf16[1216,128]{1,0:T(8,128)(2,1)S(1)} %shard_map.76.refs_0_), channel_id=1, source_target_pairs={{0,8},{1,3},{2,10},{3,1},{4,12},{5,7},{6,14},{7,5},{8,0},{9,11},{1... | collective-permute-start | bytes 933896 | tf_op jit(solution)/shard_map/ppermute | solution.py:547
  84.2 3.7 %shard_map.77 = f32[128,5120]{1,0:T(8,128)} custom-call(bf16[128,5120]{1,0:T(8,128)(2,1)S(1)} %bitcast.7, f32[8,640]{1,0:T(8,128)S(1)} %get-tuple-element.55.sums_ref, f32[8,640]{1,0:T(8,128)S(1)} %collective-permute-done.other_ref, bf16[128,5120]{1,0:T(8,128)(2,1)S(1)} %bitcast.13, bf16[128,5120]{1,0:T(8,128)(2,1)S(1)} %get-tuple-element.93.dtemp_ref, ...), custom_call_target="tpu_custom_call" | custom-call | flops 4000000000 | tf_op jit(solution)/shard_map/pallas_call | solution.py:750
  87.9 0.1 collective-permute-done.28.refs_4_
  88.1 1.5 %collective-permute-done.27.refs_2_ = bf16[1216,128]{1,0:T(8,128)(2,1)S(1)} collective-permute-done((bf16[1216,128]{1,0:T(8,128)(2,1)S(1)}, bf16[1216,128]{1,0:T(8,128)(2,1)S(1)}, u32[]{:S(2)}, u32[]{:S(2)}) %collective-permute-start.27) | collective-permute-done | bytes 311328 | tf_op jit(solution)/shard_map/ppermute | solution.py:547
  89.6 0.5 collective-permute-start.31
  90.1 1.5 %collective-permute-start.29 = (bf16[1216,128]{1,0:T(8,128)(2,1)S(1)}, bf16[1216,128]{1,0:T(8,128)(2,1)S(1)}, u32[]{:S(2)}, u32[]{:S(2)}) collective-permute-start(bf16[1216,128]{1,0:T(8,128)(2,1)S(1)} %collective-permute-done.28.refs_4_), channel_id=1, source_target_pairs={{0,8},{1,3},{2,10},{3,1},{4,12},{5,7},{6,14},{7,5},{8,0},{9,11},{1... | collective-permute-start | bytes 933896 | tf_op jit(solution)/shard_map/ppermute | solution.py:547
  91.6 0.0 collective-permute-done.31.refs_3_
  91.7 0.4 collective-permute-done.32.refs_5_
  92.1 2.4 %shard_map.78 = (f32[3,960,320]{2,1,0:T(8,128)}, f32[3,320,320]{2,1,0:T(8,128)}) custom-call(bf16[1216,128]{1,0:T(8,128)(2,1)S(1)} %shard_map.76.refs_0_, bf16[1216,128]{1,0:T(8,128)(2,1)S(1)} %collective-permute-done.30.refs_1_, bf16[1216,128]{1,0:T(8,128)(2,1)S(1)} %collective-permute-done.27.refs_2_, ...), custom_call_target="tpu_custom_call" | custom-call | flops 1000 | bytes 1000 | tf_op jit(solution)/shard_map/pallas_call | solution.py:595
  94.5 2.5 %collective-permute-done.29.refs_0_ = bf16[1216,128]{1,0:T(8,128)(2,1)S(1)} collective-permute-done((bf16[1216,128]{1,0:T(8,128)(2,1)S(1)}, bf16[1216,128]{1,0:T(8,128)(2,1)S(1)}, u32[]{:S(2)}, u32[]{:S(2)}) %collective-permute-start.29) | collective-permute-done | bytes 311328 | tf_op jit(solution)/shard_map/ppermute | solution.py:547
  97.0 1.6 %collective-permute-done.33.refs_1_ = bf16[1216,128]{1,0:T(8,128)(2,1)S(1)} collective-permute-done((bf16[1216,128]{1,0:T(8,128)(2,1)S(1)}, bf16[1216,128]{1,0:T(8,128)(2,1)S(1)}, u32[]{:S(2)}, u32[]{:S(2)}) %collective-permute-start.33) | collective-permute-done | bytes 311328 | tf_op jit(solution)/shard_map/ppermute | solution.py:609
  98.6 1.3 %shard_map.79 = (f32[3,960,320]{2,1,0:T(8,128)}, f32[3,320,320]{2,1,0:T(8,128)}) custom-call(bf16[1216,128]{1,0:T(8,128)(2,1)S(1)} %collective-permute-done.29.refs_0_, bf16[1216,128]{1,0:T(8,128)(2,1)S(1)} %collective-permute-done.33.refs_1_, f32[3,960,320]{2,1,0:T(8,128)} %get-tuple-element.103.refs_2_, ...), custom_call_target="tpu_custom_call", output_to_operand_aliasing={{0}: (2, {}), {1}: (3, {})} | custom-call | flops 1000 | bytes 1000 | tf_op jit(solution)/shard_map/pallas_call | solution.py:595
  (34 shorter events, 0.2 us)
Async XLA Ops:
  0.6 1.3 %copy-start.1 = (bf16[1,4,32,5120]{3,2,1,0:T(8,128)(2,1)S(1)}, bf16[1,4,32,5120]{3,2,1,0:T(8,128)(2,1)}, u32[]{:S(2)}) copy-start(bf16[1,4,32,5120]{3,2,1,0:T(8,128)(2,1)} %param.4) | copy-start | bytes 3932164
  1.9 1.3 %copy-start.3 = (bf16[1,4,32,5120]{3,2,1,0:T(8,128)(2,1)S(1)}, bf16[1,4,32,5120]{3,2,1,0:T(8,128)(2,1)}, u32[]{:S(2)}) copy-start(bf16[1,4,32,5120]{3,2,1,0:T(8,128)(2,1)} %param.7) | copy-start | bytes 3932164
  2.6 4.8 %collective-permute-start = (f32[8,640]{1,0:T(8,128)S(1)}, f32[8,640]{1,0:T(8,128)S(1)}, u32[]{:S(2)}, u32[]{:S(2)}) collective-permute-start(f32[8,640]{1,0:T(8,128)S(1)} %get-tuple-element.55.sums_ref), channel_id=1, source_target_pairs={{0,1},{1,0},{2,3},{3,2},{4,5},{5,4},{6,7},{7,6},{8,9},{9,8},{10,11... | collective-permute-start | bytes 61448 | tf_op jit(solution)/shard_map/ppermute | solution.py:609
  3.1 4.3 %collective-permute-start.1 = (bf16[128,384]{1,0:T(8,128)(2,1)S(1)}, bf16[128,384]{1,0:T(8,128)(2,1)S(1)}, u32[]{:S(2)}, u32[]{:S(2)}) collective-permute-start(bf16[128,384]{1,0:T(8,128)(2,1)S(1)} %get-tuple-element.56), channel_id=1, source_target_pairs={{0,1},{1,0},{2,3},{3,2},{4,5},{5,4},{6,7},{7,6},{8,9},{9,8},{10,11... | collective-permute-start | bytes 294920 | tf_op jit(solution)/shard_map/ppermute | solution.py:609
  3.3 4.2 %copy-start = (bf16[3,3,320,320]{3,2,1,0:T(8,128)(2,1)S(1)}, bf16[3,3,320,320]{3,2,1,0:T(8,128)(2,1)}, u32[]{:S(2)}) copy-start(bf16[3,3,320,320]{3,2,1,0:T(8,128)(2,1)} %kernel_ref.5) | copy-start | bytes 5529604
  3.5 20.8 %collective-permute-start.2 = (bf16[32,5120]{1,0:T(8,128)(2,1)S(1)}, bf16[32,5120]{1,0:T(8,128)(2,1)S(1)}, u32[]{:S(2)}, u32[]{:S(2)}) collective-permute-start(bf16[32,5120]{1,0:T(8,128)(2,1)S(1)} %get-tuple-element.58), channel_id=1, source_target_pairs={{0,2},{2,0},{4,6},{6,4},{1,3},{3,1},{5,7},{7,5},{8,10},{10,8},{12,... | collective-permute-start | bytes 983048 | tf_op jit(solution)/shard_map/ppermute | solution.py:288
  6.6 17.7 %copy-start.4 = (bf16[3,320,320]{2,1,0:T(8,128)(2,1)S(1)}, bf16[3,320,320]{2,1,0:T(8,128)(2,1)}, u32[]{:S(2)}) copy-start(bf16[3,320,320]{2,1,0:T(8,128)(2,1)} %kernel_ref.4) | copy-start | bytes 1843204
  6.6 17.7 %collective-permute-start.3 = (bf16[32,5120]{1,0:T(8,128)(2,1)S(1)}, bf16[32,5120]{1,0:T(8,128)(2,1)S(1)}, u32[]{:S(2)}, u32[]{:S(2)}) collective-permute-start(bf16[32,5120]{1,0:T(8,128)(2,1)S(1)} %get-tuple-element.59), channel_id=1, source_target_pairs={{2,4},{4,2},{3,5},{5,3},{10,12},{12,10},{11,13},{13,11},{18,20},{2... | collective-permute-start | bytes 983048 | tf_op jit(solution)/shard_map/ppermute | solution.py:288
  17.2 1.3 %collective-permute-start.4 = (f32[8,640]{1,0:T(8,128)S(1)}, f32[8,640]{1,0:T(8,128)S(1)}, u32[]{:S(2)}, u32[]{:S(2)}) collective-permute-start(f32[8,640]{1,0:T(8,128)S(1)} %get-tuple-element.60), channel_id=1, source_target_pairs={{0,1},{1,0},{2,3},{3,2},{4,5},{5,4},{6,7},{7,6},{8,9},{9,8},{10,11... | collective-permute-start | bytes 61448 | tf_op jit(solution)/shard_map/ppermute | solution.py:609
  18.5 9.1 %collective-permute-start.7 = (f32[8,640]{1,0:T(8,128)S(1)}, f32[8,640]{1,0:T(8,128)S(1)}, u32[]{:S(2)}, u32[]{:S(2)}) collective-permute-start(f32[8,640]{1,0:T(8,128)S(1)} %add.27.refs_0_), channel_id=1, source_target_pairs={{0,6},{2,4},{4,2},{6,0},{1,7},{3,5},{5,3},{7,1},{8,14},{10,12},{12... | collective-permute-start | bytes 61448 | tf_op jit(solution)/shard_map/ppermute | solution.py:609
  21.0 6.6 %collective-permute-start.6 = (f32[8,640]{1,0:T(8,128)S(1)}, f32[8,640]{1,0:T(8,128)S(1)}, u32[]{:S(2)}, u32[]{:S(2)}) collective-permute-start(f32[8,640]{1,0:T(8,128)S(1)} %add.27.refs_0_), channel_id=1, source_target_pairs={{0,4},{2,6},{4,0},{6,2},{1,5},{3,7},{5,1},{7,3},{8,12},{10,14},{12... | collective-permute-start | bytes 61448 | tf_op jit(solution)/shard_map/ppermute | solution.py:609
  24.3 3.8 %collective-permute-start.5 = (f32[8,640]{1,0:T(8,128)S(1)}, f32[8,640]{1,0:T(8,128)S(1)}, u32[]{:S(2)}, u32[]{:S(2)}) collective-permute-start(f32[8,640]{1,0:T(8,128)S(1)} %add.27.refs_0_), channel_id=1, source_target_pairs={{0,2},{2,0},{4,6},{6,4},{1,3},{3,1},{5,7},{7,5},{8,10},{10,8},{12,... | collective-permute-start | bytes 61448 | tf_op jit(solution)/shard_map/ppermute | solution.py:609
  30.5 9.2 %collective-permute-start.8 = (f32[384,384]{1,0:T(8,128)S(1)}, f32[384,384]{1,0:T(8,128)S(1)}, u32[]{:S(2)}, u32[]{:S(2)}) collective-permute-start(f32[384,384]{1,0:T(8,128)S(1)} %get-tuple-element.62), channel_id=1, source_target_pairs={{0,1},{1,0},{2,3},{3,2},{4,5},{5,4},{6,7},{7,6},{8,9},{9,8},{10,11... | collective-permute-start | bytes 1769480 | tf_op jit(solution)/shard_map/ppermute | solution.py:609
  30.6 2.0 %collective-permute-start.9 = (f32[8,640]{1,0:T(8,128)S(1)}, f32[8,640]{1,0:T(8,128)S(1)}, u32[]{:S(2)}, u32[]{:S(2)}) collective-permute-start(f32[8,640]{1,0:T(8,128)S(1)} %get-tuple-element.65), channel_id=1, source_target_pairs={{0,1},{1,0},{2,3},{3,2},{4,5},{5,4},{6,7},{7,6},{8,9},{9,8},{10,11... | collective-permute-start | bytes 61448 | tf_op jit(solution)/shard_map/ppermute | solution.py:609
  32.6 7.0 %collective-permute-start.12 = (f32[8,640]{1,0:T(8,128)S(1)}, f32[8,640]{1,0:T(8,128)S(1)}, u32[]{:S(2)}, u32[]{:S(2)}) collective-permute-start(f32[8,640]{1,0:T(8,128)S(1)} %add.28.refs_4_), channel_id=1, source_target_pairs={{0,6},{2,4},{4,2},{6,0},{1,7},{3,5},{5,3},{7,1},{8,14},{10,12},{12... | collective-permute-start | bytes 61448 | tf_op jit(solution)/shard_map/ppermute | solution.py:609
  33.6 6.0 %collective-permute-start.11 = (f32[8,640]{1,0:T(8,128)S(1)}, f32[8,640]{1,0:T(8,128)S(1)}, u32[]{:S(2)}, u32[]{:S(2)}) collective-permute-start(f32[8,640]{1,0:T(8,128)S(1)} %add.28.refs_4_), channel_id=1, source_target_pairs={{0,4},{2,6},{4,0},{6,2},{1,5},{3,7},{5,1},{7,3},{8,12},{10,14},{12... | collective-permute-start | bytes 61448 | tf_op jit(solution)/shard_map/ppermute | solution.py:609
  35.6 4.0 %collective-permute-start.10 = (f32[8,640]{1,0:T(8,128)S(1)}, f32[8,640]{1,0:T(8,128)S(1)}, u32[]{:S(2)}, u32[]{:S(2)}) collective-permute-start(f32[8,640]{1,0:T(8,128)S(1)} %add.28.refs_4_), channel_id=1, source_target_pairs={{0,2},{2,0},{4,6},{6,4},{1,3},{3,1},{5,7},{7,5},{8,10},{10,8},{12,... | collective-permute-start | bytes 61448 | tf_op jit(solution)/shard_map/ppermute | solution.py:609
  48.3 1.7 %collective-permute-start.14 = (bf16[1216,128]{1,0:T(8,128)(2,1)S(1)}, bf16[1216,128]{1,0:T(8,128)(2,1)S(1)}, u32[]{:S(2)}, u32[]{:S(2)}) collective-permute-start(bf16[1216,128]{1,0:T(8,128)(2,1)S(1)} %get-tuple-element.69), channel_id=1, source_target_pairs={{0,1},{1,0},{2,3},{3,2},{4,5},{5,4},{6,7},{7,6},{8,9},{9,8},{10,11... | collective-permute-start | bytes 933896 | tf_op jit(solution)/shard_map/ppermute | solution.py:609
  48.4 16.0 %collective-permute-start.13 = (bf16[1216,128]{1,0:T(8,128)(2,1)S(1)}, bf16[1216,128]{1,0:T(8,128)(2,1)S(1)}, u32[]{:S(2)}, u32[]{:S(2)}) collective-permute-start(bf16[1216,128]{1,0:T(8,128)(2,1)S(1)} %get-tuple-element.67), channel_id=1, source_target_pairs={{0,1},{1,0},{2,3},{3,2},{4,5},{5,4},{6,7},{7,6},{8,9},{9,8},{10,11... | collective-permute-start | bytes 933896 | tf_op jit(solution)/shard_map/ppermute | solution.py:609
  48.9 2.0 %collective-permute-start.15 = (bf16[1216,128]{1,0:T(8,128)(2,1)S(1)}, bf16[1216,128]{1,0:T(8,128)(2,1)S(1)}, u32[]{:S(2)}, u32[]{:S(2)}) collective-permute-start(bf16[1216,128]{1,0:T(8,128)(2,1)S(1)} %get-tuple-element.71), channel_id=1, source_target_pairs={{0,1},{1,0},{2,3},{3,2},{4,5},{5,4},{6,7},{7,6},{8,9},{9,8},{10,11... | collective-permute-start | bytes 933896 | tf_op jit(solution)/shard_map/ppermute | solution.py:609
  48.9 2.4 %collective-permute-start.16 = (bf16[1216,128]{1,0:T(8,128)(2,1)S(1)}, bf16[1216,128]{1,0:T(8,128)(2,1)S(1)}, u32[]{:S(2)}, u32[]{:S(2)}) collective-permute-start(bf16[1216,128]{1,0:T(8,128)(2,1)S(1)} %get-tuple-element.73), channel_id=1, source_target_pairs={{0,1},{1,0},{2,3},{3,2},{4,5},{5,4},{6,7},{7,6},{8,9},{9,8},{10,11... | collective-permute-start | bytes 933896 | tf_op jit(solution)/shard_map/ppermute | solution.py:609
  50.0 4.9 %copy-start.2 = (bf16[1,4,32,5120]{3,2,1,0:T(8,128)(2,1)S(1)}, bf16[1,4,32,5120]{3,2,1,0:T(8,128)(2,1)}, u32[]{:S(2)}) copy-start(bf16[1,4,32,5120]{3,2,1,0:T(8,128)(2,1)} %param.4) | copy-start | bytes 3932164
  51.4 13.0 %collective-permute-start.17 = (bf16[1216,128]{1,0:T(8,128)(2,1)S(1)}, bf16[1216,128]{1,0:T(8,128)(2,1)S(1)}, u32[]{:S(2)}, u32[]{:S(2)}) collective-permute-start(bf16[1216,128]{1,0:T(8,128)(2,1)S(1)} %add_convert_fusion.2), channel_id=1, source_target_pairs={{0,8},{1,3},{2,10},{3,1},{4,12},{5,7},{6,14},{7,5},{8,0},{9,11},{1... | collective-permute-start | bytes 933896 | tf_op jit(solution)/shard_map/ppermute | solution.py:547
  52.9 11.5 %collective-permute-start.18 = (bf16[1216,128]{1,0:T(8,128)(2,1)S(1)}, bf16[1216,128]{1,0:T(8,128)(2,1)S(1)}, u32[]{:S(2)}, u32[]{:S(2)}) collective-permute-start(bf16[1216,128]{1,0:T(8,128)(2,1)S(1)} %add_convert_fusion.1), channel_id=1, source_target_pairs={{0,16},{1,5},{2,18},{3,7},{4,20},{5,1},{6,22},{7,3},{8,24},{9,13},... | collective-permute-start | bytes 933896 | tf_op jit(solution)/shard_map/ppermute | solution.py:547
  54.5 10.0 %collective-permute-start.19 = (bf16[1216,128]{1,0:T(8,128)(2,1)S(1)}, bf16[1216,128]{1,0:T(8,128)(2,1)S(1)}, u32[]{:S(2)}, u32[]{:S(2)}) collective-permute-start(bf16[1216,128]{1,0:T(8,128)(2,1)S(1)} %add_convert_fusion), channel_id=1, source_target_pairs={{0,24},{1,7},{2,26},{3,5},{4,28},{5,3},{6,30},{7,1},{8,16},{9,15},... | collective-permute-start | bytes 933896 | tf_op jit(solution)/shard_map/ppermute | solution.py:547
  64.6 5.6 %collective-permute-start.20 = (bf16[304,128]{1,0:T(8,128)(2,1)S(1)}, bf16[304,128]{1,0:T(8,128)(2,1)S(1)}, u32[]{:S(2)}, u32[]{:S(2)}) collective-permute-start(bf16[304,128]{1,0:T(8,128)(2,1)S(1)} %get-tuple-element.85), channel_id=1, source_target_pairs={{0,2},{1,9},{2,0},{3,11},{4,6},{5,13},{6,4},{7,15},{8,10},{9,1},{1... | collective-permute-start | bytes 233480 | tf_op jit(solution)/shard_map/ppermute | solution.py:547
  65.8 6.1 %collective-permute-start.21 = (bf16[304,128]{1,0:T(8,128)(2,1)S(1)}, bf16[304,128]{1,0:T(8,128)(2,1)S(1)}, u32[]{:S(2)}, u32[]{:S(2)}) collective-permute-start(bf16[304,128]{1,0:T(8,128)(2,1)S(1)} %get-tuple-element.86), channel_id=1, source_target_pairs={{0,4},{1,17},{2,6},{3,19},{4,0},{5,21},{6,2},{7,23},{8,12},{9,25},... | collective-permute-start | bytes 233480 | tf_op jit(solution)/shard_map/ppermute | solution.py:547
  66.8 6.3 %collective-permute-start.22 = (bf16[304,128]{1,0:T(8,128)(2,1)S(1)}, bf16[304,128]{1,0:T(8,128)(2,1)S(1)}, u32[]{:S(2)}, u32[]{:S(2)}) collective-permute-start(bf16[304,128]{1,0:T(8,128)(2,1)S(1)} %get-tuple-element.87), channel_id=1, source_target_pairs={{0,6},{1,25},{2,4},{3,27},{4,2},{5,29},{6,0},{7,31},{8,14},{9,17},... | collective-permute-start | bytes 233480 | tf_op jit(solution)/shard_map/ppermute | solution.py:547
  69.1 1.2 %collective-permute-start.23 = (f32[8,640]{1,0:T(8,128)S(1)}, f32[8,640]{1,0:T(8,128)S(1)}, u32[]{:S(2)}, u32[]{:S(2)}) collective-permute-start(f32[8,640]{1,0:T(8,128)S(1)} %get-tuple-element.88.mine_ref), channel_id=1, source_target_pairs={{0,1},{1,0},{2,3},{3,2},{4,5},{5,4},{6,7},{7,6},{8,9},{9,8},{10,11... | collective-permute-start | bytes 61448 | tf_op jit(solution)/shard_map/ppermute | solution.py:609
  73.2 6.3 %collective-permute-start.26 = (bf16[304,128]{1,0:T(8,128)(2,1)S(1)}, bf16[304,128]{1,0:T(8,128)(2,1)S(1)}, u32[]{:S(2)}, u32[]{:S(2)}) collective-permute-start(bf16[304,128]{1,0:T(8,128)(2,1)S(1)} %add_convert_fusion.3.refs_0_), channel_id=1, source_target_pairs={{0,6},{1,25},{2,4},{3,27},{4,2},{5,29},{6,0},{7,31},{8,14},{9,17},... | collective-permute-start | bytes 233480 | tf_op jit(solution)/shard_map/ppermute | solution.py:547
  75.4 5.7 %collective-permute-start.25 = (bf16[304,128]{1,0:T(8,128)(2,1)S(1)}, bf16[304,128]{1,0:T(8,128)(2,1)S(1)}, u32[]{:S(2)}, u32[]{:S(2)}) collective-permute-start(bf16[304,128]{1,0:T(8,128)(2,1)S(1)} %add_convert_fusion.3.refs_0_), channel_id=1, source_target_pairs={{0,4},{1,17},{2,6},{3,19},{4,0},{5,21},{6,2},{7,23},{8,12},{9,25},... | collective-permute-start | bytes 233480 | tf_op jit(solution)/shard_map/ppermute | solution.py:547
  75.7 5.4 %collective-permute-start.24 = (bf16[304,128]{1,0:T(8,128)(2,1)S(1)}, bf16[304,128]{1,0:T(8,128)(2,1)S(1)}, u32[]{:S(2)}, u32[]{:S(2)}) collective-permute-start(bf16[304,128]{1,0:T(8,128)(2,1)S(1)} %add_convert_fusion.3.refs_0_), channel_id=1, source_target_pairs={{0,2},{1,9},{2,0},{3,11},{4,6},{5,13},{6,4},{7,15},{8,10},{9,1},{1... | collective-permute-start | bytes 233480 | tf_op jit(solution)/shard_map/ppermute | solution.py:547
  81.1 7.0 %collective-permute-start.28 = (bf16[1216,128]{1,0:T(8,128)(2,1)S(1)}, bf16[1216,128]{1,0:T(8,128)(2,1)S(1)}, u32[]{:S(2)}, u32[]{:S(2)}) collective-permute-start(bf16[1216,128]{1,0:T(8,128)(2,1)S(1)} %shard_map.76.refs_0_), channel_id=1, source_target_pairs={{0,16},{1,5},{2,18},{3,7},{4,20},{5,1},{6,22},{7,3},{8,24},{9,13},... | collective-permute-start | bytes 933896 | tf_op jit(solution)/shard_map/ppermute | solution.py:547
  82.7 6.9 %collective-permute-start.27 = (bf16[1216,128]{1,0:T(8,128)(2,1)S(1)}, bf16[1216,128]{1,0:T(8,128)(2,1)S(1)}, u32[]{:S(2)}, u32[]{:S(2)}) collective-permute-start(bf16[1216,128]{1,0:T(8,128)(2,1)S(1)} %shard_map.76.refs_0_), channel_id=1, source_target_pairs={{0,8},{1,3},{2,10},{3,1},{4,12},{5,7},{6,14},{7,5},{8,0},{9,11},{1... | collective-permute-start | bytes 933896 | tf_op jit(solution)/shard_map/ppermute | solution.py:547
  89.6 2.0 %collective-permute-start.30 = (bf16[1216,128]{1,0:T(8,128)(2,1)S(1)}, bf16[1216,128]{1,0:T(8,128)(2,1)S(1)}, u32[]{:S(2)}, u32[]{:S(2)}) collective-permute-start(bf16[1216,128]{1,0:T(8,128)(2,1)S(1)} %shard_map.76.refs_0_), channel_id=1, source_target_pairs={{0,1},{1,0},{2,3},{3,2},{4,5},{5,4},{6,7},{7,6},{8,9},{9,8},{10,11... | collective-permute-start | bytes 933896 | tf_op jit(solution)/shard_map/ppermute | solution.py:609
  89.6 2.0 %collective-permute-start.31 = (bf16[1216,128]{1,0:T(8,128)(2,1)S(1)}, bf16[1216,128]{1,0:T(8,128)(2,1)S(1)}, u32[]{:S(2)}, u32[]{:S(2)}) collective-permute-start(bf16[1216,128]{1,0:T(8,128)(2,1)S(1)} %collective-permute-done.27.refs_2_), channel_id=1, source_target_pairs={{0,1},{1,0},{2,3},{3,2},{4,5},{5,4},{6,7},{7,6},{8,9},{9,8},{10,11... | collective-permute-start | bytes 933896 | tf_op jit(solution)/shard_map/ppermute | solution.py:609
  90.1 2.0 %collective-permute-start.32 = (bf16[1216,128]{1,0:T(8,128)(2,1)S(1)}, bf16[1216,128]{1,0:T(8,128)(2,1)S(1)}, u32[]{:S(2)}, u32[]{:S(2)}) collective-permute-start(bf16[1216,128]{1,0:T(8,128)(2,1)S(1)} %collective-permute-done.28.refs_4_), channel_id=1, source_target_pairs={{0,1},{1,0},{2,3},{3,2},{4,5},{5,4},{6,7},{7,6},{8,9},{9,8},{10,11... | collective-permute-start | bytes 933896 | tf_op jit(solution)/shard_map/ppermute | solution.py:609
  90.1 6.9 %collective-permute-start.29 = (bf16[1216,128]{1,0:T(8,128)(2,1)S(1)}, bf16[1216,128]{1,0:T(8,128)(2,1)S(1)}, u32[]{:S(2)}, u32[]{:S(2)}) collective-permute-start(bf16[1216,128]{1,0:T(8,128)(2,1)S(1)} %collective-permute-done.28.refs_4_), channel_id=1, source_target_pairs={{0,8},{1,3},{2,10},{3,1},{4,12},{5,7},{6,14},{7,5},{8,0},{9,11},{1... | collective-permute-start | bytes 933896 | tf_op jit(solution)/shard_map/ppermute | solution.py:547
  97.0 1.6 %collective-permute-start.33 = (bf16[1216,128]{1,0:T(8,128)(2,1)S(1)}, bf16[1216,128]{1,0:T(8,128)(2,1)S(1)}, u32[]{:S(2)}, u32[]{:S(2)}) collective-permute-start(bf16[1216,128]{1,0:T(8,128)(2,1)S(1)} %collective-permute-done.29.refs_0_), channel_id=1, source_target_pairs={{0,1},{1,0},{2,3},{3,2},{4,5},{5,4},{6,7},{7,6},{8,9},{9,8},{10,11... | collective-permute-start | bytes 933896 | tf_op jit(solution)/shard_map/ppermute | solution.py:609

commit v7 on v6

--- a/solution.py
+++ b/solution.py
@@ -13,6 +13,7 @@
 F32 = jnp.float32
 BF16 = jnp.bfloat16
 VMEM_LIMIT = 20 * 1024 * 1024
+CONV_LIMIT = 28 * 1024 * 1024
 SMALL_LIMIT = 4 * 1024 * 1024
 CONV_COST = 12_000_000_000
 
@@ -147,29 +148,72 @@
         )
 
 
-def forward_weights(kernel_ref, even_ref, odd_ref, sizes):
-    channels, slack, window = sizes.channels, sizes.slack, sizes.window
-    for weights in (even_ref, odd_ref):
-        weights[...] = jnp.zeros(weights.shape, BF16)
-    for i in range(3):
-        for j in range(3):
-            taps = kernel_ref[i, j]
-            zeros = jnp.zeros((channels, slack), BF16)
-            at = i * window + j * channels
-            even_ref[at + slack : at + slack + channels, :] = jnp.concatenate([taps, zeros], axis=1)
-            odd_ref[at : at + channels, :] = jnp.concatenate([zeros, taps], axis=1)
-
-
-def backward_weights(kernel_ref, even_ref, odd_ref, sizes):
-    channels, slack, window = sizes.channels, sizes.slack, sizes.window
-    for weights in (even_ref, odd_ref):
-        weights[...] = jnp.zeros(weights.shape, BF16)
-    zeros = jnp.zeros((channels, slack), BF16)
-    for i in range(3):
-        taps = [kernel_ref[2 - i, 2 - j] for j in range(3)]
-        lanes = slice(i * window, (i + 1) * window)
-        even_ref[0:channels, lanes] = jnp.concatenate([zeros] + taps, axis=1)
-        odd_ref[slack : slack + channels, lanes] = jnp.concatenate(taps + [zeros], axis=1)
+class Tile:
+    def __init__(self, t, sizes):
+        channels = sizes.channels
+        low, high = 256 * t // channels, (256 * t + 255) // channels
+        self.lanes = slice(256 * t, 256 * t + 256)
+        self.columns = []
+        for column in range(low, high + 1):
+            first = max(256 * t, column * channels)
+            last = min(256 * t + 256, (column + 1) * channels)
+            self.columns.append((column, first - column * channels, last - column * channels, first - 256 * t))
+        self.taken = range(low - 1, high + 2)
+        begin = sizes.edge + (low - 1) * channels
+        end = sizes.edge + (high + 2) * channels
+        self.start = begin // 128 * 128
+        self.head = begin - self.start
+        self.size = -(-(end - self.start) // 128) * 128
+        self.tail = self.size - self.head - len(self.taken) * channels
+
+
+def tiles_of(sizes):
+    return [Tile(t, sizes) for t in range(4 * sizes.channels // 256)]
+
+
+def tile_scratch(sizes):
+    return [pltpu.VMEM((3 * tile.size, 256), BF16) for tile in tiles_of(sizes)]
+
+
+def tile_scratch_back(sizes):
+    return [pltpu.VMEM((256, 3 * tile.size), BF16) for tile in tiles_of(sizes)]
+
+
+def forward_weights(kernel_ref, tiles, targets, sizes):
+    channels = sizes.channels
+    for tile, target in zip(tiles, targets):
+        for i in range(3):
+            at = i * tile.size
+            if tile.head:
+                target[at : at + tile.head, :] = jnp.zeros((tile.head, 256), BF16)
+            at += tile.head
+            for taken in tile.taken:
+                parts = []
+                for column, first, last, _ in tile.columns:
+                    j = taken - column + 1
+                    inside = 0 <= j <= 2
+                    parts.append(kernel_ref[i, j][:, first:last] if inside else jnp.zeros((channels, last - first), BF16))
+                target[at : at + channels, :] = jnp.concatenate(parts, axis=1) if len(parts) > 1 else parts[0]
+                at += channels
+            if tile.tail:
+                target[at : at + tile.tail, :] = jnp.zeros((tile.tail, 256), BF16)
+
+
+def backward_weights(kernel_ref, tiles, targets, sizes):
+    channels = sizes.channels
+    for tile, target in zip(tiles, targets):
+        for i in range(3):
+            lanes = slice(i * tile.size, (i + 1) * tile.size)
+            for column, first, last, at in tile.columns:
+                count = last - first
+                parts = [jnp.zeros((count, tile.head), BF16)] if tile.head else []
+                for taken in tile.taken:
+                    j = taken - column + 1
+                    inside = 0 <= j <= 2
+                    parts.append(kernel_ref[2 - i, 2 - j][first:last, :] if inside else jnp.zeros((count, channels), BF16))
+                if tile.tail:
+                    parts.append(jnp.zeros((count, tile.tail), BF16))
+                target[at : at + count, lanes] = jnp.concatenate(parts, axis=1)
 
 
 def temporal_weights(kernel_ref, even_ref, odd_ref, sizes):
@@ -183,11 +227,10 @@
         odd_ref[slack : slack + channels, lanes] = jnp.concatenate([zeros, kernel_ref[i]], axis=1)
 
 
-def windows(padded_ref, p, count, odd, sizes):
+def windows(padded_ref, tile, sizes):
     found = []
-    for q in range(count):
-        start = pl.multiple_of((p + q) * sizes.pair, 128) + (sizes.edge if odd else 0)
-        lanes = pl.ds(pl.multiple_of(start, 128), sizes.window)
+    for start in range(tile.start, tile.start + sizes.width, 2 * sizes.pair):
+        lanes = slice(start, start + tile.size)
         found.append(jnp.concatenate([padded_ref[i, :, lanes] for i in range(3)], axis=1))
     return jnp.concatenate(found, axis=0)
 
@@ -198,10 +241,11 @@
 
 
 def forward_body(
-    sizes, frame_entries, block, x_ref, sums_ref, other_ref, rim_ref, kernel_ref,
-    hidden_ref, act_ref, clip_ref, padded, even_ref, odd_ref,
+    sizes, frame_entries, x_ref, sums_ref, other_ref, rim_ref, kernel_ref,
+    hidden_ref, act_ref, clip_ref, padded, plain, square, *weights
 ):
-    forward_weights(kernel_ref, even_ref, odd_ref, sizes)
+    tiles = tiles_of(sizes)
+    forward_weights(kernel_ref, tiles, weights, sizes)
     mean, rate = moments(sums_ref[...] + other_ref[...], sizes.frames, frame_entries, sizes)
 
     def rim(rows, f, before):
@@ -222,25 +266,18 @@
     lax.fori_loop(0, sizes.pairs, activate, 0)
     act_ref[...] = padded[1]
 
-    def step(b, carry):
-        plain, square = carry
-        p = b * block
-        even = jnp.dot(windows(padded, p, block, False, sizes), even_ref[...], preferred_element_type=F32)
-        odd = jnp.dot(windows(padded, p, block, True, sizes), odd_ref[...], preferred_element_type=F32)
-        for q in range(block):
-            rows = slice(q * sizes.pixels, (q + 1) * sizes.pixels)
-            spatial = join(even[rows], odd[rows], sizes)
-            lanes = pair_lanes(p + q, sizes)
-            hidden = (x_ref[:, lanes].astype(F32) + spatial).astype(BF16)
+    for tile, weight in zip(tiles, weights):
+        spatial = jnp.dot(windows(padded, tile, sizes), weight[...], preferred_element_type=F32)
+        sums = [jnp.zeros((8, 256), F32)] * 2
+        for q in range(sizes.pairs // 2):
+            lanes = slice(q * 2 * sizes.pair + tile.lanes.start, q * 2 * sizes.pair + tile.lanes.stop)
+            hidden = x_ref[:, lanes].astype(F32) + spatial[q * sizes.pixels : (q + 1) * sizes.pixels]
+            hidden = hidden.astype(BF16)
             hidden_ref[:, lanes] = hidden
             wide = hidden.astype(F32)
-            plain = plain + fold(wide)
-            square = square + fold(wide * wide)
-        return plain, square
-
-    zero = jnp.zeros((8, sizes.pair), F32)
-    plain, square = lax.fori_loop(0, sizes.pairs // block, step, (zero, zero))
-    put_sums(clip_ref, plain, square)
+            sums = [sums[0] + fold(wide), sums[1] + fold(wide * wide)]
+        plain[:, tile.lanes], square[:, tile.lanes] = sums
+    put_sums(clip_ref, *(both[:, : sizes.pair] + both[:, sizes.pair :] for both in (plain, square)))
 
 
 def add_up(refs):
@@ -459,10 +496,11 @@
 
 
 def backward_body(
-    sizes, frame_entries, block, x_ref, sums_ref, other_ref, dspat_ref, kernel_ref,
-    grad_ref, out_ref, padded, plains, even_ref, odd_ref,
+    sizes, frame_entries, x_ref, sums_ref, other_ref, dspat_ref, kernel_ref,
+    grad_ref, out_ref, padded, plains, *weights
 ):
-    backward_weights(kernel_ref, even_ref, odd_ref, sizes)
+    tiles = tiles_of(sizes)
+    backward_weights(kernel_ref, tiles, weights, sizes)
     mean, rate = moments(sums_ref[...] + other_ref[...], sizes.frames, frame_entries, sizes)
 
     def spread(k, _):
@@ -473,34 +511,26 @@
         return 0
 
     lax.fori_loop(0, sizes.padded // 128, spread, 0)
-    plains[...] = jnp.zeros(plains.shape, F32)
-    contract = (((1,), (1,)), ((), ()))
-
-    def step(b, _):
-        p = b * block
-        even = lax.dot_general(
-            windows(padded, p, block, False, sizes), even_ref[...], contract, preferred_element_type=F32
+    mean, rate = (jnp.concatenate([values, values], axis=1) for values in (mean, rate))
+    for tile, weight in zip(tiles, weights):
+        dact = lax.dot_general(
+            windows(padded, tile, sizes), weight[...], (((1,), (1,)), ((), ())), preferred_element_type=F32
         )
-        odd = lax.dot_general(
-            windows(padded, p, block, True, sizes), odd_ref[...], contract, preferred_element_type=F32
-        )
-        for q in range(block):
-            base = q * sizes.pixels
-            for f in range(sizes.frames):
-                at = slice(base + f * sizes.rows, base + (f + 1) * sizes.rows)
-                dact = join(even[at], odd[at], sizes)
-                rows, lanes = pl.ds(f * sizes.rows, sizes.rows), pair_lanes(p + q, sizes)
-                normed = (x_ref[rows, lanes].astype(F32) - mean[f : f + 1]) * rate[f : f + 1]
+        for f in range(sizes.frames):
+            rows = pl.ds(f * sizes.rows, sizes.rows)
+            sums = [jnp.zeros((8, 256), F32)] * 2
+            for q in range(sizes.pairs // 2):
+                lanes = slice(q * 2 * sizes.pair + tile.lanes.start, q * 2 * sizes.pair + tile.lanes.stop)
+                normed = (x_ref[rows, lanes].astype(F32) - mean[f : f + 1, tile.lanes]) * rate[f : f + 1, tile.lanes]
                 _, s = silu_parts(normed)
-                grad = dact * (s * (1.0 + normed * (1.0 - s)))
+                at = q * sizes.pixels + f * sizes.rows
+                grad = dact[at : at + sizes.rows] * (s * (1.0 + normed * (1.0 - s)))
                 grad_ref[rows, lanes] = grad
-                plains[f] += fold(grad)
-                plains[sizes.frames + f] += fold(grad * normed)
-        return 0
-
-    lax.fori_loop(0, sizes.pairs // block, step, 0)
+                sums = [sums[0] + fold(grad), sums[1] + fold(grad * normed)]
+            plains[f, :, tile.lanes], plains[sizes.frames + f, :, tile.lanes] = sums
     for k in range(2 * sizes.frames):
-        out_ref[k : k + 1, :] = jnp.sum(plains[k], axis=0, keepdims=True)
+        both = jnp.sum(plains[k], axis=0, keepdims=True)
+        out_ref[k : k + 1, :] = both[:, : sizes.pair] + both[:, sizes.pair :]
 
 
 def finish_body(
@@ -684,10 +714,11 @@
     other = swap(sums, "col", 1)
     rim = swap(edge, "col", 1)
     hidden, act, clip = call(
-        functools.partial(forward_body, sizes, frame_entries, min(4, sizes.pairs)),
+        functools.partial(forward_body, sizes, frame_entries),
         [struct((sizes.pixels, width), BF16), struct((sizes.pixels, sizes.padded), BF16), sum_shape],
-        [padded_scratch] + [pltpu.VMEM((3 * sizes.window, sizes.edge), BF16)] * 2,
+        [padded_scratch] + [pltpu.VMEM((8, 2 * sizes.pair), F32)] * 2 + tile_scratch(sizes),
         flops=CONV_COST,
+        limit=CONV_LIMIT,
     )(x, sums, other, rim, spatial_kernel)
     clips = from_all(clip + swap(clip, "col", 1), "seq")
     dact = call(
@@ -737,11 +768,11 @@
     sends, dspat = lax.optimization_barrier((sends, dspat))
     found = [exchange(values, 0, n + 1) for n, values in enumerate(sends)]
     dnormed, mine = call(
-        functools.partial(backward_body, sizes, frame_entries, min(4, sizes.pairs)),
+        functools.partial(backward_body, sizes, frame_entries),
         [struct((sizes.pixels, width), F32), frame_shape],
-        [padded_scratch, pltpu.VMEM((2 * frames, 8, sizes.pair), F32)]
-        + [pltpu.VMEM((sizes.edge, 3 * sizes.window), BF16)] * 2,
+        [padded_scratch, pltpu.VMEM((2 * frames, 8, 2 * sizes.pair), F32)] + tile_scratch_back(sizes),
         flops=CONV_COST,
+        limit=CONV_LIMIT,
     )(x, sums, other, dspat, spatial_kernel)
     found, (dnormed, mine) = lax.optimization_barrier((found, (dnormed, mine)))
     theirs = swap(mine, "col", 1)

time: 100 us -> 98.6 us (0.986)
  Pallas kernels: 44.5 us -> 42.7 us
    pallas_call x2, Pallas kernels: 19.2 us -> 17.3 us  [the longest x1 8.91 us: shards(): call(functools.partial(forward_body, sizes, frame_entries), [struct((size...]
  transfers between devices with their start and end apart: 34 -> 34, of which waited for: 16 -> 16; matrix products, arithmetic and copies ran while one was open for 0% -> 0% of each run, Pallas kernels for 31% -> 30%
where the time goes in v7:
time: 98.6 us; the launch traced here: 98.4 us
  Pallas kernels  42.7 us (43%)
  starting transfers between devices  34.5 us (35%)
  waiting for transfers between devices  18.3 us (19%)
  local copies, waits for them, and re-layouts  1.42 us (1%)
  between operations  1.09 us (1%)
    ppermute x12, starting transfers between devices, exchange(): return lax.ppermute(values, names, pairs)  17 us
    ppermute x20, starting transfers between devices, swap(): return lax.ppermute(values, axis, [(i, i ^ bit) for i in range(count)])  13.6 us
    ppermute x12, waiting for transfers between devices, exchange(): return lax.ppermute(values, names, pairs)  10.5 us
    pallas_call x1, Pallas kernels, shards(): call(functools.partial(forward_body, sizes, frame_entries), [struct((size...  8.91 us
    pallas_call x1, Pallas kernels, shards(): call(functools.partial(spatial_grad_body, sizes, clip_entries, seqs), [st...  8.62 us
    pallas_call x1, Pallas kernels, shards(): call(functools.partial(backward_body, sizes, frame_entries), [struct((siz...  8.38 us
    ppermute x20, waiting for transfers between devices, swap(): return lax.ppermute(values, axis, [(i, i ^ bit) for i in range(count)])  7.88 us
    ppermute x2, starting transfers between devices, neighbour_frames(): found.append(lax.ppermute(values, 'seq', pairs))  3.89 us
  transfers between devices with their start and end apart: 34, of which 16 were waited for; matrix products, arithmetic and copies ran while one was open for 0% of the time, Pallas kernels for 30%

profile of v7, /device:TPU:0, one launch (start us, length us, event | category | flops | bytes accessed | tf_op | source)
XLA Modules:
  0.0 98.4 jit_solution(18321317826939187818)
XLA Ops:
  0.6 1.3 %copy-done.1 = bf16[1,4,32,5120]{3,2,1,0:T(8,128)(2,1)S(1)} copy-done((bf16[1,4,32,5120]{3,2,1,0:T(8,128)(2,1)S(1)}, bf16[1,4,32,5120]{3,2,1,0:T(8,128)(2,1)}, u32[]{:S(2)}) %copy-start.1) | copy-done | bytes 1310744
  2.0 0.6 shard_map.67
  2.6 0.5 collective-permute-start
  3.1 0.1 collective-permute-start.1
  3.2 0.1 copy-done.3
  3.3 0.2 shard_map.69
  3.5 3.1 %collective-permute-start.2 = (bf16[32,5120]{1,0:T(8,128)(2,1)S(1)}, bf16[32,5120]{1,0:T(8,128)(2,1)S(1)}, u32[]{:S(2)}, u32[]{:S(2)}) collective-permute-start(bf16[32,5120]{1,0:T(8,128)(2,1)S(1)} %get-tuple-element.58), channel_id=1, source_target_pairs={{0,2},{2,0},{4,6},{6,4},{1,3},{3,1},{5,7},{7,5},{8,10},{10,8},{12,... | collective-permute-start | bytes 983048 | tf_op jit(solution)/shard_map/ppermute | solution.py:325
  6.6 0.8 collective-permute-start.3
  7.4 8.9 %shard_map.68 = (bf16[128,5120]{1,0:T(8,128)(2,1)S(1)}, bf16[128,5888]{1,0:T(8,128)(2,1)S(1)}, f32[8,640]{1,0:T(8,128)S(1)}) custom-call(bf16[128,5120]{1,0:T(8,128)(2,1)S(1)} %bitcast.5, f32[8,640]{1,0:T(8,128)S(1)} %get-tuple-element.55.sums_ref, f32[8,640]{1,0:T(8,128)S(1)} %collective-permute-done.other_ref, ...), custom_call_target="tpu_custom_call" | custom-call | flops 12000000000 | tf_op jit(solution)/shard_map/pallas_call | solution.py:716
  16.4 0.1 collective-permute-start.4
  16.4 1.2 %collective-permute-done.4 = f32[8,640]{1,0:T(8,128)S(1)} collective-permute-done((f32[8,640]{1,0:T(8,128)S(1)}, f32[8,640]{1,0:T(8,128)S(1)}, u32[]{:S(2)}, u32[]{:S(2)}) %collective-permute-start.4) | collective-permute-done | bytes 20512 | tf_op jit(solution)/shard_map/ppermute | solution.py:639
  17.6 2.9 %collective-permute-start.7 = (f32[8,640]{1,0:T(8,128)S(1)}, f32[8,640]{1,0:T(8,128)S(1)}, u32[]{:S(2)}, u32[]{:S(2)}) collective-permute-start(f32[8,640]{1,0:T(8,128)S(1)} %add.27.refs_0_), channel_id=1, source_target_pairs={{0,6},{2,4},{4,2},{6,0},{1,7},{3,5},{5,3},{7,1},{8,14},{10,12},{12... | collective-permute-start | bytes 61448 | tf_op jit(solution)/shard_map/ppermute | solution.py:639
  20.5 3.0 %collective-permute-start.6 = (f32[8,640]{1,0:T(8,128)S(1)}, f32[8,640]{1,0:T(8,128)S(1)}, u32[]{:S(2)}, u32[]{:S(2)}) collective-permute-start(f32[8,640]{1,0:T(8,128)S(1)} %add.27.refs_0_), channel_id=1, source_target_pairs={{0,4},{2,6},{4,0},{6,2},{1,5},{3,7},{5,1},{7,3},{8,12},{10,14},{12... | collective-permute-start | bytes 61448 | tf_op jit(solution)/shard_map/ppermute | solution.py:639
  23.5 3.3 %shard_map.70.dact_ref = f32[128,5120]{1,0:T(8,128)S(1)} custom-call(bf16[128,5120]{1,0:T(8,128)(2,1)S(1)} %bitcast.9, bf16[32,5120]{1,0:T(8,128)(2,1)S(1)} %collective-permute-done.2.before_ref, bf16[32,5120]{1,0:T(8,128)(2,1)S(1)} %collective-permute-done.3.after_ref, bf16[3,320,320]{2,1,0:T(8,128)(2,1)S(1)} %copy-done.4), custom_call_target="tpu_custom_call" | custom-call | flops 4000000000 | tf_op jit(solution)/shard_map/pallas_call | solution.py:724
  26.8 0.5 collective-permute-done.5.refs_1_
  27.2 2.4 %shard_map.71 = (bf16[128,5120]{1,0:T(8,128)(2,1)S(1)}, f32[128,5120]{1,0:T(8,128)S(1)}, f32[8,640]{1,0:T(8,128)S(1)}, f32[384,384]{1,0:T(8,128)S(1)}) custom-call(bf16[128,5120]{1,0:T(8,128)(2,1)S(1)} %get-tuple-element.57.hidden_ref, bf16[128,5120]{1,0:T(8,128)(2,1)S(1)} %bitcast.10, f32[128,5120]{1,0:T(8,128)S(1)} %shard_map.70.dact_ref, ...), custom_call_target="tpu_custom_call" | custom-call | flops 4000000000 | tf_op jit(solution)/shard_map/pallas_call | solution.py:730
  29.7 0.1 collective-permute-start.8
  29.8 0.5 collective-permute-start.9
  30.2 1.5 %collective-permute-done.9 = f32[8,640]{1,0:T(8,128)S(1)} collective-permute-done((f32[8,640]{1,0:T(8,128)S(1)}, f32[8,640]{1,0:T(8,128)S(1)}, u32[]{:S(2)}, u32[]{:S(2)}) %collective-permute-start.9) | collective-permute-done | bytes 20512 | tf_op jit(solution)/shard_map/ppermute | solution.py:639
  31.8 1.0 %collective-permute-start.12 = (f32[8,640]{1,0:T(8,128)S(1)}, f32[8,640]{1,0:T(8,128)S(1)}, u32[]{:S(2)}, u32[]{:S(2)}) collective-permute-start(f32[8,640]{1,0:T(8,128)S(1)} %add.28.refs_4_), channel_id=1, source_target_pairs={{0,6},{2,4},{4,2},{6,0},{1,7},{3,5},{5,3},{7,1},{8,14},{10,12},{12... | collective-permute-start | bytes 61448 | tf_op jit(solution)/shard_map/ppermute | solution.py:639
  32.8 2.0 %collective-permute-start.11 = (f32[8,640]{1,0:T(8,128)S(1)}, f32[8,640]{1,0:T(8,128)S(1)}, u32[]{:S(2)}, u32[]{:S(2)}) collective-permute-start(f32[8,640]{1,0:T(8,128)S(1)} %add.28.refs_4_), channel_id=1, source_target_pairs={{0,4},{2,6},{4,0},{6,2},{1,5},{3,7},{5,1},{7,3},{8,12},{10,14},{12... | collective-permute-start | bytes 61448 | tf_op jit(solution)/shard_map/ppermute | solution.py:639
  34.8 1.4 %collective-permute-start.10 = (f32[8,640]{1,0:T(8,128)S(1)}, f32[8,640]{1,0:T(8,128)S(1)}, u32[]{:S(2)}, u32[]{:S(2)}) collective-permute-start(f32[8,640]{1,0:T(8,128)S(1)} %add.28.refs_4_), channel_id=1, source_target_pairs={{0,2},{2,0},{4,6},{6,4},{1,3},{3,1},{5,7},{7,5},{8,10},{10,8},{12,... | collective-permute-start | bytes 61448 | tf_op jit(solution)/shard_map/ppermute | solution.py:639
  36.2 2.7 %shard_map.72.time_ref = f32[320,960]{1,0:T(8,128)S(1)} custom-call(bf16[128,5120]{1,0:T(8,128)(2,1)S(1)} %get-tuple-element.64.act_ref, bf16[128,5120]{1,0:T(8,128)(2,1)S(1)} %bitcast.11, bf16[32,5120]{1,0:T(8,128)(2,1)S(1)} %collective-permute-done.2.before_ref, bf16[32,5120]{1,0:T(8,128)(2,1)S(1)} %collective-permute-done.3.after_ref), custom_call_target="tpu_custom_call" | custom-call | flops 4000000000 | tf_op jit(solution)/shard_map/pallas_call | solution.py:743
  38.9 8.6 %shard_map.73 = (bf16[128,5120]{1,0:T(8,128)(2,1)S(1)}, bf16[128,5888]{1,0:T(8,128)(2,1)S(1)}, f32[1216,128]{1,0:T(8,128)S(1)}, f32[1216,128]{1,0:T(8,128)S(1)},...) custom-call(bf16[128,5120]{1,0:T(8,128)(2,1)S(1)} %get-tuple-element, ...), custom_call_target="tpu_custom_call" | custom-call | flops 12000000000 | tf_op jit(solution)/shard_map/pallas_call | solution.py:752
  47.5 0.1 collective-permute-start.14
  47.6 0.5 collective-permute-start.13
  48.1 0.1 collective-permute-start.15
  48.1 0.4 collective-permute-start.16
  48.6 0.6 collective-permute-done.14
  49.2 0.1 add_convert_fusion.2
  49.2 0.8 collective-permute-done.15
  50.0 0.1 add_convert_fusion.1
  50.1 0.4 collective-permute-done.16
  50.5 0.1 add_convert_fusion
  50.6 1.6 %collective-permute-start.17 = (bf16[1216,128]{1,0:T(8,128)(2,1)S(1)}, bf16[1216,128]{1,0:T(8,128)(2,1)S(1)}, u32[]{:S(2)}, u32[]{:S(2)}) collective-permute-start(bf16[1216,128]{1,0:T(8,128)(2,1)S(1)} %add_convert_fusion.2), channel_id=1, source_target_pairs={{0,8},{1,3},{2,10},{3,1},{4,12},{5,7},{6,14},{7,5},{8,0},{9,11},{1... | collective-permute-start | bytes 933896 | tf_op jit(solution)/shard_map/ppermute | solution.py:577
  52.2 1.5 %collective-permute-start.18 = (bf16[1216,128]{1,0:T(8,128)(2,1)S(1)}, bf16[1216,128]{1,0:T(8,128)(2,1)S(1)}, u32[]{:S(2)}, u32[]{:S(2)}) collective-permute-start(bf16[1216,128]{1,0:T(8,128)(2,1)S(1)} %add_convert_fusion.1), channel_id=1, source_target_pairs={{0,16},{1,5},{2,18},{3,7},{4,20},{5,1},{6,22},{7,3},{8,24},{9,13},... | collective-permute-start | bytes 933896 | tf_op jit(solution)/shard_map/ppermute | solution.py:577
  53.7 0.5 collective-permute-start.19
  54.1 8.4 %shard_map.74 = (f32[128,5120]{1,0:T(8,128)S(1)}, f32[8,640]{1,0:T(8,128)S(1)}) custom-call(bf16[128,5120]{1,0:T(8,128)(2,1)S(1)} %bitcast.6, f32[8,640]{1,0:T(8,128)S(1)} %get-tuple-element.55.sums_ref, f32[8,640]{1,0:T(8,128)S(1)} %collective-permute-done.other_ref, bf16[128,5888]{1,0:T(8,128)(2,1)S(1)} %get-tuple-element.78.dspat_ref, ...), custom_call_target="tpu_custom_call" | custom-call | flops 12000000000 | tf_op jit(solution)/shard_map/pallas_call | solution.py:770
  62.5 0.1 convert_add_fusion.refs_0_
  62.6 0.2 shard_map.75
  62.8 1.1 %collective-permute-start.20 = (bf16[304,128]{1,0:T(8,128)(2,1)S(1)}, bf16[304,128]{1,0:T(8,128)(2,1)S(1)}, u32[]{:S(2)}, u32[]{:S(2)}) collective-permute-start(bf16[304,128]{1,0:T(8,128)(2,1)S(1)} %get-tuple-element.85), channel_id=1, source_target_pairs={{0,2},{1,9},{2,0},{3,11},{4,6},{5,13},{6,4},{7,15},{8,10},{9,1},{1... | collective-permute-start | bytes 233480 | tf_op jit(solution)/shard_map/ppermute | solution.py:577
  64.0 1.0 %collective-permute-start.21 = (bf16[304,128]{1,0:T(8,128)(2,1)S(1)}, bf16[304,128]{1,0:T(8,128)(2,1)S(1)}, u32[]{:S(2)}, u32[]{:S(2)}) collective-permute-start(bf16[304,128]{1,0:T(8,128)(2,1)S(1)} %get-tuple-element.86), channel_id=1, source_target_pairs={{0,4},{1,17},{2,6},{3,19},{4,0},{5,21},{6,2},{7,23},{8,12},{9,25},... | collective-permute-start | bytes 233480 | tf_op jit(solution)/shard_map/ppermute | solution.py:577
  65.0 2.3 %collective-permute-start.22 = (bf16[304,128]{1,0:T(8,128)(2,1)S(1)}, bf16[304,128]{1,0:T(8,128)(2,1)S(1)}, u32[]{:S(2)}, u32[]{:S(2)}) collective-permute-start(bf16[304,128]{1,0:T(8,128)(2,1)S(1)} %get-tuple-element.87), channel_id=1, source_target_pairs={{0,6},{1,25},{2,4},{3,27},{4,2},{5,29},{6,0},{7,31},{8,14},{9,17},... | collective-permute-start | bytes 233480 | tf_op jit(solution)/shard_map/ppermute | solution.py:577
  67.3 0.5 collective-permute-start.23
  67.8 0.8 collective-permute-done.23.theirs_ref
  68.7 1.5 %collective-permute-done.21 = bf16[304,128]{1,0:T(8,128)(2,1)S(1)} collective-permute-done((bf16[304,128]{1,0:T(8,128)(2,1)S(1)}, bf16[304,128]{1,0:T(8,128)(2,1)S(1)}, u32[]{:S(2)}, u32[]{:S(2)}) %collective-permute-start.21) | collective-permute-done | bytes 77856 | tf_op jit(solution)/shard_map/ppermute | solution.py:577
  70.1 1.2 %collective-permute-done.22 = bf16[304,128]{1,0:T(8,128)(2,1)S(1)} collective-permute-done((bf16[304,128]{1,0:T(8,128)(2,1)S(1)}, bf16[304,128]{1,0:T(8,128)(2,1)S(1)}, u32[]{:S(2)}, u32[]{:S(2)}) %collective-permute-start.22) | collective-permute-done | bytes 77856 | tf_op jit(solution)/shard_map/ppermute | solution.py:577
  71.3 2.3 %collective-permute-start.26 = (bf16[304,128]{1,0:T(8,128)(2,1)S(1)}, bf16[304,128]{1,0:T(8,128)(2,1)S(1)}, u32[]{:S(2)}, u32[]{:S(2)}) collective-permute-start(bf16[304,128]{1,0:T(8,128)(2,1)S(1)} %add_convert_fusion.3.refs_0_), channel_id=1, source_target_pairs={{0,6},{1,25},{2,4},{3,27},{4,2},{5,29},{6,0},{7,31},{8,14},{9,17},... | collective-permute-start | bytes 233480 | tf_op jit(solution)/shard_map/ppermute | solution.py:577
  73.6 0.6 collective-permute-start.25
  74.2 1.6 %collective-permute-start.24 = (bf16[304,128]{1,0:T(8,128)(2,1)S(1)}, bf16[304,128]{1,0:T(8,128)(2,1)S(1)}, u32[]{:S(2)}, u32[]{:S(2)}) collective-permute-start(bf16[304,128]{1,0:T(8,128)(2,1)S(1)} %add_convert_fusion.3.refs_0_), channel_id=1, source_target_pairs={{0,2},{1,9},{2,0},{3,11},{4,6},{5,13},{6,4},{7,15},{8,10},{9,1},{1... | collective-permute-start | bytes 233480 | tf_op jit(solution)/shard_map/ppermute | solution.py:577
  75.8 1.8 %collective-permute-done.26.refs_3_ = bf16[304,128]{1,0:T(8,128)(2,1)S(1)} collective-permute-done((bf16[304,128]{1,0:T(8,128)(2,1)S(1)}, bf16[304,128]{1,0:T(8,128)(2,1)S(1)}, u32[]{:S(2)}, u32[]{:S(2)}) %collective-permute-start.26) | collective-permute-done | bytes 77856 | tf_op jit(solution)/shard_map/ppermute | solution.py:577
  77.6 1.8 %collective-permute-done.25.refs_2_ = bf16[304,128]{1,0:T(8,128)(2,1)S(1)} collective-permute-done((bf16[304,128]{1,0:T(8,128)(2,1)S(1)}, bf16[304,128]{1,0:T(8,128)(2,1)S(1)}, u32[]{:S(2)}, u32[]{:S(2)}) %collective-permute-start.25) | collective-permute-done | bytes 77856 | tf_op jit(solution)/shard_map/ppermute | solution.py:577
  79.4 1.6 %collective-permute-start.28 = (bf16[1216,128]{1,0:T(8,128)(2,1)S(1)}, bf16[1216,128]{1,0:T(8,128)(2,1)S(1)}, u32[]{:S(2)}, u32[]{:S(2)}) collective-permute-start(bf16[1216,128]{1,0:T(8,128)(2,1)S(1)} %shard_map.76.refs_0_), channel_id=1, source_target_pairs={{0,16},{1,5},{2,18},{3,7},{4,20},{5,1},{6,22},{7,3},{8,24},{9,13},... | collective-permute-start | bytes 933896 | tf_op jit(solution)/shard_map/ppermute | solution.py:577
  81.0 1.5 %collective-permute-start.27 = (bf16[1216,128]{1,0:T(8,128)(2,1)S(1)}, bf16[1216,128]{1,0:T(8,128)(2,1)S(1)}, u32[]{:S(2)}, u32[]{:S(2)}) collective-permute-start(bf16[1216,128]{1,0:T(8,128)(2,1)S(1)} %shard_map.76.refs_0_), channel_id=1, source_target_pairs={{0,8},{1,3},{2,10},{3,1},{4,12},{5,7},{6,14},{7,5},{8,0},{9,11},{1... | collective-permute-start | bytes 933896 | tf_op jit(solution)/shard_map/ppermute | solution.py:577
  82.5 3.7 %shard_map.77 = f32[128,5120]{1,0:T(8,128)} custom-call(bf16[128,5120]{1,0:T(8,128)(2,1)S(1)} %bitcast.7, f32[8,640]{1,0:T(8,128)S(1)} %get-tuple-element.55.sums_ref, f32[8,640]{1,0:T(8,128)S(1)} %collective-permute-done.other_ref, bf16[128,5120]{1,0:T(8,128)(2,1)S(1)} %bitcast.13, bf16[128,5120]{1,0:T(8,128)(2,1)S(1)} %get-tuple-element.93.dtemp_ref, ...), custom_call_target="tpu_custom_call" | custom-call | flops 4000000000 | tf_op jit(solution)/shard_map/pallas_call | solution.py:781
  86.2 0.1 collective-permute-done.28.refs_4_
  86.4 1.5 %collective-permute-done.27.refs_2_ = bf16[1216,128]{1,0:T(8,128)(2,1)S(1)} collective-permute-done((bf16[1216,128]{1,0:T(8,128)(2,1)S(1)}, bf16[1216,128]{1,0:T(8,128)(2,1)S(1)}, u32[]{:S(2)}, u32[]{:S(2)}) %collective-permute-start.27) | collective-permute-done | bytes 311328 | tf_op jit(solution)/shard_map/ppermute | solution.py:577
  87.9 0.5 collective-permute-start.31
  88.4 1.5 %collective-permute-start.29 = (bf16[1216,128]{1,0:T(8,128)(2,1)S(1)}, bf16[1216,128]{1,0:T(8,128)(2,1)S(1)}, u32[]{:S(2)}, u32[]{:S(2)}) collective-permute-start(bf16[1216,128]{1,0:T(8,128)(2,1)S(1)} %collective-permute-done.28.refs_4_), channel_id=1, source_target_pairs={{0,8},{1,3},{2,10},{3,1},{4,12},{5,7},{6,14},{7,5},{8,0},{9,11},{1... | collective-permute-start | bytes 933896 | tf_op jit(solution)/shard_map/ppermute | solution.py:577
  90.0 0.4 collective-permute-done.32.refs_5_
  90.4 2.4 %shard_map.78 = (f32[3,960,320]{2,1,0:T(8,128)}, f32[3,320,320]{2,1,0:T(8,128)}) custom-call(bf16[1216,128]{1,0:T(8,128)(2,1)S(1)} %shard_map.76.refs_0_, bf16[1216,128]{1,0:T(8,128)(2,1)S(1)} %collective-permute-done.30.refs_1_, bf16[1216,128]{1,0:T(8,128)(2,1)S(1)} %collective-permute-done.27.refs_2_, ...), custom_call_target="tpu_custom_call" | custom-call | flops 1000 | bytes 1000 | tf_op jit(solution)/shard_map/pallas_call | solution.py:625
  92.8 2.6 %collective-permute-done.29.refs_0_ = bf16[1216,128]{1,0:T(8,128)(2,1)S(1)} collective-permute-done((bf16[1216,128]{1,0:T(8,128)(2,1)S(1)}, bf16[1216,128]{1,0:T(8,128)(2,1)S(1)}, u32[]{:S(2)}, u32[]{:S(2)}) %collective-permute-start.29) | collective-permute-done | bytes 311328 | tf_op jit(solution)/shard_map/ppermute | solution.py:577
  95.3 1.6 %collective-permute-done.33.refs_1_ = bf16[1216,128]{1,0:T(8,128)(2,1)S(1)} collective-permute-done((bf16[1216,128]{1,0:T(8,128)(2,1)S(1)}, bf16[1216,128]{1,0:T(8,128)(2,1)S(1)}, u32[]{:S(2)}, u32[]{:S(2)}) %collective-permute-start.33) | collective-permute-done | bytes 311328 | tf_op jit(solution)/shard_map/ppermute | solution.py:639
  97.0 1.3 %shard_map.79 = (f32[3,960,320]{2,1,0:T(8,128)}, f32[3,320,320]{2,1,0:T(8,128)}) custom-call(bf16[1216,128]{1,0:T(8,128)(2,1)S(1)} %collective-permute-done.29.refs_0_, bf16[1216,128]{1,0:T(8,128)(2,1)S(1)} %collective-permute-done.33.refs_1_, f32[3,960,320]{2,1,0:T(8,128)} %get-tuple-element.103.refs_2_, ...), custom_call_target="tpu_custom_call", output_to_operand_aliasing={{0}: (2, {}), {1}: (3, {})} | custom-call | flops 1000 | bytes 1000 | tf_op jit(solution)/shard_map/pallas_call | solution.py:625
  (34 shorter events, 0.2 us)
Async XLA Ops:
  0.6 1.3 %copy-start.1 = (bf16[1,4,32,5120]{3,2,1,0:T(8,128)(2,1)S(1)}, bf16[1,4,32,5120]{3,2,1,0:T(8,128)(2,1)}, u32[]{:S(2)}) copy-start(bf16[1,4,32,5120]{3,2,1,0:T(8,128)(2,1)} %param.4) | copy-start | bytes 3932164
  1.9 1.3 %copy-start.3 = (bf16[1,4,32,5120]{3,2,1,0:T(8,128)(2,1)S(1)}, bf16[1,4,32,5120]{3,2,1,0:T(8,128)(2,1)}, u32[]{:S(2)}) copy-start(bf16[1,4,32,5120]{3,2,1,0:T(8,128)(2,1)} %param.7) | copy-start | bytes 3932164
  2.6 4.8 %collective-permute-start = (f32[8,640]{1,0:T(8,128)S(1)}, f32[8,640]{1,0:T(8,128)S(1)}, u32[]{:S(2)}, u32[]{:S(2)}) collective-permute-start(f32[8,640]{1,0:T(8,128)S(1)} %get-tuple-element.55.sums_ref), channel_id=1, source_target_pairs={{0,1},{1,0},{2,3},{3,2},{4,5},{5,4},{6,7},{7,6},{8,9},{9,8},{10,11... | collective-permute-start | bytes 61448 | tf_op jit(solution)/shard_map/ppermute | solution.py:639
  3.1 4.3 %collective-permute-start.1 = (bf16[128,384]{1,0:T(8,128)(2,1)S(1)}, bf16[128,384]{1,0:T(8,128)(2,1)S(1)}, u32[]{:S(2)}, u32[]{:S(2)}) collective-permute-start(bf16[128,384]{1,0:T(8,128)(2,1)S(1)} %get-tuple-element.56), channel_id=1, source_target_pairs={{0,1},{1,0},{2,3},{3,2},{4,5},{5,4},{6,7},{7,6},{8,9},{9,8},{10,11... | collective-permute-start | bytes 294920 | tf_op jit(solution)/shard_map/ppermute | solution.py:639
  3.3 4.2 %copy-start = (bf16[3,3,320,320]{3,2,1,0:T(8,128)(2,1)S(1)}, bf16[3,3,320,320]{3,2,1,0:T(8,128)(2,1)}, u32[]{:S(2)}) copy-start(bf16[3,3,320,320]{3,2,1,0:T(8,128)(2,1)} %kernel_ref.5) | copy-start | bytes 5529604
  3.3 4.2 %copy-start.2 = (bf16[1,4,32,5120]{3,2,1,0:T(8,128)(2,1)S(1)}, bf16[1,4,32,5120]{3,2,1,0:T(8,128)(2,1)}, u32[]{:S(2)}) copy-start(bf16[1,4,32,5120]{3,2,1,0:T(8,128)(2,1)} %param.4) | copy-start | bytes 3932164
  3.5 20.0 %collective-permute-start.2 = (bf16[32,5120]{1,0:T(8,128)(2,1)S(1)}, bf16[32,5120]{1,0:T(8,128)(2,1)S(1)}, u32[]{:S(2)}, u32[]{:S(2)}) collective-permute-start(bf16[32,5120]{1,0:T(8,128)(2,1)S(1)} %get-tuple-element.58), channel_id=1, source_target_pairs={{0,2},{2,0},{4,6},{6,4},{1,3},{3,1},{5,7},{7,5},{8,10},{10,8},{12,... | collective-permute-start | bytes 983048 | tf_op jit(solution)/shard_map/ppermute | solution.py:325
  6.6 16.9 %copy-start.4 = (bf16[3,320,320]{2,1,0:T(8,128)(2,1)S(1)}, bf16[3,320,320]{2,1,0:T(8,128)(2,1)}, u32[]{:S(2)}) copy-start(bf16[3,320,320]{2,1,0:T(8,128)(2,1)} %kernel_ref.4) | copy-start | bytes 1843204
  6.6 16.9 %collective-permute-start.3 = (bf16[32,5120]{1,0:T(8,128)(2,1)S(1)}, bf16[32,5120]{1,0:T(8,128)(2,1)S(1)}, u32[]{:S(2)}, u32[]{:S(2)}) collective-permute-start(bf16[32,5120]{1,0:T(8,128)(2,1)S(1)} %get-tuple-element.59), channel_id=1, source_target_pairs={{2,4},{4,2},{3,5},{5,3},{10,12},{12,10},{11,13},{13,11},{18,20},{2... | collective-permute-start | bytes 983048 | tf_op jit(solution)/shard_map/ppermute | solution.py:325
  16.4 1.3 %collective-permute-start.4 = (f32[8,640]{1,0:T(8,128)S(1)}, f32[8,640]{1,0:T(8,128)S(1)}, u32[]{:S(2)}, u32[]{:S(2)}) collective-permute-start(f32[8,640]{1,0:T(8,128)S(1)} %get-tuple-element.60), channel_id=1, source_target_pairs={{0,1},{1,0},{2,3},{3,2},{4,5},{5,4},{6,7},{7,6},{8,9},{9,8},{10,11... | collective-permute-start | bytes 61448 | tf_op jit(solution)/shard_map/ppermute | solution.py:639
  17.6 9.1 %collective-permute-start.7 = (f32[8,640]{1,0:T(8,128)S(1)}, f32[8,640]{1,0:T(8,128)S(1)}, u32[]{:S(2)}, u32[]{:S(2)}) collective-permute-start(f32[8,640]{1,0:T(8,128)S(1)} %add.27.refs_0_), channel_id=1, source_target_pairs={{0,6},{2,4},{4,2},{6,0},{1,7},{3,5},{5,3},{7,1},{8,14},{10,12},{12... | collective-permute-start | bytes 61448 | tf_op jit(solution)/shard_map/ppermute | solution.py:639
  20.5 6.3 %collective-permute-start.6 = (f32[8,640]{1,0:T(8,128)S(1)}, f32[8,640]{1,0:T(8,128)S(1)}, u32[]{:S(2)}, u32[]{:S(2)}) collective-permute-start(f32[8,640]{1,0:T(8,128)S(1)} %add.27.refs_0_), channel_id=1, source_target_pairs={{0,4},{2,6},{4,0},{6,2},{1,5},{3,7},{5,1},{7,3},{8,12},{10,14},{12... | collective-permute-start | bytes 61448 | tf_op jit(solution)/shard_map/ppermute | solution.py:639
  23.5 3.8 %collective-permute-start.5 = (f32[8,640]{1,0:T(8,128)S(1)}, f32[8,640]{1,0:T(8,128)S(1)}, u32[]{:S(2)}, u32[]{:S(2)}) collective-permute-start(f32[8,640]{1,0:T(8,128)S(1)} %add.27.refs_0_), channel_id=1, source_target_pairs={{0,2},{2,0},{4,6},{6,4},{1,3},{3,1},{5,7},{7,5},{8,10},{10,8},{12,... | collective-permute-start | bytes 61448 | tf_op jit(solution)/shard_map/ppermute | solution.py:639
  29.7 9.2 %collective-permute-start.8 = (f32[384,384]{1,0:T(8,128)S(1)}, f32[384,384]{1,0:T(8,128)S(1)}, u32[]{:S(2)}, u32[]{:S(2)}) collective-permute-start(f32[384,384]{1,0:T(8,128)S(1)} %get-tuple-element.62), channel_id=1, source_target_pairs={{0,1},{1,0},{2,3},{3,2},{4,5},{5,4},{6,7},{7,6},{8,9},{9,8},{10,11... | collective-permute-start | bytes 1769480 | tf_op jit(solution)/shard_map/ppermute | solution.py:639
  29.8 2.0 %collective-permute-start.9 = (f32[8,640]{1,0:T(8,128)S(1)}, f32[8,640]{1,0:T(8,128)S(1)}, u32[]{:S(2)}, u32[]{:S(2)}) collective-permute-start(f32[8,640]{1,0:T(8,128)S(1)} %get-tuple-element.65), channel_id=1, source_target_pairs={{0,1},{1,0},{2,3},{3,2},{4,5},{5,4},{6,7},{7,6},{8,9},{9,8},{10,11... | collective-permute-start | bytes 61448 | tf_op jit(solution)/shard_map/ppermute | solution.py:639
  31.8 7.1 %collective-permute-start.12 = (f32[8,640]{1,0:T(8,128)S(1)}, f32[8,640]{1,0:T(8,128)S(1)}, u32[]{:S(2)}, u32[]{:S(2)}) collective-permute-start(f32[8,640]{1,0:T(8,128)S(1)} %add.28.refs_4_), channel_id=1, source_target_pairs={{0,6},{2,4},{4,2},{6,0},{1,7},{3,5},{5,3},{7,1},{8,14},{10,12},{12... | collective-permute-start | bytes 61448 | tf_op jit(solution)/shard_map/ppermute | solution.py:639
  32.8 6.1 %collective-permute-start.11 = (f32[8,640]{1,0:T(8,128)S(1)}, f32[8,640]{1,0:T(8,128)S(1)}, u32[]{:S(2)}, u32[]{:S(2)}) collective-permute-start(f32[8,640]{1,0:T(8,128)S(1)} %add.28.refs_4_), channel_id=1, source_target_pairs={{0,4},{2,6},{4,0},{6,2},{1,5},{3,7},{5,1},{7,3},{8,12},{10,14},{12... | collective-permute-start | bytes 61448 | tf_op jit(solution)/shard_map/ppermute | solution.py:639
  34.8 4.0 %collective-permute-start.10 = (f32[8,640]{1,0:T(8,128)S(1)}, f32[8,640]{1,0:T(8,128)S(1)}, u32[]{:S(2)}, u32[]{:S(2)}) collective-permute-start(f32[8,640]{1,0:T(8,128)S(1)} %add.28.refs_4_), channel_id=1, source_target_pairs={{0,2},{2,0},{4,6},{6,4},{1,3},{3,1},{5,7},{7,5},{8,10},{10,8},{12,... | collective-permute-start | bytes 61448 | tf_op jit(solution)/shard_map/ppermute | solution.py:639
  47.5 1.7 %collective-permute-start.14 = (bf16[1216,128]{1,0:T(8,128)(2,1)S(1)}, bf16[1216,128]{1,0:T(8,128)(2,1)S(1)}, u32[]{:S(2)}, u32[]{:S(2)}) collective-permute-start(bf16[1216,128]{1,0:T(8,128)(2,1)S(1)} %get-tuple-element.69), channel_id=1, source_target_pairs={{0,1},{1,0},{2,3},{3,2},{4,5},{5,4},{6,7},{7,6},{8,9},{9,8},{10,11... | collective-permute-start | bytes 933896 | tf_op jit(solution)/shard_map/ppermute | solution.py:639
  47.6 15.0 %collective-permute-start.13 = (bf16[1216,128]{1,0:T(8,128)(2,1)S(1)}, bf16[1216,128]{1,0:T(8,128)(2,1)S(1)}, u32[]{:S(2)}, u32[]{:S(2)}) collective-permute-start(bf16[1216,128]{1,0:T(8,128)(2,1)S(1)} %get-tuple-element.67), channel_id=1, source_target_pairs={{0,1},{1,0},{2,3},{3,2},{4,5},{5,4},{6,7},{7,6},{8,9},{9,8},{10,11... | collective-permute-start | bytes 933896 | tf_op jit(solution)/shard_map/ppermute | solution.py:639
  48.1 2.0 %collective-permute-start.15 = (bf16[1216,128]{1,0:T(8,128)(2,1)S(1)}, bf16[1216,128]{1,0:T(8,128)(2,1)S(1)}, u32[]{:S(2)}, u32[]{:S(2)}) collective-permute-start(bf16[1216,128]{1,0:T(8,128)(2,1)S(1)} %get-tuple-element.71), channel_id=1, source_target_pairs={{0,1},{1,0},{2,3},{3,2},{4,5},{5,4},{6,7},{7,6},{8,9},{9,8},{10,11... | collective-permute-start | bytes 933896 | tf_op jit(solution)/shard_map/ppermute | solution.py:639
  48.1 2.4 %collective-permute-start.16 = (bf16[1216,128]{1,0:T(8,128)(2,1)S(1)}, bf16[1216,128]{1,0:T(8,128)(2,1)S(1)}, u32[]{:S(2)}, u32[]{:S(2)}) collective-permute-start(bf16[1216,128]{1,0:T(8,128)(2,1)S(1)} %get-tuple-element.73), channel_id=1, source_target_pairs={{0,1},{1,0},{2,3},{3,2},{4,5},{5,4},{6,7},{7,6},{8,9},{9,8},{10,11... | collective-permute-start | bytes 933896 | tf_op jit(solution)/shard_map/ppermute | solution.py:639
  50.6 12.0 %collective-permute-start.17 = (bf16[1216,128]{1,0:T(8,128)(2,1)S(1)}, bf16[1216,128]{1,0:T(8,128)(2,1)S(1)}, u32[]{:S(2)}, u32[]{:S(2)}) collective-permute-start(bf16[1216,128]{1,0:T(8,128)(2,1)S(1)} %add_convert_fusion.2), channel_id=1, source_target_pairs={{0,8},{1,3},{2,10},{3,1},{4,12},{5,7},{6,14},{7,5},{8,0},{9,11},{1... | collective-permute-start | bytes 933896 | tf_op jit(solution)/shard_map/ppermute | solution.py:577
  52.2 10.5 %collective-permute-start.18 = (bf16[1216,128]{1,0:T(8,128)(2,1)S(1)}, bf16[1216,128]{1,0:T(8,128)(2,1)S(1)}, u32[]{:S(2)}, u32[]{:S(2)}) collective-permute-start(bf16[1216,128]{1,0:T(8,128)(2,1)S(1)} %add_convert_fusion.1), channel_id=1, source_target_pairs={{0,16},{1,5},{2,18},{3,7},{4,20},{5,1},{6,22},{7,3},{8,24},{9,13},... | collective-permute-start | bytes 933896 | tf_op jit(solution)/shard_map/ppermute | solution.py:577
  53.7 9.0 %collective-permute-start.19 = (bf16[1216,128]{1,0:T(8,128)(2,1)S(1)}, bf16[1216,128]{1,0:T(8,128)(2,1)S(1)}, u32[]{:S(2)}, u32[]{:S(2)}) collective-permute-start(bf16[1216,128]{1,0:T(8,128)(2,1)S(1)} %add_convert_fusion), channel_id=1, source_target_pairs={{0,24},{1,7},{2,26},{3,5},{4,28},{5,3},{6,30},{7,1},{8,16},{9,15},... | collective-permute-start | bytes 933896 | tf_op jit(solution)/shard_map/ppermute | solution.py:577
  62.8 5.8 %collective-permute-start.20 = (bf16[304,128]{1,0:T(8,128)(2,1)S(1)}, bf16[304,128]{1,0:T(8,128)(2,1)S(1)}, u32[]{:S(2)}, u32[]{:S(2)}) collective-permute-start(bf16[304,128]{1,0:T(8,128)(2,1)S(1)} %get-tuple-element.85), channel_id=1, source_target_pairs={{0,2},{1,9},{2,0},{3,11},{4,6},{5,13},{6,4},{7,15},{8,10},{9,1},{1... | collective-permute-start | bytes 233480 | tf_op jit(solution)/shard_map/ppermute | solution.py:577
  64.0 6.2 %collective-permute-start.21 = (bf16[304,128]{1,0:T(8,128)(2,1)S(1)}, bf16[304,128]{1,0:T(8,128)(2,1)S(1)}, u32[]{:S(2)}, u32[]{:S(2)}) collective-permute-start(bf16[304,128]{1,0:T(8,128)(2,1)S(1)} %get-tuple-element.86), channel_id=1, source_target_pairs={{0,4},{1,17},{2,6},{3,19},{4,0},{5,21},{6,2},{7,23},{8,12},{9,25},... | collective-permute-start | bytes 233480 | tf_op jit(solution)/shard_map/ppermute | solution.py:577
  65.0 6.3 %collective-permute-start.22 = (bf16[304,128]{1,0:T(8,128)(2,1)S(1)}, bf16[304,128]{1,0:T(8,128)(2,1)S(1)}, u32[]{:S(2)}, u32[]{:S(2)}) collective-permute-start(bf16[304,128]{1,0:T(8,128)(2,1)S(1)} %get-tuple-element.87), channel_id=1, source_target_pairs={{0,6},{1,25},{2,4},{3,27},{4,2},{5,29},{6,0},{7,31},{8,14},{9,17},... | collective-permute-start | bytes 233480 | tf_op jit(solution)/shard_map/ppermute | solution.py:577
  67.3 1.4 %collective-permute-start.23 = (f32[8,640]{1,0:T(8,128)S(1)}, f32[8,640]{1,0:T(8,128)S(1)}, u32[]{:S(2)}, u32[]{:S(2)}) collective-permute-start(f32[8,640]{1,0:T(8,128)S(1)} %get-tuple-element.88.mine_ref), channel_id=1, source_target_pairs={{0,1},{1,0},{2,3},{3,2},{4,5},{5,4},{6,7},{7,6},{8,9},{9,8},{10,11... | collective-permute-start | bytes 61448 | tf_op jit(solution)/shard_map/ppermute | solution.py:639
  71.3 6.3 %collective-permute-start.26 = (bf16[304,128]{1,0:T(8,128)(2,1)S(1)}, bf16[304,128]{1,0:T(8,128)(2,1)S(1)}, u32[]{:S(2)}, u32[]{:S(2)}) collective-permute-start(bf16[304,128]{1,0:T(8,128)(2,1)S(1)} %add_convert_fusion.3.refs_0_), channel_id=1, source_target_pairs={{0,6},{1,25},{2,4},{3,27},{4,2},{5,29},{6,0},{7,31},{8,14},{9,17},... | collective-permute-start | bytes 233480 | tf_op jit(solution)/shard_map/ppermute | solution.py:577
  73.6 5.8 %collective-permute-start.25 = (bf16[304,128]{1,0:T(8,128)(2,1)S(1)}, bf16[304,128]{1,0:T(8,128)(2,1)S(1)}, u32[]{:S(2)}, u32[]{:S(2)}) collective-permute-start(bf16[304,128]{1,0:T(8,128)(2,1)S(1)} %add_convert_fusion.3.refs_0_), channel_id=1, source_target_pairs={{0,4},{1,17},{2,6},{3,19},{4,0},{5,21},{6,2},{7,23},{8,12},{9,25},... | collective-permute-start | bytes 233480 | tf_op jit(solution)/shard_map/ppermute | solution.py:577
  74.2 5.2 %collective-permute-start.24 = (bf16[304,128]{1,0:T(8,128)(2,1)S(1)}, bf16[304,128]{1,0:T(8,128)(2,1)S(1)}, u32[]{:S(2)}, u32[]{:S(2)}) collective-permute-start(bf16[304,128]{1,0:T(8,128)(2,1)S(1)} %add_convert_fusion.3.refs_0_), channel_id=1, source_target_pairs={{0,2},{1,9},{2,0},{3,11},{4,6},{5,13},{6,4},{7,15},{8,10},{9,1},{1... | collective-permute-start | bytes 233480 | tf_op jit(solution)/shard_map/ppermute | solution.py:577
  79.4 7.0 %collective-permute-start.28 = (bf16[1216,128]{1,0:T(8,128)(2,1)S(1)}, bf16[1216,128]{1,0:T(8,128)(2,1)S(1)}, u32[]{:S(2)}, u32[]{:S(2)}) collective-permute-start(bf16[1216,128]{1,0:T(8,128)(2,1)S(1)} %shard_map.76.refs_0_), channel_id=1, source_target_pairs={{0,16},{1,5},{2,18},{3,7},{4,20},{5,1},{6,22},{7,3},{8,24},{9,13},... | collective-permute-start | bytes 933896 | tf_op jit(solution)/shard_map/ppermute | solution.py:577
  81.0 6.9 %collective-permute-start.27 = (bf16[1216,128]{1,0:T(8,128)(2,1)S(1)}, bf16[1216,128]{1,0:T(8,128)(2,1)S(1)}, u32[]{:S(2)}, u32[]{:S(2)}) collective-permute-start(bf16[1216,128]{1,0:T(8,128)(2,1)S(1)} %shard_map.76.refs_0_), channel_id=1, source_target_pairs={{0,8},{1,3},{2,10},{3,1},{4,12},{5,7},{6,14},{7,5},{8,0},{9,11},{1... | collective-permute-start | bytes 933896 | tf_op jit(solution)/shard_map/ppermute | solution.py:577
  87.9 2.0 %collective-permute-start.30 = (bf16[1216,128]{1,0:T(8,128)(2,1)S(1)}, bf16[1216,128]{1,0:T(8,128)(2,1)S(1)}, u32[]{:S(2)}, u32[]{:S(2)}) collective-permute-start(bf16[1216,128]{1,0:T(8,128)(2,1)S(1)} %shard_map.76.refs_0_), channel_id=1, source_target_pairs={{0,1},{1,0},{2,3},{3,2},{4,5},{5,4},{6,7},{7,6},{8,9},{9,8},{10,11... | collective-permute-start | bytes 933896 | tf_op jit(solution)/shard_map/ppermute | solution.py:639
  87.9 2.0 %collective-permute-start.31 = (bf16[1216,128]{1,0:T(8,128)(2,1)S(1)}, bf16[1216,128]{1,0:T(8,128)(2,1)S(1)}, u32[]{:S(2)}, u32[]{:S(2)}) collective-permute-start(bf16[1216,128]{1,0:T(8,128)(2,1)S(1)} %collective-permute-done.27.refs_2_), channel_id=1, source_target_pairs={{0,1},{1,0},{2,3},{3,2},{4,5},{5,4},{6,7},{7,6},{8,9},{9,8},{10,11... | collective-permute-start | bytes 933896 | tf_op jit(solution)/shard_map/ppermute | solution.py:639
  88.4 2.0 %collective-permute-start.32 = (bf16[1216,128]{1,0:T(8,128)(2,1)S(1)}, bf16[1216,128]{1,0:T(8,128)(2,1)S(1)}, u32[]{:S(2)}, u32[]{:S(2)}) collective-permute-start(bf16[1216,128]{1,0:T(8,128)(2,1)S(1)} %collective-permute-done.28.refs_4_), channel_id=1, source_target_pairs={{0,1},{1,0},{2,3},{3,2},{4,5},{5,4},{6,7},{7,6},{8,9},{9,8},{10,11... | collective-permute-start | bytes 933896 | tf_op jit(solution)/shard_map/ppermute | solution.py:639
  88.4 6.9 %collective-permute-start.29 = (bf16[1216,128]{1,0:T(8,128)(2,1)S(1)}, bf16[1216,128]{1,0:T(8,128)(2,1)S(1)}, u32[]{:S(2)}, u32[]{:S(2)}) collective-permute-start(bf16[1216,128]{1,0:T(8,128)(2,1)S(1)} %collective-permute-done.28.refs_4_), channel_id=1, source_target_pairs={{0,8},{1,3},{2,10},{3,1},{4,12},{5,7},{6,14},{7,5},{8,0},{9,11},{1... | collective-permute-start | bytes 933896 | tf_op jit(solution)/shard_map/ppermute | solution.py:577
  95.3 1.6 %collective-permute-start.33 = (bf16[1216,128]{1,0:T(8,128)(2,1)S(1)}, bf16[1216,128]{1,0:T(8,128)(2,1)S(1)}, u32[]{:S(2)}, u32[]{:S(2)}) collective-permute-start(bf16[1216,128]{1,0:T(8,128)(2,1)S(1)} %collective-permute-done.29.refs_0_), channel_id=1, source_target_pairs={{0,1},{1,0},{2,3},{3,2},{4,5},{5,4},{6,7},{7,6},{8,9},{9,8},{10,11... | collective-permute-start | bytes 933896 | tf_op jit(solution)/shard_map/ppermute | solution.py:639
